TPU v7x, 32 devices: a whole 2x2x4 slice. The times are simulated.
32 devices in a mesh: lists: 16 (over z, y, x), users: 2 (over core).
Axes of the slice: x: 2, y: 2, z: 4, core: 2. Of those that a mesh axis runs over, the one named last changes fastest.
Arguments:
- user_vectors: bfloat16 [64, 512], P('lists'), may hold values from -6 to 6
- probe_lists: int32 [64, 32], P('lists'), may hold values from 0 to 15, as said below
- list_items: bfloat16 [16, 4096, 512], P('lists', 'users'), may hold values from -6 to 6
- candidate_ids: int32 [16, 512], P('lists'), may hold values from 0 to 65535, as said below
- history: bfloat16 [16, 256, 512], P('lists', 'users'), may hold values from -6 to 6
- history_lengths: int32 [16], P('lists'), may hold values from 1 to 256, as said below
- query_weight: bfloat16 [512, 512], replicated, may hold values from -4 to 4
- key_value_weight: bfloat16 [512, 1024], replicated, may hold values from -4 to 4
- out_weight: bfloat16 [512, 512], replicated, may hold values from -3 to 3
Outputs:
- list_scores: bfloat16 [64, 32, 4096], P('lists', None, 'users')
- ranked: bfloat16 [16, 512, 512], P('lists', 'users')
Inputs may be any that keep to these rules, and one draw needn't show every extreme that they name: `probe_lists`: among the probes of the 4 users of one index of lists, no list occurs more than 24 times, and some list exactly 24 times. `candidate_ids`: item i lies in list i // 4096. Among the candidates of the 1 users of one index of lists, at most 48 lie in the same group of 1 lists (list) and the same group of 2048 slots (slot // 2048), and some such pair of groups holds exactly 48. `history_lengths`: the first ranked user has 256 valid events.
All inputs are finite; a program needn't handle non-finite values.
Results may differ from a plain program's by a relative error of at most 0.018.
Values may be sent and summed in bfloat16 or wider, within the bound.
No kernel may reach another device: no remote copies, remote signals or barrier semaphores. Data moves between devices by JAX's collectives and lax.ppermute only.
A program may use at most 128 MiB of HBM per device.

v0:
```python
import jax
import jax.numpy as jnp
from jax import lax
from jax.sharding import PartitionSpec as P

HEADS = 8


def merged(value, axis, join):
    pieces = jax.tree.map(lambda part: lax.all_gather(part, axis), value)
    head = jax.tree.map(lambda part: part[0], pieces)
    tail = jax.tree.map(lambda part: part[1:], pieces)
    running, _ = lax.scan(lambda running, share: (join(running, share), None), head, tail)
    return running


def bucket_slots(bucket, keep, buckets, most):
    onehot = (bucket[:, None] == jnp.arange(buckets, dtype=jnp.int32)[None, :]).astype(
        jnp.int32
    ) * keep[:, None]
    before = jnp.cumsum(onehot, axis=0) - onehot
    return bucket * most + jnp.sum(before * onehot, axis=1)


def softmax_combine(first, second):
    top = jnp.maximum(first[0], second[0])
    left = jnp.exp(first[0] - top)
    right = jnp.exp(second[0] - top)
    return (
        top,
        first[1] * left + second[1] * right,
        first[2] * left[..., None] + second[2] * right[..., None],
    )


def shards(
    user_vectors,
    probe_lists,
    list_items,
    candidate_ids,
    history,
    history_lengths,
    query_weight,
    key_value_weight,
    out_weight,
):
    n_lists = lax.axis_size("lists")
    n_users = lax.axis_size("users")
    list_dev, items_loc, width = list_items.shape
    user_dev, probes = probe_lists.shape
    total_lists = list_dev * n_lists
    cap_lists = max(2, 3 * user_dev * probes // total_lists)
    scale = width ** (-0.5)
    flat_probes = probe_lists.reshape(-1)
    all_ones = jnp.ones(flat_probes.shape, jnp.int32)
    probe_slot = bucket_slots(flat_probes, all_ones, total_lists, cap_lists)
    repeated = jnp.repeat(user_vectors, probes, axis=0)
    outgoing = (
        jnp.zeros((total_lists * cap_lists, width), jnp.bfloat16).at[probe_slot].set(repeated)
    )
    outgoing = outgoing.reshape(n_lists, list_dev, cap_lists, width)
    scores = jnp.einsum(
        "skcd,kjd->skcj",
        lax.all_to_all(outgoing, "lists", split_axis=0, concat_axis=0, tiled=True),
        list_items,
        preferred_element_type=jnp.float32,
    )
    scores = (scores * scale).astype(jnp.bfloat16)
    returned = lax.all_to_all(scores, "lists", split_axis=0, concat_axis=0, tiled=True)
    returned = returned.reshape(total_lists * cap_lists, items_loc)
    list_scores = returned[probe_slot].reshape(user_dev, probes, items_loc)
    rank_dev, cands = candidate_ids.shape
    grouped = rank_dev * cands
    items_list = items_loc * n_users
    cap_rows = max(2, 3 * grouped // (n_lists * n_users))
    flat_ids = candidate_ids.reshape(-1)
    list_of = flat_ids // items_list
    slot_of = flat_ids % items_list
    owner_row = list_of // list_dev
    owner_col = slot_of // items_loc
    local_index = list_of % list_dev * items_loc + slot_of % items_loc
    flat_items = list_items.reshape(list_dev * items_loc, width)
    column = lax.axis_index("users")
    keep = (owner_col == column).astype(jnp.int32)
    row_slot = bucket_slots(owner_row, keep, n_lists, cap_rows)
    dump = n_lists * cap_rows
    request = (
        jnp.zeros((dump + 1,), jnp.int32).at[jnp.where(keep == 1, row_slot, dump)].set(local_index)
    )
    request = request[:dump].reshape(n_lists, cap_rows)
    fetched = lax.all_to_all(
        flat_items[lax.all_to_all(request, "lists", split_axis=0, concat_axis=0, tiled=True)],
        "lists",
        split_axis=0,
        concat_axis=0,
        tiled=True,
    )
    fetched = fetched.reshape(dump, width)
    mine = jnp.where(
        keep[:, None] == 1,
        fetched[jnp.minimum(row_slot, dump - 1)].astype(jnp.float32),
        jnp.float32(0.0),
    )
    cand_rows = lax.psum(mine.astype(jnp.bfloat16), "users")
    head_dim = width // HEADS
    hist_dev = history.shape[1]
    queries = (
        jnp.dot(cand_rows, query_weight, preferred_element_type=jnp.float32) * head_dim ** (-0.5)
    ).astype(jnp.bfloat16)
    queries = queries.reshape(rank_dev, cands, HEADS, head_dim)
    pairs = jnp.dot(
        history.reshape(-1, width), key_value_weight, preferred_element_type=jnp.float32
    ).astype(jnp.bfloat16)
    pairs = pairs.reshape(rank_dev, hist_dev, 2, HEADS, head_dim)
    positions = column * hist_dev + jnp.arange(hist_dev, dtype=jnp.int32)
    valid_events = positions[None, :] < history_lengths[:, None]

    def attend(packed):
        user_queries, user_pairs, valid = packed
        scores = jnp.einsum(
            "chd,ehd->che", user_queries, user_pairs[:, 0], preferred_element_type=jnp.float32
        )
        mask = valid[None, None, :]
        scores = jnp.where(mask, scores, jnp.float32(-1e30))
        top = jnp.max(scores, axis=-1)
        exponentials = jnp.where(mask, jnp.exp(scores - top[..., None]), jnp.float32(0.0))
        total = jnp.sum(exponentials, axis=-1)
        probs = exponentials.astype(jnp.bfloat16)
        mixed = jnp.einsum(
            "che,ehd->chd", probs, user_pairs[:, 1], preferred_element_type=jnp.float32
        )
        return (top, total, mixed)

    top, total, mixed = lax.map(attend, (queries, pairs, valid_events))
    own = cands // n_users
    top, total, mixed = merged((top, total, mixed), "users", softmax_combine)
    mixed = lax.dynamic_slice_in_dim(mixed, column * own, own, 1)
    total = lax.dynamic_slice_in_dim(total, column * own, own, 1)
    attended = (mixed / total[..., None]).reshape(rank_dev * own, width).astype(jnp.bfloat16)
    ranked = jnp.dot(attended, out_weight, preferred_element_type=jnp.float32).astype(jnp.bfloat16)
    return (list_scores, ranked.reshape(rank_dev, own, width))


def solution(mesh):
    placed = (
        P("lists", None),
        P("lists", None),
        P("lists", "users", None),
        P("lists", None),
        P("lists", "users", None),
        P("lists"),
        P(),
        P(),
        P(),
    )
    return jax.shard_map(
        shards,
        mesh=mesh,
        in_specs=placed,
        out_specs=(P("lists", None, "users"), P("lists", "users", None)),
        check_vma=False,
    )
```

profile of v0, /device:TPU:12, one launch (start us, length us, event | category | flops | bytes accessed | tf_op | source)
XLA Modules:
  0.0 128.9 jit_solution(7908107669680048828)
XLA Ops:
  7.2 0.8 add_select_fusion.4
  8.0 0.7 fusion.42
  8.7 0.7 broadcast_compare_fusion.1
  9.4 0.7 add_select_fusion
  10.1 1.2 reduce-window.6
  11.7 0.7 compare_select_fusion.1
  12.4 0.7 compare_select_fusion.2
  13.1 2.4 %scatter_custom_fusion.1 = s32[769]{0:T(1024)S(1)} fusion(s32[512]{0:T(512)S(1)} %bitcast.134, s32[512]{0:T(512)S(1)} %get-tuple-element.56, s32[]{:T(128)} %constant.129.clone.1), kind=kCustom, calls=%fused_computation.112 | custom fusion | bytes 3080 | tf_op jit(solution)/shard_map/scatter | solution.py:88
  15.6 12.0 %all_to_all.27 = s32[16,1,48]{2,1,0:T(1,128)S(1)} all-to-all(s32[16,1,48]{2,1,0:T(1,128)S(1)} %all_to_all.19), channel_id=1, replica_groups=mesh['lists'=16,'users'=2] {'lists'}, dimensions={0} | all-to-all | bytes 6144 | tf_op jit(solution)/shard_map/all_to_all | solution.py:92
  27.7 3.3 %gather_fusion.1 = bf16[768,512]{1,0:T(8,128)(2,1)} fusion(bf16[2048,512]{1,0:T(8,128)(2,1)S(1)} %bitcast.117, s32[1024]{0:T(1024)S(1)} %pad_clamp_fusion.1), kind=kCustom, calls=%fused_computation.1 | custom fusion | bytes 1575936 | tf_op jit(solution)/shard_map/gather | solution.py:92
  31.1 5.8 %all-to-all-start.3 = ((bf16[16,48,512]{2,1,0:T(8,128)(2,1)}), bf16[16,48,512]{2,1,0:T(8,128)(2,1)S(1)}, u32[]{:S(2)}, u32[]{:S(2)}) async-start(bf16[16,48,512]{2,1,0:T(8,128)(2,1)} %bitcast.119), calls=%async_computation.3 | async-start | bytes 1572864 | tf_op jit(solution)/shard_map/all_to_all | solution.py:91
  37.5 1.8 %scatter_custom_fusion = bf16[384,512]{1,0:T(8,128)(2,1)} fusion(s32[128]{0:T(128)S(1)} %fusion.44, bf16[128,512]{1,0:T(8,128)(2,1)S(1)} %bitcast.125, bf16[]{:T(256)} %constant.127.clone.1), kind=kCustom, calls=%fused_computation.34 | custom fusion | bytes 393218 | tf_op jit(solution)/shard_map/scatter | solution.py:59
  39.3 16.0 %all-to-all-done.3 = bf16[16,48,512]{2,1,0:T(8,128)(2,1)S(1)} async-done(((bf16[16,48,512]{2,1,0:T(8,128)(2,1)}), bf16[16,48,512]{2,1,0:T(8,128)(2,1)S(1)}, u32[]{:S(2)}, u32[]{:S(2)}) %all-to-all-start.3) | async-done | bytes 786464 | tf_op jit(solution)/shard_map/all_to_all | solution.py:91
  55.3 5.0 %all-to-all-start = ((bf16[16,1,24,512]{3,2,1,0:T(8,128)(2,1)}), bf16[16,1,24,512]{3,2,1,0:T(8,128)(2,1)}, u32[]{:S(2)}, u32[]{:S(2)}) async-start(bf16[16,1,24,512]{3,2,1,0:T(8,128)(2,1)} %bitcast.3), calls=%async_computation | async-start | bytes 786432 | tf_op jit(solution)/shard_map/all_to_all | solution.py:64
  60.4 2.0 %gather_fusion.2 = bf16[512,512]{1,0:T(8,128)(2,1)S(1)} fusion(bf16[768,512]{1,0:T(8,128)(2,1)S(1)} %bitcast.118, s32[1024]{0:T(1024)S(1)} %pad_clamp_fusion), kind=kCustom, calls=%fused_computation.2 | custom fusion | bytes 1050624 | tf_op jit(solution)/shard_map/gather | solution.py:101
  62.4 1.0 select_convert_fusion
  63.4 1.5 %convolution_convert_fusion.1 = bf16[128,1024]{1,0:T(8,128)(2,1)S(1)} fusion(bf16[512,1024]{1,0:T(8,128)(2,1)} %param.16, bf16[1,128,512]{2,1,0:T(8,128)(2,1)S(1)} %copy-done.3), kind=kOutput, calls=%fused_computation.18 | convolution fusion | flops 134348800 | bytes 1441792 | tf_op jit(solution)/shard_map/dot_general | solution.py:111
  65.8 4.6 %all-to-all-done = bf16[16,1,24,512]{3,2,1,0:T(8,128)(2,1)} async-done(((bf16[16,1,24,512]{3,2,1,0:T(8,128)(2,1)}), bf16[16,1,24,512]{3,2,1,0:T(8,128)(2,1)}, u32[]{:S(2)}, u32[]{:S(2)}) %all-to-all-start) | async-done | bytes 393248 | tf_op jit(solution)/shard_map/all_to_all | solution.py:64
  70.4 3.3 %fusion = bf16[16,1,24,2048]{3,2,1,0:T(8,128)(2,1)} fusion(bf16[1,2048,512]{2,1,0:T(8,128)(2,1)S(1)} %copy-done, bf16[16,1,24,512]{3,2,1,0:T(8,128)(2,1)} %all-to-all-done), kind=kOutput, calls=%fused_computation.6 | convolution fusion | flops 806879232 | bytes 4063232 | tf_op jit(solution)/shard_map/skcd,kjd->skcj/dot_general | solution.py:62
  73.7 5.7 %all-to-all-start.1 = ((bf16[16,1,24,2048]{3,2,1,0:T(8,128)(2,1)}), bf16[16,1,24,2048]{3,2,1,0:T(8,128)(2,1)}, u32[]{:S(2)}, u32[]{:S(2)}) async-start(bf16[16,1,24,2048]{3,2,1,0:T(8,128)(2,1)} %fusion), calls=%async_computation.1 | async-start | bytes 3145728 | tf_op jit(solution)/shard_map/all_to_all | solution.py:69
  79.5 4.5 %all-reduce.2.cloned.1.call-done = bf16[512,512]{1,0:T(8,128)(2,1)} async-done(((bf16[512,512]{1,0:T(8,128)(2,1)}), bf16[512,512]{1,0:T(8,128)(2,1)}) %all-reduce.2.cloned.1.call-update) | async-done | bytes 524304 | tf_op jit(solution)/shard_map/psum | solution.py:104
  84.0 1.5 %fusion.6 = bf16[512,512]{0,1:T(8,128)(2,1)S(1)} fusion(bf16[512,512]{1,0:T(8,128)(2,1)} %all-reduce.2.cloned.1.call-done, bf16[512,512]{1,0:T(8,128)(2,1)S(1)} %copy-done.6), kind=kOutput, calls=%fused_computation.16 | convolution fusion | flops 268959744 | bytes 1572864 | tf_op jit(solution)/shard_map/dot_general | solution.py:108
  85.5 0.5 bitcast_reduce_fusion
  86.0 1.3 copy-done.1
  87.3 1.6 %convolution_bitcast_fusion = f32[512,8,64]{0,2,1:T(8,128)} fusion(f32[8,128,512]{2,1,0:T(8,128)S(1)} %get-tuple-element.59, f32[512,8]{0,1:T(8,128)S(1)} %get-tuple-element.58, pred[128]{0:T(512)(128)(4,1)S(1)} %add_compare_fusion, bf16[128,2,8,64]{0,3,2,1:T(8,128)(2,1)S(1)} %bitcast.121), kind=kOutput, calls=%fused_computation.14 | convolution fusion | flops 69206016 | bytes 3294208 | tf_op jit(solution)/shard_map/while/body/eval_jaxpr/che,ehd->chd/dot_general | solution.py:129
  88.9 1.8 %all-gather.1 = f32[1024,8]{0,1:T(8,128)S(1)} all-gather(f32[512,8]{0,1:T(8,128)S(1)} %get-tuple-element.58), channel_id=3, replica_groups=mesh['lists'=16,'users'=2] {'users'}, dimensions={0}, use_global_device_ids=true | all-gather | bytes 49152 | tf_op jit(solution)/shard_map/all_gather | solution.py:10
  90.8 2.1 %fusion.4 = f32[512,8]{0,1:T(8,128)S(1)} fusion(f32[8,128,512]{2,1,0:T(8,128)} %copy-done.1, f32[512,8]{0,1:T(8,128)S(1)} %get-tuple-element.58, pred[128]{0:T(512)(128)(4,1)S(1)} %add_compare_fusion), kind=kLoop, calls=%fused_computation.12 | loop fusion | flops 2093056 | bytes 2130048 | tf_op jit(solution)/shard_map/while/body/eval_jaxpr/reduce_sum | solution.py:127
  92.9 1.8 %all-gather.2 = f32[1024,8]{0,1:T(8,128)S(1)} all-gather(f32[512,8]{0,1:T(8,128)S(1)} %fusion.4), channel_id=4, replica_groups=mesh['lists'=16,'users'=2] {'users'}, dimensions={0}, use_global_device_ids=true | all-gather | bytes 49152 | tf_op jit(solution)/shard_map/all_gather | solution.py:10
  94.8 20.4 %all-to-all-done.1 = bf16[16,1,24,2048]{3,2,1,0:T(8,128)(2,1)} async-done(((bf16[16,1,24,2048]{3,2,1,0:T(8,128)(2,1)}), bf16[16,1,24,2048]{3,2,1,0:T(8,128)(2,1)}, u32[]{:S(2)}, u32[]{:S(2)}) %all-to-all-start.1) | async-done | bytes 1572896 | tf_op jit(solution)/shard_map/all_to_all | solution.py:69
  115.2 3.8 %gather_fusion = bf16[128,2048]{1,0:T(8,128)(2,1)} fusion(bf16[384,2048]{1,0:T(8,128)(2,1)} %bitcast.11, s32[1024]{0:T(1024)S(1)} %pad_clamp_fusion.2), kind=kCustom, calls=%fused_computation | custom fusion | bytes 1049088 | tf_op jit(solution)/shard_map/gather | solution.py:71
  119.0 1.8 %slice_bitcast_fusion.1 = (f32[1,512,8,64]{1,3,2,0:T(8,128)S(1)}, f32[1,512,8,64]{1,3,2,0:T(8,128)S(1)}) fusion(f32[1024,8,64]{0,2,1:T(8,128)} %all-gather.5.cloned.1.call-done), kind=kLoop, calls=%fused_computation.21 | loop fusion | bytes 4194304 | tf_op jit(solution)/shard_map/squeeze | solution.py:11
  121.0 1.0 fusion.7
  (44 shorter events, 1.7 us)
Async XLA Ops:
  7.2 20.5 %copy-start = (bf16[1,2048,512]{2,1,0:T(8,128)(2,1)S(1)}, bf16[1,2048,512]{2,1,0:T(8,128)(2,1)}, u32[]{:S(2)}) copy-start(bf16[1,2048,512]{2,1,0:T(8,128)(2,1)} %param.11) | copy-start | bytes 6291460
  27.7 9.1 %copy-start.4 = (s32[4,32]{1,0:T(4,128)S(1)}, s32[4,32]{1,0:T(4,128)}, u32[]{:S(2)}) copy-start(s32[4,32]{1,0:T(4,128)} %param.10) | copy-start | bytes 1540
  27.7 9.7 %copy-start.5 = (bf16[4,512]{1,0:T(4,128)(2,1)S(1)}, bf16[4,512]{1,0:T(4,128)(2,1)}, u32[]{:S(2)}) copy-start(bf16[4,512]{1,0:T(4,128)(2,1)} %param.9) | copy-start | bytes 12292
  31.1 24.2 %all-to-all-start.3 = ((bf16[16,48,512]{2,1,0:T(8,128)(2,1)}), bf16[16,48,512]{2,1,0:T(8,128)(2,1)S(1)}, u32[]{:S(2)}, u32[]{:S(2)}) async-start(bf16[16,48,512]{2,1,0:T(8,128)(2,1)} %bitcast.119), calls=%async_computation.3 | async-start | bytes 1572864 | tf_op jit(solution)/shard_map/all_to_all | solution.py:91
  55.3 15.1 %all-to-all-start = ((bf16[16,1,24,512]{3,2,1,0:T(8,128)(2,1)}), bf16[16,1,24,512]{3,2,1,0:T(8,128)(2,1)}, u32[]{:S(2)}, u32[]{:S(2)}) async-start(bf16[16,1,24,512]{3,2,1,0:T(8,128)(2,1)} %bitcast.3), calls=%async_computation | async-start | bytes 786432 | tf_op jit(solution)/shard_map/all_to_all | solution.py:64
  60.3 23.6 %all-reduce.2.cloned.1.call-start = ((), (), s32[]{:S(2)}) async-start(), calls=%async_computation.4 | async-start | bytes 1048576 | tf_op jit(solution)/shard_map/psum | solution.py:104
  60.4 3.0 %copy-start.3 = (bf16[1,128,512]{2,1,0:T(8,128)(2,1)S(1)}, bf16[1,128,512]{2,1,0:T(8,128)(2,1)}, u32[]{:S(2)}) copy-start(bf16[1,128,512]{2,1,0:T(8,128)(2,1)} %param.13) | copy-start | bytes 393220
  73.7 10.3 %copy-start.6 = (bf16[512,512]{1,0:T(8,128)(2,1)S(1)}, bf16[512,512]{1,0:T(8,128)(2,1)}, u32[]{:S(2)}) copy-start(bf16[512,512]{1,0:T(8,128)(2,1)} %param.15) | copy-start | bytes 1572868
  73.7 41.5 %all-to-all-start.1 = ((bf16[16,1,24,2048]{3,2,1,0:T(8,128)(2,1)}), bf16[16,1,24,2048]{3,2,1,0:T(8,128)(2,1)}, u32[]{:S(2)}, u32[]{:S(2)}) async-start(bf16[16,1,24,2048]{3,2,1,0:T(8,128)(2,1)} %fusion), calls=%async_computation.1 | async-start | bytes 3145728 | tf_op jit(solution)/shard_map/all_to_all | solution.py:69
  79.4 39.6 %all-gather.5.cloned.1.call-start = ((), (), s32[]{:S(2)}) async-start(), calls=%async_computation.5 | async-start | bytes 3145728 | tf_op jit(solution)/shard_map/all_gather | solution.py:10
  86.0 1.3 %copy-start.1 = (f32[8,128,512]{2,1,0:T(8,128)}, f32[8,128,512]{2,1,0:T(8,128)S(1)}, u32[]{:S(2)}) copy-start(f32[8,128,512]{2,1,0:T(8,128)S(1)} %get-tuple-element.59) | copy-start | bytes 6291460
  119.0 2.0 %copy-start.2 = (bf16[512,512]{1,0:T(8,128)(2,1)S(1)}, bf16[512,512]{1,0:T(8,128)(2,1)}, u32[]{:S(2)}) copy-start(bf16[512,512]{1,0:T(8,128)(2,1)} %param.17) | copy-start | bytes 1572868
Sparse Core Ops, SparseCore 0:
  64.1 19.8 all-reduce.1
  89.0 11.7 all-gather.4
where the time goes:
time: 130 us; the launch traced here: 129 us
  waiting for transfers between devices  45.5 us (35%)
  local copies, waits for them, and re-layouts  17.3 us (13%)
  starting transfers between devices  16.6 us (13%)
  blocking collectives  15.7 us (12%)
  between operations  14.9 us (11%)
  matrix products  9.47 us (7%)
  other arithmetic  9.42 us (7%)
    all_to_all x1, waiting for transfers between devices, shards(): lax.all_to_all(scores, 'lists', split_axis=0, concat_axis=0, tiled=True)  20.4 us
    all_to_all x1, waiting for transfers between devices, shards(): lax.all_to_all(flat_items[lax.all_to_all(request, 'lists', split_axis=0,...  16 us
    all_to_all x1, blocking collectives, shards(): lax.all_to_all(request, 'lists', split_axis=0, concat_axis=0, tiled=True)  12 us
    all_to_all x1, starting transfers between devices, shards(): lax.all_to_all(flat_items[lax.all_to_all(request, 'lists', split_axis=0,...  5.77 us
    all_to_all x1, starting transfers between devices, shards(): lax.all_to_all(scores, 'lists', split_axis=0, concat_axis=0, tiled=True)  5.74 us
    all_to_all x1, starting transfers between devices, shards(): lax.all_to_all(outgoing, 'lists', split_axis=0, concat_axis=0, tiled=True)  5.03 us
    all_to_all x1, waiting for transfers between devices, shards(): lax.all_to_all(outgoing, 'lists', split_axis=0, concat_axis=0, tiled=True)  4.63 us
    psum x1, waiting for transfers between devices, shards(): cand_rows = lax.psum(mine.astype(jnp.bfloat16), 'users')  4.48 us
  transfers between devices with their start and end apart: 5, of which 4 were waited for; matrix products, arithmetic and copies ran while one was open for 16% of the time, Pallas kernels for 0%

commit v1 on v0

v1 whole, which is shorter than its diff:
```python
import functools

import jax
import jax.numpy as jnp
from jax import lax
from jax.experimental import pallas as pl
from jax.experimental.pallas import tpu as pltpu
from jax.sharding import PartitionSpec as P

HEADS = 8
BASE = 256
LANES = 128
ROW_TILE = 16
VMEM_BYTES = 28 * 1024 * 1024
ALL_VMEM_BYTES = 62 * 1024 * 1024


def round_up(value, step):
    return (value + step - 1) // step * step


def picks(index, count):
    place = lax.broadcasted_iota(jnp.int32, (index.shape[0], count), 1)
    return jnp.where(index == place, 1.0, 0.0).astype(jnp.bfloat16)


def pack_kernel(digits, ids_ref, vectors_ref, pack_ref):
    width = vectors_ref.shape[1]
    vectors = vectors_ref[...].astype(jnp.float32)
    ids = ids_ref[...]
    spans = [slice(start, start + LANES) for start in range(0, width, LANES)]
    rows = [vectors[:, span] for span in spans]
    for digit in range(digits):
        value = ((ids >> (8 * digit)) & (BASE - 1)).astype(jnp.float32)
        rows += [value[:, span] for span in spans]
    count = sum(row.shape[0] for row in rows)
    if pack_ref.shape[1] > count:
        rows.append(jnp.zeros((pack_ref.shape[1] - count, LANES), jnp.float32))
    pack_ref[...] = jnp.broadcast_to(jnp.concatenate(rows, axis=0).astype(jnp.bfloat16)[None], pack_ref.shape)


def earlier(count):
    row = lax.broadcasted_iota(jnp.int32, (count, count), 0)
    column = lax.broadcasted_iota(jnp.int32, (count, count), 1)
    return jnp.where(row < column, 1.0, 0.0).astype(jnp.bfloat16)


def items_kernel(items_hbm, items_ref, sems):
    part = items_ref.shape[0] // sems.shape[0]
    loads = []
    for p in range(sems.shape[0]):
        rows = pl.ds(p * part, part)
        loads.append(pltpu.make_async_copy(items_hbm.at[rows], items_ref.at[rows], sems.at[p]))
        loads[-1].start()
    for load in loads:
        load.wait()


def slot_kernel(n_lists, items_loc, n_users, block, col_ref, ids_ref, probes_ref, slot_ref, probe_ref):
    ids = ids_ref[...]
    cands = ids.shape[1]
    bins = ids // items_loc
    mine = bins % n_users == col_ref[0]
    owner = bins // n_users
    lists = lax.broadcasted_iota(jnp.int32, (n_lists, cands), 0)
    hot = jnp.where((lists == owner) & mine, 1.0, 0.0)
    before = jnp.dot(hot.astype(jnp.bfloat16), earlier(cands), preferred_element_type=jnp.float32)
    rank = jnp.sum(before * hot, axis=0, keepdims=True)
    slot = jnp.where(mine, owner.astype(jnp.float32) * block + rank, -1.0)
    slot_ref[...] = jnp.broadcast_to(slot, slot_ref.shape)
    probes = probes_ref[...].astype(jnp.float32)
    flat = jnp.concatenate([probes[u : u + 1] for u in range(probes.shape[0])], axis=1)
    probe_ref[...] = jnp.broadcast_to(flat, probe_ref.shape)


def pairs_kernel(n_parts, *refs):
    parts, (weight_ref, query_ref, keys_ref, values_ref, turned_ref) = refs[:n_parts], refs[n_parts:]
    events = jnp.concatenate([part[...] for part in parts], axis=0)
    pairs = jnp.dot(events, weight_ref[...], preferred_element_type=jnp.float32)
    heads, _, head_dim = keys_ref.shape
    width = heads * head_dim
    for h in range(heads):
        keys_ref[h] = pairs[:, h * head_dim : (h + 1) * head_dim].astype(jnp.bfloat16)
    values_ref[...] = jnp.transpose(pairs[:, width:]).astype(jnp.bfloat16)
    turned_ref[...] = jnp.transpose(query_ref[...].astype(jnp.float32)).astype(jnp.bfloat16)


def owner_kernel(n_lists, user_dev, digits, cap, scale, base_ref, gathered_ref, items_ref, *refs):
    out_hbm, out_ref, out_sems = refs
    pack_rows = gathered_ref.shape[0] // n_lists
    items_loc, width = items_ref.shape
    spans = width // LANES
    entry = lax.broadcasted_iota(jnp.int32, ((user_dev + digits) * n_lists, 1), 0)
    asker, field = entry % n_lists, entry // n_lists
    unpacked = []
    for span in range(spans):
        line = jnp.where(field < user_dev, span * user_dev + field, (user_dev + field - user_dev) * spans + span)
        unpacked.append(
            jnp.dot(
                picks(asker * pack_rows + line, n_lists * pack_rows),
                gathered_ref[...],
                preferred_element_type=jnp.float32,
            )
        )
    unpacked = jnp.concatenate(unpacked, axis=1)
    ids = jnp.zeros((n_lists, width), jnp.float32)
    for digit in range(digits):
        ids = ids + unpacked[(user_dev + digit) * n_lists : (user_dev + digit + 1) * n_lists] * float(BASE**digit)
    local = ids - base_ref[0].astype(jnp.float32)
    mine = (local >= 0.0) & (local < items_loc)
    hot = jnp.where(mine, 1.0, 0.0).astype(jnp.bfloat16)
    rank = jnp.dot(hot, earlier(width), preferred_element_type=jnp.float32)
    rank = jnp.where(mine, rank, -1.0)
    place = lax.broadcasted_iota(jnp.int32, (cap, width), 0).astype(jnp.float32)
    index = []
    for r in range(n_lists):
        picked = jnp.where(rank[r : r + 1] == place, local[r : r + 1], 0.0)
        index.append(jnp.sum(picked, axis=1, keepdims=True).astype(jnp.int32))
    scores = lax.dot_general(
        unpacked[: user_dev * n_lists].astype(jnp.bfloat16),
        items_ref[...],
        (((1,), (1,)), ((), ())),
        preferred_element_type=jnp.float32,
    )
    scores = (scores * scale).astype(jnp.bfloat16)
    pieces = items_loc // width
    stacked = jnp.concatenate(
        [scores[:, piece * width : (piece + 1) * width] for piece in range(pieces)], axis=0
    )
    kept = out_ref.shape[1] - cap
    entry = lax.broadcasted_iota(jnp.int32, (n_lists * kept, 1), 0)
    wanted = jnp.where(entry % kept < pieces * user_dev, entry % kept * n_lists + entry // kept, -1)
    spread = jnp.dot(
        picks(wanted, stacked.shape[0]), stacked, preferred_element_type=jnp.float32
    ).astype(jnp.bfloat16)
    out_ref[:, cap:, :] = spread.reshape(n_lists, kept, width)
    step = max(1, 256 // cap)
    sends = []
    for number, first in enumerate(range(0, n_lists, step)):
        last = min(n_lists, first + step)
        rows = jnp.dot(
            picks(jnp.concatenate(index[first:last], axis=0), items_loc),
            items_ref[...],
            preferred_element_type=jnp.float32,
        ).astype(jnp.bfloat16)
        out_ref[first:last, :cap, :] = rows.reshape(last - first, cap, width)
        send = pltpu.make_async_copy(out_ref.at[first:last], out_hbm.at[first:last], out_sems.at[number])
        send.start()
        sends.append(send)
    for send in sends:
        send.wait()


def place_kernel(n_users, col_ref, slot_ref, fetched_ref, own_ref, *rest):
    sent_refs, scratch = rest[:-1], rest[-1]
    n_lists, block, width = fetched_ref.shape
    rows = n_lists * block
    share = own_ref.shape[0]
    slot = jnp.transpose(slot_ref[...])[:, :1].astype(jnp.int32)
    scratch[...] = jnp.dot(
        picks(slot, rows), fetched_ref[...].reshape(rows, width), preferred_element_type=jnp.float32
    ).astype(jnp.bfloat16)
    for shift, ref in enumerate((own_ref, *sent_refs)):
        start = (col_ref[0] + shift) % n_users * share
        ref[...] = scratch[pl.ds(pl.multiple_of(start, share), share), :]


def attend_kernel(n_parts, col_ref, length_ref, *refs):
    parts, (keys_ref, values_ref, turned_ref, out_weight_ref, out_ref) = refs[:n_parts], refs[n_parts:]
    heads, events, head_dim = keys_ref.shape
    hist_dev = events // n_parts
    rows = parts[0][...]
    for part in parts[1:]:
        rows = rows + part[...]
    queries = lax.dot_general(
        turned_ref[...], rows, (((1,), (1,)), ((), ())), preferred_element_type=jnp.float32
    )
    queries = (queries * head_dim ** (-0.5)).astype(jnp.bfloat16)
    event = lax.broadcasted_iota(jnp.int32, (events, 1), 0)
    piece = event // hist_dev
    position = (col_ref[0] - piece + n_parts) % n_parts * hist_dev + event % hist_dev
    valid = position < length_ref[0]
    mixed = []
    for h in range(heads):
        span = slice(h * head_dim, (h + 1) * head_dim)
        scores = jnp.dot(keys_ref[h], queries[span], preferred_element_type=jnp.float32)
        scores = jnp.where(valid, scores, -1e30)
        exponentials = jnp.exp(scores - jnp.max(scores, axis=0, keepdims=True))
        total = jnp.sum(exponentials, axis=0, keepdims=True)
        head = jnp.dot(values_ref[span, :], exponentials.astype(jnp.bfloat16), preferred_element_type=jnp.float32)
        mixed.append(head / total)
    attended = jnp.transpose(jnp.concatenate(mixed, axis=0)).astype(jnp.bfloat16)
    out_ref[...] = jnp.dot(attended, out_weight_ref[...], preferred_element_type=jnp.float32).astype(jnp.bfloat16)


def expand_kernel(user_dev, pieces, cap, probes_ref, fetched_ref, out_ref):
    n_lists, block, width = fetched_ref.shape
    kept = block - cap
    rows = n_lists * kept
    returned = fetched_ref[:, cap:, :].reshape(rows, width)
    count = out_ref.shape[0]
    probe = jnp.transpose(probes_ref[...])[:, :1].astype(jnp.int32)
    user = lax.broadcasted_iota(jnp.int32, (count, 1), 0) // (count // user_dev)
    for piece in range(pieces):
        wanted = probe * kept + piece * user_dev + user
        out_ref[:, piece * width : (piece + 1) * width] = jnp.dot(
            picks(wanted, rows), returned, preferred_element_type=jnp.float32
        ).astype(jnp.bfloat16)


SMEM = pl.BlockSpec(memory_space=pltpu.SMEM)
VMEM = pl.BlockSpec(memory_space=pltpu.VMEM)
HBM = pl.BlockSpec(memory_space=pltpu.HBM)
PARAMS = pltpu.CompilerParams(vmem_limit_bytes=VMEM_BYTES)


def shards(
    user_vectors,
    probe_lists,
    list_items,
    candidate_ids,
    history,
    history_lengths,
    query_weight,
    key_value_weight,
    out_weight,
):
    n_lists = lax.axis_size("lists")
    n_users = lax.axis_size("users")
    _, items_loc, width = list_items.shape
    user_dev, probes = probe_lists.shape
    _, cands = candidate_ids.shape
    bf16 = jnp.bfloat16
    cap = max(2, 3 * cands // (n_lists * n_users))
    cap = round_up(cap, ROW_TILE)
    kept = round_up(items_loc // width * user_dev, ROW_TILE)
    share = cands // n_users
    pieces = items_loc // width
    digits = 1
    while BASE**digits < n_lists * n_users * items_loc:
        digits += 1
    pack_rows = round_up((user_dev + digits) * (width // LANES), 8)
    line = lax.axis_index("lists").astype(jnp.int32)
    col = lax.axis_index("users").astype(jnp.int32)
    col_arg = col.reshape(1)
    base_arg = ((line * n_users + col) * items_loc).reshape(1)

    flat_items = list_items.reshape(items_loc, width)
    pack = pl.pallas_call(
        functools.partial(pack_kernel, digits),
        out_shape=jax.ShapeDtypeStruct((n_lists, pack_rows, LANES), bf16),
        in_specs=[VMEM, VMEM],
        out_specs=VMEM,
        compiler_params=pltpu.CompilerParams(vmem_limit_bytes=ALL_VMEM_BYTES),
    )(candidate_ids, user_vectors)
    gathered = lax.all_to_all(pack, "lists", split_axis=0, concat_axis=0, tiled=True)
    gathered = gathered.reshape(n_lists * pack_rows, LANES)

    items = pl.pallas_call(
        items_kernel,
        out_shape=jax.ShapeDtypeStruct((items_loc, width), bf16),
        in_specs=[HBM],
        out_specs=VMEM,
        scratch_shapes=[pltpu.SemaphoreType.DMA((4,))],
        compiler_params=PARAMS,
    )(flat_items)
    gathered, items = lax.optimization_barrier((gathered, items))

    slot, probe_row = pl.pallas_call(
        functools.partial(slot_kernel, n_lists, items_loc, n_users, cap + kept),
        out_shape=(
            jax.ShapeDtypeStruct((8, cands), jnp.float32),
            jax.ShapeDtypeStruct((8, user_dev * probes), jnp.float32),
        ),
        in_specs=[SMEM, VMEM, VMEM],
        out_specs=(VMEM, VMEM),
        compiler_params=PARAMS,
    )(col_arg, candidate_ids, probe_lists)

    events = history.reshape(-1, width)
    hist = [events]
    for shift in range(1, n_users):
        hist.append(lax.ppermute(events, "users", [(i, (i + shift) % n_users) for i in range(n_users)]))
    total_events = n_users * events.shape[0]
    keys, values, turned = pl.pallas_call(
        functools.partial(pairs_kernel, n_users),
        out_shape=(
            jax.ShapeDtypeStruct((HEADS, total_events, width // HEADS), bf16),
            jax.ShapeDtypeStruct((width, total_events), bf16),
            jax.ShapeDtypeStruct((width, width), bf16),
        ),
        in_specs=[VMEM] * (n_users + 2),
        out_specs=(VMEM, VMEM, VMEM),
        compiler_params=PARAMS,
    )(*hist, key_value_weight, query_weight)

    step = max(1, 256 // cap)
    answers = pl.pallas_call(
        functools.partial(owner_kernel, n_lists, user_dev, digits, cap, width ** (-0.5)),
        out_shape=jax.ShapeDtypeStruct((n_lists, cap + kept, width), bf16),
        in_specs=[SMEM, VMEM, VMEM],
        out_specs=pl.BlockSpec(memory_space=pl.ANY),
        scratch_shapes=[
            pltpu.VMEM((n_lists, cap + kept, width), bf16),
            pltpu.SemaphoreType.DMA((-(-n_lists // step),)),
        ],
        compiler_params=PARAMS,
    )(base_arg, gathered, items)
    fetched = lax.all_to_all(answers, "lists", split_axis=0, concat_axis=0, tiled=True)
    fetched, slot, probe_row, keys, values, turned = lax.optimization_barrier(
        (fetched, slot, probe_row, keys, values, turned)
    )

    placed = pl.pallas_call(
        functools.partial(place_kernel, n_users),
        out_shape=tuple(jax.ShapeDtypeStruct((share, width), bf16) for _ in range(n_users)),
        in_specs=[SMEM, VMEM, VMEM],
        out_specs=tuple(VMEM for _ in range(n_users)),
        scratch_shapes=[pltpu.VMEM((cands, width), bf16)],
        compiler_params=PARAMS,
    )(col_arg, slot, fetched)
    parts = [placed[0]]
    for shift in range(1, n_users):
        parts.append(
            lax.ppermute(placed[shift], "users", [(i, (i + shift) % n_users) for i in range(n_users)])
        )
    ranked = pl.pallas_call(
        functools.partial(attend_kernel, n_users),
        out_shape=jax.ShapeDtypeStruct((share, width), bf16),
        in_specs=[SMEM, SMEM] + [VMEM] * (n_users + 4),
        out_specs=VMEM,
        compiler_params=PARAMS,
    )(col_arg, history_lengths, *parts, keys, values, turned, out_weight)

    list_scores = pl.pallas_call(
        functools.partial(expand_kernel, user_dev, pieces, cap),
        out_shape=jax.ShapeDtypeStruct((user_dev * probes, items_loc), bf16),
        in_specs=[VMEM, VMEM],
        out_specs=VMEM,
        compiler_params=PARAMS,
    )(probe_row, fetched)
    return (list_scores.reshape(user_dev, probes, items_loc), ranked.reshape(1, share, width))


def solution(mesh):
    placed = (
        P("lists", None),
        P("lists", None),
        P("lists", "users", None),
        P("lists", None),
        P("lists", "users", None),
        P("lists"),
        P(),
        P(),
        P(),
    )
    return jax.shard_map(
        shards,
        mesh=mesh,
        in_specs=placed,
        out_specs=(P("lists", None, "users"), P("lists", "users", None)),
        check_vma=False,
    )
```

time: 130 us -> 56.9 us (0.44)
  the two profiles are of different devices: /device:TPU:12 before, /device:TPU:0 now
where the time goes in v1:
time: 56.9 us; the launch traced here: 55.9 us
  waiting for transfers between devices  26 us (46%)
  starting transfers between devices  12.3 us (22%)
  Pallas kernels  11.7 us (21%)
  local copies, waits for them, and re-layouts  4.5 us (8%)
  between operations  1.44 us (3%)
    all_to_all x1, waiting for transfers between devices, shards(): lax.all_to_all(answers, 'lists', split_axis=0, concat_axis=0, tiled=True)  19.6 us
    all_to_all x1, starting transfers between devices, shards(): lax.all_to_all(pack, 'lists', split_axis=0, concat_axis=0, tiled=True)  8.31 us
    all_to_all x1, waiting for transfers between devices, shards(): lax.all_to_all(pack, 'lists', split_axis=0, concat_axis=0, tiled=True)  5.86 us
    unnamed x26, local copies, waits for them, and re-layouts  4.5 us
    all_to_all x1, starting transfers between devices, shards(): lax.all_to_all(answers, 'lists', split_axis=0, concat_axis=0, tiled=True)  3.8 us
    pallas_call x1, Pallas kernels, shards(): pl.pallas_call(functools.partial(owner_kernel, n_lists, user_dev, digits,...  3.8 us
    pallas_call x1, Pallas kernels, shards(): pl.pallas_call(functools.partial(attend_kernel, n_users), out_shape=jax.S...  3.35 us
    pallas_call x1, Pallas kernels, shards(): pl.pallas_call(functools.partial(pack_kernel, digits), out_shape=jax.Shap...  1.36 us
  transfers between devices with their start and end apart: 4, of which 3 were waited for; matrix products, arithmetic and copies ran while one was open for 0% of the time, Pallas kernels for 4%

profile of v1, /device:TPU:0, one launch (start us, length us, event | category | flops | bytes accessed | tf_op | source)
XLA Modules:
  0.0 55.9 jit_solution(14704133661992508859)
XLA Ops:
  0.6 1.4 %shard_map.104 = bf16[16,24,128]{2,1,0:T(8,128)(2,1)} custom-call(s32[1,512]{1,0:T(1,128)} %ids_ref.3, bf16[4,512]{1,0:T(4,128)(2,1)} %vectors_ref.1), custom_call_target="tpu_custom_call" | custom-call | tf_op jit(solution)/shard_map/pallas_call | solution.py:249
  2.0 8.3 %all-to-all-start = ((bf16[16,24,128]{2,1,0:T(8,128)(2,1)}), bf16[16,24,128]{2,1,0:T(8,128)(2,1)S(1)}, u32[]{:S(2)}, u32[]{:S(2)}) async-start(bf16[16,24,128]{2,1,0:T(8,128)(2,1)} %shard_map.104), calls=%async_computation | async-start | bytes 196608 | tf_op jit(solution)/shard_map/all_to_all | solution.py:256
  10.3 0.0 copy-start
  10.3 1.6 %copy-done = bf16[1,2048,512]{2,1,0:T(8,128)(2,1)S(1)} copy-done((bf16[1,2048,512]{2,1,0:T(8,128)(2,1)S(1)}, bf16[1,2048,512]{2,1,0:T(8,128)(2,1)}, u32[]{:S(2)}) %copy-start) | copy-done | bytes 2097176
  11.9 0.2 shard_map.105.items_ref
  12.1 5.9 %all-to-all-done = bf16[16,24,128]{2,1,0:T(8,128)(2,1)S(1)} async-done(((bf16[16,24,128]{2,1,0:T(8,128)(2,1)}), bf16[16,24,128]{2,1,0:T(8,128)(2,1)S(1)}, u32[]{:S(2)}, u32[]{:S(2)}) %all-to-all-start) | async-done | bytes 98336 | tf_op jit(solution)/shard_map/all_to_all | solution.py:256
  18.0 3.8 %shard_map.106 = bf16[16,64,512]{2,1,0:T(8,128)(2,1)} custom-call(s32[1]{0:T(128)} %bitcast.base_ref, bf16[384,128]{1,0:T(8,128)(2,1)S(1)} %bitcast.8, bf16[2048,512]{1,0:T(8,128)(2,1)S(1)} %shard_map.105.items_ref), custom_call_target="tpu_custom_call" | custom-call | tf_op jit(solution)/shard_map/pallas_call | solution.py:298
  21.8 0.0 copy-start.2
  21.8 3.8 %all-to-all-start.1 = ((bf16[16,64,512]{2,1,0:T(8,128)(2,1)}), bf16[16,64,512]{2,1,0:T(8,128)(2,1)S(1)}, u32[]{:S(2)}, u32[]{:S(2)}) async-start(bf16[16,64,512]{2,1,0:T(8,128)(2,1)} %shard_map.106), calls=%async_computation.1 | async-start | bytes 2097152 | tf_op jit(solution)/shard_map/all_to_all | solution.py:309
  25.6 0.0 copy-done.8
  25.6 0.1 collective-permute-start
  25.7 0.0 copy-done.9
  25.7 0.0 copy-done.12
  25.7 0.2 shard_map.107
  25.9 0.0 copy-start.10
  25.9 0.6 %copy-done.10 = f32[8,128]{1,0:T(8,128)} copy-done((f32[8,128]{1,0:T(8,128)}, f32[8,128]{1,0:T(8,128)S(1)}, u32[]{:S(2)}) %copy-start.10) | copy-done | bytes 4120
  26.5 0.5 collective-permute-done.refs_1_
  27.0 0.0 copy-done.1
  27.0 0.0 copy-done.2
  27.0 0.6 %shard_map.108 = (bf16[8,256,64]{2,1,0:T(8,128)(2,1)S(1)}, bf16[512,256]{1,0:T(8,128)(2,1)S(1)}, bf16[512,512]{1,0:T(8,128)(2,1)S(1)}) custom-call(bf16[128,512]{1,0:T(8,128)(2,1)S(1)} %bitcast.10, bf16[128,512]{1,0:T(8,128)(2,1)S(1)} %collective-permute-done.refs_1_, bf16[512,1024]{1,0:T(8,128)(2,1)S(1)} %copy-done.1, bf16[512,512]{1,0:T(8,128)(2,1)S(1)} %copy-done.2), custom_call_target="tpu_custom_call" | custom-call | tf_op jit(solution)/shard_map/pallas_call | solution.py:285
  27.6 0.0 copy-start.4
  27.6 0.8 %copy-done.4 = bf16[8,256,64]{2,1,0:T(8,128)(2,1)} copy-done((bf16[8,256,64]{2,1,0:T(8,128)(2,1)}, bf16[8,256,64]{2,1,0:T(8,128)(2,1)S(1)}, u32[]{:S(2)}) %copy-start.4) | copy-done | bytes 262168
  28.4 0.8 %copy-done.6 = bf16[512,512]{1,0:T(8,128)(2,1)} copy-done((bf16[512,512]{1,0:T(8,128)(2,1)}, bf16[512,512]{1,0:T(8,128)(2,1)S(1)}, u32[]{:S(2)}) %copy-start.6) | copy-done | bytes 524312
  29.2 19.6 %all-to-all-done.1.fetched_ref = bf16[16,64,512]{2,1,0:T(8,128)(2,1)S(1)} async-done(((bf16[16,64,512]{2,1,0:T(8,128)(2,1)}), bf16[16,64,512]{2,1,0:T(8,128)(2,1)S(1)}, u32[]{:S(2)}, u32[]{:S(2)}) %all-to-all-start.1) | async-done | bytes 1048608 | tf_op jit(solution)/shard_map/all_to_all | solution.py:309
  48.9 1.0 %shard_map.110 = (bf16[256,512]{1,0:T(8,128)(2,1)S(1)}, bf16[256,512]{1,0:T(8,128)(2,1)S(1)}) custom-call(s32[1]{0:T(128)} %bitcast.3.col_ref, f32[8,512]{1,0:T(8,128)S(1)} %get-tuple-element.26.slot_ref, bf16[16,64,512]{2,1,0:T(8,128)(2,1)S(1)} %all-to-all-done.1.fetched_ref), custom_call_target="tpu_custom_call" | custom-call | tf_op jit(solution)/shard_map/pallas_call | solution.py:314
  49.9 0.1 collective-permute-start.1
  50.6 0.0 copy-start.11
  50.7 0.7 %copy-done.11 = f32[8,128]{1,0:T(8,128)S(1)} copy-done((f32[8,128]{1,0:T(8,128)S(1)}, f32[8,128]{1,0:T(8,128)}, u32[]{:S(2)}) %copy-start.11) | copy-done | bytes 4120
  51.3 1.2 %shard_map.109 = bf16[128,2048]{1,0:T(8,128)(2,1)} custom-call(f32[8,128]{1,0:T(8,128)S(1)} %copy-done.11, bf16[16,64,512]{2,1,0:T(8,128)(2,1)S(1)} %all-to-all-done.1.fetched_ref), custom_call_target="tpu_custom_call" | custom-call | tf_op jit(solution)/shard_map/pallas_call | solution.py:335
  52.5 0.0 collective-permute-done.1.refs_1_
  52.5 0.0 copy-done.3
  52.6 3.3 %shard_map.111 = bf16[256,512]{1,0:T(8,128)(2,1)} custom-call(s32[1]{0:T(128)} %bitcast.3.col_ref, s32[1]{0:T(128)S(6)} %copy.11.length_ref, bf16[256,512]{1,0:T(8,128)(2,1)S(1)} %get-tuple-element.27.refs_0_, bf16[256,512]{1,0:T(8,128)(2,1)S(1)} %collective-permute-done.1.refs_1_, bf16[8,256,64]{2,1,0:T(8,128)(2,1)S(1)} %copy-done.5, ...), custom_call_target="tpu_custom_call" | custom-call | tf_op jit(solution)/shard_map/pallas_call | solution.py:327
  (10 shorter events, 0.0 us)
Async XLA Ops:
  2.0 16.0 %all-to-all-start = ((bf16[16,24,128]{2,1,0:T(8,128)(2,1)}), bf16[16,24,128]{2,1,0:T(8,128)(2,1)S(1)}, u32[]{:S(2)}, u32[]{:S(2)}) async-start(bf16[16,24,128]{2,1,0:T(8,128)(2,1)} %shard_map.104), calls=%async_computation | async-start | bytes 196608 | tf_op jit(solution)/shard_map/all_to_all | solution.py:256
  10.3 1.6 %copy-start = (bf16[1,2048,512]{2,1,0:T(8,128)(2,1)S(1)}, bf16[1,2048,512]{2,1,0:T(8,128)(2,1)}, u32[]{:S(2)}) copy-start(bf16[1,2048,512]{2,1,0:T(8,128)(2,1)} %param.11) | copy-start | bytes 6291460
  18.0 7.6 %copy-start.8 = (bf16[1,128,512]{2,1,0:T(8,128)(2,1)S(1)}, bf16[1,128,512]{2,1,0:T(8,128)(2,1)}, u32[]{:S(2)}) copy-start(bf16[1,128,512]{2,1,0:T(8,128)(2,1)} %param.13) | copy-start | bytes 393220
  18.0 7.7 %copy-start.9 = (s32[1,512]{1,0:T(1,128)S(1)}, s32[1,512]{1,0:T(1,128)}, u32[]{:S(2)}) copy-start(s32[1,512]{1,0:T(1,128)} %ids_ref.3) | copy-start | bytes 6148
  18.0 7.7 %copy-start.12 = (s32[4,32]{1,0:T(4,128)S(1)}, s32[4,32]{1,0:T(4,128)}, u32[]{:S(2)}) copy-start(s32[4,32]{1,0:T(4,128)} %probes_ref.1) | copy-start | bytes 1540
  18.0 9.1 %copy-start.1 = (bf16[512,1024]{1,0:T(8,128)(2,1)S(1)}, bf16[512,1024]{1,0:T(8,128)(2,1)}, u32[]{:S(2)}) copy-start(bf16[512,1024]{1,0:T(8,128)(2,1)} %refs_2_.1) | copy-start | bytes 3145732
  21.8 5.2 %copy-start.2 = (bf16[512,512]{1,0:T(8,128)(2,1)S(1)}, bf16[512,512]{1,0:T(8,128)(2,1)}, u32[]{:S(2)}) copy-start(bf16[512,512]{1,0:T(8,128)(2,1)} %refs_3_.1) | copy-start | bytes 1572868
  21.8 27.1 %all-to-all-start.1 = ((bf16[16,64,512]{2,1,0:T(8,128)(2,1)}), bf16[16,64,512]{2,1,0:T(8,128)(2,1)S(1)}, u32[]{:S(2)}, u32[]{:S(2)}) async-start(bf16[16,64,512]{2,1,0:T(8,128)(2,1)} %shard_map.106), calls=%async_computation.1 | async-start | bytes 2097152 | tf_op jit(solution)/shard_map/all_to_all | solution.py:309
  25.6 1.4 %collective-permute-start = (bf16[128,512]{1,0:T(8,128)(2,1)S(1)}, bf16[128,512]{1,0:T(8,128)(2,1)S(1)}, u32[]{:S(2)}, u32[]{:S(2)}) collective-permute-start(bf16[128,512]{1,0:T(8,128)(2,1)S(1)} %bitcast.9), channel_id=1, source_target_pairs={{0,1},{1,0},{2,3},{3,2},{4,5},{5,4},{6,7},{7,6},{8,9},{9,8},{10,11... | collective-permute-start | bytes 393224 | tf_op jit(solution)/shard_map/ppermute | solution.py:283
  25.9 0.6 %copy-start.10 = (f32[8,128]{1,0:T(8,128)}, f32[8,128]{1,0:T(8,128)S(1)}, u32[]{:S(2)}) copy-start(f32[8,128]{1,0:T(8,128)S(1)} %get-tuple-element.24.probes_ref) | copy-start | bytes 12292
  26.5 26.0 %copy-start.3 = (bf16[512,512]{1,0:T(8,128)(2,1)S(1)}, bf16[512,512]{1,0:T(8,128)(2,1)}, u32[]{:S(2)}) copy-start(bf16[512,512]{1,0:T(8,128)(2,1)} %refs_5_.1) | copy-start | bytes 1572868
  27.6 0.8 %copy-start.4 = (bf16[8,256,64]{2,1,0:T(8,128)(2,1)}, bf16[8,256,64]{2,1,0:T(8,128)(2,1)S(1)}, u32[]{:S(2)}) copy-start(bf16[8,256,64]{2,1,0:T(8,128)(2,1)S(1)} %get-tuple-element.29.refs_2_) | copy-start | bytes 786436
  28.4 0.8 %copy-start.6 = (bf16[512,512]{1,0:T(8,128)(2,1)}, bf16[512,512]{1,0:T(8,128)(2,1)S(1)}, u32[]{:S(2)}) copy-start(bf16[512,512]{1,0:T(8,128)(2,1)S(1)} %get-tuple-element.31.refs_4_) | copy-start | bytes 1572868
  48.9 3.7 %copy-start.5 = (bf16[8,256,64]{2,1,0:T(8,128)(2,1)S(1)}, bf16[8,256,64]{2,1,0:T(8,128)(2,1)}, u32[]{:S(2)}) copy-start(bf16[8,256,64]{2,1,0:T(8,128)(2,1)} %copy-done.4) | copy-start | bytes 786436
  48.9 3.7 %copy-start.7 = (bf16[512,512]{1,0:T(8,128)(2,1)S(1)}, bf16[512,512]{1,0:T(8,128)(2,1)}, u32[]{:S(2)}) copy-start(bf16[512,512]{1,0:T(8,128)(2,1)} %copy-done.6) | copy-start | bytes 1572868
  49.9 2.6 %collective-permute-start.1 = (bf16[256,512]{1,0:T(8,128)(2,1)S(1)}, bf16[256,512]{1,0:T(8,128)(2,1)S(1)}, u32[]{:S(2)}, u32[]{:S(2)}) collective-permute-start(bf16[256,512]{1,0:T(8,128)(2,1)S(1)} %get-tuple-element.28), channel_id=1, source_target_pairs={{0,1},{1,0},{2,3},{3,2},{4,5},{5,4},{6,7},{7,6},{8,9},{9,8},{10,11... | collective-permute-start | bytes 786440 | tf_op jit(solution)/shard_map/ppermute | solution.py:325
  50.6 0.7 %copy-start.11 = (f32[8,128]{1,0:T(8,128)S(1)}, f32[8,128]{1,0:T(8,128)}, u32[]{:S(2)}) copy-start(f32[8,128]{1,0:T(8,128)} %copy-done.10) | copy-start | bytes 12292

commit v2 on v1

v2 whole, which is shorter than its diff:
```python
import functools

import jax
import jax.numpy as jnp
from jax import lax
from jax.experimental import pallas as pl
from jax.experimental.pallas import tpu as pltpu
from jax.sharding import PartitionSpec as P

HEADS = 8
BASE = 256
LANES = 128
ROW_TILE = 16
VMEM_BYTES = 28 * 1024 * 1024
ALL_VMEM_BYTES = 62 * 1024 * 1024


def round_up(value, step):
    return (value + step - 1) // step * step


def picks(index, count):
    place = lax.broadcasted_iota(jnp.int32, (index.shape[0], count), 1)
    return jnp.where(index == place, 1.0, 0.0).astype(jnp.bfloat16)


def pack_kernel(digits, ids_ref, vectors_ref, pack_ref):
    width = vectors_ref.shape[1]
    vectors = vectors_ref[...].astype(jnp.float32)
    ids = ids_ref[...]
    spans = [slice(start, start + LANES) for start in range(0, width, LANES)]
    rows = [vectors[:, span] for span in spans]
    for digit in range(digits):
        value = ((ids >> (8 * digit)) & (BASE - 1)).astype(jnp.float32)
        rows += [value[:, span] for span in spans]
    count = sum(row.shape[0] for row in rows)
    if pack_ref.shape[1] > count:
        rows.append(jnp.zeros((pack_ref.shape[1] - count, LANES), jnp.float32))
    pack_ref[...] = jnp.broadcast_to(jnp.concatenate(rows, axis=0).astype(jnp.bfloat16)[None], pack_ref.shape)


def earlier(count):
    row = lax.broadcasted_iota(jnp.int32, (count, count), 0)
    column = lax.broadcasted_iota(jnp.int32, (count, count), 1)
    return jnp.where(row < column, 1.0, 0.0).astype(jnp.bfloat16)


def items_kernel(items_hbm, items_ref, sems):
    part = items_ref.shape[0] // sems.shape[0]
    loads = []
    for p in range(sems.shape[0]):
        rows = pl.ds(p * part, part)
        loads.append(pltpu.make_async_copy(items_hbm.at[rows], items_ref.at[rows], sems.at[p]))
        loads[-1].start()
    for load in loads:
        load.wait()


def unpack(gathered_ref, n_lists, user_dev, digits, turn):
    pack_rows = gathered_ref.shape[0] // n_lists
    spans = pack_rows // (user_dev + digits)
    entry = lax.broadcasted_iota(jnp.int32, ((user_dev + digits) * n_lists, 1), 0)
    asker, field = (entry % n_lists) ^ turn, entry // n_lists
    fields = jnp.concatenate(
        [
            jnp.dot(
                picks(
                    asker * pack_rows
                    + jnp.where(field < user_dev, span * user_dev + field, field * spans + span),
                    n_lists * pack_rows,
                ),
                gathered_ref[...],
                preferred_element_type=jnp.float32,
            )
            for span in range(spans)
        ],
        axis=1,
    )
    ids = jnp.zeros((n_lists, fields.shape[1]), jnp.float32)
    for digit in range(digits):
        ids = ids + fields[(user_dev + digit) * n_lists : (user_dev + digit + 1) * n_lists] * float(BASE**digit)
    return fields[: user_dev * n_lists], ids


def asked(ids, base, items_loc, first, count):
    local = ids - base
    mine = (local >= 0.0) & (local < items_loc)
    hot = jnp.where(mine, 1.0, 0.0).astype(jnp.bfloat16)
    rank = jnp.dot(hot, earlier(ids.shape[1]), preferred_element_type=jnp.float32)
    rank = jnp.where(mine, rank, -1.0)
    place = lax.broadcasted_iota(jnp.int32, (count, ids.shape[1]), 0).astype(jnp.float32) + float(first)
    index = []
    for r in range(ids.shape[0]):
        picked = jnp.where(rank[r : r + 1] == place, local[r : r + 1] + 1.0, 0.0)
        index.append(jnp.sum(picked, axis=1, keepdims=True).astype(jnp.int32) - 1)
    return index


def slot_kernel(n_lists, items_loc, n_users, block, place_ref, ids_ref, slot_ref):
    ids = ids_ref[...]
    cands = ids.shape[1]
    bins = ids // items_loc
    mine = bins % n_users == place_ref[1]
    owner = bins // n_users
    lists = lax.broadcasted_iota(jnp.int32, (n_lists, cands), 0)
    hot = jnp.where((lists == owner) & mine, 1.0, 0.0)
    before = jnp.dot(hot.astype(jnp.bfloat16), earlier(cands), preferred_element_type=jnp.float32)
    rank = jnp.sum(before * hot, axis=0, keepdims=True)
    slot = owner.astype(jnp.float32) * block + rank
    slot_ref[...] = jnp.broadcast_to(jnp.where(mine, slot, -1.0), slot_ref.shape)


def pairs_kernel(n_parts, place_ref, length_ref, *refs):
    parts, (weight_ref, query_ref, keys_ref, values_ref, turned_ref) = refs[:n_parts], refs[n_parts:]
    history = jnp.concatenate([part[...] for part in parts], axis=0)
    pairs = jnp.dot(history, weight_ref[...], preferred_element_type=jnp.float32)
    heads, events, features = keys_ref.shape
    head_dim = features - ROW_TILE
    width = heads * head_dim
    hist_dev = events // n_parts
    event = lax.broadcasted_iota(jnp.int32, (events, ROW_TILE), 0)
    feature = lax.broadcasted_iota(jnp.int32, (events, ROW_TILE), 1)
    position = (place_ref[1] - event // hist_dev + n_parts) % n_parts * hist_dev + event % hist_dev
    mask = jnp.where((position >= length_ref[0]) & (feature == 0), -1e30, 0.0)
    for h in range(heads):
        keys = pairs[:, h * head_dim : (h + 1) * head_dim]
        keys_ref[h] = jnp.concatenate([keys, mask], axis=1).astype(jnp.bfloat16)
    values_ref[...] = jnp.transpose(pairs[:, width:]).astype(jnp.bfloat16)
    turned_ref[...] = jnp.transpose(query_ref[...].astype(jnp.float32)).astype(jnp.bfloat16)


def owner_kernel(n_lists, n_users, user_dev, digits, cap, scale, place_ref, gathered_ref, items_ref, *refs):
    out_hbm, out_ref, out_sems = refs
    items_loc, width = items_ref.shape
    vectors, ids = unpack(gathered_ref, n_lists, user_dev, digits, 0)
    base = ((place_ref[0] * n_users + place_ref[1]) * items_loc).astype(jnp.float32)
    index = asked(ids, base, items_loc, 0, cap)
    scores = lax.dot_general(
        vectors.astype(jnp.bfloat16),
        items_ref[...],
        (((1,), (1,)), ((), ())),
        preferred_element_type=jnp.float32,
    )
    scores = (scores * scale).astype(jnp.bfloat16)
    pieces = items_loc // width
    stacked = jnp.concatenate(
        [scores[:, piece * width : (piece + 1) * width] for piece in range(pieces)], axis=0
    )
    kept = out_ref.shape[1] - cap
    entry = lax.broadcasted_iota(jnp.int32, (n_lists * kept, 1), 0)
    wanted = jnp.where(entry % kept < pieces * user_dev, entry % kept * n_lists + entry // kept, -1)
    spread = jnp.dot(
        picks(wanted, stacked.shape[0]), stacked, preferred_element_type=jnp.float32
    ).astype(jnp.bfloat16)
    out_ref[:, cap:, :] = spread.reshape(n_lists, kept, width)
    step = max(1, 256 // cap)
    sends = []
    for number, first in enumerate(range(0, n_lists, step)):
        last = min(n_lists, first + step)
        rows = jnp.dot(
            picks(jnp.concatenate(index[first:last], axis=0), items_loc),
            items_ref[...],
            preferred_element_type=jnp.float32,
        ).astype(jnp.bfloat16)
        out_ref[first:last, :cap, :] = rows.reshape(last - first, cap, width)
        send = pltpu.make_async_copy(out_ref.at[first:last], out_hbm.at[first:last], out_sems.at[number])
        send.start()
        sends.append(send)
    for send in sends:
        send.wait()


def place_kernel(n_users, place_ref, slot_ref, fetched_ref, *refs):
    share_refs, scratch = refs[:-1], refs[-1]
    n_lists, block, width = fetched_ref.shape
    fetched = fetched_ref[...].reshape(n_lists * block, width)
    share = share_refs[0].shape[0]
    slot = jnp.transpose(slot_ref[...])[:, :1].astype(jnp.int32)
    scratch[...] = jnp.dot(
        picks(slot, fetched.shape[0]), fetched, preferred_element_type=jnp.float32
    ).astype(jnp.bfloat16)
    for shift, ref in enumerate(share_refs):
        start = (place_ref[1] + shift) % n_users * share
        ref[...] = scratch[pl.ds(pl.multiple_of(start, share), share), :]


def attend_kernel(n_parts, *refs):
    parts, (keys_ref, values_ref, turned_ref, out_weight_ref, out_ref) = refs[:n_parts], refs[n_parts:]
    heads, events, features = keys_ref.shape
    head_dim = features - ROW_TILE
    rows = parts[0][...]
    for part in parts[1:]:
        rows = rows + part[...]
    queries = lax.dot_general(
        turned_ref[...], rows, (((1,), (1,)), ((), ())), preferred_element_type=jnp.float32
    )
    queries = (queries * head_dim ** (-0.5)).astype(jnp.bfloat16)
    feature = lax.broadcasted_iota(jnp.int32, (ROW_TILE, rows.shape[0]), 0)
    one = jnp.where(feature == 0, 1.0, 0.0).astype(jnp.bfloat16)

    def score(h):
        query = jnp.concatenate([queries[h * head_dim : (h + 1) * head_dim], one], axis=0)
        return jnp.dot(keys_ref[h], query, preferred_element_type=jnp.float32)

    ahead = [score(h) for h in range(min(2, heads))]
    mixed = []
    for h in range(heads):
        if h + 2 < heads:
            ahead.append(score(h + 2))
        exponentials = jnp.exp(ahead[h] - jnp.max(ahead[h], axis=0, keepdims=True))
        total = jnp.sum(exponentials, axis=0, keepdims=True)
        span = slice(h * head_dim, (h + 1) * head_dim)
        head = jnp.dot(values_ref[span, :], exponentials.astype(jnp.bfloat16), preferred_element_type=jnp.float32)
        mixed.append(head / total)
    attended = jnp.transpose(jnp.concatenate(mixed, axis=0)).astype(jnp.bfloat16)
    out_ref[...] = jnp.dot(attended, out_weight_ref[...], preferred_element_type=jnp.float32).astype(jnp.bfloat16)


def expand_kernel(user_dev, pieces, cap, probes_ref, fetched_ref, out_hbm, out_ref, sems):
    n_lists, block, width = fetched_ref.shape
    kept = block - cap
    rows = n_lists * kept
    returned = fetched_ref[:, cap:, :].reshape(rows, width)
    count = out_ref.shape[0]
    probes = probes_ref[...].astype(jnp.float32)
    flat = jnp.concatenate([probes[u : u + 1] for u in range(user_dev)], axis=1)
    probe = jnp.transpose(jnp.broadcast_to(flat, (8, count)))[:, :1].astype(jnp.int32)
    user = lax.broadcasted_iota(jnp.int32, (count, 1), 0) // (count // user_dev)
    sends = []
    for piece in range(pieces):
        wanted = probe * kept + piece * user_dev + user
        span = pl.ds(piece * width, width)
        out_ref[:, span] = jnp.dot(picks(wanted, rows), returned, preferred_element_type=jnp.float32).astype(
            jnp.bfloat16
        )
        sends.append(pltpu.make_async_copy(out_ref.at[:, span], out_hbm.at[:, span], sems.at[piece]))
        sends[-1].start()
    for send in sends:
        send.wait()


SMEM = pl.BlockSpec(memory_space=pltpu.SMEM)
VMEM = pl.BlockSpec(memory_space=pltpu.VMEM)
HBM = pl.BlockSpec(memory_space=pltpu.HBM)
PARAMS = pltpu.CompilerParams(vmem_limit_bytes=VMEM_BYTES)


def shards(
    user_vectors,
    probe_lists,
    list_items,
    candidate_ids,
    history,
    history_lengths,
    query_weight,
    key_value_weight,
    out_weight,
):
    n_lists = lax.axis_size("lists")
    n_users = lax.axis_size("users")
    _, items_loc, width = list_items.shape
    user_dev, probes = probe_lists.shape
    _, cands = candidate_ids.shape
    bf16 = jnp.bfloat16
    cap = max(2, 3 * cands // (n_lists * n_users))
    cap = round_up(cap, ROW_TILE)
    kept = round_up(items_loc // width * user_dev, ROW_TILE)
    share = cands // n_users
    pieces = items_loc // width
    digits = 1
    while BASE**digits < n_lists * n_users * items_loc:
        digits += 1
    pack_rows = round_up((user_dev + digits) * (width // LANES), 8)
    line = lax.axis_index("lists").astype(jnp.int32)
    col = lax.axis_index("users").astype(jnp.int32)
    place_arg = jnp.stack([line, col])
    block = cap + kept

    flat_items = list_items.reshape(items_loc, width)
    pack = pl.pallas_call(
        functools.partial(pack_kernel, digits),
        out_shape=jax.ShapeDtypeStruct((n_lists, pack_rows, LANES), bf16),
        in_specs=[VMEM, VMEM],
        out_specs=VMEM,
        compiler_params=pltpu.CompilerParams(vmem_limit_bytes=ALL_VMEM_BYTES),
    )(candidate_ids, user_vectors)
    gathered = lax.all_to_all(pack, "lists", split_axis=0, concat_axis=0, tiled=True)
    gathered = gathered.reshape(n_lists * pack_rows, LANES)

    items = pl.pallas_call(
        items_kernel,
        out_shape=jax.ShapeDtypeStruct((items_loc, width), bf16),
        in_specs=[HBM],
        out_specs=VMEM,
        scratch_shapes=[pltpu.SemaphoreType.DMA((4,))],
        compiler_params=PARAMS,
    )(flat_items)
    gathered, items = lax.optimization_barrier((gathered, items))

    events = history.reshape(-1, width)
    hist = [events]
    for shift in range(1, n_users):
        hist.append(lax.ppermute(events, "users", [(i, (i + shift) % n_users) for i in range(n_users)]))
    total_events = n_users * events.shape[0]
    keys, values, turned = pl.pallas_call(
        functools.partial(pairs_kernel, n_users),
        out_shape=(
            jax.ShapeDtypeStruct((HEADS, total_events, width // HEADS + ROW_TILE), bf16),
            jax.ShapeDtypeStruct((width, total_events), bf16),
            jax.ShapeDtypeStruct((width, width), bf16),
        ),
        in_specs=[SMEM, SMEM] + [VMEM] * (n_users + 2),
        out_specs=(VMEM, VMEM, VMEM),
        compiler_params=PARAMS,
    )(place_arg, history_lengths, *hist, key_value_weight, query_weight)

    step = max(1, 256 // cap)
    answers = pl.pallas_call(
        functools.partial(owner_kernel, n_lists, n_users, user_dev, digits, cap, width ** (-0.5)),
        out_shape=jax.ShapeDtypeStruct((n_lists, block, width), bf16),
        in_specs=[SMEM, VMEM, VMEM],
        out_specs=pl.BlockSpec(memory_space=pl.ANY),
        scratch_shapes=[
            pltpu.VMEM((n_lists, block, width), bf16),
            pltpu.SemaphoreType.DMA((-(-n_lists // step),)),
        ],
        compiler_params=PARAMS,
    )(place_arg, gathered, items)
    fetched = lax.all_to_all(answers, "lists", split_axis=0, concat_axis=0, tiled=True)

    slot = pl.pallas_call(
        functools.partial(slot_kernel, n_lists, items_loc, n_users, block),
        out_shape=jax.ShapeDtypeStruct((8, cands), jnp.float32),
        in_specs=[SMEM, VMEM],
        out_specs=VMEM,
        compiler_params=PARAMS,
    )(place_arg, candidate_ids)
    fetched, slot, keys, values, turned = lax.optimization_barrier((fetched, slot, keys, values, turned))

    placed = pl.pallas_call(
        functools.partial(place_kernel, n_users),
        out_shape=tuple(jax.ShapeDtypeStruct((share, width), bf16) for _ in range(n_users)),
        in_specs=[SMEM, VMEM, VMEM],
        out_specs=tuple(VMEM for _ in range(n_users)),
        scratch_shapes=[pltpu.VMEM((cands, width), bf16)],
        compiler_params=PARAMS,
    )(place_arg, slot, fetched)
    parts = [placed[0]]
    for shift in range(1, n_users):
        parts.append(
            lax.ppermute(placed[shift], "users", [(i, (i + shift) % n_users) for i in range(n_users)])
        )
    ranked = pl.pallas_call(
        functools.partial(attend_kernel, n_users),
        out_shape=jax.ShapeDtypeStruct((share, width), bf16),
        in_specs=[VMEM] * (n_users + 4),
        out_specs=VMEM,
        compiler_params=PARAMS,
    )(*parts, keys, values, turned, out_weight)

    list_scores = pl.pallas_call(
        functools.partial(expand_kernel, user_dev, pieces, cap),
        out_shape=jax.ShapeDtypeStruct((user_dev * probes, items_loc), bf16),
        in_specs=[VMEM, VMEM],
        out_specs=pl.BlockSpec(memory_space=pl.ANY),
        scratch_shapes=[
            pltpu.VMEM((user_dev * probes, items_loc), bf16),
            pltpu.SemaphoreType.DMA((pieces,)),
        ],
        compiler_params=PARAMS,
    )(probe_lists, fetched)
    return (list_scores.reshape(user_dev, probes, items_loc), ranked.reshape(1, share, width))


def solution(mesh):
    placed = (
        P("lists", None),
        P("lists", None),
        P("lists", "users", None),
        P("lists", None),
        P("lists", "users", None),
        P("lists"),
        P(),
        P(),
        P(),
    )
    return jax.shard_map(
        shards,
        mesh=mesh,
        in_specs=placed,
        out_specs=(P("lists", None, "users"), P("lists", "users", None)),
        check_vma=False,
    )
```

time: 56.9 us -> 57.1 us (level)
  waiting for transfers between devices: 26 us -> 24.1 us
  Pallas kernels: 11.7 us -> 12.9 us
  local copies, waits for them, and re-layouts: 4.5 us -> 5.35 us
    all_to_all x1, waiting for transfers between devices: 19.6 us -> 18.3 us  [shards(): lax.all_to_all(answers, 'lists', split_axis=0, concat_axis=0, tiled=True)]
    pallas_call x1, Pallas kernels: 3.35 us -> 2.32 us  [shards(): pl.pallas_call(functools.partial(attend_kernel, n_users), out_shape=jax.S...]
    unnamed x26 -> x28, local copies, waits for them, and re-layouts: 4.5 us -> 5.35 us
    pallas_call x1, Pallas kernels: 3.8 us -> 4.37 us  [shards(): pl.pallas_call(functools.partial(owner_kernel, n_lists, n_users, user_dev...]
  transfers between devices with their start and end apart: 4 -> 4, of which waited for: 3 -> 2; matrix products, arithmetic and copies ran while one was open for 0% -> 0% of each run, Pallas kernels for 4% -> 6%
where the time goes in v2:
time: 57.1 us; the launch traced here: 56.1 us
  waiting for transfers between devices  24.1 us (42%)
  Pallas kernels  12.9 us (23%)
  starting transfers between devices  12.3 us (22%)
  local copies, waits for them, and re-layouts  5.35 us (9%)
  between operations  1.49 us (3%)
    all_to_all x1, waiting for transfers between devices, shards(): lax.all_to_all(answers, 'lists', split_axis=0, concat_axis=0, tiled=True)  18.3 us
    all_to_all x1, starting transfers between devices, shards(): lax.all_to_all(pack, 'lists', split_axis=0, concat_axis=0, tiled=True)  8.31 us
    all_to_all x1, waiting for transfers between devices, shards(): lax.all_to_all(pack, 'lists', split_axis=0, concat_axis=0, tiled=True)  5.79 us
    unnamed x28, local copies, waits for them, and re-layouts  5.35 us
    pallas_call x1, Pallas kernels, shards(): pl.pallas_call(functools.partial(owner_kernel, n_lists, n_users, user_dev...  4.37 us
    all_to_all x1, starting transfers between devices, shards(): lax.all_to_all(answers, 'lists', split_axis=0, concat_axis=0, tiled=True)  3.8 us
    pallas_call x1, Pallas kernels, shards(): pl.pallas_call(functools.partial(attend_kernel, n_users), out_shape=jax.S...  2.32 us
    pallas_call x1, Pallas kernels, shards(): pl.pallas_call(functools.partial(place_kernel, n_users), out_shape=tuple(...  1.59 us
  transfers between devices with their start and end apart: 4, of which 2 were waited for; matrix products, arithmetic and copies ran while one was open for 0% of the time, Pallas kernels for 6%

profile of v2, /device:TPU:0, one launch (start us, length us, event | category | flops | bytes accessed | tf_op | source)
XLA Modules:
  0.0 56.1 jit_solution(16758360854279435410)
XLA Ops:
  0.6 1.4 %shard_map.104 = bf16[16,24,128]{2,1,0:T(8,128)(2,1)} custom-call(s32[1,512]{1,0:T(1,128)} %ids_ref.3, bf16[4,512]{1,0:T(4,128)(2,1)} %vectors_ref.1), custom_call_target="tpu_custom_call" | custom-call | tf_op jit(solution)/shard_map/pallas_call | solution.py:280
  2.0 8.3 %all-to-all-start = ((bf16[16,24,128]{2,1,0:T(8,128)(2,1)}), bf16[16,24,128]{2,1,0:T(8,128)(2,1)S(1)}, u32[]{:S(2)}, u32[]{:S(2)}) async-start(bf16[16,24,128]{2,1,0:T(8,128)(2,1)} %shard_map.104), calls=%async_computation | async-start | bytes 196608 | tf_op jit(solution)/shard_map/all_to_all | solution.py:287
  10.3 0.0 copy-start
  10.3 1.6 %copy-done = bf16[1,2048,512]{2,1,0:T(8,128)(2,1)S(1)} copy-done((bf16[1,2048,512]{2,1,0:T(8,128)(2,1)S(1)}, bf16[1,2048,512]{2,1,0:T(8,128)(2,1)}, u32[]{:S(2)}) %copy-start) | copy-done | bytes 2097176
  11.9 0.2 shard_map.105.items_ref
  12.1 0.1 pad_add_fusion.place_ref
  12.2 5.8 %all-to-all-done = bf16[16,24,128]{2,1,0:T(8,128)(2,1)S(1)} async-done(((bf16[16,24,128]{2,1,0:T(8,128)(2,1)}), bf16[16,24,128]{2,1,0:T(8,128)(2,1)S(1)}, u32[]{:S(2)}, u32[]{:S(2)}) %all-to-all-start) | async-done | bytes 98336 | tf_op jit(solution)/shard_map/all_to_all | solution.py:287
  18.0 4.4 %shard_map.106 = bf16[16,64,512]{2,1,0:T(8,128)(2,1)} custom-call(s32[2]{0:T(128)S(1)} %pad_add_fusion.place_ref, bf16[384,128]{1,0:T(8,128)(2,1)S(1)} %bitcast.8, bf16[2048,512]{1,0:T(8,128)(2,1)S(1)} %shard_map.105.items_ref), custom_call_target="tpu_custom_call" | custom-call | tf_op jit(solution)/shard_map/pallas_call | solution.py:318
  22.4 0.0 copy-start.2
  22.4 3.8 %all-to-all-start.1 = ((bf16[16,64,512]{2,1,0:T(8,128)(2,1)}), bf16[16,64,512]{2,1,0:T(8,128)(2,1)S(1)}, u32[]{:S(2)}, u32[]{:S(2)}) async-start(bf16[16,64,512]{2,1,0:T(8,128)(2,1)} %shard_map.106), calls=%async_computation.1 | async-start | bytes 2097152 | tf_op jit(solution)/shard_map/all_to_all | solution.py:329
  26.2 0.0 copy-done.8
  26.2 0.1 collective-permute-start
  26.3 0.0 copy-done.10
  26.3 0.0 copy-done.9
  26.3 0.7 %shard_map.107.slot_ref = f32[8,512]{1,0:T(8,128)S(1)} custom-call(s32[2]{0:T(128)S(1)} %pad_add_fusion.place_ref, s32[1,512]{1,0:T(1,128)S(1)} %copy-done.9), custom_call_target="tpu_custom_call" | custom-call | tf_op jit(solution)/shard_map/pallas_call | solution.py:331
  27.7 0.0 copy-start.3
  27.7 0.0 collective-permute-done.refs_1_
  27.7 0.0 copy-done.1
  27.7 0.0 copy-start.11
  27.7 0.7 %copy-done.11 = s32[2]{0:T(128)S(1)} copy-done((s32[2]{0:T(128)S(1)}, s32[2]{0:T(128)}, u32[]{:S(2)}) %copy-start.11) | copy-done | bytes 32
  28.4 1.1 %shard_map.108 = (bf16[8,256,80]{2,1,0:T(8,128)(2,1)S(1)}, bf16[512,256]{1,0:T(8,128)(2,1)S(1)}, bf16[512,512]{1,0:T(8,128)(2,1)S(1)}) custom-call(s32[2]{0:T(128)S(1)} %copy-done.11, s32[1]{0:T(128)S(6)} %copy.11.length_ref, bf16[128,512]{1,0:T(8,128)(2,1)S(1)} %bitcast.10, bf16[128,512]{1,0:T(8,128)(2,1)S(1)} %collective-permute-done.refs_1_, ...), custom_call_target="tpu_custom_call" | custom-call | tf_op jit(solution)/shard_map/pallas_call | solution.py:305
  29.6 0.8 %copy-done.4 = bf16[8,256,80]{2,1,0:T(8,128)(2,1)} copy-done((bf16[8,256,80]{2,1,0:T(8,128)(2,1)}, bf16[8,256,80]{2,1,0:T(8,128)(2,1)S(1)}, u32[]{:S(2)}) %copy-start.4) | copy-done | bytes 327704
  30.4 0.8 %copy-done.6 = bf16[512,512]{1,0:T(8,128)(2,1)} copy-done((bf16[512,512]{1,0:T(8,128)(2,1)}, bf16[512,512]{1,0:T(8,128)(2,1)S(1)}, u32[]{:S(2)}) %copy-start.6) | copy-done | bytes 524312
  31.2 18.3 %all-to-all-done.1.fetched_ref = bf16[16,64,512]{2,1,0:T(8,128)(2,1)S(1)} async-done(((bf16[16,64,512]{2,1,0:T(8,128)(2,1)}), bf16[16,64,512]{2,1,0:T(8,128)(2,1)S(1)}, u32[]{:S(2)}, u32[]{:S(2)}) %all-to-all-start.1) | async-done | bytes 1048608 | tf_op jit(solution)/shard_map/all_to_all | solution.py:329
  49.4 0.7 %copy-done.12 = s32[2]{0:T(128)S(1)} copy-done((s32[2]{0:T(128)S(1)}, s32[2]{0:T(128)}, u32[]{:S(2)}) %copy-start.12) | copy-done | bytes 32
  50.2 1.6 %shard_map.110 = (bf16[256,512]{1,0:T(8,128)(2,1)S(1)}, bf16[256,512]{1,0:T(8,128)(2,1)S(1)}) custom-call(s32[2]{0:T(128)S(1)} %copy-done.12, f32[8,512]{1,0:T(8,128)S(1)} %shard_map.107.slot_ref, bf16[16,64,512]{2,1,0:T(8,128)(2,1)S(1)} %all-to-all-done.1.fetched_ref), custom_call_target="tpu_custom_call" | custom-call | tf_op jit(solution)/shard_map/pallas_call | solution.py:340
  51.8 0.1 collective-permute-start.1
  51.9 0.0 copy-start.13
  51.9 0.7 %copy-done.13 = s32[4,32]{1,0:T(4,128)S(1)} copy-done((s32[4,32]{1,0:T(4,128)S(1)}, s32[4,32]{1,0:T(4,128)}, u32[]{:S(2)}) %copy-start.13) | copy-done | bytes 536
  52.5 1.2 %shard_map.109 = bf16[128,2048]{1,0:T(8,128)(2,1)} custom-call(s32[4,32]{1,0:T(4,128)S(1)} %copy-done.13, bf16[16,64,512]{2,1,0:T(8,128)(2,1)S(1)} %all-to-all-done.1.fetched_ref), custom_call_target="tpu_custom_call" | custom-call | tf_op jit(solution)/shard_map/pallas_call | solution.py:361
  53.8 0.0 collective-permute-done.1.refs_1_
  53.8 2.3 %shard_map.111 = bf16[256,512]{1,0:T(8,128)(2,1)} custom-call(bf16[256,512]{1,0:T(8,128)(2,1)S(1)} %get-tuple-element.21.refs_0_, bf16[256,512]{1,0:T(8,128)(2,1)S(1)} %collective-permute-done.1.refs_1_, bf16[8,256,80]{2,1,0:T(8,128)(2,1)S(1)} %copy-done.5, bf16[512,256]{1,0:T(8,128)(2,1)S(1)} %get-tuple-element.24.refs_3_, bf16[512,512]{1,0:T(8,128)(2,1)S(1)} %copy-done.7, ...), custom_call_target="tpu_custom_call" | custom-call | tf_op jit(solution)/shard_map/pallas_call | solution.py:353
  (13 shorter events, 0.0 us)
Async XLA Ops:
  2.0 16.0 %all-to-all-start = ((bf16[16,24,128]{2,1,0:T(8,128)(2,1)}), bf16[16,24,128]{2,1,0:T(8,128)(2,1)S(1)}, u32[]{:S(2)}, u32[]{:S(2)}) async-start(bf16[16,24,128]{2,1,0:T(8,128)(2,1)} %shard_map.104), calls=%async_computation | async-start | bytes 196608 | tf_op jit(solution)/shard_map/all_to_all | solution.py:287
  10.3 1.6 %copy-start = (bf16[1,2048,512]{2,1,0:T(8,128)(2,1)S(1)}, bf16[1,2048,512]{2,1,0:T(8,128)(2,1)}, u32[]{:S(2)}) copy-start(bf16[1,2048,512]{2,1,0:T(8,128)(2,1)} %param.11) | copy-start | bytes 6291460
  12.2 14.1 %copy-start.10 = (s32[2]{0:T(128)}, s32[2]{0:T(128)S(1)}, u32[]{:S(2)}) copy-start(s32[2]{0:T(128)S(1)} %pad_add_fusion.place_ref) | copy-start | bytes 28
  18.0 8.2 %copy-start.8 = (bf16[1,128,512]{2,1,0:T(8,128)(2,1)S(1)}, bf16[1,128,512]{2,1,0:T(8,128)(2,1)}, u32[]{:S(2)}) copy-start(bf16[1,128,512]{2,1,0:T(8,128)(2,1)} %param.13) | copy-start | bytes 393220
  18.0 8.3 %copy-start.9 = (s32[1,512]{1,0:T(1,128)S(1)}, s32[1,512]{1,0:T(1,128)}, u32[]{:S(2)}) copy-start(s32[1,512]{1,0:T(1,128)} %ids_ref.3) | copy-start | bytes 6148
  18.0 9.7 %copy-start.1 = (bf16[512,1024]{1,0:T(8,128)(2,1)S(1)}, bf16[512,1024]{1,0:T(8,128)(2,1)}, u32[]{:S(2)}) copy-start(bf16[512,1024]{1,0:T(8,128)(2,1)} %refs_2_.1) | copy-start | bytes 3145732
  22.4 5.4 %copy-start.2 = (bf16[512,512]{1,0:T(8,128)(2,1)S(1)}, bf16[512,512]{1,0:T(8,128)(2,1)}, u32[]{:S(2)}) copy-start(bf16[512,512]{1,0:T(8,128)(2,1)} %refs_3_.1) | copy-start | bytes 1572868
  22.4 27.1 %all-to-all-start.1 = ((bf16[16,64,512]{2,1,0:T(8,128)(2,1)}), bf16[16,64,512]{2,1,0:T(8,128)(2,1)S(1)}, u32[]{:S(2)}, u32[]{:S(2)}) async-start(bf16[16,64,512]{2,1,0:T(8,128)(2,1)} %shard_map.106), calls=%async_computation.1 | async-start | bytes 2097152 | tf_op jit(solution)/shard_map/all_to_all | solution.py:329
  26.2 1.5 %collective-permute-start = (bf16[128,512]{1,0:T(8,128)(2,1)S(1)}, bf16[128,512]{1,0:T(8,128)(2,1)S(1)}, u32[]{:S(2)}, u32[]{:S(2)}) collective-permute-start(bf16[128,512]{1,0:T(8,128)(2,1)S(1)} %bitcast.9), channel_id=1, source_target_pairs={{0,1},{1,0},{2,3},{3,2},{4,5},{5,4},{6,7},{7,6},{8,9},{9,8},{10,11... | collective-permute-start | bytes 393224 | tf_op jit(solution)/shard_map/ppermute | solution.py:303
  27.7 26.1 %copy-start.3 = (bf16[512,512]{1,0:T(8,128)(2,1)S(1)}, bf16[512,512]{1,0:T(8,128)(2,1)}, u32[]{:S(2)}) copy-start(bf16[512,512]{1,0:T(8,128)(2,1)} %refs_5_.1) | copy-start | bytes 1572868
  27.7 0.7 %copy-start.11 = (s32[2]{0:T(128)S(1)}, s32[2]{0:T(128)}, u32[]{:S(2)}) copy-start(s32[2]{0:T(128)} %copy-done.10) | copy-start | bytes 28
  29.5 0.8 %copy-start.4 = (bf16[8,256,80]{2,1,0:T(8,128)(2,1)}, bf16[8,256,80]{2,1,0:T(8,128)(2,1)S(1)}, u32[]{:S(2)}) copy-start(bf16[8,256,80]{2,1,0:T(8,128)(2,1)S(1)} %get-tuple-element.23.refs_2_) | copy-start | bytes 983044
  30.3 0.8 %copy-start.6 = (bf16[512,512]{1,0:T(8,128)(2,1)}, bf16[512,512]{1,0:T(8,128)(2,1)S(1)}, u32[]{:S(2)}) copy-start(bf16[512,512]{1,0:T(8,128)(2,1)S(1)} %get-tuple-element.25.refs_4_) | copy-start | bytes 1572868
  49.4 4.3 %copy-start.5 = (bf16[8,256,80]{2,1,0:T(8,128)(2,1)S(1)}, bf16[8,256,80]{2,1,0:T(8,128)(2,1)}, u32[]{:S(2)}) copy-start(bf16[8,256,80]{2,1,0:T(8,128)(2,1)} %copy-done.4) | copy-start | bytes 983044
  49.4 4.4 %copy-start.7 = (bf16[512,512]{1,0:T(8,128)(2,1)S(1)}, bf16[512,512]{1,0:T(8,128)(2,1)}, u32[]{:S(2)}) copy-start(bf16[512,512]{1,0:T(8,128)(2,1)} %copy-done.6) | copy-start | bytes 1572868
  49.4 0.7 %copy-start.12 = (s32[2]{0:T(128)S(1)}, s32[2]{0:T(128)}, u32[]{:S(2)}) copy-start(s32[2]{0:T(128)} %copy-done.10) | copy-start | bytes 28
  51.8 2.0 %collective-permute-start.1 = (bf16[256,512]{1,0:T(8,128)(2,1)S(1)}, bf16[256,512]{1,0:T(8,128)(2,1)S(1)}, u32[]{:S(2)}, u32[]{:S(2)}) collective-permute-start(bf16[256,512]{1,0:T(8,128)(2,1)S(1)} %get-tuple-element.22), channel_id=1, source_target_pairs={{0,1},{1,0},{2,3},{3,2},{4,5},{5,4},{6,7},{7,6},{8,9},{9,8},{10,11... | collective-permute-start | bytes 786440 | tf_op jit(solution)/shard_map/ppermute | solution.py:351
  51.9 0.7 %copy-start.13 = (s32[4,32]{1,0:T(4,128)S(1)}, s32[4,32]{1,0:T(4,128)}, u32[]{:S(2)}) copy-start(s32[4,32]{1,0:T(4,128)} %probes_ref.1) | copy-start | bytes 1540

commit v3 on v2

--- a/solution.py
+++ b/solution.py
@@ -43,17 +43,6 @@
     row = lax.broadcasted_iota(jnp.int32, (count, count), 0)
     column = lax.broadcasted_iota(jnp.int32, (count, count), 1)
     return jnp.where(row < column, 1.0, 0.0).astype(jnp.bfloat16)
-
-
-def items_kernel(items_hbm, items_ref, sems):
-    part = items_ref.shape[0] // sems.shape[0]
-    loads = []
-    for p in range(sems.shape[0]):
-        rows = pl.ds(p * part, part)
-        loads.append(pltpu.make_async_copy(items_hbm.at[rows], items_ref.at[rows], sems.at[p]))
-        loads[-1].start()
-    for load in loads:
-        load.wait()
 
 
 def unpack(gathered_ref, n_lists, user_dev, digits, turn):
@@ -96,21 +85,32 @@
     return index
 
 
-def slot_kernel(n_lists, items_loc, n_users, block, place_ref, ids_ref, slot_ref):
+def early_kernel(n_lists, n_users, block, col_ref, ids_ref, probes_ref, items_hbm, known_ref, items_ref, sems):
+    items_loc = items_ref.shape[0]
+    part = items_loc // sems.shape[0]
+    loads = []
+    for p in range(sems.shape[0]):
+        span = pl.ds(p * part, part)
+        loads.append(pltpu.make_async_copy(items_hbm.at[span], items_ref.at[span], sems.at[p]))
+        loads[-1].start()
     ids = ids_ref[...]
     cands = ids.shape[1]
     bins = ids // items_loc
-    mine = bins % n_users == place_ref[1]
+    mine = bins % n_users == col_ref[0]
     owner = bins // n_users
     lists = lax.broadcasted_iota(jnp.int32, (n_lists, cands), 0)
     hot = jnp.where((lists == owner) & mine, 1.0, 0.0)
     before = jnp.dot(hot.astype(jnp.bfloat16), earlier(cands), preferred_element_type=jnp.float32)
     rank = jnp.sum(before * hot, axis=0, keepdims=True)
-    slot = owner.astype(jnp.float32) * block + rank
-    slot_ref[...] = jnp.broadcast_to(jnp.where(mine, slot, -1.0), slot_ref.shape)
-
-
-def pairs_kernel(n_parts, place_ref, length_ref, *refs):
+    slot = jnp.where(mine, owner.astype(jnp.float32) * block + rank, -1.0)
+    probes = probes_ref[...].astype(jnp.float32)
+    known = jnp.concatenate([slot] + [probes[u : u + 1] for u in range(probes.shape[0])], axis=1)
+    known_ref[...] = jnp.broadcast_to(known, known_ref.shape)
+    for load in loads:
+        load.wait()
+
+
+def pairs_kernel(n_parts, col_ref, length_ref, *refs):
     parts, (weight_ref, query_ref, keys_ref, values_ref, turned_ref) = refs[:n_parts], refs[n_parts:]
     history = jnp.concatenate([part[...] for part in parts], axis=0)
     pairs = jnp.dot(history, weight_ref[...], preferred_element_type=jnp.float32)
@@ -120,7 +120,7 @@
     hist_dev = events // n_parts
     event = lax.broadcasted_iota(jnp.int32, (events, ROW_TILE), 0)
     feature = lax.broadcasted_iota(jnp.int32, (events, ROW_TILE), 1)
-    position = (place_ref[1] - event // hist_dev + n_parts) % n_parts * hist_dev + event % hist_dev
+    position = (col_ref[0] - event // hist_dev + n_parts) % n_parts * hist_dev + event % hist_dev
     mask = jnp.where((position >= length_ref[0]) & (feature == 0), -1e30, 0.0)
     for h in range(heads):
         keys = pairs[:, h * head_dim : (h + 1) * head_dim]
@@ -129,12 +129,11 @@
     turned_ref[...] = jnp.transpose(query_ref[...].astype(jnp.float32)).astype(jnp.bfloat16)
 
 
-def owner_kernel(n_lists, n_users, user_dev, digits, cap, scale, place_ref, gathered_ref, items_ref, *refs):
+def owner_kernel(n_lists, user_dev, digits, cap, scale, base_ref, gathered_ref, items_ref, *refs):
     out_hbm, out_ref, out_sems = refs
     items_loc, width = items_ref.shape
     vectors, ids = unpack(gathered_ref, n_lists, user_dev, digits, 0)
-    base = ((place_ref[0] * n_users + place_ref[1]) * items_loc).astype(jnp.float32)
-    index = asked(ids, base, items_loc, 0, cap)
+    index = asked(ids, base_ref[0].astype(jnp.float32), items_loc, 0, cap)
     scores = lax.dot_general(
         vectors.astype(jnp.bfloat16),
         items_ref[...],
@@ -170,17 +169,17 @@
         send.wait()
 
 
-def place_kernel(n_users, place_ref, slot_ref, fetched_ref, *refs):
+def place_kernel(n_users, col_ref, known_ref, fetched_ref, *refs):
     share_refs, scratch = refs[:-1], refs[-1]
     n_lists, block, width = fetched_ref.shape
     fetched = fetched_ref[...].reshape(n_lists * block, width)
     share = share_refs[0].shape[0]
-    slot = jnp.transpose(slot_ref[...])[:, :1].astype(jnp.int32)
+    slot = jnp.transpose(known_ref[:, : share * n_users])[:, :1].astype(jnp.int32)
     scratch[...] = jnp.dot(
         picks(slot, fetched.shape[0]), fetched, preferred_element_type=jnp.float32
     ).astype(jnp.bfloat16)
     for shift, ref in enumerate(share_refs):
-        start = (place_ref[1] + shift) % n_users * share
+        start = (col_ref[0] + shift) % n_users * share
         ref[...] = scratch[pl.ds(pl.multiple_of(start, share), share), :]
 
 
@@ -216,15 +215,14 @@
     out_ref[...] = jnp.dot(attended, out_weight_ref[...], preferred_element_type=jnp.float32).astype(jnp.bfloat16)
 
 
-def expand_kernel(user_dev, pieces, cap, probes_ref, fetched_ref, out_hbm, out_ref, sems):
+def expand_kernel(user_dev, pieces, cap, known_ref, fetched_ref, out_hbm, out_ref, sems):
     n_lists, block, width = fetched_ref.shape
     kept = block - cap
     rows = n_lists * kept
     returned = fetched_ref[:, cap:, :].reshape(rows, width)
     count = out_ref.shape[0]
-    probes = probes_ref[...].astype(jnp.float32)
-    flat = jnp.concatenate([probes[u : u + 1] for u in range(user_dev)], axis=1)
-    probe = jnp.transpose(jnp.broadcast_to(flat, (8, count)))[:, :1].astype(jnp.int32)
+    first = known_ref.shape[1] - count
+    probe = jnp.transpose(known_ref[:, first:])[:, :1].astype(jnp.int32)
     user = lax.broadcasted_iota(jnp.int32, (count, 1), 0) // (count // user_dev)
     sends = []
     for piece in range(pieces):
@@ -273,7 +271,8 @@
     pack_rows = round_up((user_dev + digits) * (width // LANES), 8)
     line = lax.axis_index("lists").astype(jnp.int32)
     col = lax.axis_index("users").astype(jnp.int32)
-    place_arg = jnp.stack([line, col])
+    col_arg = col.reshape(1)
+    base_arg = ((line * n_users + col) * items_loc).reshape(1)
     block = cap + kept
 
     flat_items = list_items.reshape(items_loc, width)
@@ -287,15 +286,18 @@
     gathered = lax.all_to_all(pack, "lists", split_axis=0, concat_axis=0, tiled=True)
     gathered = gathered.reshape(n_lists * pack_rows, LANES)
 
-    items = pl.pallas_call(
-        items_kernel,
-        out_shape=jax.ShapeDtypeStruct((items_loc, width), bf16),
-        in_specs=[HBM],
-        out_specs=VMEM,
+    known, items = pl.pallas_call(
+        functools.partial(early_kernel, n_lists, n_users, block),
+        out_shape=(
+            jax.ShapeDtypeStruct((8, cands + user_dev * probes), jnp.float32),
+            jax.ShapeDtypeStruct((items_loc, width), bf16),
+        ),
+        in_specs=[SMEM, VMEM, VMEM, HBM],
+        out_specs=(VMEM, VMEM),
         scratch_shapes=[pltpu.SemaphoreType.DMA((4,))],
         compiler_params=PARAMS,
-    )(flat_items)
-    gathered, items = lax.optimization_barrier((gathered, items))
+    )(col_arg, candidate_ids, probe_lists, flat_items)
+    gathered, known, items = lax.optimization_barrier((gathered, known, items))
 
     events = history.reshape(-1, width)
     hist = [events]
@@ -312,11 +314,11 @@
         in_specs=[SMEM, SMEM] + [VMEM] * (n_users + 2),
         out_specs=(VMEM, VMEM, VMEM),
         compiler_params=PARAMS,
-    )(place_arg, history_lengths, *hist, key_value_weight, query_weight)
+    )(col_arg, history_lengths, *hist, key_value_weight, query_weight)
 
     step = max(1, 256 // cap)
     answers = pl.pallas_call(
-        functools.partial(owner_kernel, n_lists, n_users, user_dev, digits, cap, width ** (-0.5)),
+        functools.partial(owner_kernel, n_lists, user_dev, digits, cap, width ** (-0.5)),
         out_shape=jax.ShapeDtypeStruct((n_lists, block, width), bf16),
         in_specs=[SMEM, VMEM, VMEM],
         out_specs=pl.BlockSpec(memory_space=pl.ANY),
@@ -325,17 +327,10 @@
             pltpu.SemaphoreType.DMA((-(-n_lists // step),)),
         ],
         compiler_params=PARAMS,
-    )(place_arg, gathered, items)
+    )(base_arg, gathered, items)
     fetched = lax.all_to_all(answers, "lists", split_axis=0, concat_axis=0, tiled=True)
 
-    slot = pl.pallas_call(
-        functools.partial(slot_kernel, n_lists, items_loc, n_users, block),
-        out_shape=jax.ShapeDtypeStruct((8, cands), jnp.float32),
-        in_specs=[SMEM, VMEM],
-        out_specs=VMEM,
-        compiler_params=PARAMS,
-    )(place_arg, candidate_ids)
-    fetched, slot, keys, values, turned = lax.optimization_barrier((fetched, slot, keys, values, turned))
+    fetched, keys, values, turned = lax.optimization_barrier((fetched, keys, values, turned))
 
     placed = pl.pallas_call(
         functools.partial(place_kernel, n_users),
@@ -344,7 +339,7 @@
         out_specs=tuple(VMEM for _ in range(n_users)),
         scratch_shapes=[pltpu.VMEM((cands, width), bf16)],
         compiler_params=PARAMS,
-    )(place_arg, slot, fetched)
+    )(col_arg, known, fetched)
     parts = [placed[0]]
     for shift in range(1, n_users):
         parts.append(
@@ -368,7 +363,7 @@
             pltpu.SemaphoreType.DMA((pieces,)),
         ],
         compiler_params=PARAMS,
-    )(probe_lists, fetched)
+    )(known, fetched)
     return (list_scores.reshape(user_dev, probes, items_loc), ranked.reshape(1, share, width))
 
 

time: 57.1 us -> 55.6 us (0.974)
  Pallas kernels: 12.9 us -> 10.7 us
  local copies, waits for them, and re-layouts: 5.35 us -> 6 us
    all_to_all x1, waiting for transfers between devices: 5.79 us -> 3.7 us  [shards(): lax.all_to_all(pack, 'lists', split_axis=0, concat_axis=0, tiled=True)]
    all_to_all x1, waiting for transfers between devices: 18.3 us -> 19.8 us  [shards(): lax.all_to_all(answers, 'lists', split_axis=0, concat_axis=0, tiled=True)]
    pallas_call x3 -> x2, Pallas kernels: 5.29 us -> 4.21 us  [the longest x1 3.82 us: shards(): pl.pallas_call(functools.partial(owner_kernel, n_lists, user_dev, digits,...]
    ppermute x1, waiting for transfers between devices: 0.01 us -> 0.68 us  [shards(): lax.ppermute(events, 'users', [(i, (i + shift) % n_users) for i in range(...]
    unnamed x28 -> x26, local copies, waits for them, and re-layouts: 5.35 us -> 6 us
  transfers between devices with their start and end apart: 4 -> 4, of which waited for: 2 -> 4; matrix products, arithmetic and copies ran while one was open for 0% -> 0% of each run, Pallas kernels for 6% -> 4%
where the time goes in v3:
time: 55.6 us; the launch traced here: 54.9 us
  waiting for transfers between devices  24.6 us (44%)
  starting transfers between devices  12.3 us (22%)
  Pallas kernels  10.7 us (19%)
  local copies, waits for them, and re-layouts  6 us (11%)
  between operations  1.42 us (3%)
    all_to_all x1, waiting for transfers between devices, shards(): lax.all_to_all(answers, 'lists', split_axis=0, concat_axis=0, tiled=True)  19.8 us
    all_to_all x1, starting transfers between devices, shards(): lax.all_to_all(pack, 'lists', split_axis=0, concat_axis=0, tiled=True)  8.31 us
    unnamed x26, local copies, waits for them, and re-layouts  6 us
    pallas_call x1, Pallas kernels, shards(): pl.pallas_call(functools.partial(owner_kernel, n_lists, user_dev, digits,...  3.82 us
    all_to_all x1, starting transfers between devices, shards(): lax.all_to_all(answers, 'lists', split_axis=0, concat_axis=0, tiled=True)  3.8 us
    all_to_all x1, waiting for transfers between devices, shards(): lax.all_to_all(pack, 'lists', split_axis=0, concat_axis=0, tiled=True)  3.7 us
    pallas_call x1, Pallas kernels, shards(): pl.pallas_call(functools.partial(attend_kernel, n_users), out_shape=jax.S...  2.33 us
    pallas_call x1, Pallas kernels, shards(): pl.pallas_call(functools.partial(pack_kernel, digits), out_shape=jax.Shap...  1.36 us
  transfers between devices with their start and end apart: 4, of which 4 were waited for; matrix products, arithmetic and copies ran while one was open for 0% of the time, Pallas kernels for 4%

profile of v3, /device:TPU:0, one launch (start us, length us, event | category | flops | bytes accessed | tf_op | source)
XLA Modules:
  0.0 54.9 jit_solution(810146087842715947)
XLA Ops:
  0.6 1.4 %shard_map.104 = bf16[16,24,128]{2,1,0:T(8,128)(2,1)} custom-call(s32[1,512]{1,0:T(1,128)} %ids_ref.3, bf16[4,512]{1,0:T(4,128)(2,1)} %vectors_ref.1), custom_call_target="tpu_custom_call" | custom-call | tf_op jit(solution)/shard_map/pallas_call | solution.py:279
  2.0 8.3 %all-to-all-start = ((bf16[16,24,128]{2,1,0:T(8,128)(2,1)}), bf16[16,24,128]{2,1,0:T(8,128)(2,1)S(1)}, u32[]{:S(2)}, u32[]{:S(2)}) async-start(bf16[16,24,128]{2,1,0:T(8,128)(2,1)} %shard_map.104), calls=%async_computation | async-start | bytes 196608 | tf_op jit(solution)/shard_map/all_to_all | solution.py:286
  10.3 0.0 copy-start
  10.3 1.6 %copy-done = bf16[1,2048,512]{2,1,0:T(8,128)(2,1)S(1)} copy-done((bf16[1,2048,512]{2,1,0:T(8,128)(2,1)S(1)}, bf16[1,2048,512]{2,1,0:T(8,128)(2,1)}, u32[]{:S(2)}) %copy-start) | copy-done | bytes 2097176
  11.9 0.7 %copy-done.11 = s32[1,512]{1,0:T(1,128)S(1)} copy-done((s32[1,512]{1,0:T(1,128)S(1)}, s32[1,512]{1,0:T(1,128)}, u32[]{:S(2)}) %copy-start.11) | copy-done | bytes 2072
  12.6 0.7 %copy-done.12 = s32[4,32]{1,0:T(4,128)S(1)} copy-done((s32[4,32]{1,0:T(4,128)S(1)}, s32[4,32]{1,0:T(4,128)}, u32[]{:S(2)}) %copy-start.12) | copy-done | bytes 536
  13.3 0.4 shard_map.105
  13.7 0.0 copy-start.9
  13.7 0.6 %copy-done.9 = f32[8,640]{1,0:T(8,128)} copy-done((f32[8,640]{1,0:T(8,128)}, f32[8,640]{1,0:T(8,128)S(1)}, u32[]{:S(2)}) %copy-start.9) | copy-done | bytes 20504
  14.3 3.7 %all-to-all-done = bf16[16,24,128]{2,1,0:T(8,128)(2,1)S(1)} async-done(((bf16[16,24,128]{2,1,0:T(8,128)(2,1)}), bf16[16,24,128]{2,1,0:T(8,128)(2,1)S(1)}, u32[]{:S(2)}, u32[]{:S(2)}) %all-to-all-start) | async-done | bytes 98336 | tf_op jit(solution)/shard_map/all_to_all | solution.py:286
  18.0 3.8 %shard_map.106 = bf16[16,64,512]{2,1,0:T(8,128)(2,1)} custom-call(s32[1]{0:T(128)} %bitcast.3.base_ref, bf16[384,128]{1,0:T(8,128)(2,1)S(1)} %bitcast.8, bf16[2048,512]{1,0:T(8,128)(2,1)S(1)} %get-tuple-element.20.items_ref), custom_call_target="tpu_custom_call" | custom-call | tf_op jit(solution)/shard_map/pallas_call | solution.py:320
  21.8 0.0 copy-start.2
  21.8 3.8 %all-to-all-start.1 = ((bf16[16,64,512]{2,1,0:T(8,128)(2,1)}), bf16[16,64,512]{2,1,0:T(8,128)(2,1)S(1)}, u32[]{:S(2)}, u32[]{:S(2)}) async-start(bf16[16,64,512]{2,1,0:T(8,128)(2,1)} %shard_map.106), calls=%async_computation.1 | async-start | bytes 2097152 | tf_op jit(solution)/shard_map/all_to_all | solution.py:331
  25.6 0.0 copy-done.8
  25.6 0.1 collective-permute-start
  26.4 0.0 copy-start.3
  26.4 0.7 %collective-permute-done.refs_1_ = bf16[128,512]{1,0:T(8,128)(2,1)S(1)} collective-permute-done((bf16[128,512]{1,0:T(8,128)(2,1)S(1)}, bf16[128,512]{1,0:T(8,128)(2,1)S(1)}, u32[]{:S(2)}, u32[]{:S(2)}) %collective-permute-start) | collective-permute-done | bytes 131104 | tf_op jit(solution)/shard_map/ppermute | solution.py:305
  27.0 0.0 copy-done.1
  27.1 0.0 copy-done.2
  27.1 0.6 %shard_map.107 = (bf16[8,256,80]{2,1,0:T(8,128)(2,1)S(1)}, bf16[512,256]{1,0:T(8,128)(2,1)S(1)}, bf16[512,512]{1,0:T(8,128)(2,1)S(1)}) custom-call(s32[1]{0:T(128)} %bitcast.1.col_ref, s32[1]{0:T(128)S(6)} %copy.11.length_ref, bf16[128,512]{1,0:T(8,128)(2,1)S(1)} %bitcast.10, bf16[128,512]{1,0:T(8,128)(2,1)S(1)} %collective-permute-done.refs_1_, ...), custom_call_target="tpu_custom_call" | custom-call | tf_op jit(solution)/shard_map/pallas_call | solution.py:307
  27.6 0.0 copy-start.4
  27.6 0.8 %copy-done.4 = bf16[8,256,80]{2,1,0:T(8,128)(2,1)} copy-done((bf16[8,256,80]{2,1,0:T(8,128)(2,1)}, bf16[8,256,80]{2,1,0:T(8,128)(2,1)S(1)}, u32[]{:S(2)}) %copy-start.4) | copy-done | bytes 327704
  28.4 0.8 %copy-done.6 = bf16[512,512]{1,0:T(8,128)(2,1)} copy-done((bf16[512,512]{1,0:T(8,128)(2,1)}, bf16[512,512]{1,0:T(8,128)(2,1)S(1)}, u32[]{:S(2)}) %copy-start.6) | copy-done | bytes 524312
  29.3 19.8 %all-to-all-done.1.fetched_ref = bf16[16,64,512]{2,1,0:T(8,128)(2,1)S(1)} async-done(((bf16[16,64,512]{2,1,0:T(8,128)(2,1)}), bf16[16,64,512]{2,1,0:T(8,128)(2,1)S(1)}, u32[]{:S(2)}, u32[]{:S(2)}) %all-to-all-start.1) | async-done | bytes 1048608 | tf_op jit(solution)/shard_map/all_to_all | solution.py:331
  49.1 0.8 %copy-done.10 = f32[8,640]{1,0:T(8,128)S(1)} copy-done((f32[8,640]{1,0:T(8,128)S(1)}, f32[8,640]{1,0:T(8,128)}, u32[]{:S(2)}) %copy-start.10) | copy-done | bytes 20504
  49.9 1.0 %shard_map.109 = (bf16[256,512]{1,0:T(8,128)(2,1)S(1)}, bf16[256,512]{1,0:T(8,128)(2,1)S(1)}) custom-call(s32[1]{0:T(128)} %bitcast.1.col_ref, f32[8,640]{1,0:T(8,128)S(1)} %copy-done.10, bf16[16,64,512]{2,1,0:T(8,128)(2,1)S(1)} %all-to-all-done.1.fetched_ref), custom_call_target="tpu_custom_call" | custom-call | tf_op jit(solution)/shard_map/pallas_call | solution.py:335
  51.0 0.1 collective-permute-start.1
  51.0 1.1 %shard_map.108 = bf16[128,2048]{1,0:T(8,128)(2,1)} custom-call(f32[8,640]{1,0:T(8,128)S(1)} %copy-done.10, bf16[16,64,512]{2,1,0:T(8,128)(2,1)S(1)} %all-to-all-done.1.fetched_ref), custom_call_target="tpu_custom_call" | custom-call | tf_op jit(solution)/shard_map/pallas_call | solution.py:356
  52.2 0.4 collective-permute-done.1.refs_1_
  52.6 0.0 copy-done.3
  52.6 0.0 copy-done.5
  52.6 2.3 %shard_map.110 = bf16[256,512]{1,0:T(8,128)(2,1)} custom-call(bf16[256,512]{1,0:T(8,128)(2,1)S(1)} %get-tuple-element.25.refs_0_, bf16[256,512]{1,0:T(8,128)(2,1)S(1)} %collective-permute-done.1.refs_1_, bf16[8,256,80]{2,1,0:T(8,128)(2,1)S(1)} %copy-done.5, bf16[512,256]{1,0:T(8,128)(2,1)S(1)} %get-tuple-element.28.refs_3_, bf16[512,512]{1,0:T(8,128)(2,1)S(1)} %copy-done.7, ...), custom_call_target="tpu_custom_call" | custom-call | tf_op jit(solution)/shard_map/pallas_call | solution.py:348
  (9 shorter events, 0.0 us)
Async XLA Ops:
  2.0 16.0 %all-to-all-start = ((bf16[16,24,128]{2,1,0:T(8,128)(2,1)}), bf16[16,24,128]{2,1,0:T(8,128)(2,1)S(1)}, u32[]{:S(2)}, u32[]{:S(2)}) async-start(bf16[16,24,128]{2,1,0:T(8,128)(2,1)} %shard_map.104), calls=%async_computation | async-start | bytes 196608 | tf_op jit(solution)/shard_map/all_to_all | solution.py:286
  10.3 1.6 %copy-start = (bf16[1,2048,512]{2,1,0:T(8,128)(2,1)S(1)}, bf16[1,2048,512]{2,1,0:T(8,128)(2,1)}, u32[]{:S(2)}) copy-start(bf16[1,2048,512]{2,1,0:T(8,128)(2,1)} %param.11) | copy-start | bytes 6291460
  11.9 0.7 %copy-start.11 = (s32[1,512]{1,0:T(1,128)S(1)}, s32[1,512]{1,0:T(1,128)}, u32[]{:S(2)}) copy-start(s32[1,512]{1,0:T(1,128)} %ids_ref.3) | copy-start | bytes 6148
  12.6 0.7 %copy-start.12 = (s32[4,32]{1,0:T(4,128)S(1)}, s32[4,32]{1,0:T(4,128)}, u32[]{:S(2)}) copy-start(s32[4,32]{1,0:T(4,128)} %probes_ref.1) | copy-start | bytes 1540
  13.7 0.6 %copy-start.9 = (f32[8,640]{1,0:T(8,128)}, f32[8,640]{1,0:T(8,128)S(1)}, u32[]{:S(2)}) copy-start(f32[8,640]{1,0:T(8,128)S(1)} %get-tuple-element.18.known_ref) | copy-start | bytes 61444
  18.0 7.7 %copy-start.8 = (bf16[1,128,512]{2,1,0:T(8,128)(2,1)S(1)}, bf16[1,128,512]{2,1,0:T(8,128)(2,1)}, u32[]{:S(2)}) copy-start(bf16[1,128,512]{2,1,0:T(8,128)(2,1)} %param.13) | copy-start | bytes 393220
  18.0 9.1 %copy-start.1 = (bf16[512,1024]{1,0:T(8,128)(2,1)S(1)}, bf16[512,1024]{1,0:T(8,128)(2,1)}, u32[]{:S(2)}) copy-start(bf16[512,1024]{1,0:T(8,128)(2,1)} %refs_2_.1) | copy-start | bytes 3145732
  21.8 5.2 %copy-start.2 = (bf16[512,512]{1,0:T(8,128)(2,1)S(1)}, bf16[512,512]{1,0:T(8,128)(2,1)}, u32[]{:S(2)}) copy-start(bf16[512,512]{1,0:T(8,128)(2,1)} %refs_3_.1) | copy-start | bytes 1572868
  21.8 27.3 %all-to-all-start.1 = ((bf16[16,64,512]{2,1,0:T(8,128)(2,1)}), bf16[16,64,512]{2,1,0:T(8,128)(2,1)S(1)}, u32[]{:S(2)}, u32[]{:S(2)}) async-start(bf16[16,64,512]{2,1,0:T(8,128)(2,1)} %shard_map.106), calls=%async_computation.1 | async-start | bytes 2097152 | tf_op jit(solution)/shard_map/all_to_all | solution.py:331
  25.6 1.4 %collective-permute-start = (bf16[128,512]{1,0:T(8,128)(2,1)S(1)}, bf16[128,512]{1,0:T(8,128)(2,1)S(1)}, u32[]{:S(2)}, u32[]{:S(2)}) collective-permute-start(bf16[128,512]{1,0:T(8,128)(2,1)S(1)} %bitcast.9), channel_id=1, source_target_pairs={{0,1},{1,0},{2,3},{3,2},{4,5},{5,4},{6,7},{7,6},{8,9},{9,8},{10,11... | collective-permute-start | bytes 393224 | tf_op jit(solution)/shard_map/ppermute | solution.py:305
  26.4 26.2 %copy-start.3 = (bf16[512,512]{1,0:T(8,128)(2,1)S(1)}, bf16[512,512]{1,0:T(8,128)(2,1)}, u32[]{:S(2)}) copy-start(bf16[512,512]{1,0:T(8,128)(2,1)} %refs_5_.1) | copy-start | bytes 1572868
  27.6 0.8 %copy-start.4 = (bf16[8,256,80]{2,1,0:T(8,128)(2,1)}, bf16[8,256,80]{2,1,0:T(8,128)(2,1)S(1)}, u32[]{:S(2)}) copy-start(bf16[8,256,80]{2,1,0:T(8,128)(2,1)S(1)} %get-tuple-element.27.refs_2_) | copy-start | bytes 983044
  28.4 0.8 %copy-start.6 = (bf16[512,512]{1,0:T(8,128)(2,1)}, bf16[512,512]{1,0:T(8,128)(2,1)S(1)}, u32[]{:S(2)}) copy-start(bf16[512,512]{1,0:T(8,128)(2,1)S(1)} %get-tuple-element.29.refs_4_) | copy-start | bytes 1572868
  49.1 3.5 %copy-start.5 = (bf16[8,256,80]{2,1,0:T(8,128)(2,1)S(1)}, bf16[8,256,80]{2,1,0:T(8,128)(2,1)}, u32[]{:S(2)}) copy-start(bf16[8,256,80]{2,1,0:T(8,128)(2,1)} %copy-done.4) | copy-start | bytes 983044
  49.1 3.5 %copy-start.7 = (bf16[512,512]{1,0:T(8,128)(2,1)S(1)}, bf16[512,512]{1,0:T(8,128)(2,1)}, u32[]{:S(2)}) copy-start(bf16[512,512]{1,0:T(8,128)(2,1)} %copy-done.6) | copy-start | bytes 1572868
  49.1 0.8 %copy-start.10 = (f32[8,640]{1,0:T(8,128)S(1)}, f32[8,640]{1,0:T(8,128)}, u32[]{:S(2)}) copy-start(f32[8,640]{1,0:T(8,128)} %copy-done.9) | copy-start | bytes 61444
  51.0 1.6 %collective-permute-start.1 = (bf16[256,512]{1,0:T(8,128)(2,1)S(1)}, bf16[256,512]{1,0:T(8,128)(2,1)S(1)}, u32[]{:S(2)}, u32[]{:S(2)}) collective-permute-start(bf16[256,512]{1,0:T(8,128)(2,1)S(1)} %get-tuple-element.26), channel_id=1, source_target_pairs={{0,1},{1,0},{2,3},{3,2},{4,5},{5,4},{6,7},{7,6},{8,9},{9,8},{10,11... | collective-permute-start | bytes 786440 | tf_op jit(solution)/shard_map/ppermute | solution.py:346

commit v4 on v3

--- a/solution.py
+++ b/solution.py
@@ -34,9 +34,9 @@
         value = ((ids >> (8 * digit)) & (BASE - 1)).astype(jnp.float32)
         rows += [value[:, span] for span in spans]
     count = sum(row.shape[0] for row in rows)
-    if pack_ref.shape[1] > count:
-        rows.append(jnp.zeros((pack_ref.shape[1] - count, LANES), jnp.float32))
-    pack_ref[...] = jnp.broadcast_to(jnp.concatenate(rows, axis=0).astype(jnp.bfloat16)[None], pack_ref.shape)
+    if pack_ref.shape[0] > count:
+        rows.append(jnp.zeros((pack_ref.shape[0] - count, LANES), jnp.float32))
+    pack_ref[...] = jnp.concatenate(rows, axis=0).astype(jnp.bfloat16)
 
 
 def earlier(count):
@@ -85,14 +85,20 @@
     return index
 
 
-def early_kernel(n_lists, n_users, block, col_ref, ids_ref, probes_ref, items_hbm, known_ref, items_ref, sems):
-    items_loc = items_ref.shape[0]
-    part = items_loc // sems.shape[0]
+def items_kernel(items_hbm, after_ref, items_ref, sems):
+    part = items_ref.shape[0] // sems.shape[0]
     loads = []
     for p in range(sems.shape[0]):
         span = pl.ds(p * part, part)
         loads.append(pltpu.make_async_copy(items_hbm.at[span], items_ref.at[span], sems.at[p]))
         loads[-1].start()
+    for load in loads:
+        load.wait()
+
+
+def slot_kernel(
+    n_lists, items_loc, n_users, block, col_ref, ids_ref, probes_ref, after_ref, slot_ref, probe_ref
+):
     ids = ids_ref[...]
     cands = ids.shape[1]
     bins = ids // items_loc
@@ -103,14 +109,13 @@
     before = jnp.dot(hot.astype(jnp.bfloat16), earlier(cands), preferred_element_type=jnp.float32)
     rank = jnp.sum(before * hot, axis=0, keepdims=True)
     slot = jnp.where(mine, owner.astype(jnp.float32) * block + rank, -1.0)
+    slot_ref[...] = jnp.broadcast_to(slot, slot_ref.shape)
     probes = probes_ref[...].astype(jnp.float32)
-    known = jnp.concatenate([slot] + [probes[u : u + 1] for u in range(probes.shape[0])], axis=1)
-    known_ref[...] = jnp.broadcast_to(known, known_ref.shape)
-    for load in loads:
-        load.wait()
-
-
-def pairs_kernel(n_parts, col_ref, length_ref, *refs):
+    flat = jnp.concatenate([probes[u : u + 1] for u in range(probes.shape[0])], axis=1)
+    probe_ref[...] = jnp.broadcast_to(flat, probe_ref.shape)
+
+
+def pairs_kernel(n_parts, col_ref, length_ref, after_ref, *refs):
     parts, (weight_ref, query_ref, keys_ref, values_ref, turned_ref) = refs[:n_parts], refs[n_parts:]
     history = jnp.concatenate([part[...] for part in parts], axis=0)
     pairs = jnp.dot(history, weight_ref[...], preferred_element_type=jnp.float32)
@@ -129,11 +134,10 @@
     turned_ref[...] = jnp.transpose(query_ref[...].astype(jnp.float32)).astype(jnp.bfloat16)
 
 
-def owner_kernel(n_lists, user_dev, digits, cap, scale, base_ref, gathered_ref, items_ref, *refs):
+def owner_kernel(n_lists, user_dev, digits, cap, scale, line_ref, base_ref, gathered_ref, items_ref, *refs):
     out_hbm, out_ref, out_sems = refs
     items_loc, width = items_ref.shape
-    vectors, ids = unpack(gathered_ref, n_lists, user_dev, digits, 0)
-    index = asked(ids, base_ref[0].astype(jnp.float32), items_loc, 0, cap)
+    vectors, ids = unpack(gathered_ref, n_lists, user_dev, digits, line_ref[0])
     scores = lax.dot_general(
         vectors.astype(jnp.bfloat16),
         items_ref[...],
@@ -141,6 +145,7 @@
         preferred_element_type=jnp.float32,
     )
     scores = (scores * scale).astype(jnp.bfloat16)
+    index = asked(ids, base_ref[0].astype(jnp.float32), items_loc, 0, cap)
     pieces = items_loc // width
     stacked = jnp.concatenate(
         [scores[:, piece * width : (piece + 1) * width] for piece in range(pieces)], axis=0
@@ -169,12 +174,12 @@
         send.wait()
 
 
-def place_kernel(n_users, col_ref, known_ref, fetched_ref, *refs):
+def place_kernel(n_users, col_ref, slot_ref, fetched_ref, *refs):
     share_refs, scratch = refs[:-1], refs[-1]
     n_lists, block, width = fetched_ref.shape
     fetched = fetched_ref[...].reshape(n_lists * block, width)
     share = share_refs[0].shape[0]
-    slot = jnp.transpose(known_ref[:, : share * n_users])[:, :1].astype(jnp.int32)
+    slot = jnp.transpose(slot_ref[...])[:, :1].astype(jnp.int32)
     scratch[...] = jnp.dot(
         picks(slot, fetched.shape[0]), fetched, preferred_element_type=jnp.float32
     ).astype(jnp.bfloat16)
@@ -215,14 +220,13 @@
     out_ref[...] = jnp.dot(attended, out_weight_ref[...], preferred_element_type=jnp.float32).astype(jnp.bfloat16)
 
 
-def expand_kernel(user_dev, pieces, cap, known_ref, fetched_ref, out_hbm, out_ref, sems):
+def expand_kernel(user_dev, pieces, cap, probe_ref, fetched_ref, out_hbm, out_ref, sems):
     n_lists, block, width = fetched_ref.shape
     kept = block - cap
     rows = n_lists * kept
     returned = fetched_ref[:, cap:, :].reshape(rows, width)
     count = out_ref.shape[0]
-    first = known_ref.shape[1] - count
-    probe = jnp.transpose(known_ref[:, first:])[:, :1].astype(jnp.int32)
+    probe = jnp.transpose(probe_ref[...])[:, :1].astype(jnp.int32)
     user = lax.broadcasted_iota(jnp.int32, (count, 1), 0) // (count // user_dev)
     sends = []
     for piece in range(pieces):
@@ -271,6 +275,7 @@
     pack_rows = round_up((user_dev + digits) * (width // LANES), 8)
     line = lax.axis_index("lists").astype(jnp.int32)
     col = lax.axis_index("users").astype(jnp.int32)
+    line_arg = line.reshape(1)
     col_arg = col.reshape(1)
     base_arg = ((line * n_users + col) * items_loc).reshape(1)
     block = cap + kept
@@ -278,32 +283,55 @@
     flat_items = list_items.reshape(items_loc, width)
     pack = pl.pallas_call(
         functools.partial(pack_kernel, digits),
-        out_shape=jax.ShapeDtypeStruct((n_lists, pack_rows, LANES), bf16),
+        out_shape=jax.ShapeDtypeStruct((pack_rows, LANES), bf16),
         in_specs=[VMEM, VMEM],
         out_specs=VMEM,
         compiler_params=pltpu.CompilerParams(vmem_limit_bytes=ALL_VMEM_BYTES),
     )(candidate_ids, user_vectors)
-    gathered = lax.all_to_all(pack, "lists", split_axis=0, concat_axis=0, tiled=True)
-    gathered = gathered.reshape(n_lists * pack_rows, LANES)
-
-    known, items = pl.pallas_call(
-        functools.partial(early_kernel, n_lists, n_users, block),
-        out_shape=(
-            jax.ShapeDtypeStruct((8, cands + user_dev * probes), jnp.float32),
-            jax.ShapeDtypeStruct((items_loc, width), bf16),
-        ),
-        in_specs=[SMEM, VMEM, VMEM, HBM],
-        out_specs=(VMEM, VMEM),
+    gathered, reach = pack, 1
+    while reach < n_lists:
+        ahead = gathered
+        came = lax.ppermute(gathered, "lists", [(i, i ^ reach) for i in range(n_lists)])
+        gathered, reach = jnp.concatenate([gathered, came], axis=0), reach * 2
+
+    items = pl.pallas_call(
+        items_kernel,
+        out_shape=jax.ShapeDtypeStruct((items_loc, width), bf16),
+        in_specs=[HBM, pl.BlockSpec(memory_space=pl.ANY)],
+        out_specs=VMEM,
         scratch_shapes=[pltpu.SemaphoreType.DMA((4,))],
         compiler_params=PARAMS,
-    )(col_arg, candidate_ids, probe_lists, flat_items)
-    gathered, known, items = lax.optimization_barrier((gathered, known, items))
+    )(flat_items, ahead)
 
     events = history.reshape(-1, width)
     hist = [events]
     for shift in range(1, n_users):
         hist.append(lax.ppermute(events, "users", [(i, (i + shift) % n_users) for i in range(n_users)]))
     total_events = n_users * events.shape[0]
+    step = max(1, 256 // cap)
+    answers = pl.pallas_call(
+        functools.partial(owner_kernel, n_lists, user_dev, digits, cap, width ** (-0.5)),
+        out_shape=jax.ShapeDtypeStruct((n_lists, block, width), bf16),
+        in_specs=[SMEM, SMEM, VMEM, VMEM],
+        out_specs=pl.BlockSpec(memory_space=pl.ANY),
+        scratch_shapes=[
+            pltpu.VMEM((n_lists, block, width), bf16),
+            pltpu.SemaphoreType.DMA((-(-n_lists // step),)),
+        ],
+        compiler_params=PARAMS,
+    )(line_arg, base_arg, gathered, items)
+    fetched = lax.all_to_all(answers, "lists", split_axis=0, concat_axis=0, tiled=True)
+    slot, probe_row = pl.pallas_call(
+        functools.partial(slot_kernel, n_lists, items_loc, n_users, block),
+        out_shape=(
+            jax.ShapeDtypeStruct((8, cands), jnp.float32),
+            jax.ShapeDtypeStruct((8, user_dev * probes), jnp.float32),
+        ),
+        in_specs=[SMEM, VMEM, VMEM, pl.BlockSpec(memory_space=pl.ANY)],
+        out_specs=(VMEM, VMEM),
+        compiler_params=PARAMS,
+    )(col_arg, candidate_ids, probe_lists, answers)
+
     keys, values, turned = pl.pallas_call(
         functools.partial(pairs_kernel, n_users),
         out_shape=(
@@ -311,26 +339,14 @@
             jax.ShapeDtypeStruct((width, total_events), bf16),
             jax.ShapeDtypeStruct((width, width), bf16),
         ),
-        in_specs=[SMEM, SMEM] + [VMEM] * (n_users + 2),
+        in_specs=[SMEM, SMEM, pl.BlockSpec(memory_space=pl.ANY)] + [VMEM] * (n_users + 2),
         out_specs=(VMEM, VMEM, VMEM),
         compiler_params=PARAMS,
-    )(col_arg, history_lengths, *hist, key_value_weight, query_weight)
-
-    step = max(1, 256 // cap)
-    answers = pl.pallas_call(
-        functools.partial(owner_kernel, n_lists, user_dev, digits, cap, width ** (-0.5)),
-        out_shape=jax.ShapeDtypeStruct((n_lists, block, width), bf16),
-        in_specs=[SMEM, VMEM, VMEM],
-        out_specs=pl.BlockSpec(memory_space=pl.ANY),
-        scratch_shapes=[
-            pltpu.VMEM((n_lists, block, width), bf16),
-            pltpu.SemaphoreType.DMA((-(-n_lists // step),)),
-        ],
-        compiler_params=PARAMS,
-    )(base_arg, gathered, items)
-    fetched = lax.all_to_all(answers, "lists", split_axis=0, concat_axis=0, tiled=True)
-
-    fetched, keys, values, turned = lax.optimization_barrier((fetched, keys, values, turned))
+    )(col_arg, history_lengths, answers, *hist, key_value_weight, query_weight)
+
+    fetched, slot, probe_row, keys, values, turned = lax.optimization_barrier(
+        (fetched, slot, probe_row, keys, values, turned)
+    )
 
     placed = pl.pallas_call(
         functools.partial(place_kernel, n_users),
@@ -339,7 +355,7 @@
         out_specs=tuple(VMEM for _ in range(n_users)),
         scratch_shapes=[pltpu.VMEM((cands, width), bf16)],
         compiler_params=PARAMS,
-    )(col_arg, known, fetched)
+    )(col_arg, slot, fetched)
     parts = [placed[0]]
     for shift in range(1, n_users):
         parts.append(
@@ -363,7 +379,7 @@
             pltpu.SemaphoreType.DMA((pieces,)),
         ],
         compiler_params=PARAMS,
-    )(known, fetched)
+    )(probe_row, fetched)
     return (list_scores.reshape(user_dev, probes, items_loc), ranked.reshape(1, share, width))
 
 

time: 55.6 us -> 59.9 us (1.077)
  starting transfers between devices: 12.3 us -> 18.1 us
  waiting for transfers between devices: 24.6 us -> 21.5 us
  other arithmetic: 0 us -> 2.08 us
    ppermute x0 -> x4, starting transfers between devices: none -> 10.4 us  [shards(): lax.ppermute(gathered, 'lists', [(i, i ^ reach) for i in range(n_lists)])]
    all_to_all x1 -> x0, starting transfers between devices: 8.31 us -> none  [shards(): lax.all_to_all(pack, 'lists', split_axis=0, concat_axis=0, tiled=True)]
    ppermute x0 -> x4, waiting for transfers between devices: none -> 4.82 us  [shards(): lax.ppermute(gathered, 'lists', [(i, i ^ reach) for i in range(n_lists)])]
    all_to_all x1, starting transfers between devices: 3.8 us -> 7.62 us  [shards(): lax.all_to_all(answers, 'lists', split_axis=0, concat_axis=0, tiled=True)]
    all_to_all x1 -> x0, waiting for transfers between devices: 3.7 us -> none  [shards(): lax.all_to_all(pack, 'lists', split_axis=0, concat_axis=0, tiled=True)]
    all_to_all x1, waiting for transfers between devices: 19.8 us -> 16.7 us  [shards(): lax.all_to_all(answers, 'lists', split_axis=0, concat_axis=0, tiled=True)]
    concatenate x0 -> x3, other arithmetic: none -> 2.08 us  [shards(): gathered, reach = (jnp.concatenate([gathered, came], axis=0), reach * 2)]
    ppermute x1, waiting for transfers between devices: 0.68 us -> 0.01 us  [shards(): lax.ppermute(events, 'users', [(i, (i + shift) % n_users) for i in range(...]
  transfers between devices with their start and end apart: 4 -> 7, of which waited for: 4 -> 5; matrix products, arithmetic and copies ran while one was open for 0% -> 1% of each run, Pallas kernels for 4% -> 4%
where the time goes in v4:
time: 59.9 us; the launch traced here: 59.4 us
  waiting for transfers between devices  21.5 us (36%)
  starting transfers between devices  18.1 us (30%)
  Pallas kernels  10.6 us (18%)
  local copies, waits for them, and re-layouts  5.54 us (9%)
  other arithmetic  2.08 us (3%)
  between operations  1.47 us (2%)
    all_to_all x1, waiting for transfers between devices, shards(): lax.all_to_all(answers, 'lists', split_axis=0, concat_axis=0, tiled=True)  16.7 us
    ppermute x4, starting transfers between devices, shards(): lax.ppermute(gathered, 'lists', [(i, i ^ reach) for i in range(n_lists)])  10.4 us
    all_to_all x1, starting transfers between devices, shards(): lax.all_to_all(answers, 'lists', split_axis=0, concat_axis=0, tiled=True)  7.62 us
    unnamed x26, local copies, waits for them, and re-layouts  5.53 us
    ppermute x4, waiting for transfers between devices, shards(): lax.ppermute(gathered, 'lists', [(i, i ^ reach) for i in range(n_lists)])  4.82 us
    pallas_call x1, Pallas kernels, shards(): pl.pallas_call(functools.partial(owner_kernel, n_lists, user_dev, digits,...  3.9 us
    pallas_call x1, Pallas kernels, shards(): pl.pallas_call(functools.partial(attend_kernel, n_users), out_shape=jax.S...  2.32 us
    concatenate x3, other arithmetic, shards(): gathered, reach = (jnp.concatenate([gathered, came], axis=0), reach * 2)  2.08 us
  transfers between devices with their start and end apart: 7, of which 5 were waited for; matrix products, arithmetic and copies ran while one was open for 1% of the time, Pallas kernels for 4%

profile of v4, /device:TPU:0, one launch (start us, length us, event | category | flops | bytes accessed | tf_op | source)
XLA Modules:
  0.0 59.4 jit_solution(5689955421699646427)
XLA Ops:
  0.6 1.3 %shard_map.104 = bf16[24,128]{1,0:T(8,128)(2,1)} custom-call(s32[1,512]{1,0:T(1,128)} %ids_ref.3, bf16[4,512]{1,0:T(4,128)(2,1)} %vectors_ref.1), custom_call_target="tpu_custom_call" | custom-call | tf_op jit(solution)/shard_map/pallas_call | solution.py:284
  1.9 2.9 %collective-permute-start = (bf16[24,128]{1,0:T(8,128)(2,1)}, bf16[24,128]{1,0:T(8,128)(2,1)S(1)}, u32[]{:S(2)}, u32[]{:S(2)}) collective-permute-start(bf16[24,128]{1,0:T(8,128)(2,1)} %shard_map.104), channel_id=1, source_target_pairs={{0,2},{2,0},{4,6},{6,4},{8,10},{10,8},{12,14},{14,12},{16,18},{18,... | collective-permute-start | bytes 18440 | tf_op jit(solution)/shard_map/ppermute | solution.py:294
  4.9 0.7 %constant_dynamic-update-slice_fusion.4 = bf16[384,128]{1,0:T(8,128)(2,1)S(1)} fusion(bf16[24,128]{1,0:T(8,128)(2,1)} %shard_map.104), kind=kLoop, calls=%fused_computation.7 | loop fusion | bytes 12288
  5.6 1.1 %collective-permute-done = bf16[24,128]{1,0:T(8,128)(2,1)S(1)} collective-permute-done((bf16[24,128]{1,0:T(8,128)(2,1)}, bf16[24,128]{1,0:T(8,128)(2,1)S(1)}, u32[]{:S(2)}, u32[]{:S(2)}) %collective-permute-start) | collective-permute-done | bytes 6176 | tf_op jit(solution)/shard_map/ppermute | solution.py:294
  6.7 0.7 %pad_maximum_fusion.2 = bf16[48,128]{1,0:T(8,128)(2,1)S(1)} fusion(bf16[24,128]{1,0:T(8,128)(2,1)S(1)} %collective-permute-done, bf16[24,128]{1,0:T(8,128)(2,1)} %shard_map.104), kind=kLoop, calls=%fused_computation.2 | loop fusion | flops 24576 | bytes 24576 | tf_op jit(solution)/shard_map/concatenate | solution.py:295
  7.4 2.1 %collective-permute-start.1 = (bf16[48,128]{1,0:T(8,128)(2,1)S(1)}, bf16[48,128]{1,0:T(8,128)(2,1)S(1)}, u32[]{:S(2)}, u32[]{:S(2)}) collective-permute-start(bf16[48,128]{1,0:T(8,128)(2,1)S(1)} %pad_maximum_fusion.2), channel_id=1, source_target_pairs={{0,4},{2,6},{4,0},{6,2},{8,12},{10,14},{12,8},{14,10},{16,20},{18,... | collective-permute-start | bytes 36872 | tf_op jit(solution)/shard_map/ppermute | solution.py:294
  9.4 1.7 %collective-permute-done.1 = bf16[48,128]{1,0:T(8,128)(2,1)S(1)} collective-permute-done((bf16[48,128]{1,0:T(8,128)(2,1)S(1)}, bf16[48,128]{1,0:T(8,128)(2,1)S(1)}, u32[]{:S(2)}, u32[]{:S(2)}) %collective-permute-start.1) | collective-permute-done | bytes 12320 | tf_op jit(solution)/shard_map/ppermute | solution.py:294
  11.1 0.7 %pad_maximum_fusion.1 = bf16[96,128]{1,0:T(8,128)(2,1)S(1)} fusion(bf16[48,128]{1,0:T(8,128)(2,1)S(1)} %collective-permute-done.1, bf16[24,128]{1,0:T(8,128)(2,1)S(1)} %collective-permute-done, bf16[24,128]{1,0:T(8,128)(2,1)} %shard_map.104), kind=kLoop, calls=%fused_computation.1 | loop fusion | flops 73728 | bytes 49152 | tf_op jit(solution)/shard_map/concatenate | solution.py:295
  11.8 2.1 %collective-permute-start.2 = (bf16[96,128]{1,0:T(8,128)(2,1)S(1)}, bf16[96,128]{1,0:T(8,128)(2,1)S(1)}, u32[]{:S(2)}, u32[]{:S(2)}) collective-permute-start(bf16[96,128]{1,0:T(8,128)(2,1)S(1)} %pad_maximum_fusion.1), channel_id=1, source_target_pairs={{0,8},{2,10},{4,12},{6,14},{8,0},{10,2},{12,4},{14,6},{16,24},{18,... | collective-permute-start | bytes 73736 | tf_op jit(solution)/shard_map/ppermute | solution.py:294
  13.9 1.8 %collective-permute-done.2 = bf16[96,128]{1,0:T(8,128)(2,1)S(1)} collective-permute-done((bf16[96,128]{1,0:T(8,128)(2,1)S(1)}, bf16[96,128]{1,0:T(8,128)(2,1)S(1)}, u32[]{:S(2)}, u32[]{:S(2)}) %collective-permute-start.2) | collective-permute-done | bytes 24608 | tf_op jit(solution)/shard_map/ppermute | solution.py:294
  15.7 0.7 %pad_maximum_fusion.after_ref = bf16[192,128]{1,0:T(8,128)(2,1)S(1)} fusion(bf16[96,128]{1,0:T(8,128)(2,1)S(1)} %collective-permute-done.2, bf16[48,128]{1,0:T(8,128)(2,1)S(1)} %collective-permute-done.1, bf16[24,128]{1,0:T(8,128)(2,1)S(1)} %collective-permute-done, bf16[24,128]{1,0:T(8,128)(2,1)} %shard_map.104), kind=kLoop, calls=%fused_computation | loop fusion | flops 196608 | bytes 98304 | tf_op jit(solution)/shard_map/concatenate | solution.py:295
  16.4 3.3 %collective-permute-start.3 = (bf16[192,128]{1,0:T(8,128)(2,1)S(1)}, bf16[192,128]{1,0:T(8,128)(2,1)S(1)}, u32[]{:S(2)}, u32[]{:S(2)}) collective-permute-start(bf16[192,128]{1,0:T(8,128)(2,1)S(1)} %pad_maximum_fusion.after_ref), channel_id=1, source_target_pairs={{0,16},{2,18},{4,20},{6,22},{8,24},{10,26},{12,28},{14,30},{16,0},... | collective-permute-start | bytes 147464 | tf_op jit(solution)/shard_map/ppermute | solution.py:294
  19.7 1.6 %copy-done = bf16[1,2048,512]{2,1,0:T(8,128)(2,1)S(1)} copy-done((bf16[1,2048,512]{2,1,0:T(8,128)(2,1)S(1)}, bf16[1,2048,512]{2,1,0:T(8,128)(2,1)}, u32[]{:S(2)}) %copy-start) | copy-done | bytes 2097176
  21.3 0.2 shard_map.105.items_ref
  21.5 0.3 collective-permute-done.3
  21.8 0.0 copy-start.6
  21.8 3.9 %shard_map.106.after_ref = bf16[16,64,512]{2,1,0:T(8,128)(2,1)} custom-call(s32[1]{0:T(128)} %bitcast.line_ref, s32[1]{0:T(128)} %bitcast.1.base_ref, bf16[384,128]{1,0:T(8,128)(2,1)S(1)} %constant_dynamic-update-slice_fusion.gathered_ref, bf16[2048,512]{1,0:T(8,128)(2,1)S(1)} %shard_map.105.items_ref), custom_call_target="tpu_custom_call" | custom-call | tf_op jit(solution)/shard_map/pallas_call | solution.py:312
  25.7 0.0 copy-start.1
  25.7 7.6 %all-to-all-start = ((bf16[16,64,512]{2,1,0:T(8,128)(2,1)}), bf16[16,64,512]{2,1,0:T(8,128)(2,1)S(1)}, u32[]{:S(2)}, u32[]{:S(2)}) async-start(bf16[16,64,512]{2,1,0:T(8,128)(2,1)} %shard_map.106.after_ref), calls=%async_computation | async-start | bytes 2097152 | tf_op jit(solution)/shard_map/all_to_all | solution.py:323
  33.3 0.1 collective-permute-start.4
  34.1 0.2 shard_map.107
  34.3 0.0 copy-start.8
  34.3 0.6 copy-done.8
  34.9 1.1 %copy-done.5 = bf16[512,512]{1,0:T(8,128)(2,1)S(1)} copy-done((bf16[512,512]{1,0:T(8,128)(2,1)S(1)}, bf16[512,512]{1,0:T(8,128)(2,1)}, u32[]{:S(2)}) %copy-start.5) | copy-done | bytes 524312
  36.0 0.6 shard_map.108
  36.6 0.8 %copy-done.3 = bf16[512,512]{1,0:T(8,128)(2,1)} copy-done((bf16[512,512]{1,0:T(8,128)(2,1)}, bf16[512,512]{1,0:T(8,128)(2,1)S(1)}, u32[]{:S(2)}) %copy-start.3) | copy-done | bytes 524312
  37.4 16.7 %all-to-all-done.fetched_ref = bf16[16,64,512]{2,1,0:T(8,128)(2,1)S(1)} async-done(((bf16[16,64,512]{2,1,0:T(8,128)(2,1)}), bf16[16,64,512]{2,1,0:T(8,128)(2,1)S(1)}, u32[]{:S(2)}, u32[]{:S(2)}) %all-to-all-start) | async-done | bytes 1048608 | tf_op jit(solution)/shard_map/all_to_all | solution.py:323
  54.1 1.0 %shard_map.110 = (bf16[256,512]{1,0:T(8,128)(2,1)S(1)}, bf16[256,512]{1,0:T(8,128)(2,1)S(1)}) custom-call(s32[1]{0:T(128)} %bitcast.3.col_ref, f32[8,512]{1,0:T(8,128)S(1)} %get-tuple-element.22.slot_ref, bf16[16,64,512]{2,1,0:T(8,128)(2,1)S(1)} %all-to-all-done.fetched_ref), custom_call_target="tpu_custom_call" | custom-call | tf_op jit(solution)/shard_map/pallas_call | solution.py:351
  55.1 0.1 collective-permute-start.5
  55.2 0.7 %copy-done.9 = f32[8,128]{1,0:T(8,128)S(1)} copy-done((f32[8,128]{1,0:T(8,128)S(1)}, f32[8,128]{1,0:T(8,128)}, u32[]{:S(2)}) %copy-start.9) | copy-done | bytes 4120
  55.9 1.1 %shard_map.109 = bf16[128,2048]{1,0:T(8,128)(2,1)} custom-call(f32[8,128]{1,0:T(8,128)S(1)} %copy-done.9, bf16[16,64,512]{2,1,0:T(8,128)(2,1)S(1)} %all-to-all-done.fetched_ref), custom_call_target="tpu_custom_call" | custom-call | tf_op jit(solution)/shard_map/pallas_call | solution.py:372
  57.1 2.3 %shard_map.111 = bf16[256,512]{1,0:T(8,128)(2,1)} custom-call(bf16[256,512]{1,0:T(8,128)(2,1)S(1)} %get-tuple-element.23.refs_0_, bf16[256,512]{1,0:T(8,128)(2,1)S(1)} %collective-permute-done.5.refs_1_, bf16[8,256,80]{2,1,0:T(8,128)(2,1)S(1)} %get-tuple-element.25.refs_2_, bf16[512,256]{1,0:T(8,128)(2,1)S(1)} %get-tuple-element.26.refs_3_, ...), custom_call_target="tpu_custom_call" | custom-call | tf_op jit(solution)/shard_map/pallas_call | solution.py:364
  (20 shorter events, 0.1 us)
Async XLA Ops:
  1.9 4.8 %collective-permute-start = (bf16[24,128]{1,0:T(8,128)(2,1)}, bf16[24,128]{1,0:T(8,128)(2,1)S(1)}, u32[]{:S(2)}, u32[]{:S(2)}) collective-permute-start(bf16[24,128]{1,0:T(8,128)(2,1)} %shard_map.104), channel_id=1, source_target_pairs={{0,2},{2,0},{4,6},{6,4},{8,10},{10,8},{12,14},{14,12},{16,18},{18,... | collective-permute-start | bytes 18440 | tf_op jit(solution)/shard_map/ppermute | solution.py:294
  7.4 3.7 %collective-permute-start.1 = (bf16[48,128]{1,0:T(8,128)(2,1)S(1)}, bf16[48,128]{1,0:T(8,128)(2,1)S(1)}, u32[]{:S(2)}, u32[]{:S(2)}) collective-permute-start(bf16[48,128]{1,0:T(8,128)(2,1)S(1)} %pad_maximum_fusion.2), channel_id=1, source_target_pairs={{0,4},{2,6},{4,0},{6,2},{8,12},{10,14},{12,8},{14,10},{16,20},{18,... | collective-permute-start | bytes 36872 | tf_op jit(solution)/shard_map/ppermute | solution.py:294
  11.8 3.9 %collective-permute-start.2 = (bf16[96,128]{1,0:T(8,128)(2,1)S(1)}, bf16[96,128]{1,0:T(8,128)(2,1)S(1)}, u32[]{:S(2)}, u32[]{:S(2)}) collective-permute-start(bf16[96,128]{1,0:T(8,128)(2,1)S(1)} %pad_maximum_fusion.1), channel_id=1, source_target_pairs={{0,8},{2,10},{4,12},{6,14},{8,0},{10,2},{12,4},{14,6},{16,24},{18,... | collective-permute-start | bytes 73736 | tf_op jit(solution)/shard_map/ppermute | solution.py:294
  16.4 5.4 %collective-permute-start.3 = (bf16[192,128]{1,0:T(8,128)(2,1)S(1)}, bf16[192,128]{1,0:T(8,128)(2,1)S(1)}, u32[]{:S(2)}, u32[]{:S(2)}) collective-permute-start(bf16[192,128]{1,0:T(8,128)(2,1)S(1)} %pad_maximum_fusion.after_ref), channel_id=1, source_target_pairs={{0,16},{2,18},{4,20},{6,22},{8,24},{10,26},{12,28},{14,30},{16,0},... | collective-permute-start | bytes 147464 | tf_op jit(solution)/shard_map/ppermute | solution.py:294
  19.7 1.6 %copy-start = (bf16[1,2048,512]{2,1,0:T(8,128)(2,1)S(1)}, bf16[1,2048,512]{2,1,0:T(8,128)(2,1)}, u32[]{:S(2)}) copy-start(bf16[1,2048,512]{2,1,0:T(8,128)(2,1)} %param.11) | copy-start | bytes 6291460
  21.8 11.6 %copy-start.6 = (bf16[1,128,512]{2,1,0:T(8,128)(2,1)S(1)}, bf16[1,128,512]{2,1,0:T(8,128)(2,1)}, u32[]{:S(2)}) copy-start(bf16[1,128,512]{2,1,0:T(8,128)(2,1)} %param.13) | copy-start | bytes 393220
  21.8 12.3 %copy-start.7 = (s32[1,512]{1,0:T(1,128)S(1)}, s32[1,512]{1,0:T(1,128)}, u32[]{:S(2)}) copy-start(s32[1,512]{1,0:T(1,128)} %ids_ref.3) | copy-start | bytes 6148
  21.8 12.3 %copy-start.10 = (s32[4,32]{1,0:T(4,128)S(1)}, s32[4,32]{1,0:T(4,128)}, u32[]{:S(2)}) copy-start(s32[4,32]{1,0:T(4,128)} %probes_ref.1) | copy-start | bytes 1540
  25.7 9.2 %copy-start.1 = (bf16[512,1024]{1,0:T(8,128)(2,1)S(1)}, bf16[512,1024]{1,0:T(8,128)(2,1)}, u32[]{:S(2)}) copy-start(bf16[512,1024]{1,0:T(8,128)(2,1)} %refs_2_.1) | copy-start | bytes 3145732
  25.7 28.4 %all-to-all-start = ((bf16[16,64,512]{2,1,0:T(8,128)(2,1)}), bf16[16,64,512]{2,1,0:T(8,128)(2,1)S(1)}, u32[]{:S(2)}, u32[]{:S(2)}) async-start(bf16[16,64,512]{2,1,0:T(8,128)(2,1)} %shard_map.106.after_ref), calls=%async_computation | async-start | bytes 2097152 | tf_op jit(solution)/shard_map/all_to_all | solution.py:323
  33.3 1.5 %collective-permute-start.4 = (bf16[128,512]{1,0:T(8,128)(2,1)S(1)}, bf16[128,512]{1,0:T(8,128)(2,1)S(1)}, u32[]{:S(2)}, u32[]{:S(2)}) collective-permute-start(bf16[128,512]{1,0:T(8,128)(2,1)S(1)} %bitcast.8), channel_id=1, source_target_pairs={{0,1},{1,0},{2,3},{3,2},{4,5},{5,4},{6,7},{7,6},{8,9},{9,8},{10,11... | collective-permute-start | bytes 393224 | tf_op jit(solution)/shard_map/ppermute | solution.py:309
  34.3 0.6 %copy-start.8 = (f32[8,128]{1,0:T(8,128)}, f32[8,128]{1,0:T(8,128)S(1)}, u32[]{:S(2)}) copy-start(f32[8,128]{1,0:T(8,128)S(1)} %get-tuple-element.20.probe_ref) | copy-start | bytes 12292
  34.9 22.2 %copy-start.2 = (bf16[512,512]{1,0:T(8,128)(2,1)S(1)}, bf16[512,512]{1,0:T(8,128)(2,1)}, u32[]{:S(2)}) copy-start(bf16[512,512]{1,0:T(8,128)(2,1)} %refs_5_.1) | copy-start | bytes 1572868
  34.9 1.1 %copy-start.5 = (bf16[512,512]{1,0:T(8,128)(2,1)S(1)}, bf16[512,512]{1,0:T(8,128)(2,1)}, u32[]{:S(2)}) copy-start(bf16[512,512]{1,0:T(8,128)(2,1)} %refs_3_.1) | copy-start | bytes 1572868
  36.6 0.8 %copy-start.3 = (bf16[512,512]{1,0:T(8,128)(2,1)}, bf16[512,512]{1,0:T(8,128)(2,1)S(1)}, u32[]{:S(2)}) copy-start(bf16[512,512]{1,0:T(8,128)(2,1)S(1)} %get-tuple-element.27.refs_4_) | copy-start | bytes 1572868
  54.1 3.0 %copy-start.4 = (bf16[512,512]{1,0:T(8,128)(2,1)S(1)}, bf16[512,512]{1,0:T(8,128)(2,1)}, u32[]{:S(2)}) copy-start(bf16[512,512]{1,0:T(8,128)(2,1)} %copy-done.3) | copy-start | bytes 1572868
  55.1 1.9 %collective-permute-start.5 = (bf16[256,512]{1,0:T(8,128)(2,1)S(1)}, bf16[256,512]{1,0:T(8,128)(2,1)S(1)}, u32[]{:S(2)}, u32[]{:S(2)}) collective-permute-start(bf16[256,512]{1,0:T(8,128)(2,1)S(1)} %get-tuple-element.24), channel_id=1, source_target_pairs={{0,1},{1,0},{2,3},{3,2},{4,5},{5,4},{6,7},{7,6},{8,9},{9,8},{10,11... | collective-permute-start | bytes 786440 | tf_op jit(solution)/shard_map/ppermute | solution.py:362
  55.2 0.7 %copy-start.9 = (f32[8,128]{1,0:T(8,128)S(1)}, f32[8,128]{1,0:T(8,128)}, u32[]{:S(2)}) copy-start(f32[8,128]{1,0:T(8,128)} %copy-done.8) | copy-start | bytes 12292

commit v5 on v3

--- a/solution.py
+++ b/solution.py
@@ -85,14 +85,23 @@
     return index
 
 
-def early_kernel(n_lists, n_users, block, col_ref, ids_ref, probes_ref, items_hbm, known_ref, items_ref, sems):
-    items_loc = items_ref.shape[0]
-    part = items_loc // sems.shape[0]
+def position(index, count):
+    half = max(1, count // 2)
+    return index % half * 2 + index // half if count > 1 else index
+
+
+def items_kernel(items_hbm, items_ref, sems):
+    part = items_ref.shape[0] // sems.shape[0]
     loads = []
     for p in range(sems.shape[0]):
         span = pl.ds(p * part, part)
         loads.append(pltpu.make_async_copy(items_hbm.at[span], items_ref.at[span], sems.at[p]))
         loads[-1].start()
+    for load in loads:
+        load.wait()
+
+
+def known_kernel(n_lists, items_loc, n_users, block, col_ref, ids_ref, probes_ref, known_ref, order_ref):
     ids = ids_ref[...]
     cands = ids.shape[1]
     bins = ids // items_loc
@@ -102,12 +111,14 @@
     hot = jnp.where((lists == owner) & mine, 1.0, 0.0)
     before = jnp.dot(hot.astype(jnp.bfloat16), earlier(cands), preferred_element_type=jnp.float32)
     rank = jnp.sum(before * hot, axis=0, keepdims=True)
-    slot = jnp.where(mine, owner.astype(jnp.float32) * block + rank, -1.0)
-    probes = probes_ref[...].astype(jnp.float32)
-    known = jnp.concatenate([slot] + [probes[u : u + 1] for u in range(probes.shape[0])], axis=1)
-    known_ref[...] = jnp.broadcast_to(known, known_ref.shape)
-    for load in loads:
-        load.wait()
+    slot = jnp.where(mine, position(owner, n_lists).astype(jnp.float32) * block + rank, -1.0)
+    probes = position(probes_ref[...], n_lists).astype(jnp.float32)
+    flat = jnp.concatenate([probes[u : u + 1] for u in range(probes.shape[0])], axis=1)
+    if flat.shape[1] < cands:
+        flat = jnp.concatenate([flat, jnp.zeros((1, cands - flat.shape[1]), jnp.float32)], axis=1)
+    row = lax.broadcasted_iota(jnp.int32, known_ref.shape, 0)
+    known_ref[...] = jnp.where(row == 0, slot, flat)
+    order_ref[...] = jnp.zeros_like(order_ref)
 
 
 def pairs_kernel(n_parts, col_ref, length_ref, *refs):
@@ -174,7 +185,7 @@
     n_lists, block, width = fetched_ref.shape
     fetched = fetched_ref[...].reshape(n_lists * block, width)
     share = share_refs[0].shape[0]
-    slot = jnp.transpose(known_ref[:, : share * n_users])[:, :1].astype(jnp.int32)
+    slot = jnp.transpose(known_ref[...])[:, :1].astype(jnp.int32)
     scratch[...] = jnp.dot(
         picks(slot, fetched.shape[0]), fetched, preferred_element_type=jnp.float32
     ).astype(jnp.bfloat16)
@@ -215,14 +226,13 @@
     out_ref[...] = jnp.dot(attended, out_weight_ref[...], preferred_element_type=jnp.float32).astype(jnp.bfloat16)
 
 
-def expand_kernel(user_dev, pieces, cap, known_ref, fetched_ref, out_hbm, out_ref, sems):
+def expand_kernel(user_dev, pieces, cap, known_ref, order_ref, fetched_ref, out_hbm, out_ref, sems):
     n_lists, block, width = fetched_ref.shape
     kept = block - cap
     rows = n_lists * kept
     returned = fetched_ref[:, cap:, :].reshape(rows, width)
     count = out_ref.shape[0]
-    first = known_ref.shape[1] - count
-    probe = jnp.transpose(known_ref[:, first:])[:, :1].astype(jnp.int32)
+    probe = jnp.transpose(known_ref[:, :count])[:, 1:2].astype(jnp.int32)
     user = lax.broadcasted_iota(jnp.int32, (count, 1), 0) // (count // user_dev)
     sends = []
     for piece in range(pieces):
@@ -241,6 +251,14 @@
 VMEM = pl.BlockSpec(memory_space=pltpu.VMEM)
 HBM = pl.BlockSpec(memory_space=pltpu.HBM)
 PARAMS = pltpu.CompilerParams(vmem_limit_bytes=VMEM_BYTES)
+
+
+def exchange(value):
+    count = lax.axis_size("lists")
+    group = sorted(range(count), key=lambda index: position(index, count))
+    return lax.all_to_all(
+        value, "lists", split_axis=0, concat_axis=0, axis_index_groups=[group], tiled=True
+    )
 
 
 def shards(
@@ -283,21 +301,29 @@
         out_specs=VMEM,
         compiler_params=pltpu.CompilerParams(vmem_limit_bytes=ALL_VMEM_BYTES),
     )(candidate_ids, user_vectors)
-    gathered = lax.all_to_all(pack, "lists", split_axis=0, concat_axis=0, tiled=True)
+    gathered = exchange(pack)
     gathered = gathered.reshape(n_lists * pack_rows, LANES)
 
-    known, items = pl.pallas_call(
-        functools.partial(early_kernel, n_lists, n_users, block),
+    items = pl.pallas_call(
+        items_kernel,
+        out_shape=jax.ShapeDtypeStruct((items_loc, width), bf16),
+        in_specs=[HBM],
+        out_specs=VMEM,
+        scratch_shapes=[pltpu.SemaphoreType.DMA((4,))],
+        compiler_params=PARAMS,
+    )(flat_items)
+    gathered, items = lax.optimization_barrier((gathered, items))
+
+    known, order = pl.pallas_call(
+        functools.partial(known_kernel, n_lists, items_loc, n_users, block),
         out_shape=(
-            jax.ShapeDtypeStruct((8, cands + user_dev * probes), jnp.float32),
-            jax.ShapeDtypeStruct((items_loc, width), bf16),
+            jax.ShapeDtypeStruct((8, cands), jnp.float32),
+            jax.ShapeDtypeStruct((8, LANES), jnp.float32),
         ),
-        in_specs=[SMEM, VMEM, VMEM, HBM],
+        in_specs=[SMEM, VMEM, VMEM],
         out_specs=(VMEM, VMEM),
-        scratch_shapes=[pltpu.SemaphoreType.DMA((4,))],
-        compiler_params=PARAMS,
-    )(col_arg, candidate_ids, probe_lists, flat_items)
-    gathered, known, items = lax.optimization_barrier((gathered, known, items))
+        compiler_params=PARAMS,
+    )(col_arg, candidate_ids, probe_lists)
 
     events = history.reshape(-1, width)
     hist = [events]
@@ -328,9 +354,11 @@
         ],
         compiler_params=PARAMS,
     )(base_arg, gathered, items)
-    fetched = lax.all_to_all(answers, "lists", split_axis=0, concat_axis=0, tiled=True)
-
-    fetched, keys, values, turned = lax.optimization_barrier((fetched, keys, values, turned))
+    fetched = exchange(answers)
+
+    fetched, known, order, keys, values, turned = lax.optimization_barrier(
+        (fetched, known, order, keys, values, turned)
+    )
 
     placed = pl.pallas_call(
         functools.partial(place_kernel, n_users),
@@ -356,14 +384,14 @@
     list_scores = pl.pallas_call(
         functools.partial(expand_kernel, user_dev, pieces, cap),
         out_shape=jax.ShapeDtypeStruct((user_dev * probes, items_loc), bf16),
-        in_specs=[VMEM, VMEM],
+        in_specs=[VMEM, pl.BlockSpec(memory_space=pl.ANY), VMEM],
         out_specs=pl.BlockSpec(memory_space=pl.ANY),
         scratch_shapes=[
             pltpu.VMEM((user_dev * probes, items_loc), bf16),
             pltpu.SemaphoreType.DMA((pieces,)),
         ],
         compiler_params=PARAMS,
-    )(known, fetched)
+    )(known, order, fetched)
     return (list_scores.reshape(user_dev, probes, items_loc), ranked.reshape(1, share, width))
 
 

time: 55.6 us -> 55.9 us (level)
  waiting for transfers between devices: 24.6 us -> 26.7 us
  local copies, waits for them, and re-layouts: 6 us -> 4.5 us
    all_to_all x2, waiting for transfers between devices: 23.5 us -> 26.6 us  [exchange(): lax.all_to_all(value, 'lists', split_axis=0, concat_axis=0, axis_index_gr...]
    unnamed x26, local copies, waits for them, and re-layouts: 6 us -> 4.5 us
    ppermute x1, waiting for transfers between devices: 0.68 us -> 0.01 us  [shards(): lax.ppermute(events, 'users', [(i, (i + shift) % n_users) for i in range(...]
  transfers between devices with their start and end apart: 4 -> 4, of which waited for: 4 -> 2; matrix products, arithmetic and copies ran while one was open for 0% -> 0% of each run, Pallas kernels for 4% -> 4%
where the time goes in v5:
time: 55.9 us; the launch traced here: 55.5 us
  waiting for transfers between devices  26.7 us (48%)
  starting transfers between devices  12.3 us (22%)
  Pallas kernels  10.6 us (19%)
  local copies, waits for them, and re-layouts  4.5 us (8%)
  between operations  1.47 us (3%)
    all_to_all x2, waiting for transfers between devices, exchange(): lax.all_to_all(value, 'lists', split_axis=0, concat_axis=0, axis_index_gr...  26.6 us
    all_to_all x2, starting transfers between devices, exchange(): lax.all_to_all(value, 'lists', split_axis=0, concat_axis=0, axis_index_gr...  12.1 us
    unnamed x26, local copies, waits for them, and re-layouts  4.5 us
    pallas_call x1, Pallas kernels, shards(): pl.pallas_call(functools.partial(owner_kernel, n_lists, user_dev, digits,...  3.82 us
    pallas_call x1, Pallas kernels, shards(): pl.pallas_call(functools.partial(attend_kernel, n_users), out_shape=jax.S...  2.32 us
    pallas_call x1, Pallas kernels, shards(): pl.pallas_call(functools.partial(pack_kernel, digits), out_shape=jax.Shap...  1.36 us
    pallas_call x1, Pallas kernels, shards(): pl.pallas_call(functools.partial(expand_kernel, user_dev, pieces, cap), o...  1.13 us
  transfers between devices with their start and end apart: 4, of which 2 were waited for; matrix products, arithmetic and copies ran while one was open for 0% of the time, Pallas kernels for 4%

profile of v5, /device:TPU:0, one launch (start us, length us, event | category | flops | bytes accessed | tf_op | source)
XLA Modules:
  0.0 55.5 jit_solution(13959818586200043349)
XLA Ops:
  0.6 1.4 %shard_map.104 = bf16[16,24,128]{2,1,0:T(8,128)(2,1)} custom-call(s32[1,512]{1,0:T(1,128)} %ids_ref.3, bf16[4,512]{1,0:T(4,128)(2,1)} %vectors_ref.1), custom_call_target="tpu_custom_call" | custom-call | tf_op jit(solution)/shard_map/pallas_call | solution.py:297
  2.0 8.3 %all-to-all-start = ((bf16[16,24,128]{2,1,0:T(8,128)(2,1)}), bf16[16,24,128]{2,1,0:T(8,128)(2,1)S(1)}, u32[]{:S(2)}, u32[]{:S(2)}) async-start(bf16[16,24,128]{2,1,0:T(8,128)(2,1)} %shard_map.104), calls=%async_computation | async-start | bytes 196608 | tf_op jit(solution)/shard_map/all_to_all | solution.py:259
  10.3 0.0 copy-start
  10.3 1.6 %copy-done = bf16[1,2048,512]{2,1,0:T(8,128)(2,1)S(1)} copy-done((bf16[1,2048,512]{2,1,0:T(8,128)(2,1)S(1)}, bf16[1,2048,512]{2,1,0:T(8,128)(2,1)}, u32[]{:S(2)}) %copy-start) | copy-done | bytes 2097176
  11.9 0.2 shard_map.105.items_ref
  12.1 5.7 %all-to-all-done = bf16[16,24,128]{2,1,0:T(8,128)(2,1)S(1)} async-done(((bf16[16,24,128]{2,1,0:T(8,128)(2,1)}), bf16[16,24,128]{2,1,0:T(8,128)(2,1)S(1)}, u32[]{:S(2)}, u32[]{:S(2)}) %all-to-all-start) | async-done | bytes 98336 | tf_op jit(solution)/shard_map/all_to_all | solution.py:259
  17.9 3.8 %shard_map.106 = bf16[16,64,512]{2,1,0:T(8,128)(2,1)} custom-call(s32[1]{0:T(128)} %bitcast.base_ref, bf16[384,128]{1,0:T(8,128)(2,1)S(1)} %bitcast.8, bf16[2048,512]{1,0:T(8,128)(2,1)S(1)} %shard_map.105.items_ref), custom_call_target="tpu_custom_call" | custom-call | tf_op jit(solution)/shard_map/pallas_call | solution.py:346
  21.7 0.0 copy-start.2
  21.7 3.8 %all-to-all-start.1 = ((bf16[16,64,512]{2,1,0:T(8,128)(2,1)}), bf16[16,64,512]{2,1,0:T(8,128)(2,1)S(1)}, u32[]{:S(2)}, u32[]{:S(2)}) async-start(bf16[16,64,512]{2,1,0:T(8,128)(2,1)} %shard_map.106), calls=%async_computation.1 | async-start | bytes 2097152 | tf_op jit(solution)/shard_map/all_to_all | solution.py:259
  25.5 0.0 copy-done.8
  25.5 0.1 collective-permute-start
  26.2 0.0 copy-done.9
  26.2 0.0 copy-done.12
  26.3 0.2 shard_map.107
  26.5 0.0 copy-start.10
  26.5 0.6 %copy-done.10 = f32[8,128]{1,0:T(8,128)} copy-done((f32[8,128]{1,0:T(8,128)}, f32[8,128]{1,0:T(8,128)S(1)}, u32[]{:S(2)}) %copy-start.10) | copy-done | bytes 4120
  27.1 0.0 collective-permute-done.refs_1_
  27.1 0.0 copy-done.1
  27.1 0.0 copy-done.2
  27.1 0.6 %shard_map.108 = (bf16[8,256,80]{2,1,0:T(8,128)(2,1)S(1)}, bf16[512,256]{1,0:T(8,128)(2,1)S(1)}, bf16[512,512]{1,0:T(8,128)(2,1)S(1)}) custom-call(s32[1]{0:T(128)} %bitcast.3.col_ref, s32[1]{0:T(128)S(6)} %copy.11.length_ref, bf16[128,512]{1,0:T(8,128)(2,1)S(1)} %bitcast.10, bf16[128,512]{1,0:T(8,128)(2,1)S(1)} %collective-permute-done.refs_1_, ...), custom_call_target="tpu_custom_call" | custom-call | tf_op jit(solution)/shard_map/pallas_call | solution.py:333
  27.7 0.0 copy-start.4
  27.7 0.8 %copy-done.4 = bf16[8,256,80]{2,1,0:T(8,128)(2,1)} copy-done((bf16[8,256,80]{2,1,0:T(8,128)(2,1)}, bf16[8,256,80]{2,1,0:T(8,128)(2,1)S(1)}, u32[]{:S(2)}) %copy-start.4) | copy-done | bytes 327704
  28.5 0.8 %copy-done.6 = bf16[512,512]{1,0:T(8,128)(2,1)} copy-done((bf16[512,512]{1,0:T(8,128)(2,1)}, bf16[512,512]{1,0:T(8,128)(2,1)S(1)}, u32[]{:S(2)}) %copy-start.6) | copy-done | bytes 524312
  29.3 20.9 %all-to-all-done.1.fetched_ref = bf16[16,64,512]{2,1,0:T(8,128)(2,1)S(1)} async-done(((bf16[16,64,512]{2,1,0:T(8,128)(2,1)}), bf16[16,64,512]{2,1,0:T(8,128)(2,1)S(1)}, u32[]{:S(2)}, u32[]{:S(2)}) %all-to-all-start.1) | async-done | bytes 1048608 | tf_op jit(solution)/shard_map/all_to_all | solution.py:259
  50.2 1.0 %shard_map.110 = (bf16[256,512]{1,0:T(8,128)(2,1)S(1)}, bf16[256,512]{1,0:T(8,128)(2,1)S(1)}) custom-call(s32[1]{0:T(128)} %bitcast.3.col_ref, f32[8,512]{1,0:T(8,128)S(1)} %get-tuple-element.24.known_ref, bf16[16,64,512]{2,1,0:T(8,128)(2,1)S(1)} %all-to-all-done.1.fetched_ref), custom_call_target="tpu_custom_call" | custom-call | tf_op jit(solution)/shard_map/pallas_call | solution.py:363
  51.2 0.1 collective-permute-start.1
  51.3 0.0 copy-start.11
  51.3 0.7 %copy-done.11 = f32[8,128]{1,0:T(8,128)S(1)} copy-done((f32[8,128]{1,0:T(8,128)S(1)}, f32[8,128]{1,0:T(8,128)}, u32[]{:S(2)}) %copy-start.11) | copy-done | bytes 4120
  52.0 1.1 %shard_map.109 = bf16[128,2048]{1,0:T(8,128)(2,1)} custom-call(f32[8,512]{1,0:T(8,128)S(1)} %get-tuple-element.24.known_ref, f32[8,128]{1,0:T(8,128)S(1)} %copy-done.11, bf16[16,64,512]{2,1,0:T(8,128)(2,1)S(1)} %all-to-all-done.1.fetched_ref), custom_call_target="tpu_custom_call" | custom-call | tf_op jit(solution)/shard_map/pallas_call | solution.py:384
  53.2 0.0 collective-permute-done.1.refs_1_
  53.2 0.0 copy-done.3
  53.2 2.3 %shard_map.111 = bf16[256,512]{1,0:T(8,128)(2,1)} custom-call(bf16[256,512]{1,0:T(8,128)(2,1)S(1)} %get-tuple-element.27.refs_0_, bf16[256,512]{1,0:T(8,128)(2,1)S(1)} %collective-permute-done.1.refs_1_, bf16[8,256,80]{2,1,0:T(8,128)(2,1)S(1)} %copy-done.5, bf16[512,256]{1,0:T(8,128)(2,1)S(1)} %get-tuple-element.30.refs_3_, bf16[512,512]{1,0:T(8,128)(2,1)S(1)} %copy-done.7, ...), custom_call_target="tpu_custom_call" | custom-call | tf_op jit(solution)/shard_map/pallas_call | solution.py:376
  (10 shorter events, 0.0 us)
Async XLA Ops:
  2.0 15.9 %all-to-all-start = ((bf16[16,24,128]{2,1,0:T(8,128)(2,1)}), bf16[16,24,128]{2,1,0:T(8,128)(2,1)S(1)}, u32[]{:S(2)}, u32[]{:S(2)}) async-start(bf16[16,24,128]{2,1,0:T(8,128)(2,1)} %shard_map.104), calls=%async_computation | async-start | bytes 196608 | tf_op jit(solution)/shard_map/all_to_all | solution.py:259
  10.3 1.6 %copy-start = (bf16[1,2048,512]{2,1,0:T(8,128)(2,1)S(1)}, bf16[1,2048,512]{2,1,0:T(8,128)(2,1)}, u32[]{:S(2)}) copy-start(bf16[1,2048,512]{2,1,0:T(8,128)(2,1)} %param.11) | copy-start | bytes 6291460
  17.8 7.7 %copy-start.8 = (bf16[1,128,512]{2,1,0:T(8,128)(2,1)S(1)}, bf16[1,128,512]{2,1,0:T(8,128)(2,1)}, u32[]{:S(2)}) copy-start(bf16[1,128,512]{2,1,0:T(8,128)(2,1)} %param.13) | copy-start | bytes 393220
  17.8 8.4 %copy-start.9 = (s32[1,512]{1,0:T(1,128)S(1)}, s32[1,512]{1,0:T(1,128)}, u32[]{:S(2)}) copy-start(s32[1,512]{1,0:T(1,128)} %ids_ref.3) | copy-start | bytes 6148
  17.8 8.4 %copy-start.12 = (s32[4,32]{1,0:T(4,128)S(1)}, s32[4,32]{1,0:T(4,128)}, u32[]{:S(2)}) copy-start(s32[4,32]{1,0:T(4,128)} %probes_ref.1) | copy-start | bytes 1540
  17.8 9.2 %copy-start.1 = (bf16[512,1024]{1,0:T(8,128)(2,1)S(1)}, bf16[512,1024]{1,0:T(8,128)(2,1)}, u32[]{:S(2)}) copy-start(bf16[512,1024]{1,0:T(8,128)(2,1)} %refs_2_.1) | copy-start | bytes 3145732
  21.7 5.4 %copy-start.2 = (bf16[512,512]{1,0:T(8,128)(2,1)S(1)}, bf16[512,512]{1,0:T(8,128)(2,1)}, u32[]{:S(2)}) copy-start(bf16[512,512]{1,0:T(8,128)(2,1)} %refs_3_.1) | copy-start | bytes 1572868
  21.7 28.5 %all-to-all-start.1 = ((bf16[16,64,512]{2,1,0:T(8,128)(2,1)}), bf16[16,64,512]{2,1,0:T(8,128)(2,1)S(1)}, u32[]{:S(2)}, u32[]{:S(2)}) async-start(bf16[16,64,512]{2,1,0:T(8,128)(2,1)} %shard_map.106), calls=%async_computation.1 | async-start | bytes 2097152 | tf_op jit(solution)/shard_map/all_to_all | solution.py:259
  25.5 1.5 %collective-permute-start = (bf16[128,512]{1,0:T(8,128)(2,1)S(1)}, bf16[128,512]{1,0:T(8,128)(2,1)S(1)}, u32[]{:S(2)}, u32[]{:S(2)}) collective-permute-start(bf16[128,512]{1,0:T(8,128)(2,1)S(1)} %bitcast.9), channel_id=1, source_target_pairs={{0,1},{1,0},{2,3},{3,2},{4,5},{5,4},{6,7},{7,6},{8,9},{9,8},{10,11... | collective-permute-start | bytes 393224 | tf_op jit(solution)/shard_map/ppermute | solution.py:331
  26.5 0.6 %copy-start.10 = (f32[8,128]{1,0:T(8,128)}, f32[8,128]{1,0:T(8,128)S(1)}, u32[]{:S(2)}) copy-start(f32[8,128]{1,0:T(8,128)S(1)} %get-tuple-element.25.order_ref) | copy-start | bytes 12292
  27.1 26.1 %copy-start.3 = (bf16[512,512]{1,0:T(8,128)(2,1)S(1)}, bf16[512,512]{1,0:T(8,128)(2,1)}, u32[]{:S(2)}) copy-start(bf16[512,512]{1,0:T(8,128)(2,1)} %refs_5_.1) | copy-start | bytes 1572868
  27.7 0.8 %copy-start.4 = (bf16[8,256,80]{2,1,0:T(8,128)(2,1)}, bf16[8,256,80]{2,1,0:T(8,128)(2,1)S(1)}, u32[]{:S(2)}) copy-start(bf16[8,256,80]{2,1,0:T(8,128)(2,1)S(1)} %get-tuple-element.29.refs_2_) | copy-start | bytes 983044
  28.5 0.8 %copy-start.6 = (bf16[512,512]{1,0:T(8,128)(2,1)}, bf16[512,512]{1,0:T(8,128)(2,1)S(1)}, u32[]{:S(2)}) copy-start(bf16[512,512]{1,0:T(8,128)(2,1)S(1)} %get-tuple-element.31.refs_4_) | copy-start | bytes 1572868
  50.2 3.0 %copy-start.5 = (bf16[8,256,80]{2,1,0:T(8,128)(2,1)S(1)}, bf16[8,256,80]{2,1,0:T(8,128)(2,1)}, u32[]{:S(2)}) copy-start(bf16[8,256,80]{2,1,0:T(8,128)(2,1)} %copy-done.4) | copy-start | bytes 983044
  50.2 3.0 %copy-start.7 = (bf16[512,512]{1,0:T(8,128)(2,1)S(1)}, bf16[512,512]{1,0:T(8,128)(2,1)}, u32[]{:S(2)}) copy-start(bf16[512,512]{1,0:T(8,128)(2,1)} %copy-done.6) | copy-start | bytes 1572868
  51.2 1.9 %collective-permute-start.1 = (bf16[256,512]{1,0:T(8,128)(2,1)S(1)}, bf16[256,512]{1,0:T(8,128)(2,1)S(1)}, u32[]{:S(2)}, u32[]{:S(2)}) collective-permute-start(bf16[256,512]{1,0:T(8,128)(2,1)S(1)} %get-tuple-element.28), channel_id=1, source_target_pairs={{0,1},{1,0},{2,3},{3,2},{4,5},{5,4},{6,7},{7,6},{8,9},{9,8},{10,11... | collective-permute-start | bytes 786440 | tf_op jit(solution)/shard_map/ppermute | solution.py:374
  51.3 0.7 %copy-start.11 = (f32[8,128]{1,0:T(8,128)S(1)}, f32[8,128]{1,0:T(8,128)}, u32[]{:S(2)}) copy-start(f32[8,128]{1,0:T(8,128)} %copy-done.10) | copy-start | bytes 12292

commit v6 on v5

--- a/solution.py
+++ b/solution.py
@@ -11,6 +11,7 @@
 BASE = 256
 LANES = 128
 ROW_TILE = 16
+PROBE_ROWS = 1024
 VMEM_BYTES = 28 * 1024 * 1024
 ALL_VMEM_BYTES = 62 * 1024 * 1024
 
@@ -86,8 +87,13 @@
 
 
 def position(index, count):
-    half = max(1, count // 2)
-    return index % half * 2 + index // half if count > 1 else index
+    bits = count.bit_length() - 1
+    if count != 1 << bits:
+        return index
+    place = index * 0
+    for bit in range(bits):
+        place = place | (((index >> bit) & 1) << (bits - 1 - bit))
+    return place
 
 
 def items_kernel(items_hbm, items_ref, sems):
@@ -101,7 +107,7 @@
         load.wait()
 
 
-def known_kernel(n_lists, items_loc, n_users, block, col_ref, ids_ref, probes_ref, known_ref, order_ref):
+def known_kernel(n_lists, items_loc, n_users, block, col_ref, ids_ref, probes_ref, slot_ref, probe_ref):
     ids = ids_ref[...]
     cands = ids.shape[1]
     bins = ids // items_loc
@@ -114,11 +120,8 @@
     slot = jnp.where(mine, position(owner, n_lists).astype(jnp.float32) * block + rank, -1.0)
     probes = position(probes_ref[...], n_lists).astype(jnp.float32)
     flat = jnp.concatenate([probes[u : u + 1] for u in range(probes.shape[0])], axis=1)
-    if flat.shape[1] < cands:
-        flat = jnp.concatenate([flat, jnp.zeros((1, cands - flat.shape[1]), jnp.float32)], axis=1)
-    row = lax.broadcasted_iota(jnp.int32, known_ref.shape, 0)
-    known_ref[...] = jnp.where(row == 0, slot, flat)
-    order_ref[...] = jnp.zeros_like(order_ref)
+    slot_ref[...] = jnp.broadcast_to(slot, slot_ref.shape)
+    probe_ref[...] = jnp.broadcast_to(flat, probe_ref.shape)
 
 
 def pairs_kernel(n_parts, col_ref, length_ref, *refs):
@@ -180,12 +183,12 @@
         send.wait()
 
 
-def place_kernel(n_users, col_ref, known_ref, fetched_ref, *refs):
+def place_kernel(n_users, col_ref, slot_ref, fetched_ref, *refs):
     share_refs, scratch = refs[:-1], refs[-1]
     n_lists, block, width = fetched_ref.shape
     fetched = fetched_ref[...].reshape(n_lists * block, width)
     share = share_refs[0].shape[0]
-    slot = jnp.transpose(known_ref[...])[:, :1].astype(jnp.int32)
+    slot = jnp.transpose(slot_ref[...])[:, :1].astype(jnp.int32)
     scratch[...] = jnp.dot(
         picks(slot, fetched.shape[0]), fetched, preferred_element_type=jnp.float32
     ).astype(jnp.bfloat16)
@@ -226,13 +229,13 @@
     out_ref[...] = jnp.dot(attended, out_weight_ref[...], preferred_element_type=jnp.float32).astype(jnp.bfloat16)
 
 
-def expand_kernel(user_dev, pieces, cap, known_ref, order_ref, fetched_ref, out_hbm, out_ref, sems):
+def expand_kernel(user_dev, pieces, cap, probe_ref, fetched_ref, out_hbm, out_ref, sems):
     n_lists, block, width = fetched_ref.shape
     kept = block - cap
     rows = n_lists * kept
     returned = fetched_ref[:, cap:, :].reshape(rows, width)
     count = out_ref.shape[0]
-    probe = jnp.transpose(known_ref[:, :count])[:, 1:2].astype(jnp.int32)
+    probe = jnp.transpose(probe_ref[:8, :])[:, :1].astype(jnp.int32)
     user = lax.broadcasted_iota(jnp.int32, (count, 1), 0) // (count // user_dev)
     sends = []
     for piece in range(pieces):
@@ -314,11 +317,11 @@
     )(flat_items)
     gathered, items = lax.optimization_barrier((gathered, items))
 
-    known, order = pl.pallas_call(
+    slot, probe_row = pl.pallas_call(
         functools.partial(known_kernel, n_lists, items_loc, n_users, block),
         out_shape=(
             jax.ShapeDtypeStruct((8, cands), jnp.float32),
-            jax.ShapeDtypeStruct((8, LANES), jnp.float32),
+            jax.ShapeDtypeStruct((PROBE_ROWS, user_dev * probes), jnp.float32),
         ),
         in_specs=[SMEM, VMEM, VMEM],
         out_specs=(VMEM, VMEM),
@@ -356,8 +359,8 @@
     )(base_arg, gathered, items)
     fetched = exchange(answers)
 
-    fetched, known, order, keys, values, turned = lax.optimization_barrier(
-        (fetched, known, order, keys, values, turned)
+    fetched, slot, probe_row, keys, values, turned = lax.optimization_barrier(
+        (fetched, slot, probe_row, keys, values, turned)
     )
 
     placed = pl.pallas_call(
@@ -367,7 +370,7 @@
         out_specs=tuple(VMEM for _ in range(n_users)),
         scratch_shapes=[pltpu.VMEM((cands, width), bf16)],
         compiler_params=PARAMS,
-    )(col_arg, known, fetched)
+    )(col_arg, slot, fetched)
     parts = [placed[0]]
     for shift in range(1, n_users):
         parts.append(
@@ -384,14 +387,14 @@
     list_scores = pl.pallas_call(
         functools.partial(expand_kernel, user_dev, pieces, cap),
         out_shape=jax.ShapeDtypeStruct((user_dev * probes, items_loc), bf16),
-        in_specs=[VMEM, pl.BlockSpec(memory_space=pl.ANY), VMEM],
+        in_specs=[VMEM, VMEM],
         out_specs=pl.BlockSpec(memory_space=pl.ANY),
         scratch_shapes=[
             pltpu.VMEM((user_dev * probes, items_loc), bf16),
             pltpu.SemaphoreType.DMA((pieces,)),
         ],
         compiler_params=PARAMS,
-    )(known, order, fetched)
+    )(probe_row, fetched)
     return (list_scores.reshape(user_dev, probes, items_loc), ranked.reshape(1, share, width))
 
 

time: 55.9 us -> 56 us (level)
  waiting for transfers between devices: 26.7 us -> 26.1 us
where the time goes in v6:
time: 56 us; the launch traced here: 55.6 us
  waiting for transfers between devices  26.1 us (47%)
  starting transfers between devices  12.3 us (22%)
  Pallas kernels  10.6 us (19%)
  local copies, waits for them, and re-layouts  5.05 us (9%)
  between operations  1.47 us (3%)
    all_to_all x2, waiting for transfers between devices, exchange(): lax.all_to_all(value, 'lists', split_axis=0, concat_axis=0, axis_index_gr...  26.1 us
    all_to_all x2, starting transfers between devices, exchange(): lax.all_to_all(value, 'lists', split_axis=0, concat_axis=0, axis_index_gr...  12.1 us
    unnamed x26, local copies, waits for them, and re-layouts  5.05 us
    pallas_call x1, Pallas kernels, shards(): pl.pallas_call(functools.partial(owner_kernel, n_lists, user_dev, digits,...  3.82 us
    pallas_call x1, Pallas kernels, shards(): pl.pallas_call(functools.partial(attend_kernel, n_users), out_shape=jax.S...  2.32 us
    pallas_call x1, Pallas kernels, shards(): pl.pallas_call(functools.partial(pack_kernel, digits), out_shape=jax.Shap...  1.36 us
    pallas_call x1, Pallas kernels, shards(): pl.pallas_call(functools.partial(expand_kernel, user_dev, pieces, cap), o...  1.14 us
  transfers between devices with their start and end apart: 4, of which 2 were waited for; matrix products, arithmetic and copies ran while one was open for 0% of the time, Pallas kernels for 4%

profile of v6, /device:TPU:0, one launch (start us, length us, event | category | flops | bytes accessed | tf_op | source)
XLA Modules:
  0.0 55.6 jit_solution(2844090799452691574)
XLA Ops:
  0.6 1.4 %shard_map.104 = bf16[16,24,128]{2,1,0:T(8,128)(2,1)} custom-call(s32[1,512]{1,0:T(1,128)} %ids_ref.3, bf16[4,512]{1,0:T(4,128)(2,1)} %vectors_ref.1), custom_call_target="tpu_custom_call" | custom-call | tf_op jit(solution)/shard_map/pallas_call | solution.py:300
  2.0 8.3 %all-to-all-start = ((bf16[16,24,128]{2,1,0:T(8,128)(2,1)}), bf16[16,24,128]{2,1,0:T(8,128)(2,1)S(1)}, u32[]{:S(2)}, u32[]{:S(2)}) async-start(bf16[16,24,128]{2,1,0:T(8,128)(2,1)} %shard_map.104), calls=%async_computation | async-start | bytes 196608 | tf_op jit(solution)/shard_map/all_to_all | solution.py:262
  10.3 0.0 copy-start
  10.3 1.6 %copy-done = bf16[1,2048,512]{2,1,0:T(8,128)(2,1)S(1)} copy-done((bf16[1,2048,512]{2,1,0:T(8,128)(2,1)S(1)}, bf16[1,2048,512]{2,1,0:T(8,128)(2,1)}, u32[]{:S(2)}) %copy-start) | copy-done | bytes 2097176
  11.9 0.2 shard_map.105.items_ref
  12.1 5.7 %all-to-all-done = bf16[16,24,128]{2,1,0:T(8,128)(2,1)S(1)} async-done(((bf16[16,24,128]{2,1,0:T(8,128)(2,1)}), bf16[16,24,128]{2,1,0:T(8,128)(2,1)S(1)}, u32[]{:S(2)}, u32[]{:S(2)}) %all-to-all-start) | async-done | bytes 98336 | tf_op jit(solution)/shard_map/all_to_all | solution.py:262
  17.9 3.8 %shard_map.106 = bf16[16,64,512]{2,1,0:T(8,128)(2,1)} custom-call(s32[1]{0:T(128)} %bitcast.base_ref, bf16[384,128]{1,0:T(8,128)(2,1)S(1)} %bitcast.8, bf16[2048,512]{1,0:T(8,128)(2,1)S(1)} %shard_map.105.items_ref), custom_call_target="tpu_custom_call" | custom-call | tf_op jit(solution)/shard_map/pallas_call | solution.py:349
  21.7 0.0 copy-start.2
  21.7 3.8 %all-to-all-start.1 = ((bf16[16,64,512]{2,1,0:T(8,128)(2,1)}), bf16[16,64,512]{2,1,0:T(8,128)(2,1)S(1)}, u32[]{:S(2)}, u32[]{:S(2)}) async-start(bf16[16,64,512]{2,1,0:T(8,128)(2,1)} %shard_map.106), calls=%async_computation.1 | async-start | bytes 2097152 | tf_op jit(solution)/shard_map/all_to_all | solution.py:262
  25.5 0.0 copy-done.10
  25.5 0.1 collective-permute-start
  26.2 0.0 copy-done.11
  26.2 0.0 copy-done.12
  26.3 0.2 shard_map.107
  26.5 0.0 copy-start.8
  26.5 0.8 %copy-done.8 = f32[1024,128]{1,0:T(8,128)} copy-done((f32[1024,128]{1,0:T(8,128)}, f32[1024,128]{1,0:T(8,128)S(1)}, u32[]{:S(2)}) %copy-start.8) | copy-done | bytes 524312
  27.3 0.0 collective-permute-done.refs_1_
  27.3 0.0 copy-done.1
  27.3 0.6 %shard_map.108 = (bf16[8,256,80]{2,1,0:T(8,128)(2,1)S(1)}, bf16[512,256]{1,0:T(8,128)(2,1)S(1)}, bf16[512,512]{1,0:T(8,128)(2,1)S(1)}) custom-call(s32[1]{0:T(128)} %bitcast.3.col_ref, s32[1]{0:T(128)S(6)} %copy.11.length_ref, bf16[128,512]{1,0:T(8,128)(2,1)S(1)} %bitcast.10, bf16[128,512]{1,0:T(8,128)(2,1)S(1)} %collective-permute-done.refs_1_, ...), custom_call_target="tpu_custom_call" | custom-call | tf_op jit(solution)/shard_map/pallas_call | solution.py:336
  27.9 0.8 %copy-done.4 = bf16[8,256,80]{2,1,0:T(8,128)(2,1)} copy-done((bf16[8,256,80]{2,1,0:T(8,128)(2,1)}, bf16[8,256,80]{2,1,0:T(8,128)(2,1)S(1)}, u32[]{:S(2)}) %copy-start.4) | copy-done | bytes 327704
  28.7 0.8 %copy-done.6 = bf16[512,512]{1,0:T(8,128)(2,1)} copy-done((bf16[512,512]{1,0:T(8,128)(2,1)}, bf16[512,512]{1,0:T(8,128)(2,1)S(1)}, u32[]{:S(2)}) %copy-start.6) | copy-done | bytes 524312
  29.5 20.4 %all-to-all-done.1.fetched_ref = bf16[16,64,512]{2,1,0:T(8,128)(2,1)S(1)} async-done(((bf16[16,64,512]{2,1,0:T(8,128)(2,1)}), bf16[16,64,512]{2,1,0:T(8,128)(2,1)S(1)}, u32[]{:S(2)}, u32[]{:S(2)}) %all-to-all-start.1) | async-done | bytes 1048608 | tf_op jit(solution)/shard_map/all_to_all | solution.py:262
  49.9 1.1 %shard_map.110 = (bf16[256,512]{1,0:T(8,128)(2,1)S(1)}, bf16[256,512]{1,0:T(8,128)(2,1)S(1)}) custom-call(s32[1]{0:T(128)} %bitcast.3.col_ref, f32[8,512]{1,0:T(8,128)S(1)} %get-tuple-element.26.slot_ref, bf16[16,64,512]{2,1,0:T(8,128)(2,1)S(1)} %all-to-all-done.1.fetched_ref), custom_call_target="tpu_custom_call" | custom-call | tf_op jit(solution)/shard_map/pallas_call | solution.py:366
  50.9 0.1 collective-permute-start.1
  51.0 0.0 copy-start.9
  51.0 1.0 %copy-done.9 = f32[1024,128]{1,0:T(8,128)S(1)} copy-done((f32[1024,128]{1,0:T(8,128)S(1)}, f32[1024,128]{1,0:T(8,128)}, u32[]{:S(2)}) %copy-start.9) | copy-done | bytes 524312
  52.1 1.1 %shard_map.109 = bf16[128,2048]{1,0:T(8,128)(2,1)} custom-call(f32[1024,128]{1,0:T(8,128)S(1)} %copy-done.9, bf16[16,64,512]{2,1,0:T(8,128)(2,1)S(1)} %all-to-all-done.1.fetched_ref), custom_call_target="tpu_custom_call" | custom-call | tf_op jit(solution)/shard_map/pallas_call | solution.py:387
  53.2 0.0 collective-permute-done.1.refs_1_
  53.2 0.0 copy-done.3
  53.2 0.0 copy-done.5
  53.2 0.0 copy-done.7
  53.2 2.3 %shard_map.111 = bf16[256,512]{1,0:T(8,128)(2,1)} custom-call(bf16[256,512]{1,0:T(8,128)(2,1)S(1)} %get-tuple-element.27.refs_0_, bf16[256,512]{1,0:T(8,128)(2,1)S(1)} %collective-permute-done.1.refs_1_, bf16[8,256,80]{2,1,0:T(8,128)(2,1)S(1)} %copy-done.5, bf16[512,256]{1,0:T(8,128)(2,1)S(1)} %get-tuple-element.30.refs_3_, bf16[512,512]{1,0:T(8,128)(2,1)S(1)} %copy-done.7, ...), custom_call_target="tpu_custom_call" | custom-call | tf_op jit(solution)/shard_map/pallas_call | solution.py:379
  (10 shorter events, 0.0 us)
Async XLA Ops:
  2.0 15.9 %all-to-all-start = ((bf16[16,24,128]{2,1,0:T(8,128)(2,1)}), bf16[16,24,128]{2,1,0:T(8,128)(2,1)S(1)}, u32[]{:S(2)}, u32[]{:S(2)}) async-start(bf16[16,24,128]{2,1,0:T(8,128)(2,1)} %shard_map.104), calls=%async_computation | async-start | bytes 196608 | tf_op jit(solution)/shard_map/all_to_all | solution.py:262
  10.3 1.6 %copy-start = (bf16[1,2048,512]{2,1,0:T(8,128)(2,1)S(1)}, bf16[1,2048,512]{2,1,0:T(8,128)(2,1)}, u32[]{:S(2)}) copy-start(bf16[1,2048,512]{2,1,0:T(8,128)(2,1)} %param.11) | copy-start | bytes 6291460
  17.8 7.7 %copy-start.10 = (bf16[1,128,512]{2,1,0:T(8,128)(2,1)S(1)}, bf16[1,128,512]{2,1,0:T(8,128)(2,1)}, u32[]{:S(2)}) copy-start(bf16[1,128,512]{2,1,0:T(8,128)(2,1)} %param.13) | copy-start | bytes 393220
  17.8 8.4 %copy-start.11 = (s32[1,512]{1,0:T(1,128)S(1)}, s32[1,512]{1,0:T(1,128)}, u32[]{:S(2)}) copy-start(s32[1,512]{1,0:T(1,128)} %ids_ref.3) | copy-start | bytes 6148
  17.8 8.4 %copy-start.12 = (s32[4,32]{1,0:T(4,128)S(1)}, s32[4,32]{1,0:T(4,128)}, u32[]{:S(2)}) copy-start(s32[4,32]{1,0:T(4,128)} %probes_ref.1) | copy-start | bytes 1540
  17.8 9.4 %copy-start.1 = (bf16[512,1024]{1,0:T(8,128)(2,1)S(1)}, bf16[512,1024]{1,0:T(8,128)(2,1)}, u32[]{:S(2)}) copy-start(bf16[512,1024]{1,0:T(8,128)(2,1)} %refs_2_.1) | copy-start | bytes 3145732
  21.7 5.6 %copy-start.2 = (bf16[512,512]{1,0:T(8,128)(2,1)S(1)}, bf16[512,512]{1,0:T(8,128)(2,1)}, u32[]{:S(2)}) copy-start(bf16[512,512]{1,0:T(8,128)(2,1)} %refs_3_.1) | copy-start | bytes 1572868
  21.7 28.2 %all-to-all-start.1 = ((bf16[16,64,512]{2,1,0:T(8,128)(2,1)}), bf16[16,64,512]{2,1,0:T(8,128)(2,1)S(1)}, u32[]{:S(2)}, u32[]{:S(2)}) async-start(bf16[16,64,512]{2,1,0:T(8,128)(2,1)} %shard_map.106), calls=%async_computation.1 | async-start | bytes 2097152 | tf_op jit(solution)/shard_map/all_to_all | solution.py:262
  25.5 1.7 %collective-permute-start = (bf16[128,512]{1,0:T(8,128)(2,1)S(1)}, bf16[128,512]{1,0:T(8,128)(2,1)S(1)}, u32[]{:S(2)}, u32[]{:S(2)}) collective-permute-start(bf16[128,512]{1,0:T(8,128)(2,1)S(1)} %bitcast.9), channel_id=1, source_target_pairs={{0,1},{1,0},{2,3},{3,2},{4,5},{5,4},{6,7},{7,6},{8,9},{9,8},{10,11... | collective-permute-start | bytes 393224 | tf_op jit(solution)/shard_map/ppermute | solution.py:334
  26.5 0.8 %copy-start.8 = (f32[1024,128]{1,0:T(8,128)}, f32[1024,128]{1,0:T(8,128)S(1)}, u32[]{:S(2)}) copy-start(f32[1024,128]{1,0:T(8,128)S(1)} %get-tuple-element.24.probe_ref) | copy-start | bytes 1572868
  27.3 26.0 %copy-start.3 = (bf16[512,512]{1,0:T(8,128)(2,1)S(1)}, bf16[512,512]{1,0:T(8,128)(2,1)}, u32[]{:S(2)}) copy-start(bf16[512,512]{1,0:T(8,128)(2,1)} %refs_5_.1) | copy-start | bytes 1572868
  27.9 0.8 %copy-start.4 = (bf16[8,256,80]{2,1,0:T(8,128)(2,1)}, bf16[8,256,80]{2,1,0:T(8,128)(2,1)S(1)}, u32[]{:S(2)}) copy-start(bf16[8,256,80]{2,1,0:T(8,128)(2,1)S(1)} %get-tuple-element.29.refs_2_) | copy-start | bytes 983044
  28.7 0.8 %copy-start.6 = (bf16[512,512]{1,0:T(8,128)(2,1)}, bf16[512,512]{1,0:T(8,128)(2,1)S(1)}, u32[]{:S(2)}) copy-start(bf16[512,512]{1,0:T(8,128)(2,1)S(1)} %get-tuple-element.31.refs_4_) | copy-start | bytes 1572868
  49.9 3.3 %copy-start.5 = (bf16[8,256,80]{2,1,0:T(8,128)(2,1)S(1)}, bf16[8,256,80]{2,1,0:T(8,128)(2,1)}, u32[]{:S(2)}) copy-start(bf16[8,256,80]{2,1,0:T(8,128)(2,1)} %copy-done.4) | copy-start | bytes 983044
  49.9 3.4 %copy-start.7 = (bf16[512,512]{1,0:T(8,128)(2,1)S(1)}, bf16[512,512]{1,0:T(8,128)(2,1)}, u32[]{:S(2)}) copy-start(bf16[512,512]{1,0:T(8,128)(2,1)} %copy-done.6) | copy-start | bytes 1572868
  50.9 2.3 %collective-permute-start.1 = (bf16[256,512]{1,0:T(8,128)(2,1)S(1)}, bf16[256,512]{1,0:T(8,128)(2,1)S(1)}, u32[]{:S(2)}, u32[]{:S(2)}) collective-permute-start(bf16[256,512]{1,0:T(8,128)(2,1)S(1)} %get-tuple-element.28), channel_id=1, source_target_pairs={{0,1},{1,0},{2,3},{3,2},{4,5},{5,4},{6,7},{7,6},{8,9},{9,8},{10,11... | collective-permute-start | bytes 786440 | tf_op jit(solution)/shard_map/ppermute | solution.py:377
  51.0 1.0 %copy-start.9 = (f32[1024,128]{1,0:T(8,128)S(1)}, f32[1024,128]{1,0:T(8,128)}, u32[]{:S(2)}) copy-start(f32[1024,128]{1,0:T(8,128)} %copy-done.8) | copy-start | bytes 1572868

commit v7 on v5

--- a/solution.py
+++ b/solution.py
@@ -20,8 +20,9 @@
 
 
 def picks(index, count):
-    place = lax.broadcasted_iota(jnp.int32, (index.shape[0], count), 1)
-    return jnp.where(index == place, 1.0, 0.0).astype(jnp.bfloat16)
+    place = lax.broadcasted_iota(jnp.int32, (index.shape[0], count), 1).astype(jnp.int16)
+    one, zero = jnp.bfloat16(1.0), jnp.bfloat16(0.0)
+    return jnp.where(index.astype(jnp.int16) == place, one, zero)
 
 
 def pack_kernel(digits, ids_ref, vectors_ref, pack_ref):
@@ -85,11 +86,6 @@
     return index
 
 
-def position(index, count):
-    half = max(1, count // 2)
-    return index % half * 2 + index // half if count > 1 else index
-
-
 def items_kernel(items_hbm, items_ref, sems):
     part = items_ref.shape[0] // sems.shape[0]
     loads = []
@@ -101,7 +97,7 @@
         load.wait()
 
 
-def known_kernel(n_lists, items_loc, n_users, block, col_ref, ids_ref, probes_ref, known_ref, order_ref):
+def known_kernel(n_lists, items_loc, n_users, block, col_ref, ids_ref, probes_ref, known_ref):
     ids = ids_ref[...]
     cands = ids.shape[1]
     bins = ids // items_loc
@@ -111,14 +107,13 @@
     hot = jnp.where((lists == owner) & mine, 1.0, 0.0)
     before = jnp.dot(hot.astype(jnp.bfloat16), earlier(cands), preferred_element_type=jnp.float32)
     rank = jnp.sum(before * hot, axis=0, keepdims=True)
-    slot = jnp.where(mine, position(owner, n_lists).astype(jnp.float32) * block + rank, -1.0)
-    probes = position(probes_ref[...], n_lists).astype(jnp.float32)
+    slot = jnp.where(mine, owner.astype(jnp.float32) * block + rank, -1.0)
+    probes = probes_ref[...].astype(jnp.float32)
     flat = jnp.concatenate([probes[u : u + 1] for u in range(probes.shape[0])], axis=1)
     if flat.shape[1] < cands:
         flat = jnp.concatenate([flat, jnp.zeros((1, cands - flat.shape[1]), jnp.float32)], axis=1)
     row = lax.broadcasted_iota(jnp.int32, known_ref.shape, 0)
     known_ref[...] = jnp.where(row == 0, slot, flat)
-    order_ref[...] = jnp.zeros_like(order_ref)
 
 
 def pairs_kernel(n_parts, col_ref, length_ref, *refs):
@@ -226,7 +221,7 @@
     out_ref[...] = jnp.dot(attended, out_weight_ref[...], preferred_element_type=jnp.float32).astype(jnp.bfloat16)
 
 
-def expand_kernel(user_dev, pieces, cap, known_ref, order_ref, fetched_ref, out_hbm, out_ref, sems):
+def expand_kernel(user_dev, pieces, cap, known_ref, fetched_ref, out_hbm, out_ref, sems):
     n_lists, block, width = fetched_ref.shape
     kept = block - cap
     rows = n_lists * kept
@@ -254,11 +249,7 @@
 
 
 def exchange(value):
-    count = lax.axis_size("lists")
-    group = sorted(range(count), key=lambda index: position(index, count))
-    return lax.all_to_all(
-        value, "lists", split_axis=0, concat_axis=0, axis_index_groups=[group], tiled=True
-    )
+    return lax.all_to_all(value, "lists", split_axis=0, concat_axis=0, tiled=True)
 
 
 def shards(
@@ -314,14 +305,11 @@
     )(flat_items)
     gathered, items = lax.optimization_barrier((gathered, items))
 
-    known, order = pl.pallas_call(
+    known = pl.pallas_call(
         functools.partial(known_kernel, n_lists, items_loc, n_users, block),
-        out_shape=(
-            jax.ShapeDtypeStruct((8, cands), jnp.float32),
-            jax.ShapeDtypeStruct((8, LANES), jnp.float32),
-        ),
+        out_shape=jax.ShapeDtypeStruct((8, cands), jnp.float32),
         in_specs=[SMEM, VMEM, VMEM],
-        out_specs=(VMEM, VMEM),
+        out_specs=VMEM,
         compiler_params=PARAMS,
     )(col_arg, candidate_ids, probe_lists)
 
@@ -356,9 +344,7 @@
     )(base_arg, gathered, items)
     fetched = exchange(answers)
 
-    fetched, known, order, keys, values, turned = lax.optimization_barrier(
-        (fetched, known, order, keys, values, turned)
-    )
+    fetched, known, keys, values, turned = lax.optimization_barrier((fetched, known, keys, values, turned))
 
     placed = pl.pallas_call(
         functools.partial(place_kernel, n_users),
@@ -384,14 +370,14 @@
     list_scores = pl.pallas_call(
         functools.partial(expand_kernel, user_dev, pieces, cap),
         out_shape=jax.ShapeDtypeStruct((user_dev * probes, items_loc), bf16),
-        in_specs=[VMEM, pl.BlockSpec(memory_space=pl.ANY), VMEM],
+        in_specs=[VMEM, VMEM],
         out_specs=pl.BlockSpec(memory_space=pl.ANY),
         scratch_shapes=[
             pltpu.VMEM((user_dev * probes, items_loc), bf16),
             pltpu.SemaphoreType.DMA((pieces,)),
         ],
         compiler_params=PARAMS,
-    )(known, order, fetched)
+    )(known, fetched)
     return (list_scores.reshape(user_dev, probes, items_loc), ranked.reshape(1, share, width))
 
 

time: 55.9 us -> 54.4 us (0.973)
  local copies, waits for them, and re-layouts: 4.5 us -> 3.25 us
    unnamed x26 -> x22, local copies, waits for them, and re-layouts: 4.5 us -> 3.25 us
    all_to_all x2, waiting for transfers between devices: 26.6 us -> 25.5 us  [exchange(): lax.all_to_all(value, 'lists', split_axis=0, concat_axis=0, tiled=True)]
  transfers between devices with their start and end apart: 4 -> 4, of which waited for: 2 -> 4; matrix products, arithmetic and copies ran while one was open for 0% -> 0% of each run, Pallas kernels for 4% -> 4%
where the time goes in v7:
time: 54.4 us; the launch traced here: 53.8 us
  waiting for transfers between devices  26.3 us (48%)
  starting transfers between devices  12.3 us (23%)
  Pallas kernels  10.5 us (19%)
  local copies, waits for them, and re-layouts  3.25 us (6%)
  between operations  1.44 us (3%)
    all_to_all x2, waiting for transfers between devices, exchange(): lax.all_to_all(value, 'lists', split_axis=0, concat_axis=0, tiled=True)  25.5 us
    all_to_all x2, starting transfers between devices, exchange(): lax.all_to_all(value, 'lists', split_axis=0, concat_axis=0, tiled=True)  12.1 us
    pallas_call x1, Pallas kernels, shards(): pl.pallas_call(functools.partial(owner_kernel, n_lists, user_dev, digits,...  3.76 us
    unnamed x22, local copies, waits for them, and re-layouts  3.25 us
    pallas_call x1, Pallas kernels, shards(): pl.pallas_call(functools.partial(attend_kernel, n_users), out_shape=jax.S...  2.32 us
    pallas_call x1, Pallas kernels, shards(): pl.pallas_call(functools.partial(pack_kernel, digits), out_shape=jax.Shap...  1.36 us
    pallas_call x1, Pallas kernels, shards(): pl.pallas_call(functools.partial(expand_kernel, user_dev, pieces, cap), o...  1.14 us
  transfers between devices with their start and end apart: 4, of which 4 were waited for; matrix products, arithmetic and copies ran while one was open for 0% of the time, Pallas kernels for 4%

profile of v7, /device:TPU:0, one launch (start us, length us, event | category | flops | bytes accessed | tf_op | source)
XLA Modules:
  0.0 53.8 jit_solution(1108217639397754005)
XLA Ops:
  0.6 1.4 %shard_map.104 = bf16[16,24,128]{2,1,0:T(8,128)(2,1)} custom-call(s32[1,512]{1,0:T(1,128)} %ids_ref.3, bf16[4,512]{1,0:T(4,128)(2,1)} %vectors_ref.1), custom_call_target="tpu_custom_call" | custom-call | tf_op jit(solution)/shard_map/pallas_call | solution.py:288
  2.0 8.3 %all-to-all-start = ((bf16[16,24,128]{2,1,0:T(8,128)(2,1)}), bf16[16,24,128]{2,1,0:T(8,128)(2,1)S(1)}, u32[]{:S(2)}, u32[]{:S(2)}) async-start(bf16[16,24,128]{2,1,0:T(8,128)(2,1)} %shard_map.104), calls=%async_computation | async-start | bytes 196608 | tf_op jit(solution)/shard_map/all_to_all | solution.py:252
  10.3 0.0 copy-start
  10.3 1.6 %copy-done = bf16[1,2048,512]{2,1,0:T(8,128)(2,1)S(1)} copy-done((bf16[1,2048,512]{2,1,0:T(8,128)(2,1)S(1)}, bf16[1,2048,512]{2,1,0:T(8,128)(2,1)}, u32[]{:S(2)}) %copy-start) | copy-done | bytes 2097176
  11.9 0.2 shard_map.105.items_ref
  12.1 5.9 %all-to-all-done = bf16[16,24,128]{2,1,0:T(8,128)(2,1)S(1)} async-done(((bf16[16,24,128]{2,1,0:T(8,128)(2,1)}), bf16[16,24,128]{2,1,0:T(8,128)(2,1)S(1)}, u32[]{:S(2)}, u32[]{:S(2)}) %all-to-all-start) | async-done | bytes 98336 | tf_op jit(solution)/shard_map/all_to_all | solution.py:252
  18.0 0.0 copy-start.8
  18.0 3.8 %shard_map.106 = bf16[16,64,512]{2,1,0:T(8,128)(2,1)} custom-call(s32[1]{0:T(128)} %bitcast.base_ref, bf16[384,128]{1,0:T(8,128)(2,1)S(1)} %bitcast.8, bf16[2048,512]{1,0:T(8,128)(2,1)S(1)} %shard_map.105.items_ref), custom_call_target="tpu_custom_call" | custom-call | tf_op jit(solution)/shard_map/pallas_call | solution.py:334
  21.7 0.0 copy-start.2
  21.8 3.8 %all-to-all-start.1 = ((bf16[16,64,512]{2,1,0:T(8,128)(2,1)}), bf16[16,64,512]{2,1,0:T(8,128)(2,1)S(1)}, u32[]{:S(2)}, u32[]{:S(2)}) async-start(bf16[16,64,512]{2,1,0:T(8,128)(2,1)} %shard_map.106), calls=%async_computation.1 | async-start | bytes 2097152 | tf_op jit(solution)/shard_map/all_to_all | solution.py:252
  25.6 0.0 copy-done.8
  25.6 0.1 collective-permute-start
  26.3 0.0 copy-done.9
  26.3 0.0 copy-done.10
  26.3 0.2 shard_map.107.known_ref
  26.5 0.0 copy-start.3
  26.5 0.5 collective-permute-done.refs_1_
  27.0 0.0 copy-done.1
  27.0 0.0 copy-done.2
  27.0 0.6 %shard_map.108 = (bf16[8,256,80]{2,1,0:T(8,128)(2,1)S(1)}, bf16[512,256]{1,0:T(8,128)(2,1)S(1)}, bf16[512,512]{1,0:T(8,128)(2,1)S(1)}) custom-call(s32[1]{0:T(128)} %bitcast.3.col_ref, s32[1]{0:T(128)S(6)} %copy.11.length_ref, bf16[128,512]{1,0:T(8,128)(2,1)S(1)} %bitcast.10, bf16[128,512]{1,0:T(8,128)(2,1)S(1)} %collective-permute-done.refs_1_, ...), custom_call_target="tpu_custom_call" | custom-call | tf_op jit(solution)/shard_map/pallas_call | solution.py:321
  27.6 0.0 copy-start.4
  27.6 0.8 %copy-done.4 = bf16[8,256,80]{2,1,0:T(8,128)(2,1)} copy-done((bf16[8,256,80]{2,1,0:T(8,128)(2,1)}, bf16[8,256,80]{2,1,0:T(8,128)(2,1)S(1)}, u32[]{:S(2)}) %copy-start.4) | copy-done | bytes 327704
  28.4 0.8 %copy-done.6 = bf16[512,512]{1,0:T(8,128)(2,1)} copy-done((bf16[512,512]{1,0:T(8,128)(2,1)}, bf16[512,512]{1,0:T(8,128)(2,1)S(1)}, u32[]{:S(2)}) %copy-start.6) | copy-done | bytes 524312
  29.2 19.6 %all-to-all-done.1.fetched_ref = bf16[16,64,512]{2,1,0:T(8,128)(2,1)S(1)} async-done(((bf16[16,64,512]{2,1,0:T(8,128)(2,1)}), bf16[16,64,512]{2,1,0:T(8,128)(2,1)S(1)}, u32[]{:S(2)}, u32[]{:S(2)}) %all-to-all-start.1) | async-done | bytes 1048608 | tf_op jit(solution)/shard_map/all_to_all | solution.py:252
  48.8 1.0 %shard_map.110 = (bf16[256,512]{1,0:T(8,128)(2,1)S(1)}, bf16[256,512]{1,0:T(8,128)(2,1)S(1)}) custom-call(s32[1]{0:T(128)} %bitcast.3.col_ref, f32[8,512]{1,0:T(8,128)S(1)} %shard_map.107.known_ref, bf16[16,64,512]{2,1,0:T(8,128)(2,1)S(1)} %all-to-all-done.1.fetched_ref), custom_call_target="tpu_custom_call" | custom-call | tf_op jit(solution)/shard_map/pallas_call | solution.py:349
  49.8 0.1 collective-permute-start.1
  49.9 1.1 %shard_map.109 = bf16[128,2048]{1,0:T(8,128)(2,1)} custom-call(f32[8,512]{1,0:T(8,128)S(1)} %shard_map.107.known_ref, bf16[16,64,512]{2,1,0:T(8,128)(2,1)S(1)} %all-to-all-done.1.fetched_ref), custom_call_target="tpu_custom_call" | custom-call | tf_op jit(solution)/shard_map/pallas_call | solution.py:370
  51.1 0.4 collective-permute-done.1.refs_1_
  51.4 0.0 copy-done.3
  51.4 0.0 copy-done.5
  51.4 0.0 copy-done.7
  51.5 2.3 %shard_map.111 = bf16[256,512]{1,0:T(8,128)(2,1)} custom-call(bf16[256,512]{1,0:T(8,128)(2,1)S(1)} %get-tuple-element.21.refs_0_, bf16[256,512]{1,0:T(8,128)(2,1)S(1)} %collective-permute-done.1.refs_1_, bf16[8,256,80]{2,1,0:T(8,128)(2,1)S(1)} %copy-done.5, bf16[512,256]{1,0:T(8,128)(2,1)S(1)} %get-tuple-element.24.refs_3_, bf16[512,512]{1,0:T(8,128)(2,1)S(1)} %copy-done.7, ...), custom_call_target="tpu_custom_call" | custom-call | tf_op jit(solution)/shard_map/pallas_call | solution.py:362
  (6 shorter events, 0.0 us)
Async XLA Ops:
  2.0 16.0 %all-to-all-start = ((bf16[16,24,128]{2,1,0:T(8,128)(2,1)}), bf16[16,24,128]{2,1,0:T(8,128)(2,1)S(1)}, u32[]{:S(2)}, u32[]{:S(2)}) async-start(bf16[16,24,128]{2,1,0:T(8,128)(2,1)} %shard_map.104), calls=%async_computation | async-start | bytes 196608 | tf_op jit(solution)/shard_map/all_to_all | solution.py:252
  10.3 1.6 %copy-start = (bf16[1,2048,512]{2,1,0:T(8,128)(2,1)S(1)}, bf16[1,2048,512]{2,1,0:T(8,128)(2,1)}, u32[]{:S(2)}) copy-start(bf16[1,2048,512]{2,1,0:T(8,128)(2,1)} %param.11) | copy-start | bytes 6291460
  18.0 7.6 %copy-start.8 = (bf16[1,128,512]{2,1,0:T(8,128)(2,1)S(1)}, bf16[1,128,512]{2,1,0:T(8,128)(2,1)}, u32[]{:S(2)}) copy-start(bf16[1,128,512]{2,1,0:T(8,128)(2,1)} %param.13) | copy-start | bytes 393220
  18.0 8.3 %copy-start.9 = (s32[1,512]{1,0:T(1,128)S(1)}, s32[1,512]{1,0:T(1,128)}, u32[]{:S(2)}) copy-start(s32[1,512]{1,0:T(1,128)} %ids_ref.3) | copy-start | bytes 6148
  18.0 8.3 %copy-start.10 = (s32[4,32]{1,0:T(4,128)S(1)}, s32[4,32]{1,0:T(4,128)}, u32[]{:S(2)}) copy-start(s32[4,32]{1,0:T(4,128)} %probes_ref.1) | copy-start | bytes 1540
  18.0 9.0 %copy-start.1 = (bf16[512,1024]{1,0:T(8,128)(2,1)S(1)}, bf16[512,1024]{1,0:T(8,128)(2,1)}, u32[]{:S(2)}) copy-start(bf16[512,1024]{1,0:T(8,128)(2,1)} %refs_2_.1) | copy-start | bytes 3145732
  21.7 5.2 %copy-start.2 = (bf16[512,512]{1,0:T(8,128)(2,1)S(1)}, bf16[512,512]{1,0:T(8,128)(2,1)}, u32[]{:S(2)}) copy-start(bf16[512,512]{1,0:T(8,128)(2,1)} %refs_3_.1) | copy-start | bytes 1572868
  21.8 27.1 %all-to-all-start.1 = ((bf16[16,64,512]{2,1,0:T(8,128)(2,1)}), bf16[16,64,512]{2,1,0:T(8,128)(2,1)S(1)}, u32[]{:S(2)}, u32[]{:S(2)}) async-start(bf16[16,64,512]{2,1,0:T(8,128)(2,1)} %shard_map.106), calls=%async_computation.1 | async-start | bytes 2097152 | tf_op jit(solution)/shard_map/all_to_all | solution.py:252
  25.6 1.4 %collective-permute-start = (bf16[128,512]{1,0:T(8,128)(2,1)S(1)}, bf16[128,512]{1,0:T(8,128)(2,1)S(1)}, u32[]{:S(2)}, u32[]{:S(2)}) collective-permute-start(bf16[128,512]{1,0:T(8,128)(2,1)S(1)} %bitcast.9), channel_id=1, source_target_pairs={{0,1},{1,0},{2,3},{3,2},{4,5},{5,4},{6,7},{7,6},{8,9},{9,8},{10,11... | collective-permute-start | bytes 393224 | tf_op jit(solution)/shard_map/ppermute | solution.py:319
  26.5 24.9 %copy-start.3 = (bf16[512,512]{1,0:T(8,128)(2,1)S(1)}, bf16[512,512]{1,0:T(8,128)(2,1)}, u32[]{:S(2)}) copy-start(bf16[512,512]{1,0:T(8,128)(2,1)} %refs_5_.1) | copy-start | bytes 1572868
  27.6 0.8 %copy-start.4 = (bf16[8,256,80]{2,1,0:T(8,128)(2,1)}, bf16[8,256,80]{2,1,0:T(8,128)(2,1)S(1)}, u32[]{:S(2)}) copy-start(bf16[8,256,80]{2,1,0:T(8,128)(2,1)S(1)} %get-tuple-element.23.refs_2_) | copy-start | bytes 983044
  28.4 0.8 %copy-start.6 = (bf16[512,512]{1,0:T(8,128)(2,1)}, bf16[512,512]{1,0:T(8,128)(2,1)S(1)}, u32[]{:S(2)}) copy-start(bf16[512,512]{1,0:T(8,128)(2,1)S(1)} %get-tuple-element.25.refs_4_) | copy-start | bytes 1572868
  48.8 2.6 %copy-start.5 = (bf16[8,256,80]{2,1,0:T(8,128)(2,1)S(1)}, bf16[8,256,80]{2,1,0:T(8,128)(2,1)}, u32[]{:S(2)}) copy-start(bf16[8,256,80]{2,1,0:T(8,128)(2,1)} %copy-done.4) | copy-start | bytes 983044
  48.8 2.6 %copy-start.7 = (bf16[512,512]{1,0:T(8,128)(2,1)S(1)}, bf16[512,512]{1,0:T(8,128)(2,1)}, u32[]{:S(2)}) copy-start(bf16[512,512]{1,0:T(8,128)(2,1)} %copy-done.6) | copy-start | bytes 1572868
  49.8 1.6 %collective-permute-start.1 = (bf16[256,512]{1,0:T(8,128)(2,1)S(1)}, bf16[256,512]{1,0:T(8,128)(2,1)S(1)}, u32[]{:S(2)}, u32[]{:S(2)}) collective-permute-start(bf16[256,512]{1,0:T(8,128)(2,1)S(1)} %get-tuple-element.22), channel_id=1, source_target_pairs={{0,1},{1,0},{2,3},{3,2},{4,5},{5,4},{6,7},{7,6},{8,9},{9,8},{10,11... | collective-permute-start | bytes 786440 | tf_op jit(solution)/shard_map/ppermute | solution.py:360

commit v8 on v7

--- a/solution.py
+++ b/solution.py
@@ -158,7 +158,7 @@
         picks(wanted, stacked.shape[0]), stacked, preferred_element_type=jnp.float32
     ).astype(jnp.bfloat16)
     out_ref[:, cap:, :] = spread.reshape(n_lists, kept, width)
-    step = max(1, 256 // cap)
+    step = max(1, 384 // cap)
     sends = []
     for number, first in enumerate(range(0, n_lists, step)):
         last = min(n_lists, first + step)
@@ -175,18 +175,23 @@
         send.wait()
 
 
+def placed(column, known_ref, slots, fetched_ref, out_ref):
+    n_lists, block, width = fetched_ref.shape
+    share = out_ref.shape[0]
+    slots[...] = jnp.transpose(known_ref[...])
+    start = pl.multiple_of(column * share, share)
+    slot = slots[pl.ds(start, share), :][:, :1].astype(jnp.int32)
+    out_ref[...] = jnp.dot(
+        picks(slot, n_lists * block),
+        fetched_ref[...].reshape(n_lists * block, width),
+        preferred_element_type=jnp.float32,
+    ).astype(jnp.bfloat16)
+
+
 def place_kernel(n_users, col_ref, known_ref, fetched_ref, *refs):
-    share_refs, scratch = refs[:-1], refs[-1]
-    n_lists, block, width = fetched_ref.shape
-    fetched = fetched_ref[...].reshape(n_lists * block, width)
-    share = share_refs[0].shape[0]
-    slot = jnp.transpose(known_ref[...])[:, :1].astype(jnp.int32)
-    scratch[...] = jnp.dot(
-        picks(slot, fetched.shape[0]), fetched, preferred_element_type=jnp.float32
-    ).astype(jnp.bfloat16)
-    for shift, ref in enumerate(share_refs):
-        start = (col_ref[0] + shift) % n_users * share
-        ref[...] = scratch[pl.ds(pl.multiple_of(start, share), share), :]
+    sent_refs, slots = refs[:-1], refs[-1]
+    for shift, ref in enumerate(sent_refs):
+        placed((col_ref[0] + shift + 1) % n_users, known_ref, slots, fetched_ref, ref)
 
 
 def attend_kernel(n_parts, *refs):
@@ -221,7 +226,7 @@
     out_ref[...] = jnp.dot(attended, out_weight_ref[...], preferred_element_type=jnp.float32).astype(jnp.bfloat16)
 
 
-def expand_kernel(user_dev, pieces, cap, known_ref, fetched_ref, out_hbm, out_ref, sems):
+def expand_kernel(user_dev, pieces, cap, col_ref, known_ref, fetched_ref, out_hbm, own_ref, out_ref, slots, sems):
     n_lists, block, width = fetched_ref.shape
     kept = block - cap
     rows = n_lists * kept
@@ -238,6 +243,7 @@
         )
         sends.append(pltpu.make_async_copy(out_ref.at[:, span], out_hbm.at[:, span], sems.at[piece]))
         sends[-1].start()
+    placed(col_ref[0], known_ref, slots, fetched_ref, own_ref)
     for send in sends:
         send.wait()
 
@@ -330,7 +336,7 @@
         compiler_params=PARAMS,
     )(col_arg, history_lengths, *hist, key_value_weight, query_weight)
 
-    step = max(1, 256 // cap)
+    step = max(1, 384 // cap)
     answers = pl.pallas_call(
         functools.partial(owner_kernel, n_lists, user_dev, digits, cap, width ** (-0.5)),
         out_shape=jax.ShapeDtypeStruct((n_lists, block, width), bf16),
@@ -346,38 +352,44 @@
 
     fetched, known, keys, values, turned = lax.optimization_barrier((fetched, known, keys, values, turned))
 
-    placed = pl.pallas_call(
-        functools.partial(place_kernel, n_users),
-        out_shape=tuple(jax.ShapeDtypeStruct((share, width), bf16) for _ in range(n_users)),
-        in_specs=[SMEM, VMEM, VMEM],
-        out_specs=tuple(VMEM for _ in range(n_users)),
-        scratch_shapes=[pltpu.VMEM((cands, width), bf16)],
-        compiler_params=PARAMS,
-    )(col_arg, known, fetched)
-    parts = [placed[0]]
+    sent = []
+    if n_users > 1:
+        sent = pl.pallas_call(
+            functools.partial(place_kernel, n_users),
+            out_shape=tuple(jax.ShapeDtypeStruct((share, width), bf16) for _ in range(n_users - 1)),
+            in_specs=[SMEM, VMEM, VMEM],
+            out_specs=tuple(VMEM for _ in range(n_users - 1)),
+            scratch_shapes=[pltpu.VMEM((cands, 8), jnp.float32)],
+            compiler_params=PARAMS,
+        )(col_arg, known, fetched)
+    parts = []
     for shift in range(1, n_users):
         parts.append(
-            lax.ppermute(placed[shift], "users", [(i, (i + shift) % n_users) for i in range(n_users)])
+            lax.ppermute(sent[shift - 1], "users", [(i, (i + shift) % n_users) for i in range(n_users)])
         )
+
+    list_scores, own = pl.pallas_call(
+        functools.partial(expand_kernel, user_dev, pieces, cap),
+        out_shape=(
+            jax.ShapeDtypeStruct((user_dev * probes, items_loc), bf16),
+            jax.ShapeDtypeStruct((share, width), bf16),
+        ),
+        in_specs=[SMEM, VMEM, VMEM],
+        out_specs=(pl.BlockSpec(memory_space=pl.ANY), VMEM),
+        scratch_shapes=[
+            pltpu.VMEM((user_dev * probes, items_loc), bf16),
+            pltpu.VMEM((cands, 8), jnp.float32),
+            pltpu.SemaphoreType.DMA((pieces,)),
+        ],
+        compiler_params=PARAMS,
+    )(col_arg, known, fetched)
     ranked = pl.pallas_call(
         functools.partial(attend_kernel, n_users),
         out_shape=jax.ShapeDtypeStruct((share, width), bf16),
         in_specs=[VMEM] * (n_users + 4),
         out_specs=VMEM,
         compiler_params=PARAMS,
-    )(*parts, keys, values, turned, out_weight)
-
-    list_scores = pl.pallas_call(
-        functools.partial(expand_kernel, user_dev, pieces, cap),
-        out_shape=jax.ShapeDtypeStruct((user_dev * probes, items_loc), bf16),
-        in_specs=[VMEM, VMEM],
-        out_specs=pl.BlockSpec(memory_space=pl.ANY),
-        scratch_shapes=[
-            pltpu.VMEM((user_dev * probes, items_loc), bf16),
-            pltpu.SemaphoreType.DMA((pieces,)),
-        ],
-        compiler_params=PARAMS,
-    )(known, fetched)
+    )(own, *parts, keys, values, turned, out_weight)
     return (list_scores.reshape(user_dev, probes, items_loc), ranked.reshape(1, share, width))
 
 

time: 54.4 us -> 54.1 us (level)
  no operation moved by 1% of the time
where the time goes in v8:
time: 54.1 us; the launch traced here: 53.4 us
  waiting for transfers between devices  26.3 us (49%)
  starting transfers between devices  12.3 us (23%)
  Pallas kernels  10.2 us (19%)
  local copies, waits for them, and re-layouts  3.25 us (6%)
  between operations  1.44 us (3%)
    all_to_all x2, waiting for transfers between devices, exchange(): lax.all_to_all(value, 'lists', split_axis=0, concat_axis=0, tiled=True)  25.5 us
    all_to_all x2, starting transfers between devices, exchange(): lax.all_to_all(value, 'lists', split_axis=0, concat_axis=0, tiled=True)  12.1 us
    pallas_call x1, Pallas kernels, shards(): pl.pallas_call(functools.partial(owner_kernel, n_lists, user_dev, digits,...  3.69 us
    unnamed x22, local copies, waits for them, and re-layouts  3.25 us
    pallas_call x1, Pallas kernels, shards(): pl.pallas_call(functools.partial(attend_kernel, n_users), out_shape=jax.S...  2.32 us
    pallas_call x1, Pallas kernels, shards(): pl.pallas_call(functools.partial(pack_kernel, digits), out_shape=jax.Shap...  1.36 us
    pallas_call x1, Pallas kernels, shards(): pl.pallas_call(functools.partial(expand_kernel, user_dev, pieces, cap), o...  1.18 us
  transfers between devices with their start and end apart: 4, of which 4 were waited for; matrix products, arithmetic and copies ran while one was open for 0% of the time, Pallas kernels for 4%

profile of v8, /device:TPU:0, one launch (start us, length us, event | category | flops | bytes accessed | tf_op | source)
XLA Modules:
  0.0 53.4 jit_solution(9848090726887855944)
XLA Ops:
  0.6 1.4 %shard_map.104 = bf16[16,24,128]{2,1,0:T(8,128)(2,1)} custom-call(s32[1,512]{1,0:T(1,128)} %ids_ref.3, bf16[4,512]{1,0:T(4,128)(2,1)} %vectors_ref.1), custom_call_target="tpu_custom_call" | custom-call | tf_op jit(solution)/shard_map/pallas_call | solution.py:294
  2.0 8.3 %all-to-all-start = ((bf16[16,24,128]{2,1,0:T(8,128)(2,1)}), bf16[16,24,128]{2,1,0:T(8,128)(2,1)S(1)}, u32[]{:S(2)}, u32[]{:S(2)}) async-start(bf16[16,24,128]{2,1,0:T(8,128)(2,1)} %shard_map.104), calls=%async_computation | async-start | bytes 196608 | tf_op jit(solution)/shard_map/all_to_all | solution.py:258
  10.3 0.0 copy-start
  10.3 1.6 %copy-done = bf16[1,2048,512]{2,1,0:T(8,128)(2,1)S(1)} copy-done((bf16[1,2048,512]{2,1,0:T(8,128)(2,1)S(1)}, bf16[1,2048,512]{2,1,0:T(8,128)(2,1)}, u32[]{:S(2)}) %copy-start) | copy-done | bytes 2097176
  11.9 0.2 shard_map.105.items_ref
  12.1 5.9 %all-to-all-done = bf16[16,24,128]{2,1,0:T(8,128)(2,1)S(1)} async-done(((bf16[16,24,128]{2,1,0:T(8,128)(2,1)}), bf16[16,24,128]{2,1,0:T(8,128)(2,1)S(1)}, u32[]{:S(2)}, u32[]{:S(2)}) %all-to-all-start) | async-done | bytes 98336 | tf_op jit(solution)/shard_map/all_to_all | solution.py:258
  18.0 0.0 copy-start.8
  18.0 3.7 %shard_map.106 = bf16[16,64,512]{2,1,0:T(8,128)(2,1)} custom-call(s32[1]{0:T(128)} %bitcast.1.base_ref, bf16[384,128]{1,0:T(8,128)(2,1)S(1)} %bitcast.8, bf16[2048,512]{1,0:T(8,128)(2,1)S(1)} %shard_map.105.items_ref), custom_call_target="tpu_custom_call" | custom-call | tf_op jit(solution)/shard_map/pallas_call | solution.py:340
  21.7 0.0 copy-start.2
  21.7 3.8 %all-to-all-start.1 = ((bf16[16,64,512]{2,1,0:T(8,128)(2,1)}), bf16[16,64,512]{2,1,0:T(8,128)(2,1)S(1)}, u32[]{:S(2)}, u32[]{:S(2)}) async-start(bf16[16,64,512]{2,1,0:T(8,128)(2,1)} %shard_map.106), calls=%async_computation.1 | async-start | bytes 2097152 | tf_op jit(solution)/shard_map/all_to_all | solution.py:258
  25.5 0.0 copy-done.8
  25.5 0.1 collective-permute-start
  26.2 0.0 copy-done.9
  26.2 0.0 copy-done.10
  26.3 0.2 shard_map.107.known_ref
  26.5 0.0 copy-start.3
  26.5 0.5 collective-permute-done.refs_1_
  26.9 0.0 copy-done.1
  26.9 0.0 copy-done.2
  26.9 0.6 %shard_map.108 = (bf16[8,256,80]{2,1,0:T(8,128)(2,1)S(1)}, bf16[512,256]{1,0:T(8,128)(2,1)S(1)}, bf16[512,512]{1,0:T(8,128)(2,1)S(1)}) custom-call(s32[1]{0:T(128)} %bitcast.col_ref, s32[1]{0:T(128)S(6)} %copy.11.length_ref, bf16[128,512]{1,0:T(8,128)(2,1)S(1)} %bitcast.10, bf16[128,512]{1,0:T(8,128)(2,1)S(1)} %collective-permute-done.refs_1_, ...), custom_call_target="tpu_custom_call" | custom-call | tf_op jit(solution)/shard_map/pallas_call | solution.py:327
  27.5 0.0 copy-start.4
  27.5 0.8 %copy-done.4 = bf16[8,256,80]{2,1,0:T(8,128)(2,1)} copy-done((bf16[8,256,80]{2,1,0:T(8,128)(2,1)}, bf16[8,256,80]{2,1,0:T(8,128)(2,1)S(1)}, u32[]{:S(2)}) %copy-start.4) | copy-done | bytes 327704
  28.3 0.8 %copy-done.6 = bf16[512,512]{1,0:T(8,128)(2,1)} copy-done((bf16[512,512]{1,0:T(8,128)(2,1)}, bf16[512,512]{1,0:T(8,128)(2,1)S(1)}, u32[]{:S(2)}) %copy-start.6) | copy-done | bytes 524312
  29.2 19.6 %all-to-all-done.1.fetched_ref = bf16[16,64,512]{2,1,0:T(8,128)(2,1)S(1)} async-done(((bf16[16,64,512]{2,1,0:T(8,128)(2,1)}), bf16[16,64,512]{2,1,0:T(8,128)(2,1)S(1)}, u32[]{:S(2)}, u32[]{:S(2)}) %all-to-all-start.1) | async-done | bytes 1048608 | tf_op jit(solution)/shard_map/all_to_all | solution.py:258
  48.8 0.7 %shard_map.110 = bf16[256,512]{1,0:T(8,128)(2,1)S(1)} custom-call(s32[1]{0:T(128)} %bitcast.col_ref, f32[8,512]{1,0:T(8,128)S(1)} %shard_map.107.known_ref, bf16[16,64,512]{2,1,0:T(8,128)(2,1)S(1)} %all-to-all-done.1.fetched_ref), custom_call_target="tpu_custom_call" | custom-call | tf_op jit(solution)/shard_map/pallas_call | solution.py:357
  49.5 0.1 collective-permute-start.1
  49.6 1.2 %shard_map.109 = (bf16[128,2048]{1,0:T(8,128)(2,1)}, bf16[256,512]{1,0:T(8,128)(2,1)S(1)}) custom-call(s32[1]{0:T(128)} %bitcast.col_ref, f32[8,512]{1,0:T(8,128)S(1)} %shard_map.107.known_ref, bf16[16,64,512]{2,1,0:T(8,128)(2,1)S(1)} %all-to-all-done.1.fetched_ref), custom_call_target="tpu_custom_call" | custom-call | tf_op jit(solution)/shard_map/pallas_call | solution.py:371
  50.8 0.3 collective-permute-done.1.refs_1_
  51.1 0.0 copy-done.3
  51.1 0.0 copy-done.5
  51.1 0.0 copy-done.7
  51.1 2.3 %shard_map.111 = bf16[256,512]{1,0:T(8,128)(2,1)} custom-call(bf16[256,512]{1,0:T(8,128)(2,1)S(1)} %get-tuple-element.22.refs_0_, bf16[256,512]{1,0:T(8,128)(2,1)S(1)} %collective-permute-done.1.refs_1_, bf16[8,256,80]{2,1,0:T(8,128)(2,1)S(1)} %copy-done.5, bf16[512,256]{1,0:T(8,128)(2,1)S(1)} %get-tuple-element.24.refs_3_, bf16[512,512]{1,0:T(8,128)(2,1)S(1)} %copy-done.7, ...), custom_call_target="tpu_custom_call" | custom-call | tf_op jit(solution)/shard_map/pallas_call | solution.py:386
  (6 shorter events, 0.0 us)
Async XLA Ops:
  2.0 16.0 %all-to-all-start = ((bf16[16,24,128]{2,1,0:T(8,128)(2,1)}), bf16[16,24,128]{2,1,0:T(8,128)(2,1)S(1)}, u32[]{:S(2)}, u32[]{:S(2)}) async-start(bf16[16,24,128]{2,1,0:T(8,128)(2,1)} %shard_map.104), calls=%async_computation | async-start | bytes 196608 | tf_op jit(solution)/shard_map/all_to_all | solution.py:258
  10.3 1.6 %copy-start = (bf16[1,2048,512]{2,1,0:T(8,128)(2,1)S(1)}, bf16[1,2048,512]{2,1,0:T(8,128)(2,1)}, u32[]{:S(2)}) copy-start(bf16[1,2048,512]{2,1,0:T(8,128)(2,1)} %param.11) | copy-start | bytes 6291460
  18.0 7.5 %copy-start.8 = (bf16[1,128,512]{2,1,0:T(8,128)(2,1)S(1)}, bf16[1,128,512]{2,1,0:T(8,128)(2,1)}, u32[]{:S(2)}) copy-start(bf16[1,128,512]{2,1,0:T(8,128)(2,1)} %param.13) | copy-start | bytes 393220
  18.0 8.3 %copy-start.9 = (s32[1,512]{1,0:T(1,128)S(1)}, s32[1,512]{1,0:T(1,128)}, u32[]{:S(2)}) copy-start(s32[1,512]{1,0:T(1,128)} %ids_ref.3) | copy-start | bytes 6148
  18.0 8.3 %copy-start.10 = (s32[4,32]{1,0:T(4,128)S(1)}, s32[4,32]{1,0:T(4,128)}, u32[]{:S(2)}) copy-start(s32[4,32]{1,0:T(4,128)} %probes_ref.1) | copy-start | bytes 1540
  18.0 8.9 %copy-start.1 = (bf16[512,1024]{1,0:T(8,128)(2,1)S(1)}, bf16[512,1024]{1,0:T(8,128)(2,1)}, u32[]{:S(2)}) copy-start(bf16[512,1024]{1,0:T(8,128)(2,1)} %refs_2_.1) | copy-start | bytes 3145732
  21.7 5.2 %copy-start.2 = (bf16[512,512]{1,0:T(8,128)(2,1)S(1)}, bf16[512,512]{1,0:T(8,128)(2,1)}, u32[]{:S(2)}) copy-start(bf16[512,512]{1,0:T(8,128)(2,1)} %refs_3_.1) | copy-start | bytes 1572868
  21.7 27.1 %all-to-all-start.1 = ((bf16[16,64,512]{2,1,0:T(8,128)(2,1)}), bf16[16,64,512]{2,1,0:T(8,128)(2,1)S(1)}, u32[]{:S(2)}, u32[]{:S(2)}) async-start(bf16[16,64,512]{2,1,0:T(8,128)(2,1)} %shard_map.106), calls=%async_computation.1 | async-start | bytes 2097152 | tf_op jit(solution)/shard_map/all_to_all | solution.py:258
  25.5 1.4 %collective-permute-start = (bf16[128,512]{1,0:T(8,128)(2,1)S(1)}, bf16[128,512]{1,0:T(8,128)(2,1)S(1)}, u32[]{:S(2)}, u32[]{:S(2)}) collective-permute-start(bf16[128,512]{1,0:T(8,128)(2,1)S(1)} %bitcast.9), channel_id=1, source_target_pairs={{0,1},{1,0},{2,3},{3,2},{4,5},{5,4},{6,7},{7,6},{8,9},{9,8},{10,11... | collective-permute-start | bytes 393224 | tf_op jit(solution)/shard_map/ppermute | solution.py:325
  26.5 24.7 %copy-start.3 = (bf16[512,512]{1,0:T(8,128)(2,1)S(1)}, bf16[512,512]{1,0:T(8,128)(2,1)}, u32[]{:S(2)}) copy-start(bf16[512,512]{1,0:T(8,128)(2,1)} %refs_5_.1) | copy-start | bytes 1572868
  27.5 0.8 %copy-start.4 = (bf16[8,256,80]{2,1,0:T(8,128)(2,1)}, bf16[8,256,80]{2,1,0:T(8,128)(2,1)S(1)}, u32[]{:S(2)}) copy-start(bf16[8,256,80]{2,1,0:T(8,128)(2,1)S(1)} %get-tuple-element.23.refs_2_) | copy-start | bytes 983044
  28.3 0.8 %copy-start.6 = (bf16[512,512]{1,0:T(8,128)(2,1)}, bf16[512,512]{1,0:T(8,128)(2,1)S(1)}, u32[]{:S(2)}) copy-start(bf16[512,512]{1,0:T(8,128)(2,1)S(1)} %get-tuple-element.25.refs_4_) | copy-start | bytes 1572868
  48.8 2.4 %copy-start.5 = (bf16[8,256,80]{2,1,0:T(8,128)(2,1)S(1)}, bf16[8,256,80]{2,1,0:T(8,128)(2,1)}, u32[]{:S(2)}) copy-start(bf16[8,256,80]{2,1,0:T(8,128)(2,1)} %copy-done.4) | copy-start | bytes 983044
  48.8 2.4 %copy-start.7 = (bf16[512,512]{1,0:T(8,128)(2,1)S(1)}, bf16[512,512]{1,0:T(8,128)(2,1)}, u32[]{:S(2)}) copy-start(bf16[512,512]{1,0:T(8,128)(2,1)} %copy-done.6) | copy-start | bytes 1572868
  49.5 1.6 %collective-permute-start.1 = (bf16[256,512]{1,0:T(8,128)(2,1)S(1)}, bf16[256,512]{1,0:T(8,128)(2,1)S(1)}, u32[]{:S(2)}, u32[]{:S(2)}) collective-permute-start(bf16[256,512]{1,0:T(8,128)(2,1)S(1)} %shard_map.110), channel_id=1, source_target_pairs={{0,1},{1,0},{2,3},{3,2},{4,5},{5,4},{6,7},{7,6},{8,9},{9,8},{10,11... | collective-permute-start | bytes 786440 | tf_op jit(solution)/shard_map/ppermute | solution.py:368

commit v9 on v8

--- a/solution.py
+++ b/solution.py
@@ -46,42 +46,47 @@
     return jnp.where(row < column, 1.0, 0.0).astype(jnp.bfloat16)
 
 
-def unpack(gathered_ref, n_lists, user_dev, digits, turn):
-    pack_rows = gathered_ref.shape[0] // n_lists
-    spans = pack_rows // (user_dev + digits)
-    entry = lax.broadcasted_iota(jnp.int32, ((user_dev + digits) * n_lists, 1), 0)
-    asker, field = (entry % n_lists) ^ turn, entry // n_lists
-    fields = jnp.concatenate(
+def unpack(wide, n_lists, user_dev, digits, spans):
+    pack_rows = wide.shape[0] // n_lists
+
+    def line(number):
+        return wide[pl.ds(number, n_lists, stride=pack_rows), :]
+
+    vectors = jnp.concatenate(
         [
-            jnp.dot(
-                picks(
-                    asker * pack_rows
-                    + jnp.where(field < user_dev, span * user_dev + field, field * spans + span),
-                    n_lists * pack_rows,
-                ),
-                gathered_ref[...],
-                preferred_element_type=jnp.float32,
-            )
-            for span in range(spans)
+            jnp.concatenate([line(span * user_dev + u) for span in range(spans)], axis=1)
+            for u in range(user_dev)
         ],
-        axis=1,
-    )
-    ids = jnp.zeros((n_lists, fields.shape[1]), jnp.float32)
-    for digit in range(digits):
-        ids = ids + fields[(user_dev + digit) * n_lists : (user_dev + digit + 1) * n_lists] * float(BASE**digit)
-    return fields[: user_dev * n_lists], ids
-
-
-def asked(ids, base, items_loc, first, count):
-    local = ids - base
+        axis=0,
+    )
+    ids = []
+    for span in range(spans):
+        value = line(user_dev * spans + span)
+        for digit in range(1, digits):
+            value = value + line((user_dev + digit) * spans + span) * float(BASE**digit)
+        ids.append(value)
+    return vectors, ids
+
+
+def asked(ids, base, items_loc, count):
+    n_lists = ids[0].shape[0]
+    local = jnp.concatenate([part - base for part in ids], axis=0)
     mine = (local >= 0.0) & (local < items_loc)
-    hot = jnp.where(mine, 1.0, 0.0).astype(jnp.bfloat16)
-    rank = jnp.dot(hot, earlier(ids.shape[1]), preferred_element_type=jnp.float32)
-    rank = jnp.where(mine, rank, -1.0)
-    place = lax.broadcasted_iota(jnp.int32, (count, ids.shape[1]), 0).astype(jnp.float32) + float(first)
+    hot = jnp.where(mine, 1.0, 0.0)
+    rank = jnp.dot(hot.astype(jnp.bfloat16), earlier(LANES), preferred_element_type=jnp.float32)
+    totals = jnp.sum(hot, axis=1, keepdims=True)
+    before = jnp.zeros((n_lists, 1), jnp.float32)
+    ranks, locals_ = [], []
+    for span in range(len(ids)):
+        rows = slice(span * n_lists, (span + 1) * n_lists)
+        ranks.append(jnp.where(mine[rows], rank[rows] + before, -1.0))
+        locals_.append(local[rows] + 1.0)
+        before = before + totals[rows]
+    rank, local = jnp.concatenate(ranks, axis=1), jnp.concatenate(locals_, axis=1)
+    place = lax.broadcasted_iota(jnp.int32, (count, rank.shape[1]), 0).astype(jnp.float32)
     index = []
-    for r in range(ids.shape[0]):
-        picked = jnp.where(rank[r : r + 1] == place, local[r : r + 1] + 1.0, 0.0)
+    for r in range(n_lists):
+        picked = jnp.where(rank[r : r + 1] == place, local[r : r + 1], 0.0)
         index.append(jnp.sum(picked, axis=1, keepdims=True).astype(jnp.int32) - 1)
     return index
 
@@ -136,10 +141,11 @@
 
 
 def owner_kernel(n_lists, user_dev, digits, cap, scale, base_ref, gathered_ref, items_ref, *refs):
-    out_hbm, out_ref, out_sems = refs
+    out_hbm, wide, out_ref, out_sems = refs
     items_loc, width = items_ref.shape
-    vectors, ids = unpack(gathered_ref, n_lists, user_dev, digits, 0)
-    index = asked(ids, base_ref[0].astype(jnp.float32), items_loc, 0, cap)
+    wide[...] = gathered_ref[...].astype(jnp.float32)
+    vectors, ids = unpack(wide, n_lists, user_dev, digits, width // LANES)
+    index = asked(ids, base_ref[0].astype(jnp.float32), items_loc, cap)
     scores = lax.dot_general(
         vectors.astype(jnp.bfloat16),
         items_ref[...],
@@ -158,7 +164,7 @@
         picks(wanted, stacked.shape[0]), stacked, preferred_element_type=jnp.float32
     ).astype(jnp.bfloat16)
     out_ref[:, cap:, :] = spread.reshape(n_lists, kept, width)
-    step = max(1, 384 // cap)
+    step = max(1, 288 // cap)
     sends = []
     for number, first in enumerate(range(0, n_lists, step)):
         last = min(n_lists, first + step)
@@ -336,13 +342,14 @@
         compiler_params=PARAMS,
     )(col_arg, history_lengths, *hist, key_value_weight, query_weight)
 
-    step = max(1, 384 // cap)
+    step = max(1, 288 // cap)
     answers = pl.pallas_call(
         functools.partial(owner_kernel, n_lists, user_dev, digits, cap, width ** (-0.5)),
         out_shape=jax.ShapeDtypeStruct((n_lists, block, width), bf16),
         in_specs=[SMEM, VMEM, VMEM],
         out_specs=pl.BlockSpec(memory_space=pl.ANY),
         scratch_shapes=[
+            pltpu.VMEM((n_lists * pack_rows, LANES), jnp.float32),
             pltpu.VMEM((n_lists, block, width), bf16),
             pltpu.SemaphoreType.DMA((-(-n_lists // step),)),
         ],

time: 54.1 us -> 53.7 us (level)
  no operation moved by 1% of the time
where the time goes in v9:
time: 53.7 us; the launch traced here: 53.1 us
  waiting for transfers between devices  26.3 us (49%)
  starting transfers between devices  12.3 us (23%)
  Pallas kernels  9.85 us (18%)
  local copies, waits for them, and re-layouts  3.25 us (6%)
  between operations  1.44 us (3%)
    all_to_all x2, waiting for transfers between devices, exchange(): lax.all_to_all(value, 'lists', split_axis=0, concat_axis=0, tiled=True)  25.5 us
    all_to_all x2, starting transfers between devices, exchange(): lax.all_to_all(value, 'lists', split_axis=0, concat_axis=0, tiled=True)  12.1 us
    pallas_call x1, Pallas kernels, shards(): pl.pallas_call(functools.partial(owner_kernel, n_lists, user_dev, digits,...  3.3 us
    unnamed x22, local copies, waits for them, and re-layouts  3.25 us
    pallas_call x1, Pallas kernels, shards(): pl.pallas_call(functools.partial(attend_kernel, n_users), out_shape=jax.S...  2.32 us
    pallas_call x1, Pallas kernels, shards(): pl.pallas_call(functools.partial(pack_kernel, digits), out_shape=jax.Shap...  1.36 us
    pallas_call x1, Pallas kernels, shards(): pl.pallas_call(functools.partial(expand_kernel, user_dev, pieces, cap), o...  1.17 us
  transfers between devices with their start and end apart: 4, of which 4 were waited for; matrix products, arithmetic and copies ran while one was open for 0% of the time, Pallas kernels for 4%

profile of v9, /device:TPU:0, one launch (start us, length us, event | category | flops | bytes accessed | tf_op | source)
XLA Modules:
  0.0 53.1 jit_solution(8850955246060157761)
XLA Ops:
  0.6 1.4 %shard_map.104 = bf16[16,24,128]{2,1,0:T(8,128)(2,1)} custom-call(s32[1,512]{1,0:T(1,128)} %ids_ref.3, bf16[4,512]{1,0:T(4,128)(2,1)} %vectors_ref.1), custom_call_target="tpu_custom_call" | custom-call | tf_op jit(solution)/shard_map/pallas_call | solution.py:300
  2.0 8.3 %all-to-all-start = ((bf16[16,24,128]{2,1,0:T(8,128)(2,1)}), bf16[16,24,128]{2,1,0:T(8,128)(2,1)S(1)}, u32[]{:S(2)}, u32[]{:S(2)}) async-start(bf16[16,24,128]{2,1,0:T(8,128)(2,1)} %shard_map.104), calls=%async_computation | async-start | bytes 196608 | tf_op jit(solution)/shard_map/all_to_all | solution.py:264
  10.3 0.0 copy-start
  10.3 1.6 %copy-done = bf16[1,2048,512]{2,1,0:T(8,128)(2,1)S(1)} copy-done((bf16[1,2048,512]{2,1,0:T(8,128)(2,1)S(1)}, bf16[1,2048,512]{2,1,0:T(8,128)(2,1)}, u32[]{:S(2)}) %copy-start) | copy-done | bytes 2097176
  11.9 0.2 shard_map.105.items_ref
  12.1 5.9 %all-to-all-done = bf16[16,24,128]{2,1,0:T(8,128)(2,1)S(1)} async-done(((bf16[16,24,128]{2,1,0:T(8,128)(2,1)}), bf16[16,24,128]{2,1,0:T(8,128)(2,1)S(1)}, u32[]{:S(2)}, u32[]{:S(2)}) %all-to-all-start) | async-done | bytes 98336 | tf_op jit(solution)/shard_map/all_to_all | solution.py:264
  18.0 0.0 copy-start.9
  18.0 3.3 %shard_map.106 = bf16[16,64,512]{2,1,0:T(8,128)(2,1)} custom-call(s32[1]{0:T(128)} %bitcast.1.base_ref, bf16[384,128]{1,0:T(8,128)(2,1)S(1)} %bitcast.8, bf16[2048,512]{1,0:T(8,128)(2,1)S(1)} %shard_map.105.items_ref), custom_call_target="tpu_custom_call" | custom-call | tf_op jit(solution)/shard_map/pallas_call | solution.py:346
  21.3 0.0 copy-start.2
  21.3 3.8 %all-to-all-start.1 = ((bf16[16,64,512]{2,1,0:T(8,128)(2,1)}), bf16[16,64,512]{2,1,0:T(8,128)(2,1)S(1)}, u32[]{:S(2)}, u32[]{:S(2)}) async-start(bf16[16,64,512]{2,1,0:T(8,128)(2,1)} %shard_map.106), calls=%async_computation.1 | async-start | bytes 2097152 | tf_op jit(solution)/shard_map/all_to_all | solution.py:264
  25.1 0.0 copy-done.8
  25.1 0.1 collective-permute-start
  25.8 0.0 copy-done.9
  25.9 0.0 copy-done.10
  25.9 0.2 shard_map.107.known_ref
  26.1 0.0 copy-start.3
  26.1 0.5 collective-permute-done.refs_1_
  26.5 0.0 copy-done.1
  26.5 0.0 copy-done.2
  26.5 0.6 %shard_map.108 = (bf16[8,256,80]{2,1,0:T(8,128)(2,1)S(1)}, bf16[512,256]{1,0:T(8,128)(2,1)S(1)}, bf16[512,512]{1,0:T(8,128)(2,1)S(1)}) custom-call(s32[1]{0:T(128)} %bitcast.col_ref, s32[1]{0:T(128)S(6)} %copy.11.length_ref, bf16[128,512]{1,0:T(8,128)(2,1)S(1)} %bitcast.10, bf16[128,512]{1,0:T(8,128)(2,1)S(1)} %collective-permute-done.refs_1_, ...), custom_call_target="tpu_custom_call" | custom-call | tf_op jit(solution)/shard_map/pallas_call | solution.py:333
  27.1 0.0 copy-start.4
  27.1 0.8 %copy-done.4 = bf16[8,256,80]{2,1,0:T(8,128)(2,1)} copy-done((bf16[8,256,80]{2,1,0:T(8,128)(2,1)}, bf16[8,256,80]{2,1,0:T(8,128)(2,1)S(1)}, u32[]{:S(2)}) %copy-start.4) | copy-done | bytes 327704
  27.9 0.8 %copy-done.6 = bf16[512,512]{1,0:T(8,128)(2,1)} copy-done((bf16[512,512]{1,0:T(8,128)(2,1)}, bf16[512,512]{1,0:T(8,128)(2,1)S(1)}, u32[]{:S(2)}) %copy-start.6) | copy-done | bytes 524312
  28.8 19.6 %all-to-all-done.1.fetched_ref = bf16[16,64,512]{2,1,0:T(8,128)(2,1)S(1)} async-done(((bf16[16,64,512]{2,1,0:T(8,128)(2,1)}), bf16[16,64,512]{2,1,0:T(8,128)(2,1)S(1)}, u32[]{:S(2)}, u32[]{:S(2)}) %all-to-all-start.1) | async-done | bytes 1048608 | tf_op jit(solution)/shard_map/all_to_all | solution.py:264
  48.4 0.7 %shard_map.110 = bf16[256,512]{1,0:T(8,128)(2,1)S(1)} custom-call(s32[1]{0:T(128)} %bitcast.col_ref, f32[8,512]{1,0:T(8,128)S(1)} %shard_map.107.known_ref, bf16[16,64,512]{2,1,0:T(8,128)(2,1)S(1)} %all-to-all-done.1.fetched_ref), custom_call_target="tpu_custom_call" | custom-call | tf_op jit(solution)/shard_map/pallas_call | solution.py:364
  49.1 0.1 collective-permute-start.1
  49.2 1.2 %shard_map.109 = (bf16[128,2048]{1,0:T(8,128)(2,1)}, bf16[256,512]{1,0:T(8,128)(2,1)S(1)}) custom-call(s32[1]{0:T(128)} %bitcast.col_ref, f32[8,512]{1,0:T(8,128)S(1)} %shard_map.107.known_ref, bf16[16,64,512]{2,1,0:T(8,128)(2,1)S(1)} %all-to-all-done.1.fetched_ref), custom_call_target="tpu_custom_call" | custom-call | tf_op jit(solution)/shard_map/pallas_call | solution.py:378
  50.4 0.3 collective-permute-done.1.refs_1_
  50.7 0.0 copy-done.3
  50.7 0.0 copy-done.5
  50.7 0.0 copy-done.7
  50.7 2.3 %shard_map.111 = bf16[256,512]{1,0:T(8,128)(2,1)} custom-call(bf16[256,512]{1,0:T(8,128)(2,1)S(1)} %get-tuple-element.22.refs_0_, bf16[256,512]{1,0:T(8,128)(2,1)S(1)} %collective-permute-done.1.refs_1_, bf16[8,256,80]{2,1,0:T(8,128)(2,1)S(1)} %copy-done.5, bf16[512,256]{1,0:T(8,128)(2,1)S(1)} %get-tuple-element.24.refs_3_, bf16[512,512]{1,0:T(8,128)(2,1)S(1)} %copy-done.7, ...), custom_call_target="tpu_custom_call" | custom-call | tf_op jit(solution)/shard_map/pallas_call | solution.py:393
  (6 shorter events, 0.0 us)
Async XLA Ops:
  2.0 16.0 %all-to-all-start = ((bf16[16,24,128]{2,1,0:T(8,128)(2,1)}), bf16[16,24,128]{2,1,0:T(8,128)(2,1)S(1)}, u32[]{:S(2)}, u32[]{:S(2)}) async-start(bf16[16,24,128]{2,1,0:T(8,128)(2,1)} %shard_map.104), calls=%async_computation | async-start | bytes 196608 | tf_op jit(solution)/shard_map/all_to_all | solution.py:264
  10.3 1.6 %copy-start = (bf16[1,2048,512]{2,1,0:T(8,128)(2,1)S(1)}, bf16[1,2048,512]{2,1,0:T(8,128)(2,1)}, u32[]{:S(2)}) copy-start(bf16[1,2048,512]{2,1,0:T(8,128)(2,1)} %param.11) | copy-start | bytes 6291460
  18.0 7.1 %copy-start.8 = (bf16[1,128,512]{2,1,0:T(8,128)(2,1)S(1)}, bf16[1,128,512]{2,1,0:T(8,128)(2,1)}, u32[]{:S(2)}) copy-start(bf16[1,128,512]{2,1,0:T(8,128)(2,1)} %param.13) | copy-start | bytes 393220
  18.0 7.9 %copy-start.9 = (s32[1,512]{1,0:T(1,128)S(1)}, s32[1,512]{1,0:T(1,128)}, u32[]{:S(2)}) copy-start(s32[1,512]{1,0:T(1,128)} %ids_ref.3) | copy-start | bytes 6148
  18.0 7.9 %copy-start.10 = (s32[4,32]{1,0:T(4,128)S(1)}, s32[4,32]{1,0:T(4,128)}, u32[]{:S(2)}) copy-start(s32[4,32]{1,0:T(4,128)} %probes_ref.1) | copy-start | bytes 1540
  18.0 8.6 %copy-start.1 = (bf16[512,1024]{1,0:T(8,128)(2,1)S(1)}, bf16[512,1024]{1,0:T(8,128)(2,1)}, u32[]{:S(2)}) copy-start(bf16[512,1024]{1,0:T(8,128)(2,1)} %refs_2_.1) | copy-start | bytes 3145732
  21.3 5.2 %copy-start.2 = (bf16[512,512]{1,0:T(8,128)(2,1)S(1)}, bf16[512,512]{1,0:T(8,128)(2,1)}, u32[]{:S(2)}) copy-start(bf16[512,512]{1,0:T(8,128)(2,1)} %refs_3_.1) | copy-start | bytes 1572868
  21.3 27.1 %all-to-all-start.1 = ((bf16[16,64,512]{2,1,0:T(8,128)(2,1)}), bf16[16,64,512]{2,1,0:T(8,128)(2,1)S(1)}, u32[]{:S(2)}, u32[]{:S(2)}) async-start(bf16[16,64,512]{2,1,0:T(8,128)(2,1)} %shard_map.106), calls=%async_computation.1 | async-start | bytes 2097152 | tf_op jit(solution)/shard_map/all_to_all | solution.py:264
  25.1 1.4 %collective-permute-start = (bf16[128,512]{1,0:T(8,128)(2,1)S(1)}, bf16[128,512]{1,0:T(8,128)(2,1)S(1)}, u32[]{:S(2)}, u32[]{:S(2)}) collective-permute-start(bf16[128,512]{1,0:T(8,128)(2,1)S(1)} %bitcast.9), channel_id=1, source_target_pairs={{0,1},{1,0},{2,3},{3,2},{4,5},{5,4},{6,7},{7,6},{8,9},{9,8},{10,11... | collective-permute-start | bytes 393224 | tf_op jit(solution)/shard_map/ppermute | solution.py:331
  26.1 24.7 %copy-start.3 = (bf16[512,512]{1,0:T(8,128)(2,1)S(1)}, bf16[512,512]{1,0:T(8,128)(2,1)}, u32[]{:S(2)}) copy-start(bf16[512,512]{1,0:T(8,128)(2,1)} %refs_5_.1) | copy-start | bytes 1572868
  27.1 0.8 %copy-start.4 = (bf16[8,256,80]{2,1,0:T(8,128)(2,1)}, bf16[8,256,80]{2,1,0:T(8,128)(2,1)S(1)}, u32[]{:S(2)}) copy-start(bf16[8,256,80]{2,1,0:T(8,128)(2,1)S(1)} %get-tuple-element.23.refs_2_) | copy-start | bytes 983044
  27.9 0.8 %copy-start.6 = (bf16[512,512]{1,0:T(8,128)(2,1)}, bf16[512,512]{1,0:T(8,128)(2,1)S(1)}, u32[]{:S(2)}) copy-start(bf16[512,512]{1,0:T(8,128)(2,1)S(1)} %get-tuple-element.25.refs_4_) | copy-start | bytes 1572868
  48.4 2.4 %copy-start.5 = (bf16[8,256,80]{2,1,0:T(8,128)(2,1)S(1)}, bf16[8,256,80]{2,1,0:T(8,128)(2,1)}, u32[]{:S(2)}) copy-start(bf16[8,256,80]{2,1,0:T(8,128)(2,1)} %copy-done.4) | copy-start | bytes 983044
  48.4 2.4 %copy-start.7 = (bf16[512,512]{1,0:T(8,128)(2,1)S(1)}, bf16[512,512]{1,0:T(8,128)(2,1)}, u32[]{:S(2)}) copy-start(bf16[512,512]{1,0:T(8,128)(2,1)} %copy-done.6) | copy-start | bytes 1572868
  49.1 1.6 %collective-permute-start.1 = (bf16[256,512]{1,0:T(8,128)(2,1)S(1)}, bf16[256,512]{1,0:T(8,128)(2,1)S(1)}, u32[]{:S(2)}, u32[]{:S(2)}) collective-permute-start(bf16[256,512]{1,0:T(8,128)(2,1)S(1)} %shard_map.110), channel_id=1, source_target_pairs={{0,1},{1,0},{2,3},{3,2},{4,5},{5,4},{6,7},{7,6},{8,9},{9,8},{10,11... | collective-permute-start | bytes 786440 | tf_op jit(solution)/shard_map/ppermute | solution.py:375

commit v10 on v9

--- a/solution.py
+++ b/solution.py
@@ -91,6 +91,13 @@
     return index
 
 
+def position(index, count):
+    if count % 4:
+        return index
+    quarter = count // 4
+    return index // (2 * quarter) * (2 * quarter) + index % quarter * 2 + index // quarter % 2
+
+
 def items_kernel(items_hbm, items_ref, sems):
     part = items_ref.shape[0] // sems.shape[0]
     loads = []
@@ -112,8 +119,8 @@
     hot = jnp.where((lists == owner) & mine, 1.0, 0.0)
     before = jnp.dot(hot.astype(jnp.bfloat16), earlier(cands), preferred_element_type=jnp.float32)
     rank = jnp.sum(before * hot, axis=0, keepdims=True)
-    slot = jnp.where(mine, owner.astype(jnp.float32) * block + rank, -1.0)
-    probes = probes_ref[...].astype(jnp.float32)
+    slot = jnp.where(mine, position(owner, n_lists).astype(jnp.float32) * block + rank, -1.0)
+    probes = position(probes_ref[...], n_lists).astype(jnp.float32)
     flat = jnp.concatenate([probes[u : u + 1] for u in range(probes.shape[0])], axis=1)
     if flat.shape[1] < cands:
         flat = jnp.concatenate([flat, jnp.zeros((1, cands - flat.shape[1]), jnp.float32)], axis=1)
@@ -261,7 +268,11 @@
 
 
 def exchange(value):
-    return lax.all_to_all(value, "lists", split_axis=0, concat_axis=0, tiled=True)
+    count = lax.axis_size("lists")
+    group = sorted(range(count), key=lambda index: position(index, count))
+    return lax.all_to_all(
+        value, "lists", split_axis=0, concat_axis=0, axis_index_groups=[group], tiled=True
+    )
 
 
 def shards(

time: 53.7 us -> 56.2 us (1.047)
  waiting for transfers between devices: 26.3 us -> 29.1 us
    all_to_all x2, waiting for transfers between devices: 25.5 us -> 28.3 us  [exchange(): lax.all_to_all(value, 'lists', split_axis=0, concat_axis=0, axis_index_gr...]
where the time goes in v10:
time: 56.2 us; the launch traced here: 55.9 us
  waiting for transfers between devices  29.1 us (52%)
  starting transfers between devices  12.3 us (22%)
  Pallas kernels  9.84 us (18%)
  local copies, waits for them, and re-layouts  3.25 us (6%)
  between operations  1.44 us (3%)
    all_to_all x2, waiting for transfers between devices, exchange(): lax.all_to_all(value, 'lists', split_axis=0, concat_axis=0, axis_index_gr...  28.3 us
    all_to_all x2, starting transfers between devices, exchange(): lax.all_to_all(value, 'lists', split_axis=0, concat_axis=0, axis_index_gr...  12.1 us
    pallas_call x1, Pallas kernels, shards(): pl.pallas_call(functools.partial(owner_kernel, n_lists, user_dev, digits,...  3.29 us
    unnamed x22, local copies, waits for them, and re-layouts  3.25 us
    pallas_call x1, Pallas kernels, shards(): pl.pallas_call(functools.partial(attend_kernel, n_users), out_shape=jax.S...  2.32 us
    pallas_call x1, Pallas kernels, shards(): pl.pallas_call(functools.partial(pack_kernel, digits), out_shape=jax.Shap...  1.36 us
    pallas_call x1, Pallas kernels, shards(): pl.pallas_call(functools.partial(expand_kernel, user_dev, pieces, cap), o...  1.17 us
  transfers between devices with their start and end apart: 4, of which 4 were waited for; matrix products, arithmetic and copies ran while one was open for 0% of the time, Pallas kernels for 4%

profile of v10, /device:TPU:0, one launch (start us, length us, event | category | flops | bytes accessed | tf_op | source)
XLA Modules:
  0.0 55.9 jit_solution(8614794351920141410)
XLA Ops:
  0.6 1.4 %shard_map.104 = bf16[16,24,128]{2,1,0:T(8,128)(2,1)} custom-call(s32[1,512]{1,0:T(1,128)} %ids_ref.3, bf16[4,512]{1,0:T(4,128)(2,1)} %vectors_ref.1), custom_call_target="tpu_custom_call" | custom-call | tf_op jit(solution)/shard_map/pallas_call | solution.py:311
  2.0 8.3 %all-to-all-start = ((bf16[16,24,128]{2,1,0:T(8,128)(2,1)}), bf16[16,24,128]{2,1,0:T(8,128)(2,1)S(1)}, u32[]{:S(2)}, u32[]{:S(2)}) async-start(bf16[16,24,128]{2,1,0:T(8,128)(2,1)} %shard_map.104), calls=%async_computation | async-start | bytes 196608 | tf_op jit(solution)/shard_map/all_to_all | solution.py:273
  10.3 0.0 copy-start
  10.3 1.6 %copy-done = bf16[1,2048,512]{2,1,0:T(8,128)(2,1)S(1)} copy-done((bf16[1,2048,512]{2,1,0:T(8,128)(2,1)S(1)}, bf16[1,2048,512]{2,1,0:T(8,128)(2,1)}, u32[]{:S(2)}) %copy-start) | copy-done | bytes 2097176
  11.9 0.2 shard_map.105.items_ref
  12.1 5.7 %all-to-all-done = bf16[16,24,128]{2,1,0:T(8,128)(2,1)S(1)} async-done(((bf16[16,24,128]{2,1,0:T(8,128)(2,1)}), bf16[16,24,128]{2,1,0:T(8,128)(2,1)S(1)}, u32[]{:S(2)}, u32[]{:S(2)}) %all-to-all-start) | async-done | bytes 98336 | tf_op jit(solution)/shard_map/all_to_all | solution.py:273
  17.8 0.0 copy-start.8
  17.9 3.3 %shard_map.106 = bf16[16,64,512]{2,1,0:T(8,128)(2,1)} custom-call(s32[1]{0:T(128)} %bitcast.1.base_ref, bf16[384,128]{1,0:T(8,128)(2,1)S(1)} %bitcast.8, bf16[2048,512]{1,0:T(8,128)(2,1)S(1)} %shard_map.105.items_ref), custom_call_target="tpu_custom_call" | custom-call | tf_op jit(solution)/shard_map/pallas_call | solution.py:357
  21.2 0.0 copy-start.2
  21.2 3.8 %all-to-all-start.1 = ((bf16[16,64,512]{2,1,0:T(8,128)(2,1)}), bf16[16,64,512]{2,1,0:T(8,128)(2,1)S(1)}, u32[]{:S(2)}, u32[]{:S(2)}) async-start(bf16[16,64,512]{2,1,0:T(8,128)(2,1)} %shard_map.106), calls=%async_computation.1 | async-start | bytes 2097152 | tf_op jit(solution)/shard_map/all_to_all | solution.py:273
  25.0 0.0 copy-done.8
  25.0 0.1 collective-permute-start
  25.7 0.0 copy-done.9
  25.7 0.0 copy-done.10
  25.7 0.2 shard_map.107.known_ref
  25.9 0.0 copy-start.3
  25.9 0.5 collective-permute-done.refs_1_
  26.4 0.0 copy-done.1
  26.4 0.0 copy-done.2
  26.4 0.6 %shard_map.108 = (bf16[8,256,80]{2,1,0:T(8,128)(2,1)S(1)}, bf16[512,256]{1,0:T(8,128)(2,1)S(1)}, bf16[512,512]{1,0:T(8,128)(2,1)S(1)}) custom-call(s32[1]{0:T(128)} %bitcast.col_ref, s32[1]{0:T(128)S(6)} %copy.11.length_ref, bf16[128,512]{1,0:T(8,128)(2,1)S(1)} %bitcast.10, bf16[128,512]{1,0:T(8,128)(2,1)S(1)} %collective-permute-done.refs_1_, ...), custom_call_target="tpu_custom_call" | custom-call | tf_op jit(solution)/shard_map/pallas_call | solution.py:344
  27.0 0.0 copy-start.4
  27.0 0.8 %copy-done.4 = bf16[8,256,80]{2,1,0:T(8,128)(2,1)} copy-done((bf16[8,256,80]{2,1,0:T(8,128)(2,1)}, bf16[8,256,80]{2,1,0:T(8,128)(2,1)S(1)}, u32[]{:S(2)}) %copy-start.4) | copy-done | bytes 327704
  27.8 0.8 %copy-done.6 = bf16[512,512]{1,0:T(8,128)(2,1)} copy-done((bf16[512,512]{1,0:T(8,128)(2,1)}, bf16[512,512]{1,0:T(8,128)(2,1)S(1)}, u32[]{:S(2)}) %copy-start.6) | copy-done | bytes 524312
  28.6 22.6 %all-to-all-done.1.fetched_ref = bf16[16,64,512]{2,1,0:T(8,128)(2,1)S(1)} async-done(((bf16[16,64,512]{2,1,0:T(8,128)(2,1)}), bf16[16,64,512]{2,1,0:T(8,128)(2,1)S(1)}, u32[]{:S(2)}, u32[]{:S(2)}) %all-to-all-start.1) | async-done | bytes 1048608 | tf_op jit(solution)/shard_map/all_to_all | solution.py:273
  51.2 0.7 %shard_map.110 = bf16[256,512]{1,0:T(8,128)(2,1)S(1)} custom-call(s32[1]{0:T(128)} %bitcast.col_ref, f32[8,512]{1,0:T(8,128)S(1)} %shard_map.107.known_ref, bf16[16,64,512]{2,1,0:T(8,128)(2,1)S(1)} %all-to-all-done.1.fetched_ref), custom_call_target="tpu_custom_call" | custom-call | tf_op jit(solution)/shard_map/pallas_call | solution.py:375
  52.0 0.1 collective-permute-start.1
  52.0 1.2 %shard_map.109 = (bf16[128,2048]{1,0:T(8,128)(2,1)}, bf16[256,512]{1,0:T(8,128)(2,1)S(1)}) custom-call(s32[1]{0:T(128)} %bitcast.col_ref, f32[8,512]{1,0:T(8,128)S(1)} %shard_map.107.known_ref, bf16[16,64,512]{2,1,0:T(8,128)(2,1)S(1)} %all-to-all-done.1.fetched_ref), custom_call_target="tpu_custom_call" | custom-call | tf_op jit(solution)/shard_map/pallas_call | solution.py:389
  53.2 0.3 collective-permute-done.1.refs_1_
  53.6 0.0 copy-done.3
  53.6 0.0 copy-done.5
  53.6 0.0 copy-done.7
  53.6 2.3 %shard_map.111 = bf16[256,512]{1,0:T(8,128)(2,1)} custom-call(bf16[256,512]{1,0:T(8,128)(2,1)S(1)} %get-tuple-element.22.refs_0_, bf16[256,512]{1,0:T(8,128)(2,1)S(1)} %collective-permute-done.1.refs_1_, bf16[8,256,80]{2,1,0:T(8,128)(2,1)S(1)} %copy-done.5, bf16[512,256]{1,0:T(8,128)(2,1)S(1)} %get-tuple-element.24.refs_3_, bf16[512,512]{1,0:T(8,128)(2,1)S(1)} %copy-done.7, ...), custom_call_target="tpu_custom_call" | custom-call | tf_op jit(solution)/shard_map/pallas_call | solution.py:404
  (6 shorter events, 0.0 us)
Async XLA Ops:
  2.0 15.9 %all-to-all-start = ((bf16[16,24,128]{2,1,0:T(8,128)(2,1)}), bf16[16,24,128]{2,1,0:T(8,128)(2,1)S(1)}, u32[]{:S(2)}, u32[]{:S(2)}) async-start(bf16[16,24,128]{2,1,0:T(8,128)(2,1)} %shard_map.104), calls=%async_computation | async-start | bytes 196608 | tf_op jit(solution)/shard_map/all_to_all | solution.py:273
  10.3 1.6 %copy-start = (bf16[1,2048,512]{2,1,0:T(8,128)(2,1)S(1)}, bf16[1,2048,512]{2,1,0:T(8,128)(2,1)}, u32[]{:S(2)}) copy-start(bf16[1,2048,512]{2,1,0:T(8,128)(2,1)} %param.11) | copy-start | bytes 6291460
  17.8 7.1 %copy-start.8 = (bf16[1,128,512]{2,1,0:T(8,128)(2,1)S(1)}, bf16[1,128,512]{2,1,0:T(8,128)(2,1)}, u32[]{:S(2)}) copy-start(bf16[1,128,512]{2,1,0:T(8,128)(2,1)} %param.13) | copy-start | bytes 393220
  17.8 7.9 %copy-start.9 = (s32[1,512]{1,0:T(1,128)S(1)}, s32[1,512]{1,0:T(1,128)}, u32[]{:S(2)}) copy-start(s32[1,512]{1,0:T(1,128)} %ids_ref.3) | copy-start | bytes 6148
  17.8 7.9 %copy-start.10 = (s32[4,32]{1,0:T(4,128)S(1)}, s32[4,32]{1,0:T(4,128)}, u32[]{:S(2)}) copy-start(s32[4,32]{1,0:T(4,128)} %probes_ref.1) | copy-start | bytes 1540
  17.8 8.5 %copy-start.1 = (bf16[512,1024]{1,0:T(8,128)(2,1)S(1)}, bf16[512,1024]{1,0:T(8,128)(2,1)}, u32[]{:S(2)}) copy-start(bf16[512,1024]{1,0:T(8,128)(2,1)} %refs_2_.1) | copy-start | bytes 3145732
  21.2 5.2 %copy-start.2 = (bf16[512,512]{1,0:T(8,128)(2,1)S(1)}, bf16[512,512]{1,0:T(8,128)(2,1)}, u32[]{:S(2)}) copy-start(bf16[512,512]{1,0:T(8,128)(2,1)} %refs_3_.1) | copy-start | bytes 1572868
  21.2 30.0 %all-to-all-start.1 = ((bf16[16,64,512]{2,1,0:T(8,128)(2,1)}), bf16[16,64,512]{2,1,0:T(8,128)(2,1)S(1)}, u32[]{:S(2)}, u32[]{:S(2)}) async-start(bf16[16,64,512]{2,1,0:T(8,128)(2,1)} %shard_map.106), calls=%async_computation.1 | async-start | bytes 2097152 | tf_op jit(solution)/shard_map/all_to_all | solution.py:273
  25.0 1.4 %collective-permute-start = (bf16[128,512]{1,0:T(8,128)(2,1)S(1)}, bf16[128,512]{1,0:T(8,128)(2,1)S(1)}, u32[]{:S(2)}, u32[]{:S(2)}) collective-permute-start(bf16[128,512]{1,0:T(8,128)(2,1)S(1)} %bitcast.9), channel_id=1, source_target_pairs={{0,1},{1,0},{2,3},{3,2},{4,5},{5,4},{6,7},{7,6},{8,9},{9,8},{10,11... | collective-permute-start | bytes 393224 | tf_op jit(solution)/shard_map/ppermute | solution.py:342
  25.9 27.6 %copy-start.3 = (bf16[512,512]{1,0:T(8,128)(2,1)S(1)}, bf16[512,512]{1,0:T(8,128)(2,1)}, u32[]{:S(2)}) copy-start(bf16[512,512]{1,0:T(8,128)(2,1)} %refs_5_.1) | copy-start | bytes 1572868
  27.0 0.8 %copy-start.4 = (bf16[8,256,80]{2,1,0:T(8,128)(2,1)}, bf16[8,256,80]{2,1,0:T(8,128)(2,1)S(1)}, u32[]{:S(2)}) copy-start(bf16[8,256,80]{2,1,0:T(8,128)(2,1)S(1)} %get-tuple-element.23.refs_2_) | copy-start | bytes 983044
  27.8 0.8 %copy-start.6 = (bf16[512,512]{1,0:T(8,128)(2,1)}, bf16[512,512]{1,0:T(8,128)(2,1)S(1)}, u32[]{:S(2)}) copy-start(bf16[512,512]{1,0:T(8,128)(2,1)S(1)} %get-tuple-element.25.refs_4_) | copy-start | bytes 1572868
  51.2 2.4 %copy-start.5 = (bf16[8,256,80]{2,1,0:T(8,128)(2,1)S(1)}, bf16[8,256,80]{2,1,0:T(8,128)(2,1)}, u32[]{:S(2)}) copy-start(bf16[8,256,80]{2,1,0:T(8,128)(2,1)} %copy-done.4) | copy-start | bytes 983044
  51.2 2.4 %copy-start.7 = (bf16[512,512]{1,0:T(8,128)(2,1)S(1)}, bf16[512,512]{1,0:T(8,128)(2,1)}, u32[]{:S(2)}) copy-start(bf16[512,512]{1,0:T(8,128)(2,1)} %copy-done.6) | copy-start | bytes 1572868
  52.0 1.6 %collective-permute-start.1 = (bf16[256,512]{1,0:T(8,128)(2,1)S(1)}, bf16[256,512]{1,0:T(8,128)(2,1)S(1)}, u32[]{:S(2)}, u32[]{:S(2)}) collective-permute-start(bf16[256,512]{1,0:T(8,128)(2,1)S(1)} %shard_map.110), channel_id=1, source_target_pairs={{0,1},{1,0},{2,3},{3,2},{4,5},{5,4},{6,7},{7,6},{8,9},{9,8},{10,11... | collective-permute-start | bytes 786440 | tf_op jit(solution)/shard_map/ppermute | solution.py:386

commit v11 on v9

--- a/solution.py
+++ b/solution.py
@@ -68,7 +68,7 @@
     return vectors, ids
 
 
-def asked(ids, base, items_loc, count):
+def asked(ids, base, items_loc, first, count):
     n_lists = ids[0].shape[0]
     local = jnp.concatenate([part - base for part in ids], axis=0)
     mine = (local >= 0.0) & (local < items_loc)
@@ -83,12 +83,12 @@
         locals_.append(local[rows] + 1.0)
         before = before + totals[rows]
     rank, local = jnp.concatenate(ranks, axis=1), jnp.concatenate(locals_, axis=1)
-    place = lax.broadcasted_iota(jnp.int32, (count, rank.shape[1]), 0).astype(jnp.float32)
+    place = (lax.broadcasted_iota(jnp.int32, (count, rank.shape[1]), 0) + first).astype(jnp.float32)
     index = []
     for r in range(n_lists):
         picked = jnp.where(rank[r : r + 1] == place, local[r : r + 1], 0.0)
         index.append(jnp.sum(picked, axis=1, keepdims=True).astype(jnp.int32) - 1)
-    return index
+    return index, before
 
 
 def items_kernel(items_hbm, items_ref, sems):
@@ -102,17 +102,47 @@
         load.wait()
 
 
-def known_kernel(n_lists, items_loc, n_users, block, col_ref, ids_ref, probes_ref, known_ref):
+def crowded(ids, n_lists, items_loc, main, spare):
+    bins = [part.astype(jnp.int32) // items_loc for part in ids]
+    worst = jnp.zeros((n_lists, 1), jnp.float32)
+    for owner in range(n_lists):
+        count = []
+        for c in range(2):
+            hits = [jnp.where(part == owner * 2 + c, 1.0, 0.0) for part in bins]
+            count.append(jnp.sum(sum(hits[1:], hits[0]), axis=1, keepdims=True))
+        for one, other in ((0, 1), (1, 0)):
+            clash = (count[one] > float(main - spare)) & (count[other] > float(main))
+            worst = jnp.maximum(worst, jnp.where(clash, 1.0, 0.0))
+    return jnp.max(worst)
+
+
+def known_kernel(
+    n_lists, items_loc, n_users, user_dev, digits, main, spare, kept, *refs
+):
+    line_ref, col_ref, ids_ref, probes_ref, gathered_ref, known_ref, many_ref, wide = refs
+    block = kept + main
     ids = ids_ref[...]
     cands = ids.shape[1]
     bins = ids // items_loc
     mine = bins % n_users == col_ref[0]
     owner = bins // n_users
-    lists = lax.broadcasted_iota(jnp.int32, (n_lists, cands), 0)
-    hot = jnp.where((lists == owner) & mine, 1.0, 0.0)
+    lists = lax.broadcasted_iota(jnp.int32, (n_lists * n_users, cands), 0)
+    hot = jnp.where(lists == bins, 1.0, 0.0)
     before = jnp.dot(hot.astype(jnp.bfloat16), earlier(cands), preferred_element_type=jnp.float32)
     rank = jnp.sum(before * hot, axis=0, keepdims=True)
-    slot = jnp.where(mine, owner.astype(jnp.float32) * block + rank, -1.0)
+    slot = owner.astype(jnp.float32) * block + kept + rank
+    if spare:
+        wide[...] = gathered_ref[...].astype(jnp.float32)
+        _, asked_ids = unpack(wide, n_lists, user_dev, digits, cands // LANES)
+        many = crowded(asked_ids, n_lists, items_loc, main, spare)
+        many_ref[0] = many.astype(jnp.int32)
+        apart = n_lists * block + (owner ^ line_ref[0]).astype(jnp.float32) * spare + rank - main
+        apart = jnp.where(many > 0.5, apart, -1.0)
+        there = jnp.where((rank >= float(main)) & (many < 0.5), slot - spare, -1.0)
+        slot = jnp.where(mine, jnp.where(rank < float(main), slot, apart), there)
+    else:
+        many_ref[0] = jnp.int32(0)
+        slot = jnp.where(mine, slot, -1.0)
     probes = probes_ref[...].astype(jnp.float32)
     flat = jnp.concatenate([probes[u : u + 1] for u in range(probes.shape[0])], axis=1)
     if flat.shape[1] < cands:
@@ -140,12 +170,15 @@
     turned_ref[...] = jnp.transpose(query_ref[...].astype(jnp.float32)).astype(jnp.bfloat16)
 
 
-def owner_kernel(n_lists, user_dev, digits, cap, scale, base_ref, gathered_ref, items_ref, *refs):
-    out_hbm, wide, out_ref, out_sems = refs
+def owner_kernel(
+    n_lists, user_dev, digits, main, spare, scale, base_ref, other_ref, gathered_ref, items_ref, *refs
+):
+    sibling_ref = refs[0] if spare else None
+    out_hbm, wide, out_ref, out_sems = refs[-4:]
     items_loc, width = items_ref.shape
     wide[...] = gathered_ref[...].astype(jnp.float32)
     vectors, ids = unpack(wide, n_lists, user_dev, digits, width // LANES)
-    index = asked(ids, base_ref[0].astype(jnp.float32), items_loc, cap)
+    index, own = asked(ids, base_ref[0].astype(jnp.float32), items_loc, 0, main)
     scores = lax.dot_general(
         vectors.astype(jnp.bfloat16),
         items_ref[...],
@@ -157,14 +190,20 @@
     stacked = jnp.concatenate(
         [scores[:, piece * width : (piece + 1) * width] for piece in range(pieces)], axis=0
     )
-    kept = out_ref.shape[1] - cap
+    kept = out_ref.shape[1] - main
     entry = lax.broadcasted_iota(jnp.int32, (n_lists * kept, 1), 0)
     wanted = jnp.where(entry % kept < pieces * user_dev, entry % kept * n_lists + entry // kept, -1)
     spread = jnp.dot(
         picks(wanted, stacked.shape[0]), stacked, preferred_element_type=jnp.float32
     ).astype(jnp.bfloat16)
-    out_ref[:, cap:, :] = spread.reshape(n_lists, kept, width)
-    step = max(1, 288 // cap)
+    out_ref[:, :kept, :] = spread.reshape(n_lists, kept, width)
+    if spare:
+        over, _ = asked(ids, other_ref[0].astype(jnp.float32), items_loc, main, spare)
+        over = [jnp.where(own[r : r + 1] > float(main - spare), -1, over[r]) for r in range(n_lists)]
+        shared = jnp.dot(
+            picks(jnp.concatenate(over, axis=0), items_loc), sibling_ref[...], preferred_element_type=jnp.float32
+        )
+    step = max(1, 288 // main)
     sends = []
     for number, first in enumerate(range(0, n_lists, step)):
         last = min(n_lists, first + step)
@@ -172,8 +211,13 @@
             picks(jnp.concatenate(index[first:last], axis=0), items_loc),
             items_ref[...],
             preferred_element_type=jnp.float32,
-        ).astype(jnp.bfloat16)
-        out_ref[first:last, :cap, :] = rows.reshape(last - first, cap, width)
+        )
+        for r in range(first, last):
+            mine = rows[(r - first) * main : (r - first + 1) * main]
+            out_ref[r, kept : kept + main - spare, :] = mine[: main - spare].astype(jnp.bfloat16)
+            if spare:
+                both = mine[main - spare :] + shared[r * spare : (r + 1) * spare]
+                out_ref[r, kept + main - spare :, :] = both.astype(jnp.bfloat16)
         send = pltpu.make_async_copy(out_ref.at[first:last], out_hbm.at[first:last], out_sems.at[number])
         send.start()
         sends.append(send)
@@ -181,23 +225,44 @@
         send.wait()
 
 
-def placed(column, known_ref, slots, fetched_ref, out_ref):
+def spill_kernel(n_lists, user_dev, digits, main, base_ref, gathered_ref, items_ref, spill_ref, wide):
+    items_loc, width = items_ref.shape
+    spare = spill_ref.shape[1]
+    wide[...] = gathered_ref[...].astype(jnp.float32)
+    _, ids = unpack(wide, n_lists, user_dev, digits, width // LANES)
+    index, _ = asked(ids, base_ref[0].astype(jnp.float32), items_loc, main, spare)
+    rows = jnp.dot(
+        picks(jnp.concatenate(index, axis=0), items_loc), items_ref[...], preferred_element_type=jnp.float32
+    )
+    spill_ref[...] = rows.astype(jnp.bfloat16).reshape(spill_ref.shape)
+
+
+def stay_kernel(came_ref, here_ref):
+    here_ref[...] = came_ref[...]
+
+
+def placed(column, known_ref, slots, fetched_ref, extra_refs, out_ref):
     n_lists, block, width = fetched_ref.shape
     share = out_ref.shape[0]
     slots[...] = jnp.transpose(known_ref[...])
     start = pl.multiple_of(column * share, share)
     slot = slots[pl.ds(start, share), :][:, :1].astype(jnp.int32)
-    out_ref[...] = jnp.dot(
+    rows = jnp.dot(
         picks(slot, n_lists * block),
         fetched_ref[...].reshape(n_lists * block, width),
         preferred_element_type=jnp.float32,
-    ).astype(jnp.bfloat16)
+    )
+    for ref in extra_refs:
+        rows = rows + jnp.dot(
+            picks(slot - n_lists * block, ref.shape[0]), ref[...], preferred_element_type=jnp.float32
+        )
+    out_ref[...] = rows.astype(jnp.bfloat16)
 
 
 def place_kernel(n_users, col_ref, known_ref, fetched_ref, *refs):
-    sent_refs, slots = refs[:-1], refs[-1]
+    extra_refs, sent_refs, slots = refs[: -n_users], refs[-n_users:-1], refs[-1]
     for shift, ref in enumerate(sent_refs):
-        placed((col_ref[0] + shift + 1) % n_users, known_ref, slots, fetched_ref, ref)
+        placed((col_ref[0] + shift + 1) % n_users, known_ref, slots, fetched_ref, extra_refs, ref)
 
 
 def attend_kernel(n_parts, *refs):
@@ -232,11 +297,11 @@
     out_ref[...] = jnp.dot(attended, out_weight_ref[...], preferred_element_type=jnp.float32).astype(jnp.bfloat16)
 
 
-def expand_kernel(user_dev, pieces, cap, col_ref, known_ref, fetched_ref, out_hbm, own_ref, out_ref, slots, sems):
-    n_lists, block, width = fetched_ref.shape
-    kept = block - cap
+def expand_kernel(user_dev, pieces, kept, col_ref, known_ref, fetched_ref, *refs):
+    extra_refs, (out_hbm, own_ref, out_ref, slots, sems) = refs[:-5], refs[-5:]
+    n_lists, _, width = fetched_ref.shape
     rows = n_lists * kept
-    returned = fetched_ref[:, cap:, :].reshape(rows, width)
+    returned = fetched_ref[:, :kept, :].reshape(rows, width)
     count = out_ref.shape[0]
     probe = jnp.transpose(known_ref[:, :count])[:, 1:2].astype(jnp.int32)
     user = lax.broadcasted_iota(jnp.int32, (count, 1), 0) // (count // user_dev)
@@ -249,7 +314,7 @@
         )
         sends.append(pltpu.make_async_copy(out_ref.at[:, span], out_hbm.at[:, span], sems.at[piece]))
         sends[-1].start()
-    placed(col_ref[0], known_ref, slots, fetched_ref, own_ref)
+    placed(col_ref[0], known_ref, slots, fetched_ref, extra_refs, own_ref)
     for send in sends:
         send.wait()
 
@@ -293,8 +358,12 @@
     line = lax.axis_index("lists").astype(jnp.int32)
     col = lax.axis_index("users").astype(jnp.int32)
     col_arg = col.reshape(1)
+    line_arg = line.reshape(1)
     base_arg = ((line * n_users + col) * items_loc).reshape(1)
-    block = cap + kept
+    other_arg = ((line * n_users + n_users - 1 - col) * items_loc).reshape(1)
+    spare = 8 if n_users == 2 and cap >= 48 else 0
+    main = cap - spare
+    block = main + kept
 
     flat_items = list_items.reshape(items_loc, width)
     pack = pl.pallas_call(
@@ -317,13 +386,50 @@
     )(flat_items)
     gathered, items = lax.optimization_barrier((gathered, items))
 
-    known = pl.pallas_call(
-        functools.partial(known_kernel, n_lists, items_loc, n_users, block),
-        out_shape=jax.ShapeDtypeStruct((8, cands), jnp.float32),
-        in_specs=[SMEM, VMEM, VMEM],
-        out_specs=VMEM,
+    siblings = []
+    if spare:
+        siblings.append(lax.ppermute(flat_items, "users", [(0, 1), (1, 0)]))
+
+    known, many = pl.pallas_call(
+        functools.partial(known_kernel, n_lists, items_loc, n_users, user_dev, digits, main, spare, kept),
+        out_shape=(
+            jax.ShapeDtypeStruct((8, cands), jnp.float32),
+            jax.ShapeDtypeStruct((1,), jnp.int32),
+        ),
+        in_specs=[SMEM, SMEM, VMEM, VMEM, VMEM],
+        out_specs=(VMEM, SMEM),
+        scratch_shapes=[pltpu.VMEM((n_lists * pack_rows, LANES), jnp.float32)],
         compiler_params=PARAMS,
-    )(col_arg, candidate_ids, probe_lists)
+    )(line_arg, col_arg, candidate_ids, probe_lists, gathered)
+
+    extras = []
+    if spare:
+
+        def spill_apart():
+            spill = pl.pallas_call(
+                functools.partial(spill_kernel, n_lists, user_dev, digits, main),
+                out_shape=jax.ShapeDtypeStruct((n_lists, spare, width), bf16),
+                in_specs=[SMEM, VMEM, VMEM],
+                out_specs=VMEM,
+                scratch_shapes=[pltpu.VMEM((n_lists * pack_rows, LANES), jnp.float32)],
+                compiler_params=PARAMS,
+            )(base_arg, gathered, flat_items)
+            spill = spill[jnp.arange(n_lists, dtype=jnp.int32) ^ line]
+            blocks = [spill[:1]]
+            for k in range(1, n_lists):
+                blocks.append(lax.ppermute(spill[k : k + 1], "lists", [(i, i ^ k) for i in range(n_lists)]))
+            return jnp.concatenate(blocks, axis=0).reshape(n_lists * spare, width)
+
+        came = lax.cond(many[0] > 0, spill_apart, lambda: jnp.zeros((n_lists * spare, width), bf16))
+        extras.append(
+            pl.pallas_call(
+                stay_kernel,
+                out_shape=jax.ShapeDtypeStruct(came.shape, bf16),
+                in_specs=[VMEM],
+                out_specs=VMEM,
+                compiler_params=PARAMS,
+            )(came)
+        )
 
     events = history.reshape(-1, width)
     hist = [events]
@@ -342,11 +448,11 @@
         compiler_params=PARAMS,
     )(col_arg, history_lengths, *hist, key_value_weight, query_weight)
 
-    step = max(1, 288 // cap)
+    step = max(1, 288 // main)
     answers = pl.pallas_call(
-        functools.partial(owner_kernel, n_lists, user_dev, digits, cap, width ** (-0.5)),
+        functools.partial(owner_kernel, n_lists, user_dev, digits, main, spare, width ** (-0.5)),
         out_shape=jax.ShapeDtypeStruct((n_lists, block, width), bf16),
-        in_specs=[SMEM, VMEM, VMEM],
+        in_specs=[SMEM, SMEM] + [VMEM] * (2 + len(siblings)),
         out_specs=pl.BlockSpec(memory_space=pl.ANY),
         scratch_shapes=[
             pltpu.VMEM((n_lists * pack_rows, LANES), jnp.float32),
@@ -354,21 +460,23 @@
             pltpu.SemaphoreType.DMA((-(-n_lists // step),)),
         ],
         compiler_params=PARAMS,
-    )(base_arg, gathered, items)
+    )(base_arg, other_arg, gathered, items, *siblings)
     fetched = exchange(answers)
 
-    fetched, known, keys, values, turned = lax.optimization_barrier((fetched, known, keys, values, turned))
+    fetched, known, extras, keys, values, turned = lax.optimization_barrier(
+        (fetched, known, extras, keys, values, turned)
+    )
 
     sent = []
     if n_users > 1:
         sent = pl.pallas_call(
             functools.partial(place_kernel, n_users),
             out_shape=tuple(jax.ShapeDtypeStruct((share, width), bf16) for _ in range(n_users - 1)),
-            in_specs=[SMEM, VMEM, VMEM],
+            in_specs=[SMEM, VMEM, VMEM] + [VMEM] * len(extras),
             out_specs=tuple(VMEM for _ in range(n_users - 1)),
             scratch_shapes=[pltpu.VMEM((cands, 8), jnp.float32)],
             compiler_params=PARAMS,
-        )(col_arg, known, fetched)
+        )(col_arg, known, fetched, *extras)
     parts = []
     for shift in range(1, n_users):
         parts.append(
@@ -376,12 +484,12 @@
         )
 
     list_scores, own = pl.pallas_call(
-        functools.partial(expand_kernel, user_dev, pieces, cap),
+        functools.partial(expand_kernel, user_dev, pieces, kept),
         out_shape=(
             jax.ShapeDtypeStruct((user_dev * probes, items_loc), bf16),
             jax.ShapeDtypeStruct((share, width), bf16),
         ),
-        in_specs=[SMEM, VMEM, VMEM],
+        in_specs=[SMEM, VMEM, VMEM] + [VMEM] * len(extras),
         out_specs=(pl.BlockSpec(memory_space=pl.ANY), VMEM),
         scratch_shapes=[
             pltpu.VMEM((user_dev * probes, items_loc), bf16),
@@ -389,7 +497,7 @@
             pltpu.SemaphoreType.DMA((pieces,)),
         ],
         compiler_params=PARAMS,
-    )(col_arg, known, fetched)
+    )(col_arg, known, fetched, *extras)
     ranked = pl.pallas_call(
         functools.partial(attend_kernel, n_users),
         out_shape=jax.ShapeDtypeStruct((share, width), bf16),

time: 53.7 us -> 54.1 us (level)
  Pallas kernels: 9.85 us -> 15.8 us
  waiting for transfers between devices: 26.3 us -> 21 us
  local copies, waits for them, and re-layouts: 3.25 us -> 2.31 us
  between operations: 1.44 us -> 2.08 us
    all_to_all x2, waiting for transfers between devices: 25.5 us -> 20 us  [exchange(): lax.all_to_all(value, 'lists', split_axis=0, concat_axis=0, tiled=True)]
    pallas_call x1, Pallas kernels: 3.3 us -> 5.38 us  [shards(): pl.pallas_call(functools.partial(owner_kernel, n_lists, user_dev, digits,...]
    unnamed x22 -> x18, local copies, waits for them, and re-layouts: 3.25 us -> 1.64 us
    pallas_call x1, Pallas kernels: 0.2 us -> 1.68 us  [shards(): pl.pallas_call(functools.partial(known_kernel, n_lists, items_loc, n_user...]
    pallas_call x1, Pallas kernels: 0.18 us -> 1.55 us  [shards(): pl.pallas_call(items_kernel, out_shape=jax.ShapeDtypeStruct((items_loc, w...]
    pallas_call x1 -> x2, Pallas kernels: 1.17 us -> 2.16 us  [the longest x1 1.17 us: shards(): pl.pallas_call(functools.partial(expand_kernel, user_dev, pieces, kept),...]
    another operation x0 -> x1, local copies, waits for them, and re-layouts: none -> 0.67 us
  transfers between devices with their start and end apart: 4 -> 5, of which waited for: 4 -> 4; matrix products, arithmetic and copies ran while one was open for 0% -> 1% of each run, Pallas kernels for 4% -> 14%
where the time goes in v11:
time: 54.1 us; the launch traced here: 53.6 us
  waiting for transfers between devices  21 us (39%)
  Pallas kernels  15.8 us (29%)
  starting transfers between devices  12.4 us (23%)
  local copies, waits for them, and re-layouts  2.31 us (4%)
  between operations  2.08 us (4%)
    all_to_all x2, waiting for transfers between devices, exchange(): lax.all_to_all(value, 'lists', split_axis=0, concat_axis=0, tiled=True)  20 us
    all_to_all x2, starting transfers between devices, exchange(): lax.all_to_all(value, 'lists', split_axis=0, concat_axis=0, tiled=True)  11.7 us
    pallas_call x1, Pallas kernels, shards(): pl.pallas_call(functools.partial(owner_kernel, n_lists, user_dev, digits,...  5.38 us
    pallas_call x1, Pallas kernels, shards(): pl.pallas_call(functools.partial(attend_kernel, n_users), out_shape=jax.S...  2.32 us
    pallas_call x1, Pallas kernels, shards(): pl.pallas_call(functools.partial(known_kernel, n_lists, items_loc, n_user...  1.68 us
    unnamed x18, local copies, waits for them, and re-layouts  1.64 us
    pallas_call x1, Pallas kernels, shards(): pl.pallas_call(items_kernel, out_shape=jax.ShapeDtypeStruct((items_loc, w...  1.55 us
    pallas_call x1, Pallas kernels, shards(): pl.pallas_call(functools.partial(pack_kernel, digits), out_shape=jax.Shap...  1.36 us
  transfers between devices with their start and end apart: 5, of which 4 were waited for; matrix products, arithmetic and copies ran while one was open for 1% of the time, Pallas kernels for 14%

profile of v11, /device:TPU:0, one launch (start us, length us, event | category | flops | bytes accessed | tf_op | source)
XLA Modules:
  0.0 53.6 jit_solution(597753081388714215)
XLA Ops:
  0.6 0.5 collective-permute-start.15
  1.1 1.4 %shard_map.104 = bf16[16,24,128]{2,1,0:T(8,128)(2,1)} custom-call(s32[1,512]{1,0:T(1,128)} %refs_2_.2, bf16[4,512]{1,0:T(4,128)(2,1)} %vectors_ref.1), custom_call_target="tpu_custom_call" | custom-call | tf_op jit(solution)/shard_map/pallas_call | solution.py:369
  2.5 7.9 %all-to-all-start = ((bf16[16,24,128]{2,1,0:T(8,128)(2,1)}), bf16[16,24,128]{2,1,0:T(8,128)(2,1)}, u32[]{:S(2)}, u32[]{:S(2)}) async-start(bf16[16,24,128]{2,1,0:T(8,128)(2,1)} %shard_map.104), calls=%async_computation | async-start | bytes 196608 | tf_op jit(solution)/shard_map/all_to_all | solution.py:329
  10.4 1.6 %shard_map.105.items_ref = bf16[2048,512]{1,0:T(8,128)(2,1)S(1)} custom-call(bf16[2048,512]{1,0:T(8,128)(2,1)} %bitcast.16), custom_call_target="tpu_custom_call" | custom-call | tf_op jit(solution)/shard_map/pallas_call | solution.py:379
  12.0 6.2 %all-to-all-done = bf16[16,24,128]{2,1,0:T(8,128)(2,1)} async-done(((bf16[16,24,128]{2,1,0:T(8,128)(2,1)}), bf16[16,24,128]{2,1,0:T(8,128)(2,1)}, u32[]{:S(2)}, u32[]{:S(2)}) %all-to-all-start) | async-done | bytes 98336 | tf_op jit(solution)/shard_map/all_to_all | solution.py:329
  18.2 0.0 collective-permute-done.15.refs_0_
  18.2 5.4 %shard_map.106 = bf16[16,56,512]{2,1,0:T(8,128)(2,1)} custom-call(s32[1]{0:T(128)} %bitcast.3.base_ref, s32[1]{0:T(128)} %bitcast.4.other_ref, bf16[384,128]{1,0:T(8,128)(2,1)} %bitcast.5.gathered_ref.refs_4_, bf16[2048,512]{1,0:T(8,128)(2,1)S(1)} %shard_map.105.items_ref, bf16[2048,512]{1,0:T(8,128)(2,1)} %collective-permute-done.15.refs_0_), custom_call_target="tpu_custom_call" | custom-call | tf_op jit(solution)/shard_map/pallas_call | solution.py:452
  23.6 0.0 copy-start
  23.6 0.0 copy-start.1
  23.6 0.0 copy-start.7
  23.6 0.0 copy-start.8
  23.6 3.8 %all-to-all-start.1 = ((bf16[16,56,512]{2,1,0:T(8,128)(2,1)}), bf16[16,56,512]{2,1,0:T(8,128)(2,1)S(1)}, u32[]{:S(2)}, u32[]{:S(2)}) async-start(bf16[16,56,512]{2,1,0:T(8,128)(2,1)} %shard_map.106), calls=%async_computation.1 | async-start | bytes 1835008 | tf_op jit(solution)/shard_map/all_to_all | solution.py:329
  27.4 0.0 copy-done.5
  27.4 0.1 collective-permute-start.16
  28.2 0.7 %collective-permute-done.16.refs_1_ = bf16[128,512]{1,0:T(8,128)(2,1)S(1)} collective-permute-done((bf16[128,512]{1,0:T(8,128)(2,1)S(1)}, bf16[128,512]{1,0:T(8,128)(2,1)S(1)}, u32[]{:S(2)}, u32[]{:S(2)}) %collective-permute-start.16) | collective-permute-done | bytes 131104 | tf_op jit(solution)/shard_map/ppermute | solution.py:437
  28.8 0.0 copy-done
  28.8 0.0 copy-done.1
  28.9 0.9 %copy-done.6 = bf16[1,128,512]{2,1,0:T(8,128)(2,1)S(1)} copy-done((bf16[1,128,512]{2,1,0:T(8,128)(2,1)S(1)}, bf16[1,128,512]{2,1,0:T(8,128)(2,1)}, u32[]{:S(2)}) %copy-start.6) | copy-done | bytes 131096
  29.8 0.6 %shard_map.109 = (bf16[8,256,80]{2,1,0:T(8,128)(2,1)S(1)}, bf16[512,256]{1,0:T(8,128)(2,1)S(1)}, bf16[512,512]{1,0:T(8,128)(2,1)S(1)}) custom-call(s32[1]{0:T(128)} %bitcast.2.refs_1_.col_ref, s32[1]{0:T(128)S(6)} %copy.28.length_ref, bf16[128,512]{1,0:T(8,128)(2,1)S(1)} %bitcast.14, bf16[128,512]{1,0:T(8,128)(2,1)S(1)} %collective-permute-done.16.refs_1_, ...), custom_call_target="tpu_custom_call" | custom-call | tf_op jit(solution)/shard_map/pallas_call | solution.py:439
  30.4 0.0 copy-start.3
  30.4 0.7 %copy-done.3 = bf16[512,256]{1,0:T(8,128)(2,1)} copy-done((bf16[512,256]{1,0:T(8,128)(2,1)}, bf16[512,256]{1,0:T(8,128)(2,1)S(1)}, u32[]{:S(2)}) %copy-start.3) | copy-done | bytes 262168
  31.1 0.0 copy-done.7
  31.1 1.7 %shard_map.107 = (f32[8,512]{1,0:T(8,128)S(1)}, s32[1]{0:T(128)}) custom-call(s32[1]{0:T(128)} %bitcast.7.refs_0_, s32[1]{0:T(128)} %bitcast.2.refs_1_.col_ref, s32[1,512]{1,0:T(1,128)S(1)} %copy-done.7, s32[4,32]{1,0:T(4,128)S(1)} %copy-done.8, bf16[384,128]{1,0:T(8,128)(2,1)} %bitcast.5.gathered_ref.refs_4_), custom_call_target="tpu_custom_call" | custom-call | tf_op jit(solution)/shard_map/pallas_call | solution.py:393
  33.4 0.7 %conditional.1 = (bf16[128,512]{1,0:T(8,128)(2,1)}) conditional(s32[]{:T(128)} %bitcast.8, () %tuple.17, (s32[1]{0:T(128)}, bf16[384,128]{1,0:T(8,128)(2,1)}, bf16[2048,512]{1,0:T(8,128)(2,1)}, s32[]{:T(128)}) %tuple.38), branch_computations={%region_0.0_spmd, %region_1.0_spmd} | conditional | flops 1088 | bytes 1266468 | solution.py:423
  33.4 0.7 %broadcast.27 = bf16[128,512]{1,0:T(8,128)(2,1)} broadcast(bf16[]{:T(256)} %constant.7.clone), dimensions={} | broadcast | bytes 131074 | tf_op jit(solution)/shard_map/broadcast.1
  34.1 1.0 %shard_map.108.refs_0_ = bf16[128,512]{1,0:T(8,128)(2,1)S(1)} custom-call(bf16[128,512]{1,0:T(8,128)(2,1)} %get-tuple-element.63.came_ref), custom_call_target="tpu_custom_call" | custom-call | tf_op jit(solution)/shard_map/pallas_call | solution.py:425
  35.1 13.8 %all-to-all-done.1.fetched_ref = bf16[16,56,512]{2,1,0:T(8,128)(2,1)S(1)} async-done(((bf16[16,56,512]{2,1,0:T(8,128)(2,1)}), bf16[16,56,512]{2,1,0:T(8,128)(2,1)S(1)}, u32[]{:S(2)}, u32[]{:S(2)}) %all-to-all-start.1) | async-done | bytes 917536 | tf_op jit(solution)/shard_map/all_to_all | solution.py:329
  48.9 0.8 %shard_map.111 = bf16[256,512]{1,0:T(8,128)(2,1)S(1)} custom-call(s32[1]{0:T(128)} %bitcast.2.refs_1_.col_ref, f32[8,512]{1,0:T(8,128)S(1)} %get-tuple-element.39.known_ref, bf16[16,56,512]{2,1,0:T(8,128)(2,1)S(1)} %all-to-all-done.1.fetched_ref, bf16[128,512]{1,0:T(8,128)(2,1)S(1)} %shard_map.108.refs_0_), custom_call_target="tpu_custom_call" | custom-call | tf_op jit(solution)/shard_map/pallas_call | solution.py:472
  49.7 0.1 collective-permute-start.17
  49.8 1.2 %shard_map.110 = (bf16[128,2048]{1,0:T(8,128)(2,1)}, bf16[256,512]{1,0:T(8,128)(2,1)S(1)}) custom-call(s32[1]{0:T(128)} %bitcast.2.refs_1_.col_ref, f32[8,512]{1,0:T(8,128)S(1)} %get-tuple-element.39.known_ref, bf16[16,56,512]{2,1,0:T(8,128)(2,1)S(1)} %all-to-all-done.1.fetched_ref, bf16[128,512]{1,0:T(8,128)(2,1)S(1)} %shard_map.108.refs_0_), custom_call_target="tpu_custom_call" | custom-call | tf_op jit(solution)/shard_map/pallas_call | solution.py:486
  51.0 0.3 collective-permute-done.17.refs_1_
  51.3 2.3 %shard_map.112 = bf16[256,512]{1,0:T(8,128)(2,1)} custom-call(bf16[256,512]{1,0:T(8,128)(2,1)S(1)} %get-tuple-element.43.refs_0_, bf16[256,512]{1,0:T(8,128)(2,1)S(1)} %collective-permute-done.17.refs_1_, bf16[8,256,80]{2,1,0:T(8,128)(2,1)S(1)} %get-tuple-element.44.refs_2_, bf16[512,256]{1,0:T(8,128)(2,1)S(1)} %copy-done.4, ...), custom_call_target="tpu_custom_call" | custom-call | tf_op jit(solution)/shard_map/pallas_call | solution.py:501
  (7 shorter events, 0.0 us)
Async XLA Ops:
  0.6 17.6 %collective-permute-start.15 = (bf16[2048,512]{1,0:T(8,128)(2,1)}, bf16[2048,512]{1,0:T(8,128)(2,1)}, u32[]{:S(2)}, u32[]{:S(2)}) collective-permute-start(bf16[2048,512]{1,0:T(8,128)(2,1)} %bitcast.15), channel_id=1, source_target_pairs={{0,1},{1,0},{2,3},{3,2},{4,5},{5,4},{6,7},{7,6},{8,9},{9,8},{10,11... | collective-permute-start | bytes 6291464 | tf_op jit(solution)/shard_map/ppermute | solution.py:391
  2.5 15.7 %all-to-all-start = ((bf16[16,24,128]{2,1,0:T(8,128)(2,1)}), bf16[16,24,128]{2,1,0:T(8,128)(2,1)}, u32[]{:S(2)}, u32[]{:S(2)}) async-start(bf16[16,24,128]{2,1,0:T(8,128)(2,1)} %shard_map.104), calls=%async_computation | async-start | bytes 196608 | tf_op jit(solution)/shard_map/all_to_all | solution.py:329
  18.2 9.2 %copy-start.5 = (bf16[1,128,512]{2,1,0:T(8,128)(2,1)S(1)}, bf16[1,128,512]{2,1,0:T(8,128)(2,1)}, u32[]{:S(2)}) copy-start(bf16[1,128,512]{2,1,0:T(8,128)(2,1)} %param.15) | copy-start | bytes 393220
  23.6 5.3 %copy-start = (bf16[512,1024]{1,0:T(8,128)(2,1)S(1)}, bf16[512,1024]{1,0:T(8,128)(2,1)}, u32[]{:S(2)}) copy-start(bf16[512,1024]{1,0:T(8,128)(2,1)} %refs_2_.3) | copy-start | bytes 3145732
  23.6 5.2 %copy-start.1 = (bf16[512,512]{1,0:T(8,128)(2,1)S(1)}, bf16[512,512]{1,0:T(8,128)(2,1)}, u32[]{:S(2)}) copy-start(bf16[512,512]{1,0:T(8,128)(2,1)} %refs_3_.3) | copy-start | bytes 1572868
  23.6 7.4 %copy-start.7 = (s32[1,512]{1,0:T(1,128)S(1)}, s32[1,512]{1,0:T(1,128)}, u32[]{:S(2)}) copy-start(s32[1,512]{1,0:T(1,128)} %refs_2_.2) | copy-start | bytes 6148
  23.6 7.4 %copy-start.8 = (s32[4,32]{1,0:T(4,128)S(1)}, s32[4,32]{1,0:T(4,128)}, u32[]{:S(2)}) copy-start(s32[4,32]{1,0:T(4,128)} %refs_3_.2) | copy-start | bytes 1540
  23.6 25.3 %all-to-all-start.1 = ((bf16[16,56,512]{2,1,0:T(8,128)(2,1)}), bf16[16,56,512]{2,1,0:T(8,128)(2,1)S(1)}, u32[]{:S(2)}, u32[]{:S(2)}) async-start(bf16[16,56,512]{2,1,0:T(8,128)(2,1)} %shard_map.106), calls=%async_computation.1 | async-start | bytes 1835008 | tf_op jit(solution)/shard_map/all_to_all | solution.py:329
  27.4 1.4 %collective-permute-start.16 = (bf16[128,512]{1,0:T(8,128)(2,1)S(1)}, bf16[128,512]{1,0:T(8,128)(2,1)S(1)}, u32[]{:S(2)}, u32[]{:S(2)}) collective-permute-start(bf16[128,512]{1,0:T(8,128)(2,1)S(1)} %bitcast.13), channel_id=1, source_target_pairs={{0,1},{1,0},{2,3},{3,2},{4,5},{5,4},{6,7},{7,6},{8,9},{9,8},{10,11... | collective-permute-start | bytes 393224 | tf_op jit(solution)/shard_map/ppermute | solution.py:437
  28.9 0.9 %copy-start.6 = (bf16[1,128,512]{2,1,0:T(8,128)(2,1)S(1)}, bf16[1,128,512]{2,1,0:T(8,128)(2,1)}, u32[]{:S(2)}) copy-start(bf16[1,128,512]{2,1,0:T(8,128)(2,1)} %param.15) | copy-start | bytes 393220
  30.4 0.7 %copy-start.3 = (bf16[512,256]{1,0:T(8,128)(2,1)}, bf16[512,256]{1,0:T(8,128)(2,1)S(1)}, u32[]{:S(2)}) copy-start(bf16[512,256]{1,0:T(8,128)(2,1)S(1)} %get-tuple-element.45.refs_3_) | copy-start | bytes 786436
  34.1 17.2 %copy-start.2 = (bf16[512,512]{1,0:T(8,128)(2,1)S(1)}, bf16[512,512]{1,0:T(8,128)(2,1)}, u32[]{:S(2)}) copy-start(bf16[512,512]{1,0:T(8,128)(2,1)} %refs_5_.1) | copy-start | bytes 1572868
  34.1 17.2 %copy-start.4 = (bf16[512,256]{1,0:T(8,128)(2,1)S(1)}, bf16[512,256]{1,0:T(8,128)(2,1)}, u32[]{:S(2)}) copy-start(bf16[512,256]{1,0:T(8,128)(2,1)} %copy-done.3) | copy-start | bytes 786436
  49.7 1.6 %collective-permute-start.17 = (bf16[256,512]{1,0:T(8,128)(2,1)S(1)}, bf16[256,512]{1,0:T(8,128)(2,1)S(1)}, u32[]{:S(2)}, u32[]{:S(2)}) collective-permute-start(bf16[256,512]{1,0:T(8,128)(2,1)S(1)} %shard_map.111), channel_id=1, source_target_pairs={{0,1},{1,0},{2,3},{3,2},{4,5},{5,4},{6,7},{7,6},{8,9},{9,8},{10,11... | collective-permute-start | bytes 786440 | tf_op jit(solution)/shard_map/ppermute | solution.py:483

commit v12 on v11

--- a/solution.py
+++ b/solution.py
@@ -91,13 +91,18 @@
     return index, before
 
 
-def items_kernel(items_hbm, items_ref, sems):
-    part = items_ref.shape[0] // sems.shape[0]
+def items_kernel(*refs):
+    count = len(refs) // 2
+    sems = refs[-1]
+    parts = sems.shape[1]
     loads = []
-    for p in range(sems.shape[0]):
-        span = pl.ds(p * part, part)
-        loads.append(pltpu.make_async_copy(items_hbm.at[span], items_ref.at[span], sems.at[p]))
-        loads[-1].start()
+    for k in range(count):
+        source, target = refs[k], refs[count + k]
+        part = source.shape[0] // parts
+        for p in range(parts):
+            span = pl.ds(p * part, part)
+            loads.append(pltpu.make_async_copy(source.at[span], target.at[span], sems.at[k, p]))
+            loads[-1].start()
     for load in loads:
         load.wait()
 
@@ -376,19 +381,18 @@
     gathered = exchange(pack)
     gathered = gathered.reshape(n_lists * pack_rows, LANES)
 
-    items = pl.pallas_call(
+    halves = [flat_items]
+    if spare:
+        halves.append(lax.ppermute(flat_items, "users", [(0, 1), (1, 0)]))
+    items, *siblings = pl.pallas_call(
         items_kernel,
-        out_shape=jax.ShapeDtypeStruct((items_loc, width), bf16),
-        in_specs=[HBM],
-        out_specs=VMEM,
-        scratch_shapes=[pltpu.SemaphoreType.DMA((4,))],
+        out_shape=tuple(jax.ShapeDtypeStruct((items_loc, width), bf16) for _ in halves),
+        in_specs=[HBM] * len(halves),
+        out_specs=tuple(VMEM for _ in halves),
+        scratch_shapes=[pltpu.SemaphoreType.DMA((len(halves), 4))],
         compiler_params=PARAMS,
-    )(flat_items)
-    gathered, items = lax.optimization_barrier((gathered, items))
-
-    siblings = []
-    if spare:
-        siblings.append(lax.ppermute(flat_items, "users", [(0, 1), (1, 0)]))
+    )(*halves)
+    gathered, items, siblings = lax.optimization_barrier((gathered, items, siblings))
 
     known, many = pl.pallas_call(
         functools.partial(known_kernel, n_lists, items_loc, n_users, user_dev, digits, main, spare, kept),

time: 54.1 us -> 54.9 us (1.015)
  local copies, waits for them, and re-layouts: 2.31 us -> 5.25 us
  waiting for transfers between devices: 21 us -> 19 us
    unnamed x18 -> x22, local copies, waits for them, and re-layouts: 1.64 us -> 4.59 us
    all_to_all x2, waiting for transfers between devices: 20 us -> 18 us  [exchange(): lax.all_to_all(value, 'lists', split_axis=0, concat_axis=0, tiled=True)]
    pallas_call x1, Pallas kernels: 5.38 us -> 4.63 us  [shards(): pl.pallas_call(functools.partial(owner_kernel, n_lists, user_dev, digits,...]
    pallas_call x1, Pallas kernels: 1.55 us -> 2.22 us  [shards(): pl.pallas_call(items_kernel, out_shape=tuple((jax.ShapeDtypeStruct((items...]
  transfers between devices with their start and end apart: 5 -> 5, of which waited for: 4 -> 4; matrix products, arithmetic and copies ran while one was open for 1% -> 1% of each run, Pallas kernels for 14% -> 15%
where the time goes in v12:
time: 54.9 us; the launch traced here: 54.5 us
  waiting for transfers between devices  19 us (35%)
  Pallas kernels  15.8 us (29%)
  starting transfers between devices  12.4 us (23%)
  local copies, waits for them, and re-layouts  5.25 us (10%)
  between operations  2.09 us (4%)
    all_to_all x2, waiting for transfers between devices, exchange(): lax.all_to_all(value, 'lists', split_axis=0, concat_axis=0, tiled=True)  18 us
    all_to_all x2, starting transfers between devices, exchange(): lax.all_to_all(value, 'lists', split_axis=0, concat_axis=0, tiled=True)  11.7 us
    pallas_call x1, Pallas kernels, shards(): pl.pallas_call(functools.partial(owner_kernel, n_lists, user_dev, digits,...  4.63 us
    unnamed x22, local copies, waits for them, and re-layouts  4.59 us
    pallas_call x1, Pallas kernels, shards(): pl.pallas_call(functools.partial(attend_kernel, n_users), out_shape=jax.S...  2.32 us
    pallas_call x1, Pallas kernels, shards(): pl.pallas_call(items_kernel, out_shape=tuple((jax.ShapeDtypeStruct((items...  2.22 us
    pallas_call x1, Pallas kernels, shards(): pl.pallas_call(functools.partial(known_kernel, n_lists, items_loc, n_user...  1.68 us
    pallas_call x1, Pallas kernels, shards(): pl.pallas_call(functools.partial(pack_kernel, digits), out_shape=jax.Shap...  1.36 us
  transfers between devices with their start and end apart: 5, of which 4 were waited for; matrix products, arithmetic and copies ran while one was open for 1% of the time, Pallas kernels for 15%

profile of v12, /device:TPU:0, one launch (start us, length us, event | category | flops | bytes accessed | tf_op | source)
XLA Modules:
  0.0 54.5 jit_solution(4896341910075279878)
XLA Ops:
  0.6 0.5 collective-permute-start.15
  1.1 1.4 %shard_map.104 = bf16[16,24,128]{2,1,0:T(8,128)(2,1)} custom-call(s32[1,512]{1,0:T(1,128)} %refs_2_.2, bf16[4,512]{1,0:T(4,128)(2,1)} %vectors_ref.1), custom_call_target="tpu_custom_call" | custom-call | tf_op jit(solution)/shard_map/pallas_call | solution.py:374
  2.5 7.9 %all-to-all-start = ((bf16[16,24,128]{2,1,0:T(8,128)(2,1)}), bf16[16,24,128]{2,1,0:T(8,128)(2,1)}, u32[]{:S(2)}, u32[]{:S(2)}) async-start(bf16[16,24,128]{2,1,0:T(8,128)(2,1)} %shard_map.104), calls=%async_computation | async-start | bytes 196608 | tf_op jit(solution)/shard_map/all_to_all | solution.py:334
  10.4 0.0 collective-permute-done.15.refs_1_
  10.5 2.2 %shard_map.105 = (bf16[2048,512]{1,0:T(8,128)(2,1)S(1)}, bf16[2048,512]{1,0:T(8,128)(2,1)S(1)}) custom-call(bf16[2048,512]{1,0:T(8,128)(2,1)} %bitcast.16, bf16[2048,512]{1,0:T(8,128)(2,1)} %collective-permute-done.15.refs_1_), custom_call_target="tpu_custom_call" | custom-call | tf_op jit(solution)/shard_map/pallas_call | solution.py:387
  12.7 1.4 %copy-done = bf16[2048,512]{1,0:T(8,128)(2,1)} copy-done((bf16[2048,512]{1,0:T(8,128)(2,1)}, bf16[2048,512]{1,0:T(8,128)(2,1)S(1)}, u32[]{:S(2)}) %copy-start) | copy-done | bytes 2097176
  14.1 4.1 %all-to-all-done = bf16[16,24,128]{2,1,0:T(8,128)(2,1)} async-done(((bf16[16,24,128]{2,1,0:T(8,128)(2,1)}), bf16[16,24,128]{2,1,0:T(8,128)(2,1)}, u32[]{:S(2)}, u32[]{:S(2)}) %all-to-all-start) | async-done | bytes 98336 | tf_op jit(solution)/shard_map/all_to_all | solution.py:334
  18.2 1.6 %copy-done.1 = bf16[2048,512]{1,0:T(8,128)(2,1)S(1)} copy-done((bf16[2048,512]{1,0:T(8,128)(2,1)S(1)}, bf16[2048,512]{1,0:T(8,128)(2,1)}, u32[]{:S(2)}) %copy-start.1) | copy-done | bytes 2097176
  19.8 4.6 %shard_map.106 = bf16[16,56,512]{2,1,0:T(8,128)(2,1)} custom-call(s32[1]{0:T(128)} %bitcast.3.base_ref, s32[1]{0:T(128)} %bitcast.4.other_ref, bf16[384,128]{1,0:T(8,128)(2,1)} %bitcast.5.gathered_ref.refs_4_, bf16[2048,512]{1,0:T(8,128)(2,1)S(1)} %get-tuple-element.38.items_ref, bf16[2048,512]{1,0:T(8,128)(2,1)S(1)} %copy-done.1), custom_call_target="tpu_custom_call" | custom-call | tf_op jit(solution)/shard_map/pallas_call | solution.py:456
  24.4 0.0 copy-start.2
  24.4 0.0 copy-start.3
  24.5 0.0 copy-start.9
  24.5 0.0 copy-start.10
  24.5 3.8 %all-to-all-start.1 = ((bf16[16,56,512]{2,1,0:T(8,128)(2,1)}), bf16[16,56,512]{2,1,0:T(8,128)(2,1)S(1)}, u32[]{:S(2)}, u32[]{:S(2)}) async-start(bf16[16,56,512]{2,1,0:T(8,128)(2,1)} %shard_map.106), calls=%async_computation.1 | async-start | bytes 1835008 | tf_op jit(solution)/shard_map/all_to_all | solution.py:334
  28.3 0.1 collective-permute-start.16
  29.0 0.7 %collective-permute-done.16.refs_1_ = bf16[128,512]{1,0:T(8,128)(2,1)S(1)} collective-permute-done((bf16[128,512]{1,0:T(8,128)(2,1)S(1)}, bf16[128,512]{1,0:T(8,128)(2,1)S(1)}, u32[]{:S(2)}, u32[]{:S(2)}) %collective-permute-start.16) | collective-permute-done | bytes 131104 | tf_op jit(solution)/shard_map/ppermute | solution.py:441
  29.7 0.9 %copy-done.8 = bf16[1,128,512]{2,1,0:T(8,128)(2,1)S(1)} copy-done((bf16[1,128,512]{2,1,0:T(8,128)(2,1)S(1)}, bf16[1,128,512]{2,1,0:T(8,128)(2,1)}, u32[]{:S(2)}) %copy-start.8) | copy-done | bytes 131096
  30.6 0.6 %shard_map.109 = (bf16[8,256,80]{2,1,0:T(8,128)(2,1)S(1)}, bf16[512,256]{1,0:T(8,128)(2,1)S(1)}, bf16[512,512]{1,0:T(8,128)(2,1)S(1)}) custom-call(s32[1]{0:T(128)} %bitcast.2.refs_1_.col_ref, s32[1]{0:T(128)S(6)} %copy.28.length_ref, bf16[128,512]{1,0:T(8,128)(2,1)S(1)} %bitcast.14, bf16[128,512]{1,0:T(8,128)(2,1)S(1)} %collective-permute-done.16.refs_1_, ...), custom_call_target="tpu_custom_call" | custom-call | tf_op jit(solution)/shard_map/pallas_call | solution.py:443
  31.2 0.0 copy-start.5
  31.2 0.7 %copy-done.5 = bf16[512,256]{1,0:T(8,128)(2,1)} copy-done((bf16[512,256]{1,0:T(8,128)(2,1)}, bf16[512,256]{1,0:T(8,128)(2,1)S(1)}, u32[]{:S(2)}) %copy-start.5) | copy-done | bytes 262168
  31.9 0.0 copy-done.9
  31.9 1.7 %shard_map.107 = (f32[8,512]{1,0:T(8,128)S(1)}, s32[1]{0:T(128)}) custom-call(s32[1]{0:T(128)} %bitcast.7.refs_0_, s32[1]{0:T(128)} %bitcast.2.refs_1_.col_ref, s32[1,512]{1,0:T(1,128)S(1)} %copy-done.9, s32[4,32]{1,0:T(4,128)S(1)} %copy-done.10, bf16[384,128]{1,0:T(8,128)(2,1)} %bitcast.5.gathered_ref.refs_4_), custom_call_target="tpu_custom_call" | custom-call | tf_op jit(solution)/shard_map/pallas_call | solution.py:397
  34.2 0.7 %conditional.1 = (bf16[128,512]{1,0:T(8,128)(2,1)}) conditional(s32[]{:T(128)} %bitcast.8, () %tuple.17, (s32[1]{0:T(128)}, bf16[384,128]{1,0:T(8,128)(2,1)}, bf16[2048,512]{1,0:T(8,128)(2,1)}, s32[]{:T(128)}) %tuple.38), branch_computations={%region_0.0_spmd, %region_1.0_spmd} | conditional | flops 1088 | bytes 1266468 | solution.py:427
  34.2 0.7 %broadcast.27 = bf16[128,512]{1,0:T(8,128)(2,1)} broadcast(bf16[]{:T(256)} %constant.7.clone), dimensions={} | broadcast | bytes 131074 | tf_op jit(solution)/shard_map/broadcast.1
  34.9 1.0 %shard_map.108.refs_0_ = bf16[128,512]{1,0:T(8,128)(2,1)S(1)} custom-call(bf16[128,512]{1,0:T(8,128)(2,1)} %get-tuple-element.69.came_ref), custom_call_target="tpu_custom_call" | custom-call | tf_op jit(solution)/shard_map/pallas_call | solution.py:429
  35.9 13.8 %all-to-all-done.1.fetched_ref = bf16[16,56,512]{2,1,0:T(8,128)(2,1)S(1)} async-done(((bf16[16,56,512]{2,1,0:T(8,128)(2,1)}), bf16[16,56,512]{2,1,0:T(8,128)(2,1)S(1)}, u32[]{:S(2)}, u32[]{:S(2)}) %all-to-all-start.1) | async-done | bytes 917536 | tf_op jit(solution)/shard_map/all_to_all | solution.py:334
  49.7 0.8 %shard_map.111 = bf16[256,512]{1,0:T(8,128)(2,1)S(1)} custom-call(s32[1]{0:T(128)} %bitcast.2.refs_1_.col_ref, f32[8,512]{1,0:T(8,128)S(1)} %get-tuple-element.45.known_ref, bf16[16,56,512]{2,1,0:T(8,128)(2,1)S(1)} %all-to-all-done.1.fetched_ref, bf16[128,512]{1,0:T(8,128)(2,1)S(1)} %shard_map.108.refs_0_), custom_call_target="tpu_custom_call" | custom-call | tf_op jit(solution)/shard_map/pallas_call | solution.py:476
  50.5 0.1 collective-permute-start.17
  50.6 1.2 %shard_map.110 = (bf16[128,2048]{1,0:T(8,128)(2,1)}, bf16[256,512]{1,0:T(8,128)(2,1)S(1)}) custom-call(s32[1]{0:T(128)} %bitcast.2.refs_1_.col_ref, f32[8,512]{1,0:T(8,128)S(1)} %get-tuple-element.45.known_ref, bf16[16,56,512]{2,1,0:T(8,128)(2,1)S(1)} %all-to-all-done.1.fetched_ref, bf16[128,512]{1,0:T(8,128)(2,1)S(1)} %shard_map.108.refs_0_), custom_call_target="tpu_custom_call" | custom-call | tf_op jit(solution)/shard_map/pallas_call | solution.py:490
  51.8 0.3 collective-permute-done.17.refs_1_
  52.2 0.0 copy-done.4
  52.2 2.3 %shard_map.112 = bf16[256,512]{1,0:T(8,128)(2,1)} custom-call(bf16[256,512]{1,0:T(8,128)(2,1)S(1)} %get-tuple-element.49.refs_0_, bf16[256,512]{1,0:T(8,128)(2,1)S(1)} %collective-permute-done.17.refs_1_, bf16[8,256,80]{2,1,0:T(8,128)(2,1)S(1)} %get-tuple-element.50.refs_2_, bf16[512,256]{1,0:T(8,128)(2,1)S(1)} %copy-done.6, ...), custom_call_target="tpu_custom_call" | custom-call | tf_op jit(solution)/shard_map/pallas_call | solution.py:505
  (11 shorter events, 0.0 us)
Async XLA Ops:
  0.6 9.8 %collective-permute-start.15 = (bf16[2048,512]{1,0:T(8,128)(2,1)}, bf16[2048,512]{1,0:T(8,128)(2,1)}, u32[]{:S(2)}, u32[]{:S(2)}) collective-permute-start(bf16[2048,512]{1,0:T(8,128)(2,1)} %bitcast.15), channel_id=1, source_target_pairs={{0,1},{1,0},{2,3},{3,2},{4,5},{5,4},{6,7},{7,6},{8,9},{9,8},{10,11... | collective-permute-start | bytes 6291464 | tf_op jit(solution)/shard_map/ppermute | solution.py:386
  2.5 15.7 %all-to-all-start = ((bf16[16,24,128]{2,1,0:T(8,128)(2,1)}), bf16[16,24,128]{2,1,0:T(8,128)(2,1)}, u32[]{:S(2)}, u32[]{:S(2)}) async-start(bf16[16,24,128]{2,1,0:T(8,128)(2,1)} %shard_map.104), calls=%async_computation | async-start | bytes 196608 | tf_op jit(solution)/shard_map/all_to_all | solution.py:334
  12.7 1.4 %copy-start = (bf16[2048,512]{1,0:T(8,128)(2,1)}, bf16[2048,512]{1,0:T(8,128)(2,1)S(1)}, u32[]{:S(2)}) copy-start(bf16[2048,512]{1,0:T(8,128)(2,1)S(1)} %get-tuple-element.39.refs_0_) | copy-start | bytes 6291460
  18.2 1.6 %copy-start.1 = (bf16[2048,512]{1,0:T(8,128)(2,1)S(1)}, bf16[2048,512]{1,0:T(8,128)(2,1)}, u32[]{:S(2)}) copy-start(bf16[2048,512]{1,0:T(8,128)(2,1)} %copy-done) | copy-start | bytes 6291460
  19.8 8.5 %copy-start.7 = (bf16[1,128,512]{2,1,0:T(8,128)(2,1)S(1)}, bf16[1,128,512]{2,1,0:T(8,128)(2,1)}, u32[]{:S(2)}) copy-start(bf16[1,128,512]{2,1,0:T(8,128)(2,1)} %param.15) | copy-start | bytes 393220
  24.4 5.3 %copy-start.2 = (bf16[512,1024]{1,0:T(8,128)(2,1)S(1)}, bf16[512,1024]{1,0:T(8,128)(2,1)}, u32[]{:S(2)}) copy-start(bf16[512,1024]{1,0:T(8,128)(2,1)} %refs_2_.3) | copy-start | bytes 3145732
  24.4 5.2 %copy-start.3 = (bf16[512,512]{1,0:T(8,128)(2,1)S(1)}, bf16[512,512]{1,0:T(8,128)(2,1)}, u32[]{:S(2)}) copy-start(bf16[512,512]{1,0:T(8,128)(2,1)} %refs_3_.3) | copy-start | bytes 1572868
  24.5 7.4 %copy-start.9 = (s32[1,512]{1,0:T(1,128)S(1)}, s32[1,512]{1,0:T(1,128)}, u32[]{:S(2)}) copy-start(s32[1,512]{1,0:T(1,128)} %refs_2_.2) | copy-start | bytes 6148
  24.5 7.4 %copy-start.10 = (s32[4,32]{1,0:T(4,128)S(1)}, s32[4,32]{1,0:T(4,128)}, u32[]{:S(2)}) copy-start(s32[4,32]{1,0:T(4,128)} %refs_3_.2) | copy-start | bytes 1540
  24.5 25.3 %all-to-all-start.1 = ((bf16[16,56,512]{2,1,0:T(8,128)(2,1)}), bf16[16,56,512]{2,1,0:T(8,128)(2,1)S(1)}, u32[]{:S(2)}, u32[]{:S(2)}) async-start(bf16[16,56,512]{2,1,0:T(8,128)(2,1)} %shard_map.106), calls=%async_computation.1 | async-start | bytes 1835008 | tf_op jit(solution)/shard_map/all_to_all | solution.py:334
  28.3 1.4 %collective-permute-start.16 = (bf16[128,512]{1,0:T(8,128)(2,1)S(1)}, bf16[128,512]{1,0:T(8,128)(2,1)S(1)}, u32[]{:S(2)}, u32[]{:S(2)}) collective-permute-start(bf16[128,512]{1,0:T(8,128)(2,1)S(1)} %bitcast.13), channel_id=1, source_target_pairs={{0,1},{1,0},{2,3},{3,2},{4,5},{5,4},{6,7},{7,6},{8,9},{9,8},{10,11... | collective-permute-start | bytes 393224 | tf_op jit(solution)/shard_map/ppermute | solution.py:441
  29.7 0.9 %copy-start.8 = (bf16[1,128,512]{2,1,0:T(8,128)(2,1)S(1)}, bf16[1,128,512]{2,1,0:T(8,128)(2,1)}, u32[]{:S(2)}) copy-start(bf16[1,128,512]{2,1,0:T(8,128)(2,1)} %param.15) | copy-start | bytes 393220
  31.2 0.7 %copy-start.5 = (bf16[512,256]{1,0:T(8,128)(2,1)}, bf16[512,256]{1,0:T(8,128)(2,1)S(1)}, u32[]{:S(2)}) copy-start(bf16[512,256]{1,0:T(8,128)(2,1)S(1)} %get-tuple-element.51.refs_3_) | copy-start | bytes 786436
  34.9 17.2 %copy-start.4 = (bf16[512,512]{1,0:T(8,128)(2,1)S(1)}, bf16[512,512]{1,0:T(8,128)(2,1)}, u32[]{:S(2)}) copy-start(bf16[512,512]{1,0:T(8,128)(2,1)} %refs_5_.1) | copy-start | bytes 1572868
  34.9 17.2 %copy-start.6 = (bf16[512,256]{1,0:T(8,128)(2,1)S(1)}, bf16[512,256]{1,0:T(8,128)(2,1)}, u32[]{:S(2)}) copy-start(bf16[512,256]{1,0:T(8,128)(2,1)} %copy-done.5) | copy-start | bytes 786436
  50.5 1.6 %collective-permute-start.17 = (bf16[256,512]{1,0:T(8,128)(2,1)S(1)}, bf16[256,512]{1,0:T(8,128)(2,1)S(1)}, u32[]{:S(2)}, u32[]{:S(2)}) collective-permute-start(bf16[256,512]{1,0:T(8,128)(2,1)S(1)} %shard_map.111), channel_id=1, source_target_pairs={{0,1},{1,0},{2,3},{3,2},{4,5},{5,4},{6,7},{7,6},{8,9},{9,8},{10,11... | collective-permute-start | bytes 786440 | tf_op jit(solution)/shard_map/ppermute | solution.py:487

commit v13 on v11

--- a/solution.py
+++ b/solution.py
@@ -173,8 +173,16 @@
 def owner_kernel(
     n_lists, user_dev, digits, main, spare, scale, base_ref, other_ref, gathered_ref, items_ref, *refs
 ):
-    sibling_ref = refs[0] if spare else None
-    out_hbm, wide, out_ref, out_sems = refs[-4:]
+    loads = []
+    if spare:
+        sibling_hbm, out_hbm, wide, out_ref, out_sems, sibling_ref, in_sems = refs
+        part = sibling_ref.shape[0] // in_sems.shape[0]
+        for p in range(in_sems.shape[0]):
+            span = pl.ds(p * part, part)
+            loads.append(pltpu.make_async_copy(sibling_hbm.at[span], sibling_ref.at[span], in_sems.at[p]))
+            loads[-1].start()
+    else:
+        out_hbm, wide, out_ref, out_sems = refs
     items_loc, width = items_ref.shape
     wide[...] = gathered_ref[...].astype(jnp.float32)
     vectors, ids = unpack(wide, n_lists, user_dev, digits, width // LANES)
@@ -200,9 +208,6 @@
     if spare:
         over, _ = asked(ids, other_ref[0].astype(jnp.float32), items_loc, main, spare)
         over = [jnp.where(own[r : r + 1] > float(main - spare), -1, over[r]) for r in range(n_lists)]
-        shared = jnp.dot(
-            picks(jnp.concatenate(over, axis=0), items_loc), sibling_ref[...], preferred_element_type=jnp.float32
-        )
     step = max(1, 288 // main)
     sends = []
     for number, first in enumerate(range(0, n_lists, step)):
@@ -212,6 +217,14 @@
             items_ref[...],
             preferred_element_type=jnp.float32,
         )
+        if spare and first == 0:
+            for load in loads:
+                load.wait()
+            shared = jnp.dot(
+                picks(jnp.concatenate(over, axis=0), items_loc),
+                sibling_ref[...],
+                preferred_element_type=jnp.float32,
+            )
         for r in range(first, last):
             mine = rows[(r - first) * main : (r - first + 1) * main]
             out_ref[r, kept : kept + main - spare, :] = mine[: main - spare].astype(jnp.bfloat16)
@@ -452,13 +465,14 @@
     answers = pl.pallas_call(
         functools.partial(owner_kernel, n_lists, user_dev, digits, main, spare, width ** (-0.5)),
         out_shape=jax.ShapeDtypeStruct((n_lists, block, width), bf16),
-        in_specs=[SMEM, SMEM] + [VMEM] * (2 + len(siblings)),
+        in_specs=[SMEM, SMEM, VMEM, VMEM] + [pl.BlockSpec(memory_space=pl.ANY)] * len(siblings),
         out_specs=pl.BlockSpec(memory_space=pl.ANY),
         scratch_shapes=[
             pltpu.VMEM((n_lists * pack_rows, LANES), jnp.float32),
             pltpu.VMEM((n_lists, block, width), bf16),
             pltpu.SemaphoreType.DMA((-(-n_lists // step),)),
-        ],
+        ]
+        + [pltpu.VMEM((items_loc, width), bf16), pltpu.SemaphoreType.DMA((4,))] * len(siblings),
         compiler_params=PARAMS,
     )(base_arg, other_arg, gathered, items, *siblings)
     fetched = exchange(answers)

time: 54.1 us -> 53.4 us (0.987)
  Pallas kernels: 15.8 us -> 15.1 us
    pallas_call x1, Pallas kernels: 5.38 us -> 4.64 us  [shards(): pl.pallas_call(functools.partial(owner_kernel, n_lists, user_dev, digits,...]
where the time goes in v13:
time: 53.4 us; the launch traced here: 52.9 us
  waiting for transfers between devices  21 us (39%)
  Pallas kernels  15.1 us (28%)
  starting transfers between devices  12.4 us (23%)
  local copies, waits for them, and re-layouts  2.31 us (4%)
  between operations  2.08 us (4%)
    all_to_all x2, waiting for transfers between devices, exchange(): lax.all_to_all(value, 'lists', split_axis=0, concat_axis=0, tiled=True)  20 us
    all_to_all x2, starting transfers between devices, exchange(): lax.all_to_all(value, 'lists', split_axis=0, concat_axis=0, tiled=True)  11.7 us
    pallas_call x1, Pallas kernels, shards(): pl.pallas_call(functools.partial(owner_kernel, n_lists, user_dev, digits,...  4.64 us
    pallas_call x1, Pallas kernels, shards(): pl.pallas_call(functools.partial(attend_kernel, n_users), out_shape=jax.S...  2.32 us
    pallas_call x1, Pallas kernels, shards(): pl.pallas_call(functools.partial(known_kernel, n_lists, items_loc, n_user...  1.68 us
    unnamed x18, local copies, waits for them, and re-layouts  1.64 us
    pallas_call x1, Pallas kernels, shards(): pl.pallas_call(items_kernel, out_shape=jax.ShapeDtypeStruct((items_loc, w...  1.55 us
    pallas_call x1, Pallas kernels, shards(): pl.pallas_call(functools.partial(pack_kernel, digits), out_shape=jax.Shap...  1.36 us
  transfers between devices with their start and end apart: 5, of which 4 were waited for; matrix products, arithmetic and copies ran while one was open for 1% of the time, Pallas kernels for 14%

profile of v13, /device:TPU:0, one launch (start us, length us, event | category | flops | bytes accessed | tf_op | source)
XLA Modules:
  0.0 52.9 jit_solution(13929501227256347261)
XLA Ops:
  0.6 0.5 collective-permute-start.15
  1.1 1.4 %shard_map.104 = bf16[16,24,128]{2,1,0:T(8,128)(2,1)} custom-call(s32[1,512]{1,0:T(1,128)} %refs_2_.2, bf16[4,512]{1,0:T(4,128)(2,1)} %vectors_ref.1), custom_call_target="tpu_custom_call" | custom-call | tf_op jit(solution)/shard_map/pallas_call | solution.py:382
  2.5 7.9 %all-to-all-start = ((bf16[16,24,128]{2,1,0:T(8,128)(2,1)}), bf16[16,24,128]{2,1,0:T(8,128)(2,1)}, u32[]{:S(2)}, u32[]{:S(2)}) async-start(bf16[16,24,128]{2,1,0:T(8,128)(2,1)} %shard_map.104), calls=%async_computation | async-start | bytes 196608 | tf_op jit(solution)/shard_map/all_to_all | solution.py:342
  10.4 1.6 %shard_map.105.items_ref = bf16[2048,512]{1,0:T(8,128)(2,1)S(1)} custom-call(bf16[2048,512]{1,0:T(8,128)(2,1)} %bitcast.16), custom_call_target="tpu_custom_call" | custom-call | tf_op jit(solution)/shard_map/pallas_call | solution.py:392
  12.0 6.2 %all-to-all-done = bf16[16,24,128]{2,1,0:T(8,128)(2,1)} async-done(((bf16[16,24,128]{2,1,0:T(8,128)(2,1)}), bf16[16,24,128]{2,1,0:T(8,128)(2,1)}, u32[]{:S(2)}, u32[]{:S(2)}) %all-to-all-start) | async-done | bytes 98336 | tf_op jit(solution)/shard_map/all_to_all | solution.py:342
  18.2 0.0 collective-permute-done.15.refs_0_
  18.2 4.6 %shard_map.106 = bf16[16,56,512]{2,1,0:T(8,128)(2,1)} custom-call(s32[1]{0:T(128)} %bitcast.3.base_ref, s32[1]{0:T(128)} %bitcast.4.other_ref, bf16[384,128]{1,0:T(8,128)(2,1)} %bitcast.5.gathered_ref.refs_4_, bf16[2048,512]{1,0:T(8,128)(2,1)S(1)} %shard_map.105.items_ref, bf16[2048,512]{1,0:T(8,128)(2,1)} %collective-permute-done.15.refs_0_), custom_call_target="tpu_custom_call" | custom-call | tf_op jit(solution)/shard_map/pallas_call | solution.py:465
  22.8 0.0 copy-start
  22.9 0.0 copy-start.1
  22.9 0.0 copy-start.7
  22.9 0.0 copy-start.8
  22.9 3.8 %all-to-all-start.1 = ((bf16[16,56,512]{2,1,0:T(8,128)(2,1)}), bf16[16,56,512]{2,1,0:T(8,128)(2,1)S(1)}, u32[]{:S(2)}, u32[]{:S(2)}) async-start(bf16[16,56,512]{2,1,0:T(8,128)(2,1)} %shard_map.106), calls=%async_computation.1 | async-start | bytes 1835008 | tf_op jit(solution)/shard_map/all_to_all | solution.py:342
  26.7 0.0 copy-done.5
  26.7 0.1 collective-permute-start.16
  27.4 0.7 %collective-permute-done.16.refs_1_ = bf16[128,512]{1,0:T(8,128)(2,1)S(1)} collective-permute-done((bf16[128,512]{1,0:T(8,128)(2,1)S(1)}, bf16[128,512]{1,0:T(8,128)(2,1)S(1)}, u32[]{:S(2)}, u32[]{:S(2)}) %collective-permute-start.16) | collective-permute-done | bytes 131104 | tf_op jit(solution)/shard_map/ppermute | solution.py:450
  28.1 0.0 copy-done
  28.1 0.0 copy-done.1
  28.1 0.9 %copy-done.6 = bf16[1,128,512]{2,1,0:T(8,128)(2,1)S(1)} copy-done((bf16[1,128,512]{2,1,0:T(8,128)(2,1)S(1)}, bf16[1,128,512]{2,1,0:T(8,128)(2,1)}, u32[]{:S(2)}) %copy-start.6) | copy-done | bytes 131096
  29.0 0.6 %shard_map.109 = (bf16[8,256,80]{2,1,0:T(8,128)(2,1)S(1)}, bf16[512,256]{1,0:T(8,128)(2,1)S(1)}, bf16[512,512]{1,0:T(8,128)(2,1)S(1)}) custom-call(s32[1]{0:T(128)} %bitcast.2.refs_1_.col_ref, s32[1]{0:T(128)S(6)} %copy.28.length_ref, bf16[128,512]{1,0:T(8,128)(2,1)S(1)} %bitcast.14, bf16[128,512]{1,0:T(8,128)(2,1)S(1)} %collective-permute-done.16.refs_1_, ...), custom_call_target="tpu_custom_call" | custom-call | tf_op jit(solution)/shard_map/pallas_call | solution.py:452
  29.6 0.0 copy-start.3
  29.6 0.7 %copy-done.3 = bf16[512,256]{1,0:T(8,128)(2,1)} copy-done((bf16[512,256]{1,0:T(8,128)(2,1)}, bf16[512,256]{1,0:T(8,128)(2,1)S(1)}, u32[]{:S(2)}) %copy-start.3) | copy-done | bytes 262168
  30.3 0.0 copy-done.7
  30.3 1.7 %shard_map.107 = (f32[8,512]{1,0:T(8,128)S(1)}, s32[1]{0:T(128)}) custom-call(s32[1]{0:T(128)} %bitcast.7.refs_0_, s32[1]{0:T(128)} %bitcast.2.refs_1_.col_ref, s32[1,512]{1,0:T(1,128)S(1)} %copy-done.7, s32[4,32]{1,0:T(4,128)S(1)} %copy-done.8, bf16[384,128]{1,0:T(8,128)(2,1)} %bitcast.5.gathered_ref.refs_4_), custom_call_target="tpu_custom_call" | custom-call | tf_op jit(solution)/shard_map/pallas_call | solution.py:406
  32.7 0.7 %conditional.1 = (bf16[128,512]{1,0:T(8,128)(2,1)}) conditional(s32[]{:T(128)} %bitcast.8, () %tuple.17, (s32[1]{0:T(128)}, bf16[384,128]{1,0:T(8,128)(2,1)}, bf16[2048,512]{1,0:T(8,128)(2,1)}, s32[]{:T(128)}) %tuple.38), branch_computations={%region_0.0_spmd, %region_1.0_spmd} | conditional | flops 1088 | bytes 1266468 | solution.py:436
  32.7 0.7 %broadcast.27 = bf16[128,512]{1,0:T(8,128)(2,1)} broadcast(bf16[]{:T(256)} %constant.7.clone), dimensions={} | broadcast | bytes 131074 | tf_op jit(solution)/shard_map/broadcast.1
  33.3 1.0 %shard_map.108.refs_0_ = bf16[128,512]{1,0:T(8,128)(2,1)S(1)} custom-call(bf16[128,512]{1,0:T(8,128)(2,1)} %get-tuple-element.63.came_ref), custom_call_target="tpu_custom_call" | custom-call | tf_op jit(solution)/shard_map/pallas_call | solution.py:438
  34.3 13.8 %all-to-all-done.1.fetched_ref = bf16[16,56,512]{2,1,0:T(8,128)(2,1)S(1)} async-done(((bf16[16,56,512]{2,1,0:T(8,128)(2,1)}), bf16[16,56,512]{2,1,0:T(8,128)(2,1)S(1)}, u32[]{:S(2)}, u32[]{:S(2)}) %all-to-all-start.1) | async-done | bytes 917536 | tf_op jit(solution)/shard_map/all_to_all | solution.py:342
  48.2 0.8 %shard_map.111 = bf16[256,512]{1,0:T(8,128)(2,1)S(1)} custom-call(s32[1]{0:T(128)} %bitcast.2.refs_1_.col_ref, f32[8,512]{1,0:T(8,128)S(1)} %get-tuple-element.39.known_ref, bf16[16,56,512]{2,1,0:T(8,128)(2,1)S(1)} %all-to-all-done.1.fetched_ref, bf16[128,512]{1,0:T(8,128)(2,1)S(1)} %shard_map.108.refs_0_), custom_call_target="tpu_custom_call" | custom-call | tf_op jit(solution)/shard_map/pallas_call | solution.py:486
  49.0 0.1 collective-permute-start.17
  49.1 1.2 %shard_map.110 = (bf16[128,2048]{1,0:T(8,128)(2,1)}, bf16[256,512]{1,0:T(8,128)(2,1)S(1)}) custom-call(s32[1]{0:T(128)} %bitcast.2.refs_1_.col_ref, f32[8,512]{1,0:T(8,128)S(1)} %get-tuple-element.39.known_ref, bf16[16,56,512]{2,1,0:T(8,128)(2,1)S(1)} %all-to-all-done.1.fetched_ref, bf16[128,512]{1,0:T(8,128)(2,1)S(1)} %shard_map.108.refs_0_), custom_call_target="tpu_custom_call" | custom-call | tf_op jit(solution)/shard_map/pallas_call | solution.py:500
  50.2 0.3 collective-permute-done.17.refs_1_
  50.6 2.3 %shard_map.112 = bf16[256,512]{1,0:T(8,128)(2,1)} custom-call(bf16[256,512]{1,0:T(8,128)(2,1)S(1)} %get-tuple-element.43.refs_0_, bf16[256,512]{1,0:T(8,128)(2,1)S(1)} %collective-permute-done.17.refs_1_, bf16[8,256,80]{2,1,0:T(8,128)(2,1)S(1)} %get-tuple-element.44.refs_2_, bf16[512,256]{1,0:T(8,128)(2,1)S(1)} %copy-done.4, ...), custom_call_target="tpu_custom_call" | custom-call | tf_op jit(solution)/shard_map/pallas_call | solution.py:515
  (7 shorter events, 0.0 us)
Async XLA Ops:
  0.6 17.6 %collective-permute-start.15 = (bf16[2048,512]{1,0:T(8,128)(2,1)}, bf16[2048,512]{1,0:T(8,128)(2,1)}, u32[]{:S(2)}, u32[]{:S(2)}) collective-permute-start(bf16[2048,512]{1,0:T(8,128)(2,1)} %bitcast.15), channel_id=1, source_target_pairs={{0,1},{1,0},{2,3},{3,2},{4,5},{5,4},{6,7},{7,6},{8,9},{9,8},{10,11... | collective-permute-start | bytes 6291464 | tf_op jit(solution)/shard_map/ppermute | solution.py:404
  2.5 15.7 %all-to-all-start = ((bf16[16,24,128]{2,1,0:T(8,128)(2,1)}), bf16[16,24,128]{2,1,0:T(8,128)(2,1)}, u32[]{:S(2)}, u32[]{:S(2)}) async-start(bf16[16,24,128]{2,1,0:T(8,128)(2,1)} %shard_map.104), calls=%async_computation | async-start | bytes 196608 | tf_op jit(solution)/shard_map/all_to_all | solution.py:342
  18.2 8.5 %copy-start.5 = (bf16[1,128,512]{2,1,0:T(8,128)(2,1)S(1)}, bf16[1,128,512]{2,1,0:T(8,128)(2,1)}, u32[]{:S(2)}) copy-start(bf16[1,128,512]{2,1,0:T(8,128)(2,1)} %param.15) | copy-start | bytes 393220
  22.8 5.3 %copy-start = (bf16[512,1024]{1,0:T(8,128)(2,1)S(1)}, bf16[512,1024]{1,0:T(8,128)(2,1)}, u32[]{:S(2)}) copy-start(bf16[512,1024]{1,0:T(8,128)(2,1)} %refs_2_.3) | copy-start | bytes 3145732
  22.9 5.2 %copy-start.1 = (bf16[512,512]{1,0:T(8,128)(2,1)S(1)}, bf16[512,512]{1,0:T(8,128)(2,1)}, u32[]{:S(2)}) copy-start(bf16[512,512]{1,0:T(8,128)(2,1)} %refs_3_.3) | copy-start | bytes 1572868
  22.9 7.4 %copy-start.7 = (s32[1,512]{1,0:T(1,128)S(1)}, s32[1,512]{1,0:T(1,128)}, u32[]{:S(2)}) copy-start(s32[1,512]{1,0:T(1,128)} %refs_2_.2) | copy-start | bytes 6148
  22.9 7.4 %copy-start.8 = (s32[4,32]{1,0:T(4,128)S(1)}, s32[4,32]{1,0:T(4,128)}, u32[]{:S(2)}) copy-start(s32[4,32]{1,0:T(4,128)} %refs_3_.2) | copy-start | bytes 1540
  22.9 25.3 %all-to-all-start.1 = ((bf16[16,56,512]{2,1,0:T(8,128)(2,1)}), bf16[16,56,512]{2,1,0:T(8,128)(2,1)S(1)}, u32[]{:S(2)}, u32[]{:S(2)}) async-start(bf16[16,56,512]{2,1,0:T(8,128)(2,1)} %shard_map.106), calls=%async_computation.1 | async-start | bytes 1835008 | tf_op jit(solution)/shard_map/all_to_all | solution.py:342
  26.7 1.4 %collective-permute-start.16 = (bf16[128,512]{1,0:T(8,128)(2,1)S(1)}, bf16[128,512]{1,0:T(8,128)(2,1)S(1)}, u32[]{:S(2)}, u32[]{:S(2)}) collective-permute-start(bf16[128,512]{1,0:T(8,128)(2,1)S(1)} %bitcast.13), channel_id=1, source_target_pairs={{0,1},{1,0},{2,3},{3,2},{4,5},{5,4},{6,7},{7,6},{8,9},{9,8},{10,11... | collective-permute-start | bytes 393224 | tf_op jit(solution)/shard_map/ppermute | solution.py:450
  28.1 0.9 %copy-start.6 = (bf16[1,128,512]{2,1,0:T(8,128)(2,1)S(1)}, bf16[1,128,512]{2,1,0:T(8,128)(2,1)}, u32[]{:S(2)}) copy-start(bf16[1,128,512]{2,1,0:T(8,128)(2,1)} %param.15) | copy-start | bytes 393220
  29.6 0.7 %copy-start.3 = (bf16[512,256]{1,0:T(8,128)(2,1)}, bf16[512,256]{1,0:T(8,128)(2,1)S(1)}, u32[]{:S(2)}) copy-start(bf16[512,256]{1,0:T(8,128)(2,1)S(1)} %get-tuple-element.45.refs_3_) | copy-start | bytes 786436
  33.3 17.2 %copy-start.2 = (bf16[512,512]{1,0:T(8,128)(2,1)S(1)}, bf16[512,512]{1,0:T(8,128)(2,1)}, u32[]{:S(2)}) copy-start(bf16[512,512]{1,0:T(8,128)(2,1)} %refs_5_.1) | copy-start | bytes 1572868
  33.3 17.2 %copy-start.4 = (bf16[512,256]{1,0:T(8,128)(2,1)S(1)}, bf16[512,256]{1,0:T(8,128)(2,1)}, u32[]{:S(2)}) copy-start(bf16[512,256]{1,0:T(8,128)(2,1)} %copy-done.3) | copy-start | bytes 786436
  49.0 1.6 %collective-permute-start.17 = (bf16[256,512]{1,0:T(8,128)(2,1)S(1)}, bf16[256,512]{1,0:T(8,128)(2,1)S(1)}, u32[]{:S(2)}, u32[]{:S(2)}) collective-permute-start(bf16[256,512]{1,0:T(8,128)(2,1)S(1)} %shard_map.111), channel_id=1, source_target_pairs={{0,1},{1,0},{2,3},{3,2},{4,5},{5,4},{6,7},{7,6},{8,9},{9,8},{10,11... | collective-permute-start | bytes 786440 | tf_op jit(solution)/shard_map/ppermute | solution.py:497

commit v14 on v13

--- a/solution.py
+++ b/solution.py
@@ -209,31 +209,39 @@
         over, _ = asked(ids, other_ref[0].astype(jnp.float32), items_loc, main, spare)
         over = [jnp.where(own[r : r + 1] > float(main - spare), -1, over[r]) for r in range(n_lists)]
     step = max(1, 288 // main)
+    chunks = [(first, min(n_lists, first + step)) for first in range(0, n_lists, step)]
     sends = []
-    for number, first in enumerate(range(0, n_lists, step)):
-        last = min(n_lists, first + step)
+
+    def finish(number):
+        first, last = chunks[number]
+        if spare:
+            for r in range(first, last):
+                out_ref[r, kept + main - spare :, :] += shared[r * spare : (r + 1) * spare]
+        send = pltpu.make_async_copy(out_ref.at[first:last], out_hbm.at[first:last], out_sems.at[number])
+        send.start()
+        sends.append(send)
+
+    for number, (first, last) in enumerate(chunks):
         rows = jnp.dot(
             picks(jnp.concatenate(index[first:last], axis=0), items_loc),
             items_ref[...],
             preferred_element_type=jnp.float32,
-        )
-        if spare and first == 0:
-            for load in loads:
-                load.wait()
-            shared = jnp.dot(
-                picks(jnp.concatenate(over, axis=0), items_loc),
-                sibling_ref[...],
-                preferred_element_type=jnp.float32,
-            )
+        ).astype(jnp.bfloat16)
         for r in range(first, last):
-            mine = rows[(r - first) * main : (r - first + 1) * main]
-            out_ref[r, kept : kept + main - spare, :] = mine[: main - spare].astype(jnp.bfloat16)
+            out_ref[r, kept:, :] = rows[(r - first) * main : (r - first + 1) * main]
+        if number == max(0, len(chunks) - 2):
             if spare:
-                both = mine[main - spare :] + shared[r * spare : (r + 1) * spare]
-                out_ref[r, kept + main - spare :, :] = both.astype(jnp.bfloat16)
-        send = pltpu.make_async_copy(out_ref.at[first:last], out_hbm.at[first:last], out_sems.at[number])
-        send.start()
-        sends.append(send)
+                for load in loads:
+                    load.wait()
+                shared = jnp.dot(
+                    picks(jnp.concatenate(over, axis=0), items_loc),
+                    sibling_ref[...],
+                    preferred_element_type=jnp.float32,
+                ).astype(jnp.bfloat16)
+            for done in range(number + 1):
+                finish(done)
+        elif number == len(chunks) - 1:
+            finish(number)
     for send in sends:
         send.wait()
 

time: 53.4 us -> 53.3 us (level)
  no operation moved by 1% of the time
where the time goes in v14:
time: 53.3 us; the launch traced here: 52.9 us
  waiting for transfers between devices  21 us (39%)
  Pallas kernels  15.1 us (28%)
  starting transfers between devices  12.4 us (23%)
  local copies, waits for them, and re-layouts  2.31 us (4%)
  between operations  2.08 us (4%)
    all_to_all x2, waiting for transfers between devices, exchange(): lax.all_to_all(value, 'lists', split_axis=0, concat_axis=0, tiled=True)  20 us
    all_to_all x2, starting transfers between devices, exchange(): lax.all_to_all(value, 'lists', split_axis=0, concat_axis=0, tiled=True)  11.7 us
    pallas_call x1, Pallas kernels, shards(): pl.pallas_call(functools.partial(owner_kernel, n_lists, user_dev, digits,...  4.64 us
    pallas_call x1, Pallas kernels, shards(): pl.pallas_call(functools.partial(attend_kernel, n_users), out_shape=jax.S...  2.32 us
    pallas_call x1, Pallas kernels, shards(): pl.pallas_call(functools.partial(known_kernel, n_lists, items_loc, n_user...  1.68 us
    unnamed x18, local copies, waits for them, and re-layouts  1.64 us
    pallas_call x1, Pallas kernels, shards(): pl.pallas_call(items_kernel, out_shape=jax.ShapeDtypeStruct((items_loc, w...  1.55 us
    pallas_call x1, Pallas kernels, shards(): pl.pallas_call(functools.partial(pack_kernel, digits), out_shape=jax.Shap...  1.36 us
  transfers between devices with their start and end apart: 5, of which 4 were waited for; matrix products, arithmetic and copies ran while one was open for 1% of the time, Pallas kernels for 14%

profile of v14, /device:TPU:0, one launch (start us, length us, event | category | flops | bytes accessed | tf_op | source)
XLA Modules:
  0.0 52.9 jit_solution(12993783270108099095)
XLA Ops:
  0.6 0.5 collective-permute-start.15
  1.1 1.4 %shard_map.104 = bf16[16,24,128]{2,1,0:T(8,128)(2,1)} custom-call(s32[1,512]{1,0:T(1,128)} %refs_2_.2, bf16[4,512]{1,0:T(4,128)(2,1)} %vectors_ref.1), custom_call_target="tpu_custom_call" | custom-call | tf_op jit(solution)/shard_map/pallas_call | solution.py:390
  2.5 7.9 %all-to-all-start = ((bf16[16,24,128]{2,1,0:T(8,128)(2,1)}), bf16[16,24,128]{2,1,0:T(8,128)(2,1)}, u32[]{:S(2)}, u32[]{:S(2)}) async-start(bf16[16,24,128]{2,1,0:T(8,128)(2,1)} %shard_map.104), calls=%async_computation | async-start | bytes 196608 | tf_op jit(solution)/shard_map/all_to_all | solution.py:350
  10.4 1.6 %shard_map.105.items_ref = bf16[2048,512]{1,0:T(8,128)(2,1)S(1)} custom-call(bf16[2048,512]{1,0:T(8,128)(2,1)} %bitcast.16), custom_call_target="tpu_custom_call" | custom-call | tf_op jit(solution)/shard_map/pallas_call | solution.py:400
  12.0 6.2 %all-to-all-done = bf16[16,24,128]{2,1,0:T(8,128)(2,1)} async-done(((bf16[16,24,128]{2,1,0:T(8,128)(2,1)}), bf16[16,24,128]{2,1,0:T(8,128)(2,1)}, u32[]{:S(2)}, u32[]{:S(2)}) %all-to-all-start) | async-done | bytes 98336 | tf_op jit(solution)/shard_map/all_to_all | solution.py:350
  18.2 0.0 collective-permute-done.15.refs_0_
  18.2 4.6 %shard_map.106 = bf16[16,56,512]{2,1,0:T(8,128)(2,1)} custom-call(s32[1]{0:T(128)} %bitcast.3.base_ref, s32[1]{0:T(128)} %bitcast.4.other_ref, bf16[384,128]{1,0:T(8,128)(2,1)} %bitcast.5.gathered_ref.refs_4_, bf16[2048,512]{1,0:T(8,128)(2,1)S(1)} %shard_map.105.items_ref, bf16[2048,512]{1,0:T(8,128)(2,1)} %collective-permute-done.15.refs_0_), custom_call_target="tpu_custom_call" | custom-call | tf_op jit(solution)/shard_map/pallas_call | solution.py:473
  22.8 0.0 copy-start
  22.9 0.0 copy-start.1
  22.9 0.0 copy-start.7
  22.9 0.0 copy-start.8
  22.9 3.8 %all-to-all-start.1 = ((bf16[16,56,512]{2,1,0:T(8,128)(2,1)}), bf16[16,56,512]{2,1,0:T(8,128)(2,1)S(1)}, u32[]{:S(2)}, u32[]{:S(2)}) async-start(bf16[16,56,512]{2,1,0:T(8,128)(2,1)} %shard_map.106), calls=%async_computation.1 | async-start | bytes 1835008 | tf_op jit(solution)/shard_map/all_to_all | solution.py:350
  26.7 0.0 copy-done.5
  26.7 0.1 collective-permute-start.16
  27.4 0.7 %collective-permute-done.16.refs_1_ = bf16[128,512]{1,0:T(8,128)(2,1)S(1)} collective-permute-done((bf16[128,512]{1,0:T(8,128)(2,1)S(1)}, bf16[128,512]{1,0:T(8,128)(2,1)S(1)}, u32[]{:S(2)}, u32[]{:S(2)}) %collective-permute-start.16) | collective-permute-done | bytes 131104 | tf_op jit(solution)/shard_map/ppermute | solution.py:458
  28.1 0.0 copy-done
  28.1 0.0 copy-done.1
  28.1 0.9 %copy-done.6 = bf16[1,128,512]{2,1,0:T(8,128)(2,1)S(1)} copy-done((bf16[1,128,512]{2,1,0:T(8,128)(2,1)S(1)}, bf16[1,128,512]{2,1,0:T(8,128)(2,1)}, u32[]{:S(2)}) %copy-start.6) | copy-done | bytes 131096
  29.0 0.6 %shard_map.109 = (bf16[8,256,80]{2,1,0:T(8,128)(2,1)S(1)}, bf16[512,256]{1,0:T(8,128)(2,1)S(1)}, bf16[512,512]{1,0:T(8,128)(2,1)S(1)}) custom-call(s32[1]{0:T(128)} %bitcast.2.refs_1_.col_ref, s32[1]{0:T(128)S(6)} %copy.28.length_ref, bf16[128,512]{1,0:T(8,128)(2,1)S(1)} %bitcast.14, bf16[128,512]{1,0:T(8,128)(2,1)S(1)} %collective-permute-done.16.refs_1_, ...), custom_call_target="tpu_custom_call" | custom-call | tf_op jit(solution)/shard_map/pallas_call | solution.py:460
  29.6 0.0 copy-start.3
  29.6 0.7 %copy-done.3 = bf16[512,256]{1,0:T(8,128)(2,1)} copy-done((bf16[512,256]{1,0:T(8,128)(2,1)}, bf16[512,256]{1,0:T(8,128)(2,1)S(1)}, u32[]{:S(2)}) %copy-start.3) | copy-done | bytes 262168
  30.3 0.0 copy-done.7
  30.3 1.7 %shard_map.107 = (f32[8,512]{1,0:T(8,128)S(1)}, s32[1]{0:T(128)}) custom-call(s32[1]{0:T(128)} %bitcast.7.refs_0_, s32[1]{0:T(128)} %bitcast.2.refs_1_.col_ref, s32[1,512]{1,0:T(1,128)S(1)} %copy-done.7, s32[4,32]{1,0:T(4,128)S(1)} %copy-done.8, bf16[384,128]{1,0:T(8,128)(2,1)} %bitcast.5.gathered_ref.refs_4_), custom_call_target="tpu_custom_call" | custom-call | tf_op jit(solution)/shard_map/pallas_call | solution.py:414
  32.7 0.7 %conditional.1 = (bf16[128,512]{1,0:T(8,128)(2,1)}) conditional(s32[]{:T(128)} %bitcast.8, () %tuple.17, (s32[1]{0:T(128)}, bf16[384,128]{1,0:T(8,128)(2,1)}, bf16[2048,512]{1,0:T(8,128)(2,1)}, s32[]{:T(128)}) %tuple.38), branch_computations={%region_0.0_spmd, %region_1.0_spmd} | conditional | flops 1088 | bytes 1266468 | solution.py:444
  32.7 0.7 %broadcast.27 = bf16[128,512]{1,0:T(8,128)(2,1)} broadcast(bf16[]{:T(256)} %constant.7.clone), dimensions={} | broadcast | bytes 131074 | tf_op jit(solution)/shard_map/broadcast.1
  33.3 1.0 %shard_map.108.refs_0_ = bf16[128,512]{1,0:T(8,128)(2,1)S(1)} custom-call(bf16[128,512]{1,0:T(8,128)(2,1)} %get-tuple-element.63.came_ref), custom_call_target="tpu_custom_call" | custom-call | tf_op jit(solution)/shard_map/pallas_call | solution.py:446
  34.3 13.8 %all-to-all-done.1.fetched_ref = bf16[16,56,512]{2,1,0:T(8,128)(2,1)S(1)} async-done(((bf16[16,56,512]{2,1,0:T(8,128)(2,1)}), bf16[16,56,512]{2,1,0:T(8,128)(2,1)S(1)}, u32[]{:S(2)}, u32[]{:S(2)}) %all-to-all-start.1) | async-done | bytes 917536 | tf_op jit(solution)/shard_map/all_to_all | solution.py:350
  48.2 0.8 %shard_map.111 = bf16[256,512]{1,0:T(8,128)(2,1)S(1)} custom-call(s32[1]{0:T(128)} %bitcast.2.refs_1_.col_ref, f32[8,512]{1,0:T(8,128)S(1)} %get-tuple-element.39.known_ref, bf16[16,56,512]{2,1,0:T(8,128)(2,1)S(1)} %all-to-all-done.1.fetched_ref, bf16[128,512]{1,0:T(8,128)(2,1)S(1)} %shard_map.108.refs_0_), custom_call_target="tpu_custom_call" | custom-call | tf_op jit(solution)/shard_map/pallas_call | solution.py:494
  49.0 0.1 collective-permute-start.17
  49.0 1.2 %shard_map.110 = (bf16[128,2048]{1,0:T(8,128)(2,1)}, bf16[256,512]{1,0:T(8,128)(2,1)S(1)}) custom-call(s32[1]{0:T(128)} %bitcast.2.refs_1_.col_ref, f32[8,512]{1,0:T(8,128)S(1)} %get-tuple-element.39.known_ref, bf16[16,56,512]{2,1,0:T(8,128)(2,1)S(1)} %all-to-all-done.1.fetched_ref, bf16[128,512]{1,0:T(8,128)(2,1)S(1)} %shard_map.108.refs_0_), custom_call_target="tpu_custom_call" | custom-call | tf_op jit(solution)/shard_map/pallas_call | solution.py:508
  50.2 0.3 collective-permute-done.17.refs_1_
  50.6 2.3 %shard_map.112 = bf16[256,512]{1,0:T(8,128)(2,1)} custom-call(bf16[256,512]{1,0:T(8,128)(2,1)S(1)} %get-tuple-element.43.refs_0_, bf16[256,512]{1,0:T(8,128)(2,1)S(1)} %collective-permute-done.17.refs_1_, bf16[8,256,80]{2,1,0:T(8,128)(2,1)S(1)} %get-tuple-element.44.refs_2_, bf16[512,256]{1,0:T(8,128)(2,1)S(1)} %copy-done.4, ...), custom_call_target="tpu_custom_call" | custom-call | tf_op jit(solution)/shard_map/pallas_call | solution.py:523
  (7 shorter events, 0.0 us)
Async XLA Ops:
  0.6 17.6 %collective-permute-start.15 = (bf16[2048,512]{1,0:T(8,128)(2,1)}, bf16[2048,512]{1,0:T(8,128)(2,1)}, u32[]{:S(2)}, u32[]{:S(2)}) collective-permute-start(bf16[2048,512]{1,0:T(8,128)(2,1)} %bitcast.15), channel_id=1, source_target_pairs={{0,1},{1,0},{2,3},{3,2},{4,5},{5,4},{6,7},{7,6},{8,9},{9,8},{10,11... | collective-permute-start | bytes 6291464 | tf_op jit(solution)/shard_map/ppermute | solution.py:412
  2.5 15.7 %all-to-all-start = ((bf16[16,24,128]{2,1,0:T(8,128)(2,1)}), bf16[16,24,128]{2,1,0:T(8,128)(2,1)}, u32[]{:S(2)}, u32[]{:S(2)}) async-start(bf16[16,24,128]{2,1,0:T(8,128)(2,1)} %shard_map.104), calls=%async_computation | async-start | bytes 196608 | tf_op jit(solution)/shard_map/all_to_all | solution.py:350
  18.2 8.5 %copy-start.5 = (bf16[1,128,512]{2,1,0:T(8,128)(2,1)S(1)}, bf16[1,128,512]{2,1,0:T(8,128)(2,1)}, u32[]{:S(2)}) copy-start(bf16[1,128,512]{2,1,0:T(8,128)(2,1)} %param.15) | copy-start | bytes 393220
  22.8 5.3 %copy-start = (bf16[512,1024]{1,0:T(8,128)(2,1)S(1)}, bf16[512,1024]{1,0:T(8,128)(2,1)}, u32[]{:S(2)}) copy-start(bf16[512,1024]{1,0:T(8,128)(2,1)} %refs_2_.3) | copy-start | bytes 3145732
  22.9 5.2 %copy-start.1 = (bf16[512,512]{1,0:T(8,128)(2,1)S(1)}, bf16[512,512]{1,0:T(8,128)(2,1)}, u32[]{:S(2)}) copy-start(bf16[512,512]{1,0:T(8,128)(2,1)} %refs_3_.3) | copy-start | bytes 1572868
  22.9 7.4 %copy-start.7 = (s32[1,512]{1,0:T(1,128)S(1)}, s32[1,512]{1,0:T(1,128)}, u32[]{:S(2)}) copy-start(s32[1,512]{1,0:T(1,128)} %refs_2_.2) | copy-start | bytes 6148
  22.9 7.4 %copy-start.8 = (s32[4,32]{1,0:T(4,128)S(1)}, s32[4,32]{1,0:T(4,128)}, u32[]{:S(2)}) copy-start(s32[4,32]{1,0:T(4,128)} %refs_3_.2) | copy-start | bytes 1540
  22.9 25.3 %all-to-all-start.1 = ((bf16[16,56,512]{2,1,0:T(8,128)(2,1)}), bf16[16,56,512]{2,1,0:T(8,128)(2,1)S(1)}, u32[]{:S(2)}, u32[]{:S(2)}) async-start(bf16[16,56,512]{2,1,0:T(8,128)(2,1)} %shard_map.106), calls=%async_computation.1 | async-start | bytes 1835008 | tf_op jit(solution)/shard_map/all_to_all | solution.py:350
  26.7 1.4 %collective-permute-start.16 = (bf16[128,512]{1,0:T(8,128)(2,1)S(1)}, bf16[128,512]{1,0:T(8,128)(2,1)S(1)}, u32[]{:S(2)}, u32[]{:S(2)}) collective-permute-start(bf16[128,512]{1,0:T(8,128)(2,1)S(1)} %bitcast.13), channel_id=1, source_target_pairs={{0,1},{1,0},{2,3},{3,2},{4,5},{5,4},{6,7},{7,6},{8,9},{9,8},{10,11... | collective-permute-start | bytes 393224 | tf_op jit(solution)/shard_map/ppermute | solution.py:458
  28.1 0.9 %copy-start.6 = (bf16[1,128,512]{2,1,0:T(8,128)(2,1)S(1)}, bf16[1,128,512]{2,1,0:T(8,128)(2,1)}, u32[]{:S(2)}) copy-start(bf16[1,128,512]{2,1,0:T(8,128)(2,1)} %param.15) | copy-start | bytes 393220
  29.6 0.7 %copy-start.3 = (bf16[512,256]{1,0:T(8,128)(2,1)}, bf16[512,256]{1,0:T(8,128)(2,1)S(1)}, u32[]{:S(2)}) copy-start(bf16[512,256]{1,0:T(8,128)(2,1)S(1)} %get-tuple-element.45.refs_3_) | copy-start | bytes 786436
  33.3 17.2 %copy-start.2 = (bf16[512,512]{1,0:T(8,128)(2,1)S(1)}, bf16[512,512]{1,0:T(8,128)(2,1)}, u32[]{:S(2)}) copy-start(bf16[512,512]{1,0:T(8,128)(2,1)} %refs_5_.1) | copy-start | bytes 1572868
  33.3 17.2 %copy-start.4 = (bf16[512,256]{1,0:T(8,128)(2,1)S(1)}, bf16[512,256]{1,0:T(8,128)(2,1)}, u32[]{:S(2)}) copy-start(bf16[512,256]{1,0:T(8,128)(2,1)} %copy-done.3) | copy-start | bytes 786436
  49.0 1.6 %collective-permute-start.17 = (bf16[256,512]{1,0:T(8,128)(2,1)S(1)}, bf16[256,512]{1,0:T(8,128)(2,1)S(1)}, u32[]{:S(2)}, u32[]{:S(2)}) collective-permute-start(bf16[256,512]{1,0:T(8,128)(2,1)S(1)} %shard_map.111), channel_id=1, source_target_pairs={{0,1},{1,0},{2,3},{3,2},{4,5},{5,4},{6,7},{7,6},{8,9},{9,8},{10,11... | collective-permute-start | bytes 786440 | tf_op jit(solution)/shard_map/ppermute | solution.py:505

commit v15 on v13

--- a/solution.py
+++ b/solution.py
@@ -119,7 +119,8 @@
 def known_kernel(
     n_lists, items_loc, n_users, user_dev, digits, main, spare, kept, *refs
 ):
-    line_ref, col_ref, ids_ref, probes_ref, gathered_ref, known_ref, many_ref, wide = refs
+    line_ref, col_ref, ids_ref, probes_ref, gathered_ref, known_ref, many_ref, copy_ref, wide = refs
+    copy_ref[...] = gathered_ref[...]
     block = kept + main
     ids = ids_ref[...]
     cands = ids.shape[1]
@@ -403,14 +404,15 @@
     if spare:
         siblings.append(lax.ppermute(flat_items, "users", [(0, 1), (1, 0)]))
 
-    known, many = pl.pallas_call(
+    known, many, gathered_copy = pl.pallas_call(
         functools.partial(known_kernel, n_lists, items_loc, n_users, user_dev, digits, main, spare, kept),
         out_shape=(
             jax.ShapeDtypeStruct((8, cands), jnp.float32),
             jax.ShapeDtypeStruct((1,), jnp.int32),
+            jax.ShapeDtypeStruct(gathered.shape, bf16),
         ),
         in_specs=[SMEM, SMEM, VMEM, VMEM, VMEM],
-        out_specs=(VMEM, SMEM),
+        out_specs=(VMEM, SMEM, VMEM),
         scratch_shapes=[pltpu.VMEM((n_lists * pack_rows, LANES), jnp.float32)],
         compiler_params=PARAMS,
     )(line_arg, col_arg, candidate_ids, probe_lists, gathered)
@@ -426,7 +428,7 @@
                 out_specs=VMEM,
                 scratch_shapes=[pltpu.VMEM((n_lists * pack_rows, LANES), jnp.float32)],
                 compiler_params=PARAMS,
-            )(base_arg, gathered, flat_items)
+            )(base_arg, gathered_copy, flat_items)
             spill = spill[jnp.arange(n_lists, dtype=jnp.int32) ^ line]
             blocks = [spill[:1]]
             for k in range(1, n_lists):

time: 53.4 us -> 52.3 us (0.979)
  Pallas kernels: 15.1 us -> 13.3 us
  waiting for transfers between devices: 21 us -> 21.8 us
    pallas_call x1, Pallas kernels: 4.64 us -> 3.71 us  [shards(): pl.pallas_call(functools.partial(owner_kernel, n_lists, user_dev, digits,...]
    pallas_call x1, Pallas kernels: 1.68 us -> 0.8 us  [shards(): pl.pallas_call(functools.partial(known_kernel, n_lists, items_loc, n_user...]
    all_to_all x2, waiting for transfers between devices: 20 us -> 20.7 us  [exchange(): lax.all_to_all(value, 'lists', split_axis=0, concat_axis=0, tiled=True)]
  transfers between devices with their start and end apart: 5 -> 5, of which waited for: 4 -> 4; matrix products, arithmetic and copies ran while one was open for 1% -> 1% of each run, Pallas kernels for 14% -> 12%
where the time goes in v15:
time: 52.3 us; the launch traced here: 51.9 us
  waiting for transfers between devices  21.8 us (42%)
  Pallas kernels  13.3 us (25%)
  starting transfers between devices  12.3 us (24%)
  local copies, waits for them, and re-layouts  2.4 us (5%)
  between operations  2.08 us (4%)
    all_to_all x2, waiting for transfers between devices, exchange(): lax.all_to_all(value, 'lists', split_axis=0, concat_axis=0, tiled=True)  20.7 us
    all_to_all x2, starting transfers between devices, exchange(): lax.all_to_all(value, 'lists', split_axis=0, concat_axis=0, tiled=True)  11.7 us
    pallas_call x1, Pallas kernels, shards(): pl.pallas_call(functools.partial(owner_kernel, n_lists, user_dev, digits,...  3.71 us
    pallas_call x1, Pallas kernels, shards(): pl.pallas_call(functools.partial(attend_kernel, n_users), out_shape=jax.S...  2.32 us
    unnamed x18, local copies, waits for them, and re-layouts  1.73 us
    pallas_call x1, Pallas kernels, shards(): pl.pallas_call(items_kernel, out_shape=jax.ShapeDtypeStruct((items_loc, w...  1.55 us
    pallas_call x1, Pallas kernels, shards(): pl.pallas_call(functools.partial(pack_kernel, digits), out_shape=jax.Shap...  1.36 us
    pallas_call x1, Pallas kernels, shards(): pl.pallas_call(functools.partial(expand_kernel, user_dev, pieces, kept),...  1.17 us
  transfers between devices with their start and end apart: 5, of which 4 were waited for; matrix products, arithmetic and copies ran while one was open for 1% of the time, Pallas kernels for 12%

profile of v15, /device:TPU:0, one launch (start us, length us, event | category | flops | bytes accessed | tf_op | source)
XLA Modules:
  0.0 51.9 jit_solution(9450131593558742020)
XLA Ops:
  0.6 0.5 collective-permute-start.15
  1.1 1.4 %shard_map.104 = bf16[16,24,128]{2,1,0:T(8,128)(2,1)} custom-call(s32[1,512]{1,0:T(1,128)} %refs_2_.2, bf16[4,512]{1,0:T(4,128)(2,1)} %vectors_ref.1), custom_call_target="tpu_custom_call" | custom-call | tf_op jit(solution)/shard_map/pallas_call | solution.py:383
  2.5 7.9 %all-to-all-start = ((bf16[16,24,128]{2,1,0:T(8,128)(2,1)}), bf16[16,24,128]{2,1,0:T(8,128)(2,1)S(1)}, u32[]{:S(2)}, u32[]{:S(2)}) async-start(bf16[16,24,128]{2,1,0:T(8,128)(2,1)} %shard_map.104), calls=%async_computation | async-start | bytes 196608 | tf_op jit(solution)/shard_map/all_to_all | solution.py:343
  10.4 1.6 %shard_map.105.items_ref = bf16[2048,512]{1,0:T(8,128)(2,1)S(1)} custom-call(bf16[2048,512]{1,0:T(8,128)(2,1)} %bitcast.18), custom_call_target="tpu_custom_call" | custom-call | tf_op jit(solution)/shard_map/pallas_call | solution.py:393
  12.0 6.1 %all-to-all-done = bf16[16,24,128]{2,1,0:T(8,128)(2,1)S(1)} async-done(((bf16[16,24,128]{2,1,0:T(8,128)(2,1)}), bf16[16,24,128]{2,1,0:T(8,128)(2,1)S(1)}, u32[]{:S(2)}, u32[]{:S(2)}) %all-to-all-start) | async-done | bytes 98336 | tf_op jit(solution)/shard_map/all_to_all | solution.py:343
  18.1 0.0 collective-permute-done.15.refs_0_
  18.1 3.7 %shard_map.106 = bf16[16,56,512]{2,1,0:T(8,128)(2,1)} custom-call(s32[1]{0:T(128)} %bitcast.3.base_ref, s32[1]{0:T(128)} %bitcast.4.other_ref, bf16[384,128]{1,0:T(8,128)(2,1)S(1)} %bitcast.13, bf16[2048,512]{1,0:T(8,128)(2,1)S(1)} %shard_map.105.items_ref, bf16[2048,512]{1,0:T(8,128)(2,1)} %collective-permute-done.15.refs_0_), custom_call_target="tpu_custom_call" | custom-call | tf_op jit(solution)/shard_map/pallas_call | solution.py:467
  21.8 0.0 copy-start
  21.8 0.0 copy-start.1
  21.8 0.0 copy-start.7
  21.8 0.0 copy-start.8
  21.9 3.8 %all-to-all-start.1 = ((bf16[16,56,512]{2,1,0:T(8,128)(2,1)}), bf16[16,56,512]{2,1,0:T(8,128)(2,1)S(1)}, u32[]{:S(2)}, u32[]{:S(2)}) async-start(bf16[16,56,512]{2,1,0:T(8,128)(2,1)} %shard_map.106), calls=%async_computation.1 | async-start | bytes 1835008 | tf_op jit(solution)/shard_map/all_to_all | solution.py:343
  25.6 0.0 copy-done.5
  25.7 0.1 collective-permute-start.16
  26.4 0.7 %collective-permute-done.16.refs_1_ = bf16[128,512]{1,0:T(8,128)(2,1)S(1)} collective-permute-done((bf16[128,512]{1,0:T(8,128)(2,1)S(1)}, bf16[128,512]{1,0:T(8,128)(2,1)S(1)}, u32[]{:S(2)}, u32[]{:S(2)}) %collective-permute-start.16) | collective-permute-done | bytes 131104 | tf_op jit(solution)/shard_map/ppermute | solution.py:452
  27.1 0.0 copy-done
  27.1 0.0 copy-done.1
  27.1 0.9 %copy-done.6 = bf16[1,128,512]{2,1,0:T(8,128)(2,1)S(1)} copy-done((bf16[1,128,512]{2,1,0:T(8,128)(2,1)S(1)}, bf16[1,128,512]{2,1,0:T(8,128)(2,1)}, u32[]{:S(2)}) %copy-start.6) | copy-done | bytes 131096
  28.0 0.6 %shard_map.109 = (bf16[8,256,80]{2,1,0:T(8,128)(2,1)S(1)}, bf16[512,256]{1,0:T(8,128)(2,1)S(1)}, bf16[512,512]{1,0:T(8,128)(2,1)S(1)}) custom-call(s32[1]{0:T(128)} %bitcast.2.refs_1_.col_ref, s32[1]{0:T(128)S(6)} %copy.28.length_ref, bf16[128,512]{1,0:T(8,128)(2,1)S(1)} %bitcast.16, bf16[128,512]{1,0:T(8,128)(2,1)S(1)} %collective-permute-done.16.refs_1_, ...), custom_call_target="tpu_custom_call" | custom-call | tf_op jit(solution)/shard_map/pallas_call | solution.py:454
  28.6 0.8 %copy-done.3 = bf16[512,512]{1,0:T(8,128)(2,1)} copy-done((bf16[512,512]{1,0:T(8,128)(2,1)}, bf16[512,512]{1,0:T(8,128)(2,1)S(1)}, u32[]{:S(2)}) %copy-start.3) | copy-done | bytes 524312
  29.4 0.0 copy-done.7
  29.4 0.8 %shard_map.107 = (f32[8,512]{1,0:T(8,128)S(1)}, s32[1]{0:T(128)}, bf16[384,128]{1,0:T(8,128)(2,1)S(1)}) custom-call(s32[1]{0:T(128)} %bitcast.7.refs_0_, s32[1]{0:T(128)} %bitcast.2.refs_1_.col_ref, s32[1,512]{1,0:T(1,128)S(1)} %copy-done.7, s32[4,32]{1,0:T(4,128)S(1)} %copy-done.8, bf16[384,128]{1,0:T(8,128)(2,1)S(1)} %bitcast.14), custom_call_target="tpu_custom_call" | custom-call | tf_op jit(solution)/shard_map/pallas_call | solution.py:407
  30.8 0.7 %conditional.1 = (bf16[128,512]{1,0:T(8,128)(2,1)}) conditional(s32[]{:T(128)} %bitcast.8, () %tuple.17, (s32[1]{0:T(128)}, bf16[384,128]{1,0:T(8,128)(2,1)S(1)}, bf16[2048,512]{1,0:T(8,128)(2,1)}, s32[]{:T(128)}) %tuple.38), branch_computations={%region_0.0_spmd, %region_1.0_spmd} | conditional | flops 1088 | bytes 1266468 | solution.py:438
  30.8 0.7 %broadcast.27 = bf16[128,512]{1,0:T(8,128)(2,1)} broadcast(bf16[]{:T(256)} %constant.7.clone), dimensions={} | broadcast | bytes 131074 | tf_op jit(solution)/shard_map/broadcast.1
  31.5 1.0 %shard_map.108.refs_0_ = bf16[128,512]{1,0:T(8,128)(2,1)S(1)} custom-call(bf16[128,512]{1,0:T(8,128)(2,1)} %get-tuple-element.65.came_ref), custom_call_target="tpu_custom_call" | custom-call | tf_op jit(solution)/shard_map/pallas_call | solution.py:440
  32.5 14.6 %all-to-all-done.1.fetched_ref = bf16[16,56,512]{2,1,0:T(8,128)(2,1)S(1)} async-done(((bf16[16,56,512]{2,1,0:T(8,128)(2,1)}), bf16[16,56,512]{2,1,0:T(8,128)(2,1)S(1)}, u32[]{:S(2)}, u32[]{:S(2)}) %all-to-all-start.1) | async-done | bytes 917536 | tf_op jit(solution)/shard_map/all_to_all | solution.py:343
  47.1 0.8 %shard_map.111 = bf16[256,512]{1,0:T(8,128)(2,1)S(1)} custom-call(s32[1]{0:T(128)} %bitcast.2.refs_1_.col_ref, f32[8,512]{1,0:T(8,128)S(1)} %get-tuple-element.41.known_ref, bf16[16,56,512]{2,1,0:T(8,128)(2,1)S(1)} %all-to-all-done.1.fetched_ref, bf16[128,512]{1,0:T(8,128)(2,1)S(1)} %shard_map.108.refs_0_), custom_call_target="tpu_custom_call" | custom-call | tf_op jit(solution)/shard_map/pallas_call | solution.py:488
  47.9 0.1 collective-permute-start.17
  48.0 1.2 %shard_map.110 = (bf16[128,2048]{1,0:T(8,128)(2,1)}, bf16[256,512]{1,0:T(8,128)(2,1)S(1)}) custom-call(s32[1]{0:T(128)} %bitcast.2.refs_1_.col_ref, f32[8,512]{1,0:T(8,128)S(1)} %get-tuple-element.41.known_ref, bf16[16,56,512]{2,1,0:T(8,128)(2,1)S(1)} %all-to-all-done.1.fetched_ref, bf16[128,512]{1,0:T(8,128)(2,1)S(1)} %shard_map.108.refs_0_), custom_call_target="tpu_custom_call" | custom-call | tf_op jit(solution)/shard_map/pallas_call | solution.py:502
  49.2 0.3 collective-permute-done.17.refs_1_
  49.5 0.0 copy-done.4
  49.5 2.3 %shard_map.112 = bf16[256,512]{1,0:T(8,128)(2,1)} custom-call(bf16[256,512]{1,0:T(8,128)(2,1)S(1)} %get-tuple-element.45.refs_0_, bf16[256,512]{1,0:T(8,128)(2,1)S(1)} %collective-permute-done.17.refs_1_, bf16[8,256,80]{2,1,0:T(8,128)(2,1)S(1)} %get-tuple-element.46.refs_2_, bf16[512,256]{1,0:T(8,128)(2,1)S(1)} %get-tuple-element.47.refs_3_, ...), custom_call_target="tpu_custom_call" | custom-call | tf_op jit(solution)/shard_map/pallas_call | solution.py:517
  (7 shorter events, 0.0 us)
Async XLA Ops:
  0.6 17.5 %collective-permute-start.15 = (bf16[2048,512]{1,0:T(8,128)(2,1)}, bf16[2048,512]{1,0:T(8,128)(2,1)}, u32[]{:S(2)}, u32[]{:S(2)}) collective-permute-start(bf16[2048,512]{1,0:T(8,128)(2,1)} %bitcast.17), channel_id=1, source_target_pairs={{0,1},{1,0},{2,3},{3,2},{4,5},{5,4},{6,7},{7,6},{8,9},{9,8},{10,11... | collective-permute-start | bytes 6291464 | tf_op jit(solution)/shard_map/ppermute | solution.py:405
  2.5 15.6 %all-to-all-start = ((bf16[16,24,128]{2,1,0:T(8,128)(2,1)}), bf16[16,24,128]{2,1,0:T(8,128)(2,1)S(1)}, u32[]{:S(2)}, u32[]{:S(2)}) async-start(bf16[16,24,128]{2,1,0:T(8,128)(2,1)} %shard_map.104), calls=%async_computation | async-start | bytes 196608 | tf_op jit(solution)/shard_map/all_to_all | solution.py:343
  18.1 7.6 %copy-start.5 = (bf16[1,128,512]{2,1,0:T(8,128)(2,1)S(1)}, bf16[1,128,512]{2,1,0:T(8,128)(2,1)}, u32[]{:S(2)}) copy-start(bf16[1,128,512]{2,1,0:T(8,128)(2,1)} %param.15) | copy-start | bytes 393220
  21.8 5.3 %copy-start = (bf16[512,1024]{1,0:T(8,128)(2,1)S(1)}, bf16[512,1024]{1,0:T(8,128)(2,1)}, u32[]{:S(2)}) copy-start(bf16[512,1024]{1,0:T(8,128)(2,1)} %refs_2_.3) | copy-start | bytes 3145732
  21.8 5.2 %copy-start.1 = (bf16[512,512]{1,0:T(8,128)(2,1)S(1)}, bf16[512,512]{1,0:T(8,128)(2,1)}, u32[]{:S(2)}) copy-start(bf16[512,512]{1,0:T(8,128)(2,1)} %refs_3_.3) | copy-start | bytes 1572868
  21.8 7.5 %copy-start.7 = (s32[1,512]{1,0:T(1,128)S(1)}, s32[1,512]{1,0:T(1,128)}, u32[]{:S(2)}) copy-start(s32[1,512]{1,0:T(1,128)} %refs_2_.2) | copy-start | bytes 6148
  21.8 7.5 %copy-start.8 = (s32[4,32]{1,0:T(4,128)S(1)}, s32[4,32]{1,0:T(4,128)}, u32[]{:S(2)}) copy-start(s32[4,32]{1,0:T(4,128)} %refs_3_.2) | copy-start | bytes 1540
  21.9 25.3 %all-to-all-start.1 = ((bf16[16,56,512]{2,1,0:T(8,128)(2,1)}), bf16[16,56,512]{2,1,0:T(8,128)(2,1)S(1)}, u32[]{:S(2)}, u32[]{:S(2)}) async-start(bf16[16,56,512]{2,1,0:T(8,128)(2,1)} %shard_map.106), calls=%async_computation.1 | async-start | bytes 1835008 | tf_op jit(solution)/shard_map/all_to_all | solution.py:343
  25.7 1.4 %collective-permute-start.16 = (bf16[128,512]{1,0:T(8,128)(2,1)S(1)}, bf16[128,512]{1,0:T(8,128)(2,1)S(1)}, u32[]{:S(2)}, u32[]{:S(2)}) collective-permute-start(bf16[128,512]{1,0:T(8,128)(2,1)S(1)} %bitcast.15), channel_id=1, source_target_pairs={{0,1},{1,0},{2,3},{3,2},{4,5},{5,4},{6,7},{7,6},{8,9},{9,8},{10,11... | collective-permute-start | bytes 393224 | tf_op jit(solution)/shard_map/ppermute | solution.py:452
  27.1 0.9 %copy-start.6 = (bf16[1,128,512]{2,1,0:T(8,128)(2,1)S(1)}, bf16[1,128,512]{2,1,0:T(8,128)(2,1)}, u32[]{:S(2)}) copy-start(bf16[1,128,512]{2,1,0:T(8,128)(2,1)} %param.15) | copy-start | bytes 393220
  28.6 0.8 %copy-start.3 = (bf16[512,512]{1,0:T(8,128)(2,1)}, bf16[512,512]{1,0:T(8,128)(2,1)S(1)}, u32[]{:S(2)}) copy-start(bf16[512,512]{1,0:T(8,128)(2,1)S(1)} %get-tuple-element.48.refs_4_) | copy-start | bytes 1572868
  31.5 18.0 %copy-start.2 = (bf16[512,512]{1,0:T(8,128)(2,1)S(1)}, bf16[512,512]{1,0:T(8,128)(2,1)}, u32[]{:S(2)}) copy-start(bf16[512,512]{1,0:T(8,128)(2,1)} %refs_5_.1) | copy-start | bytes 1572868
  31.5 18.0 %copy-start.4 = (bf16[512,512]{1,0:T(8,128)(2,1)S(1)}, bf16[512,512]{1,0:T(8,128)(2,1)}, u32[]{:S(2)}) copy-start(bf16[512,512]{1,0:T(8,128)(2,1)} %copy-done.3) | copy-start | bytes 1572868
  47.9 1.6 %collective-permute-start.17 = (bf16[256,512]{1,0:T(8,128)(2,1)S(1)}, bf16[256,512]{1,0:T(8,128)(2,1)S(1)}, u32[]{:S(2)}, u32[]{:S(2)}) collective-permute-start(bf16[256,512]{1,0:T(8,128)(2,1)S(1)} %shard_map.111), channel_id=1, source_target_pairs={{0,1},{1,0},{2,3},{3,2},{4,5},{5,4},{6,7},{7,6},{8,9},{9,8},{10,11... | collective-permute-start | bytes 786440 | tf_op jit(solution)/shard_map/ppermute | solution.py:499

commit v16 on v14

--- a/solution.py
+++ b/solution.py
@@ -119,7 +119,8 @@
 def known_kernel(
     n_lists, items_loc, n_users, user_dev, digits, main, spare, kept, *refs
 ):
-    line_ref, col_ref, ids_ref, probes_ref, gathered_ref, known_ref, many_ref, wide = refs
+    line_ref, col_ref, ids_ref, probes_ref, gathered_ref, known_ref, many_ref, copy_ref, wide = refs
+    copy_ref[...] = gathered_ref[...]
     block = kept + main
     ids = ids_ref[...]
     cands = ids.shape[1]
@@ -411,14 +412,15 @@
     if spare:
         siblings.append(lax.ppermute(flat_items, "users", [(0, 1), (1, 0)]))
 
-    known, many = pl.pallas_call(
+    known, many, gathered_copy = pl.pallas_call(
         functools.partial(known_kernel, n_lists, items_loc, n_users, user_dev, digits, main, spare, kept),
         out_shape=(
             jax.ShapeDtypeStruct((8, cands), jnp.float32),
             jax.ShapeDtypeStruct((1,), jnp.int32),
+            jax.ShapeDtypeStruct(gathered.shape, bf16),
         ),
         in_specs=[SMEM, SMEM, VMEM, VMEM, VMEM],
-        out_specs=(VMEM, SMEM),
+        out_specs=(VMEM, SMEM, VMEM),
         scratch_shapes=[pltpu.VMEM((n_lists * pack_rows, LANES), jnp.float32)],
         compiler_params=PARAMS,
     )(line_arg, col_arg, candidate_ids, probe_lists, gathered)
@@ -434,7 +436,7 @@
                 out_specs=VMEM,
                 scratch_shapes=[pltpu.VMEM((n_lists * pack_rows, LANES), jnp.float32)],
                 compiler_params=PARAMS,
-            )(base_arg, gathered, flat_items)
+            )(base_arg, gathered_copy, flat_items)
             spill = spill[jnp.arange(n_lists, dtype=jnp.int32) ^ line]
             blocks = [spill[:1]]
             for k in range(1, n_lists):

time: 53.3 us -> 52.3 us (0.981)
  Pallas kernels: 15.1 us -> 13.3 us
  waiting for transfers between devices: 21 us -> 21.8 us
    pallas_call x1, Pallas kernels: 4.64 us -> 3.7 us  [shards(): pl.pallas_call(functools.partial(owner_kernel, n_lists, user_dev, digits,...]
    pallas_call x1, Pallas kernels: 1.68 us -> 0.8 us  [shards(): pl.pallas_call(functools.partial(known_kernel, n_lists, items_loc, n_user...]
    all_to_all x2, waiting for transfers between devices: 20 us -> 20.7 us  [exchange(): lax.all_to_all(value, 'lists', split_axis=0, concat_axis=0, tiled=True)]
  transfers between devices with their start and end apart: 5 -> 5, of which waited for: 4 -> 4; matrix products, arithmetic and copies ran while one was open for 1% -> 1% of each run, Pallas kernels for 14% -> 12%
where the time goes in v16:
time: 52.3 us; the launch traced here: 51.9 us
  waiting for transfers between devices  21.8 us (42%)
  Pallas kernels  13.3 us (25%)
  starting transfers between devices  12.3 us (24%)
  local copies, waits for them, and re-layouts  2.4 us (5%)
  between operations  2.08 us (4%)
    all_to_all x2, waiting for transfers between devices, exchange(): lax.all_to_all(value, 'lists', split_axis=0, concat_axis=0, tiled=True)  20.7 us
    all_to_all x2, starting transfers between devices, exchange(): lax.all_to_all(value, 'lists', split_axis=0, concat_axis=0, tiled=True)  11.7 us
    pallas_call x1, Pallas kernels, shards(): pl.pallas_call(functools.partial(owner_kernel, n_lists, user_dev, digits,...  3.7 us
    pallas_call x1, Pallas kernels, shards(): pl.pallas_call(functools.partial(attend_kernel, n_users), out_shape=jax.S...  2.32 us
    unnamed x18, local copies, waits for them, and re-layouts  1.73 us
    pallas_call x1, Pallas kernels, shards(): pl.pallas_call(items_kernel, out_shape=jax.ShapeDtypeStruct((items_loc, w...  1.55 us
    pallas_call x1, Pallas kernels, shards(): pl.pallas_call(functools.partial(pack_kernel, digits), out_shape=jax.Shap...  1.36 us
    pallas_call x1, Pallas kernels, shards(): pl.pallas_call(functools.partial(expand_kernel, user_dev, pieces, kept),...  1.17 us
  transfers between devices with their start and end apart: 5, of which 4 were waited for; matrix products, arithmetic and copies ran while one was open for 1% of the time, Pallas kernels for 12%

profile of v16, /device:TPU:0, one launch (start us, length us, event | category | flops | bytes accessed | tf_op | source)
XLA Modules:
  0.0 51.9 jit_solution(4415693058240103047)
XLA Ops:
  0.6 0.5 collective-permute-start.15
  1.1 1.4 %shard_map.104 = bf16[16,24,128]{2,1,0:T(8,128)(2,1)} custom-call(s32[1,512]{1,0:T(1,128)} %refs_2_.2, bf16[4,512]{1,0:T(4,128)(2,1)} %vectors_ref.1), custom_call_target="tpu_custom_call" | custom-call | tf_op jit(solution)/shard_map/pallas_call | solution.py:391
  2.5 7.9 %all-to-all-start = ((bf16[16,24,128]{2,1,0:T(8,128)(2,1)}), bf16[16,24,128]{2,1,0:T(8,128)(2,1)S(1)}, u32[]{:S(2)}, u32[]{:S(2)}) async-start(bf16[16,24,128]{2,1,0:T(8,128)(2,1)} %shard_map.104), calls=%async_computation | async-start | bytes 196608 | tf_op jit(solution)/shard_map/all_to_all | solution.py:351
  10.4 1.6 %shard_map.105.items_ref = bf16[2048,512]{1,0:T(8,128)(2,1)S(1)} custom-call(bf16[2048,512]{1,0:T(8,128)(2,1)} %bitcast.18), custom_call_target="tpu_custom_call" | custom-call | tf_op jit(solution)/shard_map/pallas_call | solution.py:401
  12.0 6.1 %all-to-all-done = bf16[16,24,128]{2,1,0:T(8,128)(2,1)S(1)} async-done(((bf16[16,24,128]{2,1,0:T(8,128)(2,1)}), bf16[16,24,128]{2,1,0:T(8,128)(2,1)S(1)}, u32[]{:S(2)}, u32[]{:S(2)}) %all-to-all-start) | async-done | bytes 98336 | tf_op jit(solution)/shard_map/all_to_all | solution.py:351
  18.1 0.0 collective-permute-done.15.refs_0_
  18.1 3.7 %shard_map.106 = bf16[16,56,512]{2,1,0:T(8,128)(2,1)} custom-call(s32[1]{0:T(128)} %bitcast.3.base_ref, s32[1]{0:T(128)} %bitcast.4.other_ref, bf16[384,128]{1,0:T(8,128)(2,1)S(1)} %bitcast.13, bf16[2048,512]{1,0:T(8,128)(2,1)S(1)} %shard_map.105.items_ref, bf16[2048,512]{1,0:T(8,128)(2,1)} %collective-permute-done.15.refs_0_), custom_call_target="tpu_custom_call" | custom-call | tf_op jit(solution)/shard_map/pallas_call | solution.py:475
  21.8 0.0 copy-start
  21.8 0.0 copy-start.1
  21.8 0.0 copy-start.7
  21.8 0.0 copy-start.8
  21.9 3.8 %all-to-all-start.1 = ((bf16[16,56,512]{2,1,0:T(8,128)(2,1)}), bf16[16,56,512]{2,1,0:T(8,128)(2,1)S(1)}, u32[]{:S(2)}, u32[]{:S(2)}) async-start(bf16[16,56,512]{2,1,0:T(8,128)(2,1)} %shard_map.106), calls=%async_computation.1 | async-start | bytes 1835008 | tf_op jit(solution)/shard_map/all_to_all | solution.py:351
  25.6 0.0 copy-done.5
  25.6 0.1 collective-permute-start.16
  26.4 0.7 %collective-permute-done.16.refs_1_ = bf16[128,512]{1,0:T(8,128)(2,1)S(1)} collective-permute-done((bf16[128,512]{1,0:T(8,128)(2,1)S(1)}, bf16[128,512]{1,0:T(8,128)(2,1)S(1)}, u32[]{:S(2)}, u32[]{:S(2)}) %collective-permute-start.16) | collective-permute-done | bytes 131104 | tf_op jit(solution)/shard_map/ppermute | solution.py:460
  27.1 0.0 copy-done
  27.1 0.0 copy-done.1
  27.1 0.9 %copy-done.6 = bf16[1,128,512]{2,1,0:T(8,128)(2,1)S(1)} copy-done((bf16[1,128,512]{2,1,0:T(8,128)(2,1)S(1)}, bf16[1,128,512]{2,1,0:T(8,128)(2,1)}, u32[]{:S(2)}) %copy-start.6) | copy-done | bytes 131096
  28.0 0.6 %shard_map.109 = (bf16[8,256,80]{2,1,0:T(8,128)(2,1)S(1)}, bf16[512,256]{1,0:T(8,128)(2,1)S(1)}, bf16[512,512]{1,0:T(8,128)(2,1)S(1)}) custom-call(s32[1]{0:T(128)} %bitcast.2.refs_1_.col_ref, s32[1]{0:T(128)S(6)} %copy.28.length_ref, bf16[128,512]{1,0:T(8,128)(2,1)S(1)} %bitcast.16, bf16[128,512]{1,0:T(8,128)(2,1)S(1)} %collective-permute-done.16.refs_1_, ...), custom_call_target="tpu_custom_call" | custom-call | tf_op jit(solution)/shard_map/pallas_call | solution.py:462
  28.6 0.0 copy-start.3
  28.6 0.8 %copy-done.3 = bf16[512,512]{1,0:T(8,128)(2,1)} copy-done((bf16[512,512]{1,0:T(8,128)(2,1)}, bf16[512,512]{1,0:T(8,128)(2,1)S(1)}, u32[]{:S(2)}) %copy-start.3) | copy-done | bytes 524312
  29.4 0.8 %shard_map.107 = (f32[8,512]{1,0:T(8,128)S(1)}, s32[1]{0:T(128)}, bf16[384,128]{1,0:T(8,128)(2,1)S(1)}) custom-call(s32[1]{0:T(128)} %bitcast.7.refs_0_, s32[1]{0:T(128)} %bitcast.2.refs_1_.col_ref, s32[1,512]{1,0:T(1,128)S(1)} %copy-done.7, s32[4,32]{1,0:T(4,128)S(1)} %copy-done.8, bf16[384,128]{1,0:T(8,128)(2,1)S(1)} %bitcast.14), custom_call_target="tpu_custom_call" | custom-call | tf_op jit(solution)/shard_map/pallas_call | solution.py:415
  30.8 0.7 %conditional.1 = (bf16[128,512]{1,0:T(8,128)(2,1)}) conditional(s32[]{:T(128)} %bitcast.8, () %tuple.17, (s32[1]{0:T(128)}, bf16[384,128]{1,0:T(8,128)(2,1)S(1)}, bf16[2048,512]{1,0:T(8,128)(2,1)}, s32[]{:T(128)}) %tuple.38), branch_computations={%region_0.0_spmd, %region_1.0_spmd} | conditional | flops 1088 | bytes 1266468 | solution.py:446
  30.8 0.7 %broadcast.27 = bf16[128,512]{1,0:T(8,128)(2,1)} broadcast(bf16[]{:T(256)} %constant.7.clone), dimensions={} | broadcast | bytes 131074 | tf_op jit(solution)/shard_map/broadcast.1
  31.5 1.0 %shard_map.108.refs_0_ = bf16[128,512]{1,0:T(8,128)(2,1)S(1)} custom-call(bf16[128,512]{1,0:T(8,128)(2,1)} %get-tuple-element.65.came_ref), custom_call_target="tpu_custom_call" | custom-call | tf_op jit(solution)/shard_map/pallas_call | solution.py:448
  32.5 14.6 %all-to-all-done.1.fetched_ref = bf16[16,56,512]{2,1,0:T(8,128)(2,1)S(1)} async-done(((bf16[16,56,512]{2,1,0:T(8,128)(2,1)}), bf16[16,56,512]{2,1,0:T(8,128)(2,1)S(1)}, u32[]{:S(2)}, u32[]{:S(2)}) %all-to-all-start.1) | async-done | bytes 917536 | tf_op jit(solution)/shard_map/all_to_all | solution.py:351
  47.1 0.8 %shard_map.111 = bf16[256,512]{1,0:T(8,128)(2,1)S(1)} custom-call(s32[1]{0:T(128)} %bitcast.2.refs_1_.col_ref, f32[8,512]{1,0:T(8,128)S(1)} %get-tuple-element.41.known_ref, bf16[16,56,512]{2,1,0:T(8,128)(2,1)S(1)} %all-to-all-done.1.fetched_ref, bf16[128,512]{1,0:T(8,128)(2,1)S(1)} %shard_map.108.refs_0_), custom_call_target="tpu_custom_call" | custom-call | tf_op jit(solution)/shard_map/pallas_call | solution.py:496
  47.9 0.1 collective-permute-start.17
  48.0 1.2 %shard_map.110 = (bf16[128,2048]{1,0:T(8,128)(2,1)}, bf16[256,512]{1,0:T(8,128)(2,1)S(1)}) custom-call(s32[1]{0:T(128)} %bitcast.2.refs_1_.col_ref, f32[8,512]{1,0:T(8,128)S(1)} %get-tuple-element.41.known_ref, bf16[16,56,512]{2,1,0:T(8,128)(2,1)S(1)} %all-to-all-done.1.fetched_ref, bf16[128,512]{1,0:T(8,128)(2,1)S(1)} %shard_map.108.refs_0_), custom_call_target="tpu_custom_call" | custom-call | tf_op jit(solution)/shard_map/pallas_call | solution.py:510
  49.2 0.3 collective-permute-done.17.refs_1_
  49.5 0.0 copy-done.4
  49.5 2.3 %shard_map.112 = bf16[256,512]{1,0:T(8,128)(2,1)} custom-call(bf16[256,512]{1,0:T(8,128)(2,1)S(1)} %get-tuple-element.45.refs_0_, bf16[256,512]{1,0:T(8,128)(2,1)S(1)} %collective-permute-done.17.refs_1_, bf16[8,256,80]{2,1,0:T(8,128)(2,1)S(1)} %get-tuple-element.46.refs_2_, bf16[512,256]{1,0:T(8,128)(2,1)S(1)} %get-tuple-element.47.refs_3_, ...), custom_call_target="tpu_custom_call" | custom-call | tf_op jit(solution)/shard_map/pallas_call | solution.py:525
  (7 shorter events, 0.0 us)
Async XLA Ops:
  0.6 17.5 %collective-permute-start.15 = (bf16[2048,512]{1,0:T(8,128)(2,1)}, bf16[2048,512]{1,0:T(8,128)(2,1)}, u32[]{:S(2)}, u32[]{:S(2)}) collective-permute-start(bf16[2048,512]{1,0:T(8,128)(2,1)} %bitcast.17), channel_id=1, source_target_pairs={{0,1},{1,0},{2,3},{3,2},{4,5},{5,4},{6,7},{7,6},{8,9},{9,8},{10,11... | collective-permute-start | bytes 6291464 | tf_op jit(solution)/shard_map/ppermute | solution.py:413
  2.5 15.6 %all-to-all-start = ((bf16[16,24,128]{2,1,0:T(8,128)(2,1)}), bf16[16,24,128]{2,1,0:T(8,128)(2,1)S(1)}, u32[]{:S(2)}, u32[]{:S(2)}) async-start(bf16[16,24,128]{2,1,0:T(8,128)(2,1)} %shard_map.104), calls=%async_computation | async-start | bytes 196608 | tf_op jit(solution)/shard_map/all_to_all | solution.py:351
  18.1 7.5 %copy-start.5 = (bf16[1,128,512]{2,1,0:T(8,128)(2,1)S(1)}, bf16[1,128,512]{2,1,0:T(8,128)(2,1)}, u32[]{:S(2)}) copy-start(bf16[1,128,512]{2,1,0:T(8,128)(2,1)} %param.15) | copy-start | bytes 393220
  21.8 5.3 %copy-start = (bf16[512,1024]{1,0:T(8,128)(2,1)S(1)}, bf16[512,1024]{1,0:T(8,128)(2,1)}, u32[]{:S(2)}) copy-start(bf16[512,1024]{1,0:T(8,128)(2,1)} %refs_2_.3) | copy-start | bytes 3145732
  21.8 5.2 %copy-start.1 = (bf16[512,512]{1,0:T(8,128)(2,1)S(1)}, bf16[512,512]{1,0:T(8,128)(2,1)}, u32[]{:S(2)}) copy-start(bf16[512,512]{1,0:T(8,128)(2,1)} %refs_3_.3) | copy-start | bytes 1572868
  21.8 7.5 %copy-start.7 = (s32[1,512]{1,0:T(1,128)S(1)}, s32[1,512]{1,0:T(1,128)}, u32[]{:S(2)}) copy-start(s32[1,512]{1,0:T(1,128)} %refs_2_.2) | copy-start | bytes 6148
  21.8 7.5 %copy-start.8 = (s32[4,32]{1,0:T(4,128)S(1)}, s32[4,32]{1,0:T(4,128)}, u32[]{:S(2)}) copy-start(s32[4,32]{1,0:T(4,128)} %refs_3_.2) | copy-start | bytes 1540
  21.9 25.3 %all-to-all-start.1 = ((bf16[16,56,512]{2,1,0:T(8,128)(2,1)}), bf16[16,56,512]{2,1,0:T(8,128)(2,1)S(1)}, u32[]{:S(2)}, u32[]{:S(2)}) async-start(bf16[16,56,512]{2,1,0:T(8,128)(2,1)} %shard_map.106), calls=%async_computation.1 | async-start | bytes 1835008 | tf_op jit(solution)/shard_map/all_to_all | solution.py:351
  25.6 1.4 %collective-permute-start.16 = (bf16[128,512]{1,0:T(8,128)(2,1)S(1)}, bf16[128,512]{1,0:T(8,128)(2,1)S(1)}, u32[]{:S(2)}, u32[]{:S(2)}) collective-permute-start(bf16[128,512]{1,0:T(8,128)(2,1)S(1)} %bitcast.15), channel_id=1, source_target_pairs={{0,1},{1,0},{2,3},{3,2},{4,5},{5,4},{6,7},{7,6},{8,9},{9,8},{10,11... | collective-permute-start | bytes 393224 | tf_op jit(solution)/shard_map/ppermute | solution.py:460
  27.1 0.9 %copy-start.6 = (bf16[1,128,512]{2,1,0:T(8,128)(2,1)S(1)}, bf16[1,128,512]{2,1,0:T(8,128)(2,1)}, u32[]{:S(2)}) copy-start(bf16[1,128,512]{2,1,0:T(8,128)(2,1)} %param.15) | copy-start | bytes 393220
  28.6 0.8 %copy-start.3 = (bf16[512,512]{1,0:T(8,128)(2,1)}, bf16[512,512]{1,0:T(8,128)(2,1)S(1)}, u32[]{:S(2)}) copy-start(bf16[512,512]{1,0:T(8,128)(2,1)S(1)} %get-tuple-element.48.refs_4_) | copy-start | bytes 1572868
  31.5 18.0 %copy-start.2 = (bf16[512,512]{1,0:T(8,128)(2,1)S(1)}, bf16[512,512]{1,0:T(8,128)(2,1)}, u32[]{:S(2)}) copy-start(bf16[512,512]{1,0:T(8,128)(2,1)} %refs_5_.1) | copy-start | bytes 1572868
  31.5 18.0 %copy-start.4 = (bf16[512,512]{1,0:T(8,128)(2,1)S(1)}, bf16[512,512]{1,0:T(8,128)(2,1)}, u32[]{:S(2)}) copy-start(bf16[512,512]{1,0:T(8,128)(2,1)} %copy-done.3) | copy-start | bytes 1572868
  47.9 1.6 %collective-permute-start.17 = (bf16[256,512]{1,0:T(8,128)(2,1)S(1)}, bf16[256,512]{1,0:T(8,128)(2,1)S(1)}, u32[]{:S(2)}, u32[]{:S(2)}) collective-permute-start(bf16[256,512]{1,0:T(8,128)(2,1)S(1)} %shard_map.111), channel_id=1, source_target_pairs={{0,1},{1,0},{2,3},{3,2},{4,5},{5,4},{6,7},{7,6},{8,9},{9,8},{10,11... | collective-permute-start | bytes 786440 | tf_op jit(solution)/shard_map/ppermute | solution.py:507

commit v17 on v16

--- a/solution.py
+++ b/solution.py
@@ -209,8 +209,9 @@
     if spare:
         over, _ = asked(ids, other_ref[0].astype(jnp.float32), items_loc, main, spare)
         over = [jnp.where(own[r : r + 1] > float(main - spare), -1, over[r]) for r in range(n_lists)]
-    step = max(1, 288 // main)
+    step = max(1, 160 // main)
     chunks = [(first, min(n_lists, first + step)) for first in range(0, n_lists, step)]
+    ready = max(0, len(chunks) // 2 - 1)
     sends = []
 
     def finish(number):
@@ -230,7 +231,7 @@
         ).astype(jnp.bfloat16)
         for r in range(first, last):
             out_ref[r, kept:, :] = rows[(r - first) * main : (r - first + 1) * main]
-        if number == max(0, len(chunks) - 2):
+        if number == ready:
             if spare:
                 for load in loads:
                     load.wait()
@@ -241,7 +242,7 @@
                 ).astype(jnp.bfloat16)
             for done in range(number + 1):
                 finish(done)
-        elif number == len(chunks) - 1:
+        elif number > ready:
             finish(number)
     for send in sends:
         send.wait()
@@ -471,7 +472,7 @@
         compiler_params=PARAMS,
     )(col_arg, history_lengths, *hist, key_value_weight, query_weight)
 
-    step = max(1, 288 // main)
+    step = max(1, 160 // main)
     answers = pl.pallas_call(
         functools.partial(owner_kernel, n_lists, user_dev, digits, main, spare, width ** (-0.5)),
         out_shape=jax.ShapeDtypeStruct((n_lists, block, width), bf16),

time: 52.3 us -> 52.2 us (level)
  no operation moved by 1% of the time
where the time goes in v17:
time: 52.2 us; the launch traced here: 51.7 us
  waiting for transfers between devices  21.8 us (42%)
  Pallas kernels  13.2 us (25%)
  starting transfers between devices  12.3 us (24%)
  local copies, waits for them, and re-layouts  2.4 us (5%)
  between operations  2.08 us (4%)
    all_to_all x2, waiting for transfers between devices, exchange(): lax.all_to_all(value, 'lists', split_axis=0, concat_axis=0, tiled=True)  20.7 us
    all_to_all x2, starting transfers between devices, exchange(): lax.all_to_all(value, 'lists', split_axis=0, concat_axis=0, tiled=True)  11.7 us
    pallas_call x1, Pallas kernels, shards(): pl.pallas_call(functools.partial(owner_kernel, n_lists, user_dev, digits,...  3.59 us
    pallas_call x1, Pallas kernels, shards(): pl.pallas_call(functools.partial(attend_kernel, n_users), out_shape=jax.S...  2.32 us
    unnamed x18, local copies, waits for them, and re-layouts  1.73 us
    pallas_call x1, Pallas kernels, shards(): pl.pallas_call(items_kernel, out_shape=jax.ShapeDtypeStruct((items_loc, w...  1.55 us
    pallas_call x1, Pallas kernels, shards(): pl.pallas_call(functools.partial(pack_kernel, digits), out_shape=jax.Shap...  1.36 us
    pallas_call x1, Pallas kernels, shards(): pl.pallas_call(functools.partial(expand_kernel, user_dev, pieces, kept),...  1.17 us
  transfers between devices with their start and end apart: 5, of which 4 were waited for; matrix products, arithmetic and copies ran while one was open for 1% of the time, Pallas kernels for 12%

profile of v17, /device:TPU:0, one launch (start us, length us, event | category | flops | bytes accessed | tf_op | source)
XLA Modules:
  0.0 51.7 jit_solution(5010636084717847097)
XLA Ops:
  0.6 0.5 %collective-permute-start.15 = (bf16[2048,512]{1,0:T(8,128)(2,1)}, bf16[2048,512]{1,0:T(8,128)(2,1)}, u32[]{:S(2)}, u32[]{:S(2)}) collective-permute-start(bf16[2048,512]{1,0:T(8,128)(2,1)} %bitcast.17), channel_id=1, source_target_pairs={{0,1},{1,0},{2,3},{3,2},{4,5},{5,4},{6,7},{7,6},{8,9},{9,8},{10,11... | collective-permute-start | bytes 6291464 | tf_op jit(solution)/shard_map/ppermute | solution.py:414
  1.1 1.4 %shard_map.104 = bf16[16,24,128]{2,1,0:T(8,128)(2,1)} custom-call(s32[1,512]{1,0:T(1,128)} %refs_2_.2, bf16[4,512]{1,0:T(4,128)(2,1)} %vectors_ref.1), custom_call_target="tpu_custom_call" | custom-call | tf_op jit(solution)/shard_map/pallas_call | solution.py:392
  2.5 7.9 %all-to-all-start = ((bf16[16,24,128]{2,1,0:T(8,128)(2,1)}), bf16[16,24,128]{2,1,0:T(8,128)(2,1)S(1)}, u32[]{:S(2)}, u32[]{:S(2)}) async-start(bf16[16,24,128]{2,1,0:T(8,128)(2,1)} %shard_map.104), calls=%async_computation | async-start | bytes 196608 | tf_op jit(solution)/shard_map/all_to_all | solution.py:352
  10.4 1.6 %shard_map.105.items_ref = bf16[2048,512]{1,0:T(8,128)(2,1)S(1)} custom-call(bf16[2048,512]{1,0:T(8,128)(2,1)} %bitcast.18), custom_call_target="tpu_custom_call" | custom-call | tf_op jit(solution)/shard_map/pallas_call | solution.py:402
  12.0 6.1 %all-to-all-done = bf16[16,24,128]{2,1,0:T(8,128)(2,1)S(1)} async-done(((bf16[16,24,128]{2,1,0:T(8,128)(2,1)}), bf16[16,24,128]{2,1,0:T(8,128)(2,1)S(1)}, u32[]{:S(2)}, u32[]{:S(2)}) %all-to-all-start) | async-done | bytes 98336 | tf_op jit(solution)/shard_map/all_to_all | solution.py:352
  18.1 0.0 collective-permute-done.15.refs_0_
  18.1 3.6 %shard_map.106 = bf16[16,56,512]{2,1,0:T(8,128)(2,1)} custom-call(s32[1]{0:T(128)} %bitcast.3.base_ref, s32[1]{0:T(128)} %bitcast.4.other_ref, bf16[384,128]{1,0:T(8,128)(2,1)S(1)} %bitcast.13, bf16[2048,512]{1,0:T(8,128)(2,1)S(1)} %shard_map.105.items_ref, bf16[2048,512]{1,0:T(8,128)(2,1)} %collective-permute-done.15.refs_0_), custom_call_target="tpu_custom_call" | custom-call | tf_op jit(solution)/shard_map/pallas_call | solution.py:476
  21.7 0.0 copy-start
  21.7 0.0 copy-start.1
  21.7 0.0 copy-start.7
  21.7 0.0 copy-start.8
  21.7 3.8 %all-to-all-start.1 = ((bf16[16,56,512]{2,1,0:T(8,128)(2,1)}), bf16[16,56,512]{2,1,0:T(8,128)(2,1)S(1)}, u32[]{:S(2)}, u32[]{:S(2)}) async-start(bf16[16,56,512]{2,1,0:T(8,128)(2,1)} %shard_map.106), calls=%async_computation.1 | async-start | bytes 1835008 | tf_op jit(solution)/shard_map/all_to_all | solution.py:352
  25.5 0.0 copy-done.5
  25.5 0.1 collective-permute-start.16
  26.3 0.7 %collective-permute-done.16.refs_1_ = bf16[128,512]{1,0:T(8,128)(2,1)S(1)} collective-permute-done((bf16[128,512]{1,0:T(8,128)(2,1)S(1)}, bf16[128,512]{1,0:T(8,128)(2,1)S(1)}, u32[]{:S(2)}, u32[]{:S(2)}) %collective-permute-start.16) | collective-permute-done | bytes 131104 | tf_op jit(solution)/shard_map/ppermute | solution.py:461
  26.9 0.0 copy-done
  27.0 0.0 copy-done.1
  27.0 0.9 %copy-done.6 = bf16[1,128,512]{2,1,0:T(8,128)(2,1)S(1)} copy-done((bf16[1,128,512]{2,1,0:T(8,128)(2,1)S(1)}, bf16[1,128,512]{2,1,0:T(8,128)(2,1)}, u32[]{:S(2)}) %copy-start.6) | copy-done | bytes 131096
  27.9 0.6 %shard_map.109 = (bf16[8,256,80]{2,1,0:T(8,128)(2,1)S(1)}, bf16[512,256]{1,0:T(8,128)(2,1)S(1)}, bf16[512,512]{1,0:T(8,128)(2,1)S(1)}) custom-call(s32[1]{0:T(128)} %bitcast.2.refs_1_.col_ref, s32[1]{0:T(128)S(6)} %copy.28.length_ref, bf16[128,512]{1,0:T(8,128)(2,1)S(1)} %bitcast.16, bf16[128,512]{1,0:T(8,128)(2,1)S(1)} %collective-permute-done.16.refs_1_, ...), custom_call_target="tpu_custom_call" | custom-call | tf_op jit(solution)/shard_map/pallas_call | solution.py:463
  28.4 0.0 copy-start.3
  28.5 0.8 %copy-done.3 = bf16[512,512]{1,0:T(8,128)(2,1)} copy-done((bf16[512,512]{1,0:T(8,128)(2,1)}, bf16[512,512]{1,0:T(8,128)(2,1)S(1)}, u32[]{:S(2)}) %copy-start.3) | copy-done | bytes 524312
  29.2 0.0 copy-done.8
  29.2 0.8 %shard_map.107 = (f32[8,512]{1,0:T(8,128)S(1)}, s32[1]{0:T(128)}, bf16[384,128]{1,0:T(8,128)(2,1)S(1)}) custom-call(s32[1]{0:T(128)} %bitcast.7.refs_0_, s32[1]{0:T(128)} %bitcast.2.refs_1_.col_ref, s32[1,512]{1,0:T(1,128)S(1)} %copy-done.7, s32[4,32]{1,0:T(4,128)S(1)} %copy-done.8, bf16[384,128]{1,0:T(8,128)(2,1)S(1)} %bitcast.14), custom_call_target="tpu_custom_call" | custom-call | tf_op jit(solution)/shard_map/pallas_call | solution.py:416
  30.7 0.7 %conditional.1 = (bf16[128,512]{1,0:T(8,128)(2,1)}) conditional(s32[]{:T(128)} %bitcast.8, () %tuple.17, (s32[1]{0:T(128)}, bf16[384,128]{1,0:T(8,128)(2,1)S(1)}, bf16[2048,512]{1,0:T(8,128)(2,1)}, s32[]{:T(128)}) %tuple.38), branch_computations={%region_0.0_spmd, %region_1.0_spmd} | conditional | flops 1088 | bytes 1266468 | solution.py:447
  30.7 0.7 %broadcast.27 = bf16[128,512]{1,0:T(8,128)(2,1)} broadcast(bf16[]{:T(256)} %constant.7.clone), dimensions={} | broadcast | bytes 131074 | tf_op jit(solution)/shard_map/broadcast.1
  31.4 1.0 %shard_map.108.refs_0_ = bf16[128,512]{1,0:T(8,128)(2,1)S(1)} custom-call(bf16[128,512]{1,0:T(8,128)(2,1)} %get-tuple-element.65.came_ref), custom_call_target="tpu_custom_call" | custom-call | tf_op jit(solution)/shard_map/pallas_call | solution.py:449
  32.4 14.6 %all-to-all-done.1.fetched_ref = bf16[16,56,512]{2,1,0:T(8,128)(2,1)S(1)} async-done(((bf16[16,56,512]{2,1,0:T(8,128)(2,1)}), bf16[16,56,512]{2,1,0:T(8,128)(2,1)S(1)}, u32[]{:S(2)}, u32[]{:S(2)}) %all-to-all-start.1) | async-done | bytes 917536 | tf_op jit(solution)/shard_map/all_to_all | solution.py:352
  47.0 0.8 %shard_map.111 = bf16[256,512]{1,0:T(8,128)(2,1)S(1)} custom-call(s32[1]{0:T(128)} %bitcast.2.refs_1_.col_ref, f32[8,512]{1,0:T(8,128)S(1)} %get-tuple-element.41.known_ref, bf16[16,56,512]{2,1,0:T(8,128)(2,1)S(1)} %all-to-all-done.1.fetched_ref, bf16[128,512]{1,0:T(8,128)(2,1)S(1)} %shard_map.108.refs_0_), custom_call_target="tpu_custom_call" | custom-call | tf_op jit(solution)/shard_map/pallas_call | solution.py:497
  47.8 0.1 collective-permute-start.17
  47.9 1.2 %shard_map.110 = (bf16[128,2048]{1,0:T(8,128)(2,1)}, bf16[256,512]{1,0:T(8,128)(2,1)S(1)}) custom-call(s32[1]{0:T(128)} %bitcast.2.refs_1_.col_ref, f32[8,512]{1,0:T(8,128)S(1)} %get-tuple-element.41.known_ref, bf16[16,56,512]{2,1,0:T(8,128)(2,1)S(1)} %all-to-all-done.1.fetched_ref, bf16[128,512]{1,0:T(8,128)(2,1)S(1)} %shard_map.108.refs_0_), custom_call_target="tpu_custom_call" | custom-call | tf_op jit(solution)/shard_map/pallas_call | solution.py:511
  49.1 0.3 collective-permute-done.17.refs_1_
  49.4 2.3 %shard_map.112 = bf16[256,512]{1,0:T(8,128)(2,1)} custom-call(bf16[256,512]{1,0:T(8,128)(2,1)S(1)} %get-tuple-element.45.refs_0_, bf16[256,512]{1,0:T(8,128)(2,1)S(1)} %collective-permute-done.17.refs_1_, bf16[8,256,80]{2,1,0:T(8,128)(2,1)S(1)} %get-tuple-element.46.refs_2_, bf16[512,256]{1,0:T(8,128)(2,1)S(1)} %get-tuple-element.47.refs_3_, ...), custom_call_target="tpu_custom_call" | custom-call | tf_op jit(solution)/shard_map/pallas_call | solution.py:526
  (7 shorter events, 0.0 us)
Async XLA Ops:
  0.6 17.5 %collective-permute-start.15 = (bf16[2048,512]{1,0:T(8,128)(2,1)}, bf16[2048,512]{1,0:T(8,128)(2,1)}, u32[]{:S(2)}, u32[]{:S(2)}) collective-permute-start(bf16[2048,512]{1,0:T(8,128)(2,1)} %bitcast.17), channel_id=1, source_target_pairs={{0,1},{1,0},{2,3},{3,2},{4,5},{5,4},{6,7},{7,6},{8,9},{9,8},{10,11... | collective-permute-start | bytes 6291464 | tf_op jit(solution)/shard_map/ppermute | solution.py:414
  2.5 15.6 %all-to-all-start = ((bf16[16,24,128]{2,1,0:T(8,128)(2,1)}), bf16[16,24,128]{2,1,0:T(8,128)(2,1)S(1)}, u32[]{:S(2)}, u32[]{:S(2)}) async-start(bf16[16,24,128]{2,1,0:T(8,128)(2,1)} %shard_map.104), calls=%async_computation | async-start | bytes 196608 | tf_op jit(solution)/shard_map/all_to_all | solution.py:352
  18.1 7.4 %copy-start.5 = (bf16[1,128,512]{2,1,0:T(8,128)(2,1)S(1)}, bf16[1,128,512]{2,1,0:T(8,128)(2,1)}, u32[]{:S(2)}) copy-start(bf16[1,128,512]{2,1,0:T(8,128)(2,1)} %param.15) | copy-start | bytes 393220
  21.7 5.3 %copy-start = (bf16[512,1024]{1,0:T(8,128)(2,1)S(1)}, bf16[512,1024]{1,0:T(8,128)(2,1)}, u32[]{:S(2)}) copy-start(bf16[512,1024]{1,0:T(8,128)(2,1)} %refs_2_.3) | copy-start | bytes 3145732
  21.7 5.2 %copy-start.1 = (bf16[512,512]{1,0:T(8,128)(2,1)S(1)}, bf16[512,512]{1,0:T(8,128)(2,1)}, u32[]{:S(2)}) copy-start(bf16[512,512]{1,0:T(8,128)(2,1)} %refs_3_.3) | copy-start | bytes 1572868
  21.7 7.5 %copy-start.7 = (s32[1,512]{1,0:T(1,128)S(1)}, s32[1,512]{1,0:T(1,128)}, u32[]{:S(2)}) copy-start(s32[1,512]{1,0:T(1,128)} %refs_2_.2) | copy-start | bytes 6148
  21.7 7.5 %copy-start.8 = (s32[4,32]{1,0:T(4,128)S(1)}, s32[4,32]{1,0:T(4,128)}, u32[]{:S(2)}) copy-start(s32[4,32]{1,0:T(4,128)} %refs_3_.2) | copy-start | bytes 1540
  21.7 25.3 %all-to-all-start.1 = ((bf16[16,56,512]{2,1,0:T(8,128)(2,1)}), bf16[16,56,512]{2,1,0:T(8,128)(2,1)S(1)}, u32[]{:S(2)}, u32[]{:S(2)}) async-start(bf16[16,56,512]{2,1,0:T(8,128)(2,1)} %shard_map.106), calls=%async_computation.1 | async-start | bytes 1835008 | tf_op jit(solution)/shard_map/all_to_all | solution.py:352
  25.5 1.4 %collective-permute-start.16 = (bf16[128,512]{1,0:T(8,128)(2,1)S(1)}, bf16[128,512]{1,0:T(8,128)(2,1)S(1)}, u32[]{:S(2)}, u32[]{:S(2)}) collective-permute-start(bf16[128,512]{1,0:T(8,128)(2,1)S(1)} %bitcast.15), channel_id=1, source_target_pairs={{0,1},{1,0},{2,3},{3,2},{4,5},{5,4},{6,7},{7,6},{8,9},{9,8},{10,11... | collective-permute-start | bytes 393224 | tf_op jit(solution)/shard_map/ppermute | solution.py:461
  27.0 0.9 %copy-start.6 = (bf16[1,128,512]{2,1,0:T(8,128)(2,1)S(1)}, bf16[1,128,512]{2,1,0:T(8,128)(2,1)}, u32[]{:S(2)}) copy-start(bf16[1,128,512]{2,1,0:T(8,128)(2,1)} %param.15) | copy-start | bytes 393220
  28.4 0.8 %copy-start.3 = (bf16[512,512]{1,0:T(8,128)(2,1)}, bf16[512,512]{1,0:T(8,128)(2,1)S(1)}, u32[]{:S(2)}) copy-start(bf16[512,512]{1,0:T(8,128)(2,1)S(1)} %get-tuple-element.48.refs_4_) | copy-start | bytes 1572868
  31.4 18.0 %copy-start.2 = (bf16[512,512]{1,0:T(8,128)(2,1)S(1)}, bf16[512,512]{1,0:T(8,128)(2,1)}, u32[]{:S(2)}) copy-start(bf16[512,512]{1,0:T(8,128)(2,1)} %refs_5_.1) | copy-start | bytes 1572868
  31.4 18.0 %copy-start.4 = (bf16[512,512]{1,0:T(8,128)(2,1)S(1)}, bf16[512,512]{1,0:T(8,128)(2,1)}, u32[]{:S(2)}) copy-start(bf16[512,512]{1,0:T(8,128)(2,1)} %copy-done.3) | copy-start | bytes 1572868
  47.8 1.6 %collective-permute-start.17 = (bf16[256,512]{1,0:T(8,128)(2,1)S(1)}, bf16[256,512]{1,0:T(8,128)(2,1)S(1)}, u32[]{:S(2)}, u32[]{:S(2)}) collective-permute-start(bf16[256,512]{1,0:T(8,128)(2,1)S(1)} %shard_map.111), channel_id=1, source_target_pairs={{0,1},{1,0},{2,3},{3,2},{4,5},{5,4},{6,7},{7,6},{8,9},{9,8},{10,11... | collective-permute-start | bytes 786440 | tf_op jit(solution)/shard_map/ppermute | solution.py:508

commit v18 on v16

--- a/solution.py
+++ b/solution.py
@@ -305,11 +305,11 @@
         query = jnp.concatenate([queries[h * head_dim : (h + 1) * head_dim], one], axis=0)
         return jnp.dot(keys_ref[h], query, preferred_element_type=jnp.float32)
 
-    ahead = [score(h) for h in range(min(2, heads))]
+    ahead = [score(h) for h in range(min(3, heads))]
     mixed = []
     for h in range(heads):
-        if h + 2 < heads:
-            ahead.append(score(h + 2))
+        if h + 3 < heads:
+            ahead.append(score(h + 3))
         exponentials = jnp.exp(ahead[h] - jnp.max(ahead[h], axis=0, keepdims=True))
         total = jnp.sum(exponentials, axis=0, keepdims=True)
         span = slice(h * head_dim, (h + 1) * head_dim)

time: 52.3 us -> 52.1 us (level)
  transfers between devices with their start and end apart: 5 -> 5, of which waited for: 4 -> 4; matrix products, arithmetic and copies ran while one was open for 1% -> 1% of each run, Pallas kernels for 12% -> 13%
where the time goes in v18:
time: 52.1 us; the launch traced here: 51.7 us
  waiting for transfers between devices  21.8 us (42%)
  Pallas kernels  13.2 us (25%)
  starting transfers between devices  12.3 us (24%)
  local copies, waits for them, and re-layouts  2.4 us (5%)
  between operations  2.08 us (4%)
    all_to_all x2, waiting for transfers between devices, exchange(): lax.all_to_all(value, 'lists', split_axis=0, concat_axis=0, tiled=True)  20.7 us
    all_to_all x2, starting transfers between devices, exchange(): lax.all_to_all(value, 'lists', split_axis=0, concat_axis=0, tiled=True)  11.7 us
    pallas_call x1, Pallas kernels, shards(): pl.pallas_call(functools.partial(owner_kernel, n_lists, user_dev, digits,...  3.7 us
    pallas_call x1, Pallas kernels, shards(): pl.pallas_call(functools.partial(attend_kernel, n_users), out_shape=jax.S...  2.2 us
    unnamed x18, local copies, waits for them, and re-layouts  1.73 us
    pallas_call x1, Pallas kernels, shards(): pl.pallas_call(items_kernel, out_shape=jax.ShapeDtypeStruct((items_loc, w...  1.55 us
    pallas_call x1, Pallas kernels, shards(): pl.pallas_call(functools.partial(pack_kernel, digits), out_shape=jax.Shap...  1.36 us
    pallas_call x1, Pallas kernels, shards(): pl.pallas_call(functools.partial(expand_kernel, user_dev, pieces, kept),...  1.17 us
  transfers between devices with their start and end apart: 5, of which 4 were waited for; matrix products, arithmetic and copies ran while one was open for 1% of the time, Pallas kernels for 13%

profile of v18, /device:TPU:0, one launch (start us, length us, event | category | flops | bytes accessed | tf_op | source)
XLA Modules:
  0.0 51.7 jit_solution(3224189849936672890)
XLA Ops:
  0.6 0.5 %collective-permute-start.15 = (bf16[2048,512]{1,0:T(8,128)(2,1)}, bf16[2048,512]{1,0:T(8,128)(2,1)}, u32[]{:S(2)}, u32[]{:S(2)}) collective-permute-start(bf16[2048,512]{1,0:T(8,128)(2,1)} %bitcast.17), channel_id=1, source_target_pairs={{0,1},{1,0},{2,3},{3,2},{4,5},{5,4},{6,7},{7,6},{8,9},{9,8},{10,11... | collective-permute-start | bytes 6291464 | tf_op jit(solution)/shard_map/ppermute | solution.py:413
  1.1 1.4 %shard_map.104 = bf16[16,24,128]{2,1,0:T(8,128)(2,1)} custom-call(s32[1,512]{1,0:T(1,128)} %refs_2_.2, bf16[4,512]{1,0:T(4,128)(2,1)} %vectors_ref.1), custom_call_target="tpu_custom_call" | custom-call | tf_op jit(solution)/shard_map/pallas_call | solution.py:391
  2.5 7.9 %all-to-all-start = ((bf16[16,24,128]{2,1,0:T(8,128)(2,1)}), bf16[16,24,128]{2,1,0:T(8,128)(2,1)S(1)}, u32[]{:S(2)}, u32[]{:S(2)}) async-start(bf16[16,24,128]{2,1,0:T(8,128)(2,1)} %shard_map.104), calls=%async_computation | async-start | bytes 196608 | tf_op jit(solution)/shard_map/all_to_all | solution.py:351
  10.4 1.6 %shard_map.105.items_ref = bf16[2048,512]{1,0:T(8,128)(2,1)S(1)} custom-call(bf16[2048,512]{1,0:T(8,128)(2,1)} %bitcast.18), custom_call_target="tpu_custom_call" | custom-call | tf_op jit(solution)/shard_map/pallas_call | solution.py:401
  12.0 6.1 %all-to-all-done = bf16[16,24,128]{2,1,0:T(8,128)(2,1)S(1)} async-done(((bf16[16,24,128]{2,1,0:T(8,128)(2,1)}), bf16[16,24,128]{2,1,0:T(8,128)(2,1)S(1)}, u32[]{:S(2)}, u32[]{:S(2)}) %all-to-all-start) | async-done | bytes 98336 | tf_op jit(solution)/shard_map/all_to_all | solution.py:351
  18.1 0.0 collective-permute-done.15.refs_0_
  18.1 3.7 %shard_map.106 = bf16[16,56,512]{2,1,0:T(8,128)(2,1)} custom-call(s32[1]{0:T(128)} %bitcast.3.base_ref, s32[1]{0:T(128)} %bitcast.4.other_ref, bf16[384,128]{1,0:T(8,128)(2,1)S(1)} %bitcast.13, bf16[2048,512]{1,0:T(8,128)(2,1)S(1)} %shard_map.105.items_ref, bf16[2048,512]{1,0:T(8,128)(2,1)} %collective-permute-done.15.refs_0_), custom_call_target="tpu_custom_call" | custom-call | tf_op jit(solution)/shard_map/pallas_call | solution.py:475
  21.8 0.0 copy-start
  21.8 0.0 copy-start.1
  21.8 0.0 copy-start.7
  21.8 0.0 copy-start.8
  21.9 3.8 %all-to-all-start.1 = ((bf16[16,56,512]{2,1,0:T(8,128)(2,1)}), bf16[16,56,512]{2,1,0:T(8,128)(2,1)S(1)}, u32[]{:S(2)}, u32[]{:S(2)}) async-start(bf16[16,56,512]{2,1,0:T(8,128)(2,1)} %shard_map.106), calls=%async_computation.1 | async-start | bytes 1835008 | tf_op jit(solution)/shard_map/all_to_all | solution.py:351
  25.6 0.0 copy-done.5
  25.6 0.1 collective-permute-start.16
  26.4 0.7 %collective-permute-done.16.refs_1_ = bf16[128,512]{1,0:T(8,128)(2,1)S(1)} collective-permute-done((bf16[128,512]{1,0:T(8,128)(2,1)S(1)}, bf16[128,512]{1,0:T(8,128)(2,1)S(1)}, u32[]{:S(2)}, u32[]{:S(2)}) %collective-permute-start.16) | collective-permute-done | bytes 131104 | tf_op jit(solution)/shard_map/ppermute | solution.py:460
  27.1 0.0 copy-done
  27.1 0.0 copy-done.1
  27.1 0.9 %copy-done.6 = bf16[1,128,512]{2,1,0:T(8,128)(2,1)S(1)} copy-done((bf16[1,128,512]{2,1,0:T(8,128)(2,1)S(1)}, bf16[1,128,512]{2,1,0:T(8,128)(2,1)}, u32[]{:S(2)}) %copy-start.6) | copy-done | bytes 131096
  28.0 0.6 %shard_map.109 = (bf16[8,256,80]{2,1,0:T(8,128)(2,1)S(1)}, bf16[512,256]{1,0:T(8,128)(2,1)S(1)}, bf16[512,512]{1,0:T(8,128)(2,1)S(1)}) custom-call(s32[1]{0:T(128)} %bitcast.2.refs_1_.col_ref, s32[1]{0:T(128)S(6)} %copy.28.length_ref, bf16[128,512]{1,0:T(8,128)(2,1)S(1)} %bitcast.16, bf16[128,512]{1,0:T(8,128)(2,1)S(1)} %collective-permute-done.16.refs_1_, ...), custom_call_target="tpu_custom_call" | custom-call | tf_op jit(solution)/shard_map/pallas_call | solution.py:462
  28.6 0.0 copy-start.3
  28.6 0.8 %copy-done.3 = bf16[512,512]{1,0:T(8,128)(2,1)} copy-done((bf16[512,512]{1,0:T(8,128)(2,1)}, bf16[512,512]{1,0:T(8,128)(2,1)S(1)}, u32[]{:S(2)}) %copy-start.3) | copy-done | bytes 524312
  29.4 0.8 %shard_map.107 = (f32[8,512]{1,0:T(8,128)S(1)}, s32[1]{0:T(128)}, bf16[384,128]{1,0:T(8,128)(2,1)S(1)}) custom-call(s32[1]{0:T(128)} %bitcast.7.refs_0_, s32[1]{0:T(128)} %bitcast.2.refs_1_.col_ref, s32[1,512]{1,0:T(1,128)S(1)} %copy-done.7, s32[4,32]{1,0:T(4,128)S(1)} %copy-done.8, bf16[384,128]{1,0:T(8,128)(2,1)S(1)} %bitcast.14), custom_call_target="tpu_custom_call" | custom-call | tf_op jit(solution)/shard_map/pallas_call | solution.py:415
  30.8 0.7 %conditional.1 = (bf16[128,512]{1,0:T(8,128)(2,1)}) conditional(s32[]{:T(128)} %bitcast.8, () %tuple.17, (s32[1]{0:T(128)}, bf16[384,128]{1,0:T(8,128)(2,1)S(1)}, bf16[2048,512]{1,0:T(8,128)(2,1)}, s32[]{:T(128)}) %tuple.38), branch_computations={%region_0.0_spmd, %region_1.0_spmd} | conditional | flops 1088 | bytes 1266468 | solution.py:446
  30.8 0.7 %broadcast.27 = bf16[128,512]{1,0:T(8,128)(2,1)} broadcast(bf16[]{:T(256)} %constant.7.clone), dimensions={} | broadcast | bytes 131074 | tf_op jit(solution)/shard_map/broadcast.1
  31.5 1.0 %shard_map.108.refs_0_ = bf16[128,512]{1,0:T(8,128)(2,1)S(1)} custom-call(bf16[128,512]{1,0:T(8,128)(2,1)} %get-tuple-element.65.came_ref), custom_call_target="tpu_custom_call" | custom-call | tf_op jit(solution)/shard_map/pallas_call | solution.py:448
  32.5 14.6 %all-to-all-done.1.fetched_ref = bf16[16,56,512]{2,1,0:T(8,128)(2,1)S(1)} async-done(((bf16[16,56,512]{2,1,0:T(8,128)(2,1)}), bf16[16,56,512]{2,1,0:T(8,128)(2,1)S(1)}, u32[]{:S(2)}, u32[]{:S(2)}) %all-to-all-start.1) | async-done | bytes 917536 | tf_op jit(solution)/shard_map/all_to_all | solution.py:351
  47.1 0.8 %shard_map.111 = bf16[256,512]{1,0:T(8,128)(2,1)S(1)} custom-call(s32[1]{0:T(128)} %bitcast.2.refs_1_.col_ref, f32[8,512]{1,0:T(8,128)S(1)} %get-tuple-element.41.known_ref, bf16[16,56,512]{2,1,0:T(8,128)(2,1)S(1)} %all-to-all-done.1.fetched_ref, bf16[128,512]{1,0:T(8,128)(2,1)S(1)} %shard_map.108.refs_0_), custom_call_target="tpu_custom_call" | custom-call | tf_op jit(solution)/shard_map/pallas_call | solution.py:496
  47.9 0.1 collective-permute-start.17
  48.0 1.2 %shard_map.110 = (bf16[128,2048]{1,0:T(8,128)(2,1)}, bf16[256,512]{1,0:T(8,128)(2,1)S(1)}) custom-call(s32[1]{0:T(128)} %bitcast.2.refs_1_.col_ref, f32[8,512]{1,0:T(8,128)S(1)} %get-tuple-element.41.known_ref, bf16[16,56,512]{2,1,0:T(8,128)(2,1)S(1)} %all-to-all-done.1.fetched_ref, bf16[128,512]{1,0:T(8,128)(2,1)S(1)} %shard_map.108.refs_0_), custom_call_target="tpu_custom_call" | custom-call | tf_op jit(solution)/shard_map/pallas_call | solution.py:510
  49.2 0.3 collective-permute-done.17.refs_1_
  49.5 0.0 copy-done.4
  49.5 2.2 %shard_map.112 = bf16[256,512]{1,0:T(8,128)(2,1)} custom-call(bf16[256,512]{1,0:T(8,128)(2,1)S(1)} %get-tuple-element.45.refs_0_, bf16[256,512]{1,0:T(8,128)(2,1)S(1)} %collective-permute-done.17.refs_1_, bf16[8,256,80]{2,1,0:T(8,128)(2,1)S(1)} %get-tuple-element.46.refs_2_, bf16[512,256]{1,0:T(8,128)(2,1)S(1)} %get-tuple-element.47.refs_3_, ...), custom_call_target="tpu_custom_call" | custom-call | tf_op jit(solution)/shard_map/pallas_call | solution.py:525
  (7 shorter events, 0.0 us)
Async XLA Ops:
  0.6 17.5 %collective-permute-start.15 = (bf16[2048,512]{1,0:T(8,128)(2,1)}, bf16[2048,512]{1,0:T(8,128)(2,1)}, u32[]{:S(2)}, u32[]{:S(2)}) collective-permute-start(bf16[2048,512]{1,0:T(8,128)(2,1)} %bitcast.17), channel_id=1, source_target_pairs={{0,1},{1,0},{2,3},{3,2},{4,5},{5,4},{6,7},{7,6},{8,9},{9,8},{10,11... | collective-permute-start | bytes 6291464 | tf_op jit(solution)/shard_map/ppermute | solution.py:413
  2.5 15.6 %all-to-all-start = ((bf16[16,24,128]{2,1,0:T(8,128)(2,1)}), bf16[16,24,128]{2,1,0:T(8,128)(2,1)S(1)}, u32[]{:S(2)}, u32[]{:S(2)}) async-start(bf16[16,24,128]{2,1,0:T(8,128)(2,1)} %shard_map.104), calls=%async_computation | async-start | bytes 196608 | tf_op jit(solution)/shard_map/all_to_all | solution.py:351
  18.1 7.5 %copy-start.5 = (bf16[1,128,512]{2,1,0:T(8,128)(2,1)S(1)}, bf16[1,128,512]{2,1,0:T(8,128)(2,1)}, u32[]{:S(2)}) copy-start(bf16[1,128,512]{2,1,0:T(8,128)(2,1)} %param.15) | copy-start | bytes 393220
  21.8 5.3 %copy-start = (bf16[512,1024]{1,0:T(8,128)(2,1)S(1)}, bf16[512,1024]{1,0:T(8,128)(2,1)}, u32[]{:S(2)}) copy-start(bf16[512,1024]{1,0:T(8,128)(2,1)} %refs_2_.3) | copy-start | bytes 3145732
  21.8 5.2 %copy-start.1 = (bf16[512,512]{1,0:T(8,128)(2,1)S(1)}, bf16[512,512]{1,0:T(8,128)(2,1)}, u32[]{:S(2)}) copy-start(bf16[512,512]{1,0:T(8,128)(2,1)} %refs_3_.3) | copy-start | bytes 1572868
  21.8 7.5 %copy-start.7 = (s32[1,512]{1,0:T(1,128)S(1)}, s32[1,512]{1,0:T(1,128)}, u32[]{:S(2)}) copy-start(s32[1,512]{1,0:T(1,128)} %refs_2_.2) | copy-start | bytes 6148
  21.8 7.5 %copy-start.8 = (s32[4,32]{1,0:T(4,128)S(1)}, s32[4,32]{1,0:T(4,128)}, u32[]{:S(2)}) copy-start(s32[4,32]{1,0:T(4,128)} %refs_3_.2) | copy-start | bytes 1540
  21.9 25.3 %all-to-all-start.1 = ((bf16[16,56,512]{2,1,0:T(8,128)(2,1)}), bf16[16,56,512]{2,1,0:T(8,128)(2,1)S(1)}, u32[]{:S(2)}, u32[]{:S(2)}) async-start(bf16[16,56,512]{2,1,0:T(8,128)(2,1)} %shard_map.106), calls=%async_computation.1 | async-start | bytes 1835008 | tf_op jit(solution)/shard_map/all_to_all | solution.py:351
  25.6 1.4 %collective-permute-start.16 = (bf16[128,512]{1,0:T(8,128)(2,1)S(1)}, bf16[128,512]{1,0:T(8,128)(2,1)S(1)}, u32[]{:S(2)}, u32[]{:S(2)}) collective-permute-start(bf16[128,512]{1,0:T(8,128)(2,1)S(1)} %bitcast.15), channel_id=1, source_target_pairs={{0,1},{1,0},{2,3},{3,2},{4,5},{5,4},{6,7},{7,6},{8,9},{9,8},{10,11... | collective-permute-start | bytes 393224 | tf_op jit(solution)/shard_map/ppermute | solution.py:460
  27.1 0.9 %copy-start.6 = (bf16[1,128,512]{2,1,0:T(8,128)(2,1)S(1)}, bf16[1,128,512]{2,1,0:T(8,128)(2,1)}, u32[]{:S(2)}) copy-start(bf16[1,128,512]{2,1,0:T(8,128)(2,1)} %param.15) | copy-start | bytes 393220
  28.6 0.8 %copy-start.3 = (bf16[512,512]{1,0:T(8,128)(2,1)}, bf16[512,512]{1,0:T(8,128)(2,1)S(1)}, u32[]{:S(2)}) copy-start(bf16[512,512]{1,0:T(8,128)(2,1)S(1)} %get-tuple-element.48.refs_4_) | copy-start | bytes 1572868
  31.5 18.0 %copy-start.2 = (bf16[512,512]{1,0:T(8,128)(2,1)S(1)}, bf16[512,512]{1,0:T(8,128)(2,1)}, u32[]{:S(2)}) copy-start(bf16[512,512]{1,0:T(8,128)(2,1)} %refs_5_.1) | copy-start | bytes 1572868
  31.5 18.0 %copy-start.4 = (bf16[512,512]{1,0:T(8,128)(2,1)S(1)}, bf16[512,512]{1,0:T(8,128)(2,1)}, u32[]{:S(2)}) copy-start(bf16[512,512]{1,0:T(8,128)(2,1)} %copy-done.3) | copy-start | bytes 1572868
  47.9 1.6 %collective-permute-start.17 = (bf16[256,512]{1,0:T(8,128)(2,1)S(1)}, bf16[256,512]{1,0:T(8,128)(2,1)S(1)}, u32[]{:S(2)}, u32[]{:S(2)}) collective-permute-start(bf16[256,512]{1,0:T(8,128)(2,1)S(1)} %shard_map.111), channel_id=1, source_target_pairs={{0,1},{1,0},{2,3},{3,2},{4,5},{5,4},{6,7},{7,6},{8,9},{9,8},{10,11... | collective-permute-start | bytes 786440 | tf_op jit(solution)/shard_map/ppermute | solution.py:507
